TPU v7x, 32 devices: a whole 2x2x4 slice. The times are simulated.
32 devices in a mesh: seq: 8 (over z, core), head: 4 (over y, x).
Axes of the slice: x: 2, y: 2, z: 4, core: 2. Of those that a mesh axis runs over, the one named last changes fastest.
Arguments:
- query_in: bfloat16 [4096, 2048], P(('seq', 'head')), may hold values from -4.6 to 4.6
- key_in: bfloat16 [4096, 2048], P(('seq', 'head')), may hold values from -4.6 to 4.6
- value_in: bfloat16 [4096, 2048], P(('seq', 'head')), may hold values from -6 to 6
- grad_out: bfloat16 [4096, 2048], P(('seq', 'head')), may hold values from -6 to 6
- module_lengths: int32 [128], replicated, may hold values from 1 to 64, 4096 in all
Outputs:
- attn_out: bfloat16 [4096, 2048], P(('seq', 'head'))
- grad_query: bfloat16 [4096, 2048], P(('seq', 'head'))
- grad_key: bfloat16 [4096, 2048], P(('seq', 'head'))
- grad_value: bfloat16 [4096, 2048], P(('seq', 'head'))
Inputs may be any that keep to these rules, and one draw needn't show every extreme that they name: `module_lengths`: the lengths sum to 4096; the longest is exactly 64.
All inputs are finite; a program needn't handle non-finite values.
Results may differ from a plain program's by a relative error of at most 0.03.
Values may be sent and summed in bfloat16 or wider, within the bound.
No kernel may reach another device: no remote copies, remote signals or barrier semaphores. Data moves between devices by JAX's collectives and lax.ppermute only.
A program may use at most 64 MiB of HBM per device.

v0:
```python
import math

import jax
import jax.numpy as jnp
from jax import lax
from jax.sharding import PartitionSpec as P

HEAD_DIM = 128


def shifted(value, axis, by):
    peers = lax.axis_size(axis)
    pairs = [(i, i + by) for i in range(peers) if 0 <= i + by < peers]
    return lax.ppermute(value, axis, pairs)


def module_ids(module_lengths, positions):
    module_ends = jnp.cumsum(module_lengths)
    counted = jnp.sum((positions[:, None] >= module_ends[None, :]).astype(jnp.int32), axis=1)
    return jnp.where(positions >= 0, counted, -1)


def allowed_pairs(module_lengths, query_pos, key_pos):
    same = (
        module_ids(module_lengths, query_pos)[:, None]
        == module_ids(module_lengths, key_pos)[None, :]
    )
    return same & (key_pos[None, :] <= query_pos[:, None])


def score_grads(grad_rows, value_block, weights, row_delta, score_scale):
    dprobs = jnp.einsum("qd,kd->qk", grad_rows, value_block, preferred_element_type=jnp.float32)
    return (weights * (dprobs - row_delta[:, None]) * score_scale).astype(jnp.bfloat16)


def key_terms(dscores, weight_bf, query_rows, grad_rows):
    key_grad = jnp.einsum("qk,qd->kd", dscores, query_rows, preferred_element_type=jnp.float32)
    value_grad = jnp.einsum("qk,qd->kd", weight_bf, grad_rows, preferred_element_type=jnp.float32)
    return (key_grad, value_grad)


def one_block(query_rows, key_block, value_block, grad_rows, allowed, score_scale):
    scores = (
        jnp.einsum("qd,kd->qk", query_rows, key_block, preferred_element_type=jnp.float32)
        * score_scale
    )
    row_top = jnp.max(jnp.where(allowed, scores, -jnp.inf), axis=1, keepdims=True)
    row_total = jnp.sum(jnp.where(allowed, jnp.exp(scores - row_top), 0.0), axis=1, keepdims=True)
    log_total = row_top + jnp.log(row_total)
    weights = jnp.where(allowed, jnp.exp(scores - log_total), 0.0)
    weight_bf = weights.astype(jnp.bfloat16)
    attn_rows = jnp.einsum(
        "qk,kd->qd", weight_bf, value_block, preferred_element_type=jnp.float32
    ).astype(jnp.bfloat16)
    row_delta = jnp.sum(grad_rows.astype(jnp.float32) * attn_rows.astype(jnp.float32), axis=1)
    dscores = score_grads(grad_rows, value_block, weights, row_delta, score_scale)
    grad_q = jnp.einsum("qk,kd->qd", dscores, key_block, preferred_element_type=jnp.float32).astype(
        jnp.bfloat16
    )
    key_grad, value_grad = key_terms(dscores, weight_bf, query_rows, grad_rows)
    return (attn_rows, grad_q, key_grad, value_grad, log_total[:, 0], row_delta)


def shards(query_in, key_in, value_in, grad_out, module_lengths):
    head_q, head_k, head_v, head_do = (
        lax.all_to_all(query_in, "head", split_axis=1, concat_axis=0, tiled=True),
        lax.all_to_all(key_in, "head", split_axis=1, concat_axis=0, tiled=True),
        lax.all_to_all(value_in, "head", split_axis=1, concat_axis=0, tiled=True),
        lax.all_to_all(grad_out, "head", split_axis=1, concat_axis=0, tiled=True),
    )
    row_count = head_q.shape[0]
    width = head_q.shape[1]
    local_heads = width // HEAD_DIM
    prior_rows = row_count // 8
    score_scale = HEAD_DIM ** (-0.5)
    tail_start = row_count - prior_rows
    prior_k, prior_v = shifted((head_k[tail_start:], head_v[tail_start:]), "seq", 1)
    row_start = lax.axis_index("seq") * row_count
    query_pos = row_start + jnp.arange(row_count, dtype=jnp.int32)
    before_pos = row_start - prior_rows + jnp.arange(prior_rows, dtype=jnp.int32)
    key_pos = jnp.concatenate([before_pos, query_pos])
    block_rows = math.gcd(row_count, 512)
    block_count = row_count // block_rows
    pos_blocks = query_pos.reshape(block_count, block_rows)

    def by_head(flat, rows):
        return jnp.moveaxis(flat.reshape(rows, local_heads, HEAD_DIM), 1, 0)

    def to_flat(stacked):
        return jnp.moveaxis(stacked, 0, 1).reshape(stacked.shape[1], width)

    query_h = by_head(head_q, row_count)
    grad_h = by_head(head_do, row_count)
    key_h = by_head(jnp.concatenate([prior_k, head_k], axis=0), row_count + prior_rows)
    value_h = by_head(jnp.concatenate([prior_v, head_v], axis=0), row_count + prior_rows)

    def run_head(packed):
        query_rows, key_block, value_block, grad_rows = packed
        query_blocks = query_rows.reshape(block_count, block_rows, HEAD_DIM)
        grad_blocks = grad_rows.reshape(block_count, block_rows, HEAD_DIM)

        def run_block(inner):
            query_part, grad_part, pos_part = inner
            allowed = allowed_pairs(module_lengths, pos_part, key_pos)
            return one_block(query_part, key_block, value_block, grad_part, allowed, score_scale)

        attn_b, grad_qb, key_b, value_b, lse_b, delta_b = lax.map(
            run_block, (query_blocks, grad_blocks, pos_blocks)
        )
        return (
            attn_b.reshape(row_count, HEAD_DIM),
            grad_qb.reshape(row_count, HEAD_DIM),
            jnp.sum(key_b, axis=0),
            jnp.sum(value_b, axis=0),
            lse_b.reshape(row_count),
            delta_b.reshape(row_count),
        )

    attn_h, grad_qh, key_grad, value_grad, log_total, row_delta = lax.map(
        run_head, (query_h, key_h, value_h, grad_h)
    )
    attn_flat = to_flat(attn_h)
    attn_back = lax.all_to_all(attn_flat, "head", split_axis=0, concat_axis=1, tiled=True)
    grad_q = to_flat(grad_qh)
    later_k, later_v = shifted((key_grad[:, :prior_rows], value_grad[:, :prior_rows]), "seq", -1)
    key_total = key_grad[:, prior_rows:].at[:, tail_start:].add(later_k)
    value_total = value_grad[:, prior_rows:].at[:, tail_start:].add(later_v)
    grad_k = to_flat(key_total.astype(jnp.bfloat16))
    grad_v = to_flat(value_total.astype(jnp.bfloat16))
    back_q, back_k, back_v = (
        lax.all_to_all(grad_q, "head", split_axis=0, concat_axis=1, tiled=True),
        lax.all_to_all(grad_k, "head", split_axis=0, concat_axis=1, tiled=True),
        lax.all_to_all(grad_v, "head", split_axis=0, concat_axis=1, tiled=True),
    )
    return (attn_back, back_q, back_k, back_v)


def solution(mesh):
    placed = (
        P(("seq", "head"), None),
        P(("seq", "head"), None),
        P(("seq", "head"), None),
        P(("seq", "head"), None),
        P(),
    )
    return jax.shard_map(
        shards,
        mesh=mesh,
        in_specs=placed,
        out_specs=(
            P(("seq", "head"), None),
            P(("seq", "head"), None),
            P(("seq", "head"), None),
            P(("seq", "head"), None),
        ),
        check_vma=False,
    )
```

profile of v0, /device:TPU:0, one launch (start us, length us, event | category | flops | bytes accessed | tf_op | source)
XLA Modules:
  0.0 123.5 jit_solution(13078051031294013816)
XLA Ops:
  0.6 1.9 %copy.121 = bf16[16,4,8,512]{3,2,0,1:T(8,128)(2,1)} copy(bf16[16,4,8,512]{3,2,1,0:T(8,128)(2,1)} %bitcast.142) | data formatting | bytes 1048576 | tf_op jit(solution)/shard_map/all_to_all | solution.py:66
  2.6 5.2 %all-to-all-start = ((bf16[128,4,512]{2,0,1:T(8,128)(2,1)}), bf16[128,4,512]{2,0,1:T(8,128)(2,1)S(1)}, u32[]{:S(2)}, u32[]{:S(2)}) async-start(bf16[128,4,512]{2,0,1:T(8,128)(2,1)} %bitcast.83), calls=%async_computation | async-start | bytes 1048576 | tf_op jit(solution)/shard_map/all_to_all | solution.py:66
  7.7 1.0 copy.93
  8.7 7.0 %all-to-all-done = bf16[128,4,512]{2,0,1:T(8,128)(2,1)S(1)} async-done(((bf16[128,4,512]{2,0,1:T(8,128)(2,1)}), bf16[128,4,512]{2,0,1:T(8,128)(2,1)S(1)}, u32[]{:S(2)}, u32[]{:S(2)}) %all-to-all-start) | async-done | bytes 524320 | tf_op jit(solution)/shard_map/all_to_all | solution.py:66
  15.8 3.5 %all-to-all-start.1 = ((bf16[128,4,512]{0,2,1:T(8,128)(2,1)}), bf16[128,4,512]{0,2,1:T(8,128)(2,1)S(1)}, u32[]{:S(2)}, u32[]{:S(2)}) async-start(bf16[128,4,512]{0,2,1:T(8,128)(2,1)} %bitcast.3), calls=%async_computation.1 | async-start | bytes 1048576 | tf_op jit(solution)/shard_map/all_to_all | solution.py:67
  19.3 1.0 copy.96
  20.3 6.1 %all-to-all-done.1 = bf16[128,4,512]{0,2,1:T(8,128)(2,1)S(1)} async-done(((bf16[128,4,512]{0,2,1:T(8,128)(2,1)}), bf16[128,4,512]{0,2,1:T(8,128)(2,1)S(1)}, u32[]{:S(2)}, u32[]{:S(2)}) %all-to-all-start.1) | async-done | bytes 524320 | tf_op jit(solution)/shard_map/all_to_all | solution.py:67
  26.4 3.5 %all-to-all-start.2 = ((bf16[128,4,512]{0,2,1:T(8,128)(2,1)}), bf16[128,4,512]{0,2,1:T(8,128)(2,1)S(1)}, u32[]{:S(2)}, u32[]{:S(2)}) async-start(bf16[128,4,512]{0,2,1:T(8,128)(2,1)} %bitcast.7), calls=%async_computation.2 | async-start | bytes 1048576 | tf_op jit(solution)/shard_map/all_to_all | solution.py:68
  29.9 1.0 copy.99
  30.9 5.5 %all-to-all-done.2 = bf16[128,4,512]{0,2,1:T(8,128)(2,1)S(1)} async-done(((bf16[128,4,512]{0,2,1:T(8,128)(2,1)}), bf16[128,4,512]{0,2,1:T(8,128)(2,1)S(1)}, u32[]{:S(2)}, u32[]{:S(2)}) %all-to-all-start.2) | async-done | bytes 524320 | tf_op jit(solution)/shard_map/all_to_all | solution.py:68
  36.4 3.5 %all-to-all-start.3 = ((bf16[128,4,512]{0,2,1:T(8,128)(2,1)}), bf16[128,4,512]{0,2,1:T(8,128)(2,1)S(1)}, u32[]{:S(2)}, u32[]{:S(2)}) async-start(bf16[128,4,512]{0,2,1:T(8,128)(2,1)} %bitcast.11), calls=%async_computation.3 | async-start | bytes 1048576 | tf_op jit(solution)/shard_map/all_to_all | solution.py:69
  40.5 1.3 %collective-permute-start = (bf16[64,512]{1,0:T(8,128)(2,1)S(1)}, bf16[64,512]{1,0:T(8,128)(2,1)S(1)}, u32[]{:S(2)}, u32[]{:S(2)}) collective-permute-start(bf16[64,512]{1,0:T(8,128)(2,1)S(1)} %slice.76), channel_id=1, source_target_pairs={{0,4},{4,8},{8,12},{12,16},{16,20},{20,24},{24,28},{1,5},{5,9},{9,... | collective-permute-start | bytes 196616 | tf_op jit(solution)/shard_map/ppermute | solution.py:14
  42.6 4.2 %collective-permute-start.1 = (bf16[64,512]{1,0:T(8,128)(2,1)S(1)}, bf16[64,512]{1,0:T(8,128)(2,1)S(1)}, u32[]{:S(2)}, u32[]{:S(2)}) collective-permute-start(bf16[64,512]{1,0:T(8,128)(2,1)S(1)} %slice.77), channel_id=1, source_target_pairs={{0,4},{4,8},{8,12},{12,16},{16,20},{20,24},{24,28},{1,5},{5,9},{9,... | collective-permute-start | bytes 196616 | tf_op jit(solution)/shard_map/ppermute | solution.py:14
  48.5 1.2 copy-done
  49.7 22.1 %while.28 = (s32[]{:T(128)}, bf16[4,512,128]{1,2,0:T(8,128)(2,1)}, bf16[4,512,128]{2,1,0:T(8,128)(2,1)}, f32[4,576,128]{2,1,0:T(8,128)}, f32[4,576,128]{2,1,0:T(...) while((s32[]{:T(128)}, bf16[4,512,128]{1,2,0:T(8,128)(2,1)}, ...), condition=%wide.region_7.8_spmd.clone, body=%wide.region_1.7_spmd.clone.sunk | while | flops 463528512 | bytes 10138509 | solution.py:119
  51.0 1.2 bitcast_dynamic-update-slice_fusion.2
  53.2 1.0 fusion.57
  54.2 1.0 fusion.58
  56.6 1.2 bitcast_dynamic-update-slice_fusion.2
  58.7 1.0 fusion.57
  59.8 1.0 fusion.58
  62.1 1.2 bitcast_dynamic-update-slice_fusion.2
  64.3 1.0 fusion.57
  65.3 1.0 fusion.58
  67.6 1.2 bitcast_dynamic-update-slice_fusion.2
  69.8 1.0 fusion.57
  70.8 1.0 fusion.58
  71.8 1.4 %copy.108 = bf16[512,4,128]{2,1,0:T(4,128)(2,1)S(1)} copy(bf16[512,4,128]{2,0,1:T(8,128)(2,1)} %bitcast.143) | data formatting | bytes 1048576 | tf_op jit(solution)/shard_map/transpose | solution.py:90
  73.3 1.0 all_to_all.126
  74.3 4.1 %all-to-all-start.5 = ((bf16[4,128,512]{2,1,0:T(8,128)(2,1)}), bf16[4,128,512]{2,1,0:T(8,128)(2,1)S(1)}, u32[]{:S(2)}, u32[]{:S(2)}) async-start(bf16[4,128,512]{2,1,0:T(8,128)(2,1)} %all_to_all.126), calls=%async_computation.5 | async-start | bytes 1048576 | tf_op jit(solution)/shard_map/all_to_all | solution.py:131
  78.5 1.1 copy.118
  79.7 7.0 %all-to-all-done.5 = bf16[4,128,512]{2,1,0:T(8,128)(2,1)S(1)} async-done(((bf16[4,128,512]{2,1,0:T(8,128)(2,1)}), bf16[4,128,512]{2,1,0:T(8,128)(2,1)S(1)}, u32[]{:S(2)}, u32[]{:S(2)}) %all-to-all-start.5) | async-done | bytes 524320 | tf_op jit(solution)/shard_map/all_to_all | solution.py:131
  86.7 3.5 %all-to-all-start.4 = ((bf16[4,128,512]{2,1,0:T(8,128)(2,1)}), bf16[4,128,512]{2,1,0:T(8,128)(2,1)S(1)}, u32[]{:S(2)}, u32[]{:S(2)}) async-start(bf16[4,128,512]{2,1,0:T(8,128)(2,1)} %copy.118), calls=%async_computation.4 | async-start | bytes 1048576 | tf_op jit(solution)/shard_map/all_to_all | solution.py:123
  90.2 1.3 %collective-permute-start.3 = (f32[4,64,128]{2,1,0:T(8,128)S(1)}, f32[4,64,128]{2,1,0:T(8,128)S(1)}, u32[]{:S(2)}, u32[]{:S(2)}) collective-permute-start(f32[4,64,128]{2,1,0:T(8,128)S(1)} %slice.75), channel_id=1, source_target_pairs={{4,0},{8,4},{12,8},{16,12},{20,16},{24,20},{28,24},{5,1},{9,5},{13... | collective-permute-start | bytes 393224 | tf_op jit(solution)/shard_map/ppermute | solution.py:14
  91.6 1.9 %collective-permute-done.3 = f32[4,64,128]{2,1,0:T(8,128)S(1)} collective-permute-done((f32[4,64,128]{2,1,0:T(8,128)S(1)}, f32[4,64,128]{2,1,0:T(8,128)S(1)}, u32[]{:S(2)}, u32[]{:S(2)}) %collective-permute-start.3) | collective-permute-done | bytes 131104 | tf_op jit(solution)/shard_map/ppermute | solution.py:14
  93.9 1.0 all_to_all.134
  94.9 2.7 %all-to-all-done.4 = bf16[4,128,512]{2,1,0:T(8,128)(2,1)S(1)} async-done(((bf16[4,128,512]{2,1,0:T(8,128)(2,1)}), bf16[4,128,512]{2,1,0:T(8,128)(2,1)S(1)}, u32[]{:S(2)}, u32[]{:S(2)}) %all-to-all-start.4) | async-done | bytes 524320 | tf_op jit(solution)/shard_map/all_to_all | solution.py:123
  97.6 3.5 %all-to-all-start.7 = ((bf16[4,128,512]{2,1,0:T(8,128)(2,1)}), bf16[4,128,512]{2,1,0:T(8,128)(2,1)S(1)}, u32[]{:S(2)}, u32[]{:S(2)}) async-start(bf16[4,128,512]{2,1,0:T(8,128)(2,1)} %all_to_all.134), calls=%async_computation.7 | async-start | bytes 1048576 | tf_op jit(solution)/shard_map/all_to_all | solution.py:133
  101.1 1.3 %collective-permute-start.2 = (f32[4,64,128]{2,1,0:T(8,128)S(1)}, f32[4,64,128]{2,1,0:T(8,128)S(1)}, u32[]{:S(2)}, u32[]{:S(2)}) collective-permute-start(f32[4,64,128]{2,1,0:T(8,128)S(1)} %slice.72), channel_id=1, source_target_pairs={{4,0},{8,4},{12,8},{16,12},{20,16},{24,20},{28,24},{5,1},{9,5},{13... | collective-permute-start | bytes 393224 | tf_op jit(solution)/shard_map/ppermute | solution.py:14
  102.5 2.0 %collective-permute-done.2 = f32[4,64,128]{2,1,0:T(8,128)S(1)} collective-permute-done((f32[4,64,128]{2,1,0:T(8,128)S(1)}, f32[4,64,128]{2,1,0:T(8,128)S(1)}, u32[]{:S(2)}, u32[]{:S(2)}) %collective-permute-start.2) | collective-permute-done | bytes 131104 | tf_op jit(solution)/shard_map/ppermute | solution.py:14
  105.0 1.0 all_to_all.130
  106.0 4.4 %all-to-all-done.7 = bf16[4,128,512]{2,1,0:T(8,128)(2,1)S(1)} async-done(((bf16[4,128,512]{2,1,0:T(8,128)(2,1)}), bf16[4,128,512]{2,1,0:T(8,128)(2,1)S(1)}, u32[]{:S(2)}, u32[]{:S(2)}) %all-to-all-start.7) | async-done | bytes 524320 | tf_op jit(solution)/shard_map/all_to_all | solution.py:133
  110.3 3.5 %all-to-all-start.6 = ((bf16[4,128,512]{2,1,0:T(8,128)(2,1)}), bf16[4,128,512]{2,1,0:T(8,128)(2,1)S(1)}, u32[]{:S(2)}, u32[]{:S(2)}) async-start(bf16[4,128,512]{2,1,0:T(8,128)(2,1)} %all_to_all.130), calls=%async_computation.6 | async-start | bytes 1048576 | tf_op jit(solution)/shard_map/all_to_all | solution.py:132
  114.1 1.0 copy.115
  115.4 1.0 copy.114
  116.7 1.0 copy.117
  117.7 4.5 %all-to-all-done.6 = bf16[4,128,512]{2,1,0:T(8,128)(2,1)S(1)} async-done(((bf16[4,128,512]{2,1,0:T(8,128)(2,1)}), bf16[4,128,512]{2,1,0:T(8,128)(2,1)S(1)}, u32[]{:S(2)}, u32[]{:S(2)}) %all-to-all-start.6) | async-done | bytes 524320 | tf_op jit(solution)/shard_map/all_to_all | solution.py:132
  122.5 1.0 copy.116
  (98 shorter events, 14.3 us)
Async XLA Ops:
  0.6 7.1 %copy-start.2 = (bf16[128,2048]{1,0:T(8,128)(2,1)S(1)}, bf16[128,2048]{1,0:T(8,128)(2,1)}, u32[]{:S(2)}) copy-start(bf16[128,2048]{1,0:T(8,128)(2,1)} %param.12) | copy-start | bytes 1572868
  2.6 13.2 %all-to-all-start = ((bf16[128,4,512]{2,0,1:T(8,128)(2,1)}), bf16[128,4,512]{2,0,1:T(8,128)(2,1)S(1)}, u32[]{:S(2)}, u32[]{:S(2)}) async-start(bf16[128,4,512]{2,0,1:T(8,128)(2,1)} %bitcast.83), calls=%async_computation | async-start | bytes 1048576 | tf_op jit(solution)/shard_map/all_to_all | solution.py:66
  7.7 11.5 %copy-start.3 = (bf16[128,2048]{1,0:T(8,128)(2,1)S(1)}, bf16[128,2048]{1,0:T(8,128)(2,1)}, u32[]{:S(2)}) copy-start(bf16[128,2048]{1,0:T(8,128)(2,1)} %param.13) | copy-start | bytes 1572868
  15.8 10.6 %all-to-all-start.1 = ((bf16[128,4,512]{0,2,1:T(8,128)(2,1)}), bf16[128,4,512]{0,2,1:T(8,128)(2,1)S(1)}, u32[]{:S(2)}, u32[]{:S(2)}) async-start(bf16[128,4,512]{0,2,1:T(8,128)(2,1)} %bitcast.3), calls=%async_computation.1 | async-start | bytes 1048576 | tf_op jit(solution)/shard_map/all_to_all | solution.py:67
  19.2 10.6 %copy-start.4 = (bf16[128,2048]{1,0:T(8,128)(2,1)S(1)}, bf16[128,2048]{1,0:T(8,128)(2,1)}, u32[]{:S(2)}) copy-start(bf16[128,2048]{1,0:T(8,128)(2,1)} %param.14) | copy-start | bytes 1572868
  26.4 10.0 %all-to-all-start.2 = ((bf16[128,4,512]{0,2,1:T(8,128)(2,1)}), bf16[128,4,512]{0,2,1:T(8,128)(2,1)S(1)}, u32[]{:S(2)}, u32[]{:S(2)}) async-start(bf16[128,4,512]{0,2,1:T(8,128)(2,1)} %bitcast.7), calls=%async_computation.2 | async-start | bytes 1048576 | tf_op jit(solution)/shard_map/all_to_all | solution.py:68
  29.8 10.1 %copy-start.6 = (s32[128]{0:T(128)S(1)}, s32[128]{0:T(128)}, u32[]{:S(2)}) copy-start(s32[128]{0:T(128)} %param.15) | copy-start | bytes 1540
  36.4 10.4 %all-to-all-start.3 = ((bf16[128,4,512]{0,2,1:T(8,128)(2,1)}), bf16[128,4,512]{0,2,1:T(8,128)(2,1)S(1)}, u32[]{:S(2)}, u32[]{:S(2)}) async-start(bf16[128,4,512]{0,2,1:T(8,128)(2,1)} %bitcast.11), calls=%async_computation.3 | async-start | bytes 1048576 | tf_op jit(solution)/shard_map/all_to_all | solution.py:69
  40.5 7.0 %collective-permute-start = (bf16[64,512]{1,0:T(8,128)(2,1)S(1)}, bf16[64,512]{1,0:T(8,128)(2,1)S(1)}, u32[]{:S(2)}, u32[]{:S(2)}) collective-permute-start(bf16[64,512]{1,0:T(8,128)(2,1)S(1)} %slice.76), channel_id=1, source_target_pairs={{0,4},{4,8},{8,12},{12,16},{16,20},{20,24},{24,28},{1,5},{5,9},{9,... | collective-permute-start | bytes 196616 | tf_op jit(solution)/shard_map/ppermute | solution.py:14
  42.6 5.4 %collective-permute-start.1 = (bf16[64,512]{1,0:T(8,128)(2,1)S(1)}, bf16[64,512]{1,0:T(8,128)(2,1)S(1)}, u32[]{:S(2)}, u32[]{:S(2)}) collective-permute-start(bf16[64,512]{1,0:T(8,128)(2,1)S(1)} %slice.77), channel_id=1, source_target_pairs={{0,4},{4,8},{8,12},{12,16},{16,20},{20,24},{24,28},{1,5},{5,9},{9,... | collective-permute-start | bytes 196616 | tf_op jit(solution)/shard_map/ppermute | solution.py:14
  48.4 1.3 %copy-start = (f32[4,576,128]{2,1,0:T(8,128)S(1)}, f32[4,576,128]{2,1,0:T(8,128)}, u32[]{:S(2)}) copy-start(f32[4,576,128]{2,1,0:T(8,128)} %custom-call.3) | copy-start | bytes 3538948
  73.3 5.1 %copy-start.5 = (bf16[4,512,128]{1,2,0:T(8,128)(2,1)S(1)}, bf16[4,512,128]{1,2,0:T(8,128)(2,1)}, u32[]{:S(2)}) copy-start(bf16[4,512,128]{1,2,0:T(8,128)(2,1)} %get-tuple-element.205) | copy-start | bytes 1572868
  74.3 12.4 %all-to-all-start.5 = ((bf16[4,128,512]{2,1,0:T(8,128)(2,1)}), bf16[4,128,512]{2,1,0:T(8,128)(2,1)S(1)}, u32[]{:S(2)}, u32[]{:S(2)}) async-start(bf16[4,128,512]{2,1,0:T(8,128)(2,1)} %all_to_all.126), calls=%async_computation.5 | async-start | bytes 1048576 | tf_op jit(solution)/shard_map/all_to_all | solution.py:131
  86.7 10.9 %all-to-all-start.4 = ((bf16[4,128,512]{2,1,0:T(8,128)(2,1)}), bf16[4,128,512]{2,1,0:T(8,128)(2,1)S(1)}, u32[]{:S(2)}, u32[]{:S(2)}) async-start(bf16[4,128,512]{2,1,0:T(8,128)(2,1)} %copy.118), calls=%async_computation.4 | async-start | bytes 1048576 | tf_op jit(solution)/shard_map/all_to_all | solution.py:123
  90.2 3.2 %collective-permute-start.3 = (f32[4,64,128]{2,1,0:T(8,128)S(1)}, f32[4,64,128]{2,1,0:T(8,128)S(1)}, u32[]{:S(2)}, u32[]{:S(2)}) collective-permute-start(f32[4,64,128]{2,1,0:T(8,128)S(1)} %slice.75), channel_id=1, source_target_pairs={{4,0},{8,4},{12,8},{16,12},{20,16},{24,20},{28,24},{5,1},{9,5},{13... | collective-permute-start | bytes 393224 | tf_op jit(solution)/shard_map/ppermute | solution.py:14
  93.9 7.2 %copy-start.1 = (f32[4,576,128]{2,1,0:T(8,128)S(1)}, f32[4,576,128]{2,1,0:T(8,128)}, u32[]{:S(2)}) copy-start(f32[4,576,128]{2,1,0:T(8,128)} %get-tuple-element.207) | copy-start | bytes 3538948
  97.6 12.7 %all-to-all-start.7 = ((bf16[4,128,512]{2,1,0:T(8,128)(2,1)}), bf16[4,128,512]{2,1,0:T(8,128)(2,1)S(1)}, u32[]{:S(2)}, u32[]{:S(2)}) async-start(bf16[4,128,512]{2,1,0:T(8,128)(2,1)} %all_to_all.134), calls=%async_computation.7 | async-start | bytes 1048576 | tf_op jit(solution)/shard_map/all_to_all | solution.py:133
  101.1 3.4 %collective-permute-start.2 = (f32[4,64,128]{2,1,0:T(8,128)S(1)}, f32[4,64,128]{2,1,0:T(8,128)S(1)}, u32[]{:S(2)}, u32[]{:S(2)}) collective-permute-start(f32[4,64,128]{2,1,0:T(8,128)S(1)} %slice.72), channel_id=1, source_target_pairs={{4,0},{8,4},{12,8},{16,12},{20,16},{24,20},{28,24},{5,1},{9,5},{13... | collective-permute-start | bytes 393224 | tf_op jit(solution)/shard_map/ppermute | solution.py:14
  110.3 11.9 %all-to-all-start.6 = ((bf16[4,128,512]{2,1,0:T(8,128)(2,1)}), bf16[4,128,512]{2,1,0:T(8,128)(2,1)S(1)}, u32[]{:S(2)}, u32[]{:S(2)}) async-start(bf16[4,128,512]{2,1,0:T(8,128)(2,1)} %all_to_all.130), calls=%async_computation.6 | async-start | bytes 1048576 | tf_op jit(solution)/shard_map/all_to_all | solution.py:132
where the time goes:
time: 124 us; the launch traced here: 123 us
  waiting for transfers between devices  41.2 us (33%)
  starting transfers between devices  38.2 us (31%)
  local copies, waits for them, and re-layouts  19.7 us (16%)
  matrix products  18.3 us (15%)
  other arithmetic  4.94 us (4%)
    unnamed x25, local copies, waits for them, and re-layouts  8.82 us
    ppermute x4, starting transfers between devices, shifted(): return lax.ppermute(value, axis, pairs)  8.1 us
    all_to_all x1, waiting for transfers between devices, shards(): lax.all_to_all(grad_q, 'head', split_axis=0, concat_axis=1, tiled=True)  7.04 us
    all_to_all x1, waiting for transfers between devices, shards(): lax.all_to_all(query_in, 'head', split_axis=1, concat_axis=0, tiled=True)  7.01 us
    all_to_all x1, waiting for transfers between devices, shards(): lax.all_to_all(key_in, 'head', split_axis=1, concat_axis=0, tiled=True)  6.09 us
    all_to_all x1, waiting for transfers between devices, shards(): lax.all_to_all(value_in, 'head', split_axis=1, concat_axis=0, tiled=True)  5.52 us
    all_to_all x1, starting transfers between devices, shards(): lax.all_to_all(query_in, 'head', split_axis=1, concat_axis=0, tiled=True)  5.16 us
    dot_general x4, matrix products, one_block(): jnp.einsum('qk,kd->qd', weight_bf, value_block, preferred_element_type=jn...  4.63 us
  transfers between devices with their start and end apart: 12, of which 9 were waited for; matrix products, arithmetic and copies ran while one was open for 9% of the time, Pallas kernels for 0%

commit v1 on v0

--- a/solution.py
+++ b/solution.py
@@ -1,11 +1,17 @@
+import functools
 import math
 
 import jax
 import jax.numpy as jnp
 from jax import lax
+from jax.experimental import pallas as pl
+from jax.experimental.pallas import tpu as pltpu
 from jax.sharding import PartitionSpec as P
 
 HEAD_DIM = 128
+SCALE = HEAD_DIM ** (-0.5)
+LOG2E = math.log2(math.e)
+MASKED = -1e30
 
 
 def shifted(value, axis, by):
@@ -61,7 +67,7 @@
     return (attn_rows, grad_q, key_grad, value_grad, log_total[:, 0], row_delta)
 
 
-def shards(query_in, key_in, value_in, grad_out, module_lengths):
+def gathered_shards(query_in, key_in, value_in, grad_out, module_lengths):
     head_q, head_k, head_v, head_do = (
         lax.all_to_all(query_in, "head", split_axis=1, concat_axis=0, tiled=True),
         lax.all_to_all(key_in, "head", split_axis=1, concat_axis=0, tiled=True),
@@ -135,6 +141,243 @@
     return (attn_back, back_q, back_k, back_v)
 
 
+def dot(left, right, left_dim, right_dim):
+    return lax.dot_general(
+        left, right, (((left_dim,), (right_dim,)), ((), ())), preferred_element_type=jnp.float32
+    )
+
+
+def module_ends_row(lengths_row):
+    count = lengths_row.shape[1]
+    row = lax.broadcasted_iota(jnp.int32, (count, count), 0)
+    col = lax.broadcasted_iota(jnp.int32, (count, count), 1)
+    lengths_col = jnp.sum(jnp.where(row == col, lengths_row, 0.0), axis=1, keepdims=True)
+    return jnp.sum(jnp.where(row <= col, lengths_col, 0.0), axis=0, keepdims=True)
+
+
+def module_ends_col(lengths_row):
+    count = lengths_row.shape[1]
+    row = lax.broadcasted_iota(jnp.int32, (count, count), 0)
+    col = lax.broadcasted_iota(jnp.int32, (count, count), 1)
+    return jnp.sum(jnp.where(col <= row, lengths_row, 0.0), axis=1, keepdims=True)
+
+
+def bias_by_query(lengths_row, first_query, queries, first_key, keys):
+    ends = module_ends_row(lengths_row)
+    query = (first_query + lax.broadcasted_iota(jnp.int32, (queries, 1), 0)).astype(jnp.float32)
+    start = jnp.max(jnp.where(ends <= query, ends, 0.0), axis=1, keepdims=True)
+    key = (first_key + lax.broadcasted_iota(jnp.int32, (queries, keys), 1)).astype(jnp.float32)
+    return jnp.where((key >= start) & (key <= query), 0.0, MASKED)
+
+
+def bias_by_key(lengths_row, first_query, queries, first_key, keys):
+    ends = module_ends_col(lengths_row)
+    query = (first_query + lax.broadcasted_iota(jnp.int32, (1, queries), 1)).astype(jnp.float32)
+    start = jnp.max(jnp.where(ends <= query, ends, 0.0), axis=0, keepdims=True)
+    key = (first_key + lax.broadcasted_iota(jnp.int32, (keys, queries), 0)).astype(jnp.float32)
+    return jnp.where((key >= start) & (key <= query), 0.0, MASKED)
+
+
+def attend(q, do, k, v, bias):
+    scores = dot(q, k, 1, 1) * (SCALE * LOG2E) + bias
+    dprobs = dot(do, v, 1, 1)
+    top = jnp.max(scores, axis=1, keepdims=True)
+    raw = jnp.exp2(scores - top)
+    weights = raw * (1.0 / jnp.sum(raw, axis=1, keepdims=True))
+    delta = jnp.sum(weights * dprobs, axis=1, keepdims=True)
+    dscores = weights * (dprobs - delta) * SCALE
+    return weights.astype(jnp.bfloat16), dscores.astype(jnp.bfloat16)
+
+
+def device_first(tok):
+    place = lax.axis_index("seq") * lax.axis_size("head") + lax.axis_index("head")
+    return place * tok
+
+
+def own_kernel(
+    prior, len_ref, q_ref, k_ref, v_ref, do_ref,
+    attn_ref, gq_ref, gk_ref, gv_ref, stat_ref, bias_ref, lead_ref,
+):
+    tok, width = q_ref.shape
+    rest = tok - prior
+    heads = width // HEAD_DIM
+
+    @pl.when(pl.program_id(0) == 0)
+    def _():
+        first = device_first(tok)
+        lengths = len_ref[...].astype(jnp.float32)
+        bias_ref[...] = bias_by_query(lengths, first + prior, rest, first, tok)
+        lead_ref[...] = bias_by_key(lengths, first, prior, first, prior)
+
+    bias, lead = bias_ref[...], lead_ref[...]
+    for h in range(heads):
+        cols = slice(h * HEAD_DIM, (h + 1) * HEAD_DIM)
+        q, k, v, do = q_ref[:, cols], k_ref[:, cols], v_ref[:, cols], do_ref[:, cols]
+        q_late, do_late = q[prior:], do[prior:]
+        weights, dscores = attend(q_late, do_late, k, v, bias)
+        attn_ref[:, cols] = dot(weights, v, 1, 0).astype(jnp.bfloat16)
+        gq_ref[:, cols] = dot(dscores, k, 1, 0).astype(jnp.bfloat16)
+        gk_ref[:, cols] = dot(dscores, q_late, 0, 0)
+        gv_ref[:, cols] = dot(weights, do_late, 0, 0)
+        scores = dot(k[:prior], q[:prior], 1, 1) * (SCALE * LOG2E) + lead
+        dprobs = dot(v[:prior], do[:prior], 1, 1)
+        top = jnp.max(scores, axis=0, keepdims=True)
+        raw = jnp.exp2(scores - top)
+        total = jnp.sum(raw, axis=0, keepdims=True)
+        stat_ref[0, h : h + 1, :] = top + jnp.log2(total)
+        stat_ref[0, heads + h : heads + h + 1, :] = (
+            jnp.sum(raw * dprobs, axis=0, keepdims=True) / total
+        )
+
+
+def lead_kernel(
+    prior, len_ref, q_ref, k_ref, v_ref, do_ref, before_ref, gk_part_ref, gv_part_ref,
+    attn_in, gq_in, attn_ref, gq_ref, gk_ref, gv_ref, bias_ref,
+):
+    width = q_ref.shape[1]
+
+    @pl.when(pl.program_id(0) == 0)
+    def _():
+        first = device_first(attn_in.shape[0])
+        lengths = len_ref[...].astype(jnp.float32)
+        bias_ref[...] = bias_by_query(lengths, first, prior, first - prior, 2 * prior)
+
+    bias = bias_ref[...]
+    for h in range(width // HEAD_DIM):
+        cols = slice(h * HEAD_DIM, (h + 1) * HEAD_DIM)
+        q, do = q_ref[:, cols], do_ref[:, cols]
+        k = jnp.concatenate([before_ref[:prior, cols], k_ref[:, cols]], axis=0)
+        v = jnp.concatenate([before_ref[prior:, cols], v_ref[:, cols]], axis=0)
+        weights, dscores = attend(q, do, k, v, bias)
+        attn_ref[:, cols] = dot(weights, v, 1, 0).astype(jnp.bfloat16)
+        gq_ref[:, cols] = dot(dscores, k, 1, 0).astype(jnp.bfloat16)
+        gk = gk_part_ref[:, cols] + dot(dscores[:, prior:], q, 0, 0)
+        gv = gv_part_ref[:, cols] + dot(weights[:, prior:], do, 0, 0)
+        gk_ref[:, cols] = gk.astype(jnp.bfloat16)
+        gv_ref[:, cols] = gv.astype(jnp.bfloat16)
+
+
+def tail_kernel(
+    prior, len_ref, k_ref, v_ref, after_ref, stat_ref, gk_part_ref, gv_part_ref,
+    gk_in, gv_in, gk_ref, gv_ref, bias_ref,
+):
+    width = k_ref.shape[1]
+    heads = width // HEAD_DIM
+
+    @pl.when(pl.program_id(0) == 0)
+    def _():
+        tok = gk_in.shape[0]
+        first = device_first(tok)
+        lengths = len_ref[...].astype(jnp.float32)
+        bias_ref[...] = bias_by_key(lengths, first + tok, prior, first + tok - prior, prior)
+
+    bias = bias_ref[...]
+    for h in range(heads):
+        cols = slice(h * HEAD_DIM, (h + 1) * HEAD_DIM)
+        q, do = after_ref[:prior, cols], after_ref[prior:, cols]
+        own_log = stat_ref[0, h : h + 1, :]
+        own_delta = stat_ref[0, heads + h : heads + h + 1, :]
+        scores = dot(k_ref[:, cols], q, 1, 1) * (SCALE * LOG2E) + bias
+        dprobs = dot(v_ref[:, cols], do, 1, 1)
+        top = jnp.maximum(jnp.max(scores, axis=0, keepdims=True), own_log)
+        raw = jnp.exp2(scores - top)
+        own_raw = jnp.exp2(own_log - top)
+        part = 1.0 / (jnp.sum(raw, axis=0, keepdims=True) + own_raw)
+        weights = raw * part
+        delta = jnp.sum(weights * dprobs, axis=0, keepdims=True) + own_raw * part * own_delta
+        dscores = weights * (dprobs - delta) * SCALE
+        gk = gk_part_ref[:, cols] + dot(dscores.astype(jnp.bfloat16), q, 1, 0)
+        gv = gv_part_ref[:, cols] + dot(weights.astype(jnp.bfloat16), do, 1, 0)
+        gk_ref[:, cols] = gk.astype(jnp.bfloat16)
+        gv_ref[:, cols] = gv.astype(jnp.bfloat16)
+
+
+def neighbour(value, by):
+    peers = lax.axis_size("seq") * lax.axis_size("head")
+    pairs = [(i, i + by) for i in range(peers) if 0 <= i + by < peers]
+    return lax.ppermute(value, ("seq", "head"), pairs)
+
+
+def cost(heads, queries, keys, products, moved):
+    return pl.CostEstimate(
+        flops=2 * heads * queries * keys * HEAD_DIM * products,
+        bytes_accessed=moved,
+        transcendentals=heads * queries * keys,
+    )
+
+
+def halo_shards(query_in, key_in, value_in, grad_out, module_lengths):
+    tok, width = query_in.shape
+    prior = tok * lax.axis_size("head") // 8
+    heads = width // HEAD_DIM
+    step = 512
+    groups = width // step
+    per = step // HEAD_DIM
+    lengths = module_lengths.reshape(1, -1)
+    len_spec = pl.BlockSpec(lengths.shape, lambda g: (0, 0))
+    whole = pl.BlockSpec((tok, step), lambda g: (0, g))
+    early = pl.BlockSpec((prior, step), lambda g: (0, g))
+    late = pl.BlockSpec((prior, step), lambda g: (tok // prior - 1, g))
+    pair = pl.BlockSpec((2 * prior, step), lambda g: (0, g))
+    stat_spec = pl.BlockSpec((1, 2 * per, prior), lambda g: (g, 0, 0))
+    keep = pl.BlockSpec(memory_space=pl.ANY)
+    full16 = jax.ShapeDtypeStruct((tok, width), jnp.bfloat16)
+    full32 = jax.ShapeDtypeStruct((tok, width), jnp.float32)
+
+    before = neighbour(jnp.concatenate([key_in[tok - prior :], value_in[tok - prior :]]), 1)
+    after = neighbour(jnp.concatenate([query_in[:prior], grad_out[:prior]]), -1)
+
+    attn, gq, gk_part, gv_part, stat = pl.pallas_call(
+        functools.partial(own_kernel, prior),
+        grid=(groups,),
+        in_specs=[len_spec, whole, whole, whole, whole],
+        out_specs=[late, late, whole, whole, stat_spec],
+        out_shape=[
+            full16, full16, full32, full32,
+            jax.ShapeDtypeStruct((groups, 2 * per, prior), jnp.float32),
+        ],
+        scratch_shapes=[
+            pltpu.VMEM((tok - prior, tok), jnp.float32),
+            pltpu.VMEM((prior, prior), jnp.float32),
+        ],
+        cost_estimate=cost(heads, tok, tok, 4, 24 * tok * width),
+        name="own_block",
+    )(lengths, query_in, key_in, value_in, grad_out)
+    stat_after = neighbour(stat, -1)
+
+    attn, gq, gk, gv = pl.pallas_call(
+        functools.partial(lead_kernel, prior),
+        grid=(groups,),
+        in_specs=[len_spec, early, early, early, early, pair, early, early, keep, keep],
+        out_specs=[early, early, early, early],
+        out_shape=[full16, full16, full16, full16],
+        scratch_shapes=[pltpu.VMEM((prior, 2 * prior), jnp.float32)],
+        input_output_aliases={8: 0, 9: 1},
+        cost_estimate=cost(heads, prior, 2 * prior, 5, 14 * tok * width),
+        name="lead_rows",
+    )(lengths, query_in, key_in, value_in, grad_out, before, gk_part, gv_part, attn, gq)
+
+    gk, gv = pl.pallas_call(
+        functools.partial(tail_kernel, prior),
+        grid=(groups,),
+        in_specs=[len_spec, late, late, pair, stat_spec, late, late, keep, keep],
+        out_specs=[late, late],
+        out_shape=[full16, full16],
+        scratch_shapes=[pltpu.VMEM((prior, prior), jnp.float32)],
+        input_output_aliases={7: 0, 8: 1},
+        cost_estimate=cost(heads, prior, prior, 4, 10 * tok * width),
+        name="tail_keys",
+    )(lengths, key_in, value_in, after, stat_after, gk_part, gv_part, gk, gv)
+    return (attn, gq, gk, gv)
+
+
+def shards(query_in, key_in, value_in, grad_out, module_lengths):
+    tok = query_in.shape[0]
+    prior = tok * lax.axis_size("head") // 8
+    plan = halo_shards if 2 * prior <= tok else gathered_shards
+    return plan(query_in, key_in, value_in, grad_out, module_lengths)
+
+
 def solution(mesh):
     placed = (
         P(("seq", "head"), None),

time: 124 us -> 43.4 us (0.35)
  waiting for transfers between devices: 41.2 us -> 3.87 us
  starting transfers between devices: 38.2 us -> 7.46 us
  Pallas kernels: 0 us -> 27.3 us
  matrix products: 18.3 us -> 0 us
  local copies, waits for them, and re-layouts: 19.7 us -> 3.67 us
  other arithmetic: 4.94 us -> 0.08 us
    all_to_all x8 -> x0, waiting for transfers between devices: 37.3 us -> none  [the longest x1 7.04 us: shards(): lax.all_to_all(grad_q, 'head', split_axis=0, concat_axis=1, tiled=True)]
    all_to_all x8 -> x0, starting transfers between devices: 30.1 us -> none  [the longest x1 5.16 us: shards(): lax.all_to_all(query_in, 'head', split_axis=1, concat_axis=0, tiled=True)]
    pallas_call x0 -> x3, Pallas kernels: none -> 27.3 us  [the longest x1 11.1 us: halo_shards(): pl.pallas_call(functools.partial(lead_kernel, prior), grid=(groups,), in_...]
    dot_general x24 -> x0, matrix products: 18.3 us -> none  [the longest x4 4.63 us: one_block(): jnp.einsum('qk,kd->qd', weight_bf, value_block, preferred_element_type=jn...]
    all_to_all x13 -> x0, local copies, waits for them, and re-layouts: 7.9 us -> none  [the longest x1 1.94 us: shards(): lax.all_to_all(query_in, 'head', split_axis=1, concat_axis=0, tiled=True)]
    unnamed x25 -> x6, local copies, waits for them, and re-layouts: 8.82 us -> 1.63 us
    reduce_sum x16 -> x0, other arithmetic: 3.62 us -> none  [the longest x8 1.98 us: module_ids(): jnp.sum((positions[:, None] >= module_ends[None, :]).astype(jnp.int32), a...]
    transpose x3 -> x0, local copies, waits for them, and re-layouts: 2.26 us -> none  [to_flat(): return jnp.moveaxis(stacked, 0, 1).reshape(stacked.shape[1], width)]
  transfers between devices with their start and end apart: 12 -> 3, of which waited for: 9 -> 1; matrix products, arithmetic and copies ran while one was open for 9% -> 0% of each run, Pallas kernels for 0% -> 50%
where the time goes in v1:
time: 43.4 us; the launch traced here: 43.1 us
  Pallas kernels  27.3 us (63%)
  starting transfers between devices  7.46 us (17%)
  waiting for transfers between devices  3.87 us (9%)
  local copies, waits for them, and re-layouts  3.67 us (8%)
  between operations  0.74 us (2%)
    pallas_call x1, Pallas kernels, halo_shards(): pl.pallas_call(functools.partial(lead_kernel, prior), grid=(groups,), in_...  11.1 us
    pallas_call x1, Pallas kernels, halo_shards(): pl.pallas_call(functools.partial(own_kernel, prior), grid=(groups,), in_s...  10.3 us
    ppermute x3, starting transfers between devices, neighbour(): return lax.ppermute(value, ('seq', 'head'), pairs)  7.46 us
    pallas_call x1, Pallas kernels, halo_shards(): pl.pallas_call(functools.partial(tail_kernel, prior), grid=(groups,), in_...  5.86 us
    ppermute x3, waiting for transfers between devices, neighbour(): return lax.ppermute(value, ('seq', 'head'), pairs)  3.87 us
    unnamed x6, local copies, waits for them, and re-layouts  1.63 us
    slice x4, local copies, waits for them, and re-layouts, halo_shards(): after = neighbour(jnp.concatenate([query_in[:prior], grad_out[:prior]]), -1)  1.02 us
    slice x2, local copies, waits for them, and re-layouts, halo_shards(): key_in[tok - prior:]  0.93 us
  transfers between devices with their start and end apart: 3, of which 1 were waited for; matrix products, arithmetic and copies ran while one was open for 0% of the time, Pallas kernels for 50%

profile of v1, /device:TPU:0, one launch (start us, length us, event | category | flops | bytes accessed | tf_op | source)
XLA Modules:
  0.0 43.1 jit_solution(17136128510542557640)
XLA Ops:
  0.6 0.0 slice-start
  0.6 0.0 slice-start.1
  0.7 0.9 %slice-done = bf16[64,2048]{1,0:T(8,128)(2,1)S(1)} async-done(((bf16[128,2048]{1,0:T(8,128)(2,1)}), bf16[64,2048]{1,0:T(8,128)(2,1)S(1)}, s32[]{:S(2)}) %slice-start) | async-done | bytes 262168 | tf_op jit(solution)/shard_map/slice | solution.py:327
  1.6 0.1 slice-done.1
  1.7 4.9 %collective-permute-start = (bf16[128,2048]{1,0:T(8,128)(2,1)S(1)}, bf16[128,2048]{1,0:T(8,128)(2,1)S(1)}, u32[]{:S(2)}, u32[]{:S(2)}) collective-permute-start(bf16[128,2048]{1,0:T(8,128)(2,1)S(1)} %pad_maximum_fusion), channel_id=1, source_target_pairs={{0,1},{1,2},{2,3},{3,4},{4,5},{5,6},{6,7},{7,8},{8,9},{9,10},{10,1... | collective-permute-start | bytes 1572872 | tf_op jit(solution)/shard_map/ppermute | solution.py:298
  6.6 0.0 slice-start.2
  6.6 0.0 slice-start.3
  6.6 0.9 %slice-done.2 = bf16[64,2048]{1,0:T(8,128)(2,1)S(1)} async-done(((bf16[128,2048]{1,0:T(8,128)(2,1)}), bf16[64,2048]{1,0:T(8,128)(2,1)S(1)}, s32[]{:S(2)}) %slice-start.2) | async-done | bytes 262168 | tf_op jit(solution)/shard_map/slice | solution.py:328
  7.6 0.1 slice-done.3
  7.7 1.3 %collective-permute-start.1 = (bf16[128,2048]{1,0:T(8,128)(2,1)S(1)}, bf16[128,2048]{1,0:T(8,128)(2,1)S(1)}, u32[]{:S(2)}, u32[]{:S(2)}) collective-permute-start(bf16[128,2048]{1,0:T(8,128)(2,1)S(1)} %pad_maximum_fusion.1), channel_id=1, source_target_pairs={{1,0},{2,1},{3,2},{4,3},{5,4},{6,5},{7,6},{8,7},{9,8},{10,9},{11,1... | collective-permute-start | bytes 1572872 | tf_op jit(solution)/shard_map/ppermute | solution.py:298
  9.0 10.3 %own_block.1 = (bf16[128,2048]{1,0:T(8,128)(2,1)}, bf16[128,2048]{1,0:T(8,128)(2,1)}, f32[128,2048]{1,0:T(8,128)}, f32[128,2048]{1,0:T(8,128)}, f32[4,8,64]{2,1,0:T(8,128)}) custom-call(s32[1,128]{1,0:T(1,128)} %bitcast.1, bf16[128,2048]{1,0:T(8,128)(2,1)} %q_ref.3, bf16[128,2048]{1,0:T(8,128)(2,1)} %k_ref.5, bf16[128,2048]{1,0:T(8,128)(2,1)} %v_ref.5, ...), custom_call_target="tpu_custom_call" | custom-call | flops 268435456 | bytes 6291456 | tf_op jit(solution)/shard_map/own_block/pallas_call | solution.py:330
  19.3 1.3 %collective-permute-start.2 = (f32[4,8,64]{2,1,0:T(8,128)}, f32[4,8,64]{2,1,0:T(8,128)S(1)}, u32[]{:S(2)}, u32[]{:S(2)}) collective-permute-start(f32[4,8,64]{2,1,0:T(8,128)} %get-tuple-element.21), channel_id=1, source_target_pairs={{1,0},{2,1},{3,2},{4,3},{5,4},{6,5},{7,6},{8,7},{9,8},{10,9},{11,1... | collective-permute-start | bytes 24584 | tf_op jit(solution)/shard_map/ppermute | solution.py:298
  20.6 3.9 %collective-permute-done.before_ref = bf16[128,2048]{1,0:T(8,128)(2,1)S(1)} collective-permute-done((bf16[128,2048]{1,0:T(8,128)(2,1)S(1)}, bf16[128,2048]{1,0:T(8,128)(2,1)S(1)}, u32[]{:S(2)}, u32[]{:S(2)}) %collective-permute-start) | collective-permute-done | bytes 524320 | tf_op jit(solution)/shard_map/ppermute | solution.py:298
  24.5 0.0 copy-start.1
  24.5 0.8 %copy-done.1 = bf16[128,2048]{1,0:T(8,128)(2,1)} copy-done((bf16[128,2048]{1,0:T(8,128)(2,1)}, bf16[128,2048]{1,0:T(8,128)(2,1)S(1)}, u32[]{:S(2)}) %copy-start.1) | copy-done | bytes 524312
  25.3 11.1 %lead_rows.1 = (bf16[128,2048]{1,0:T(8,128)(2,1)}, bf16[128,2048]{1,0:T(8,128)(2,1)}, bf16[128,2048]{1,0:T(8,128)(2,1)}, bf16[128,2048]{1,0:T(8,128)(2,1)}) custom-call(s32[1,128]{1,0:T(1,128)} %bitcast.2, bf16[128,2048]{1,0:T(8,128)(2,1)} %q_ref.3, bf16[128,2048]{1,0:T(8,128)(2,1)} %k_ref.5, ...), custom_call_target="tpu_custom_call", output_to_operand_aliasing={{0}: (8, {}), {1}: (9, {})} | custom-call | flops 167772160 | bytes 3670016 | tf_op jit(solution)/shard_map/lead_rows/pallas_call | solution.py:348
  36.4 0.0 collective-permute-done.2.stat_ref
  36.4 0.0 copy-start.2
  36.4 0.0 collective-permute-done.1.after_ref
  36.4 0.0 copy-start
  36.4 0.6 %copy-done.2 = f32[4,8,64]{2,1,0:T(8,128)} copy-done((f32[4,8,64]{2,1,0:T(8,128)}, f32[4,8,64]{2,1,0:T(8,128)S(1)}, u32[]{:S(2)}) %copy-start.2) | copy-done | bytes 8216
  37.0 0.2 copy-done
  37.2 5.9 %tail_keys.1 = (bf16[128,2048]{1,0:T(8,128)(2,1)}, bf16[128,2048]{1,0:T(8,128)(2,1)}) custom-call(s32[1,128]{1,0:T(1,128)} %bitcast.3, bf16[128,2048]{1,0:T(8,128)(2,1)} %k_ref.5, bf16[128,2048]{1,0:T(8,128)(2,1)} %v_ref.5, bf16[128,2048]{1,0:T(8,128)(2,1)} %copy-done, f32[4,8,64]{2,1,0:T(8,128)} %copy-done.2, ...), custom_call_target="tpu_custom_call", output_to_operand_aliasing={{0}: (7, {}), {1}: (8, {})} | custom-call | flops 67108864 | bytes 2621440 | tf_op jit(solution)/shard_map/tail_keys/pallas_call | solution.py:360
  (2 shorter events, 0.1 us)
Async XLA Ops:
  0.6 1.0 %slice-start = ((bf16[128,2048]{1,0:T(8,128)(2,1)}), bf16[64,2048]{1,0:T(8,128)(2,1)S(1)}, s32[]{:S(2)}) async-start(bf16[128,2048]{1,0:T(8,128)(2,1)} %k_ref.5), calls=%async_computation | async-start | bytes 524288 | tf_op jit(solution)/shard_map/slice | solution.py:327
  0.6 1.0 %slice-start.1 = ((bf16[128,2048]{1,0:T(8,128)(2,1)}), bf16[64,2048]{1,0:T(8,128)(2,1)S(1)}, s32[]{:S(2)}) async-start(bf16[128,2048]{1,0:T(8,128)(2,1)} %v_ref.5), calls=%async_computation.1 | async-start | bytes 524288 | tf_op jit(solution)/shard_map/slice | solution.py:327
  1.7 22.8 %collective-permute-start = (bf16[128,2048]{1,0:T(8,128)(2,1)S(1)}, bf16[128,2048]{1,0:T(8,128)(2,1)S(1)}, u32[]{:S(2)}, u32[]{:S(2)}) collective-permute-start(bf16[128,2048]{1,0:T(8,128)(2,1)S(1)} %pad_maximum_fusion), channel_id=1, source_target_pairs={{0,1},{1,2},{2,3},{3,4},{4,5},{5,6},{6,7},{7,8},{8,9},{9,10},{10,1... | collective-permute-start | bytes 1572872 | tf_op jit(solution)/shard_map/ppermute | solution.py:298
  6.6 1.0 %slice-start.2 = ((bf16[128,2048]{1,0:T(8,128)(2,1)}), bf16[64,2048]{1,0:T(8,128)(2,1)S(1)}, s32[]{:S(2)}) async-start(bf16[128,2048]{1,0:T(8,128)(2,1)} %q_ref.3), calls=%async_computation.2 | async-start | bytes 524288 | tf_op jit(solution)/shard_map/slice | solution.py:328
  6.6 1.0 %slice-start.3 = ((bf16[128,2048]{1,0:T(8,128)(2,1)}), bf16[64,2048]{1,0:T(8,128)(2,1)S(1)}, s32[]{:S(2)}) async-start(bf16[128,2048]{1,0:T(8,128)(2,1)} %do_ref.3), calls=%async_computation.3 | async-start | bytes 524288 | tf_op jit(solution)/shard_map/slice | solution.py:328
  7.7 28.7 %collective-permute-start.1 = (bf16[128,2048]{1,0:T(8,128)(2,1)S(1)}, bf16[128,2048]{1,0:T(8,128)(2,1)S(1)}, u32[]{:S(2)}, u32[]{:S(2)}) collective-permute-start(bf16[128,2048]{1,0:T(8,128)(2,1)S(1)} %pad_maximum_fusion.1), channel_id=1, source_target_pairs={{1,0},{2,1},{3,2},{4,3},{5,4},{6,5},{7,6},{8,7},{9,8},{10,9},{11,1... | collective-permute-start | bytes 1572872 | tf_op jit(solution)/shard_map/ppermute | solution.py:298
  19.3 17.1 %collective-permute-start.2 = (f32[4,8,64]{2,1,0:T(8,128)}, f32[4,8,64]{2,1,0:T(8,128)S(1)}, u32[]{:S(2)}, u32[]{:S(2)}) collective-permute-start(f32[4,8,64]{2,1,0:T(8,128)} %get-tuple-element.21), channel_id=1, source_target_pairs={{1,0},{2,1},{3,2},{4,3},{5,4},{6,5},{7,6},{8,7},{9,8},{10,9},{11,1... | collective-permute-start | bytes 24584 | tf_op jit(solution)/shard_map/ppermute | solution.py:298
  24.5 0.8 %copy-start.1 = (bf16[128,2048]{1,0:T(8,128)(2,1)}, bf16[128,2048]{1,0:T(8,128)(2,1)S(1)}, u32[]{:S(2)}) copy-start(bf16[128,2048]{1,0:T(8,128)(2,1)S(1)} %collective-permute-done.before_ref) | copy-start | bytes 1572868
  36.4 0.6 %copy-start.2 = (f32[4,8,64]{2,1,0:T(8,128)}, f32[4,8,64]{2,1,0:T(8,128)S(1)}, u32[]{:S(2)}) copy-start(f32[4,8,64]{2,1,0:T(8,128)S(1)} %collective-permute-done.2.stat_ref) | copy-start | bytes 24580
  36.4 0.8 %copy-start = (bf16[128,2048]{1,0:T(8,128)(2,1)}, bf16[128,2048]{1,0:T(8,128)(2,1)S(1)}, u32[]{:S(2)}) copy-start(bf16[128,2048]{1,0:T(8,128)(2,1)S(1)} %collective-permute-done.1.after_ref) | copy-start | bytes 1572868

commit v2 on v0

--- a/solution.py
+++ b/solution.py
@@ -1,11 +1,17 @@
+import functools
 import math
 
 import jax
 import jax.numpy as jnp
 from jax import lax
+from jax.experimental import pallas as pl
+from jax.experimental.pallas import tpu as pltpu
 from jax.sharding import PartitionSpec as P
 
 HEAD_DIM = 128
+SCALE = HEAD_DIM ** (-0.5)
+LOG2E = math.log2(math.e)
+MASKED = -1e30
 
 
 def shifted(value, axis, by):
@@ -61,7 +67,7 @@
     return (attn_rows, grad_q, key_grad, value_grad, log_total[:, 0], row_delta)
 
 
-def shards(query_in, key_in, value_in, grad_out, module_lengths):
+def gathered_shards(query_in, key_in, value_in, grad_out, module_lengths):
     head_q, head_k, head_v, head_do = (
         lax.all_to_all(query_in, "head", split_axis=1, concat_axis=0, tiled=True),
         lax.all_to_all(key_in, "head", split_axis=1, concat_axis=0, tiled=True),
@@ -135,6 +141,279 @@
     return (attn_back, back_q, back_k, back_v)
 
 
+def dot(left, right, left_dim, right_dim):
+    return lax.dot_general(
+        left, right, (((left_dim,), (right_dim,)), ((), ())), preferred_element_type=jnp.float32
+    )
+
+
+def module_ends_row(lengths_row):
+    count = lengths_row.shape[1]
+    row = lax.broadcasted_iota(jnp.int32, (count, count), 0)
+    col = lax.broadcasted_iota(jnp.int32, (count, count), 1)
+    lengths_col = jnp.sum(jnp.where(row == col, lengths_row, 0.0), axis=1, keepdims=True)
+    return jnp.sum(jnp.where(row <= col, lengths_col, 0.0), axis=0, keepdims=True)
+
+
+def module_ends_col(lengths_row):
+    count = lengths_row.shape[1]
+    row = lax.broadcasted_iota(jnp.int32, (count, count), 0)
+    col = lax.broadcasted_iota(jnp.int32, (count, count), 1)
+    return jnp.sum(jnp.where(col <= row, lengths_row, 0.0), axis=1, keepdims=True)
+
+
+def bias_by_query(lengths_row, first_query, queries, first_key, keys):
+    ends = module_ends_row(lengths_row)
+    query = (first_query + lax.broadcasted_iota(jnp.int32, (queries, 1), 0)).astype(jnp.float32)
+    start = jnp.max(jnp.where(ends <= query, ends, 0.0), axis=1, keepdims=True)
+    key = (first_key + lax.broadcasted_iota(jnp.int32, (queries, keys), 1)).astype(jnp.float32)
+    return jnp.where((key >= start) & (key <= query), 0.0, MASKED)
+
+
+def bias_by_key(lengths_row, first_query, queries, first_key, keys):
+    ends = module_ends_col(lengths_row)
+    query = (first_query + lax.broadcasted_iota(jnp.int32, (1, queries), 1)).astype(jnp.float32)
+    start = jnp.max(jnp.where(ends <= query, ends, 0.0), axis=0, keepdims=True)
+    key = (first_key + lax.broadcasted_iota(jnp.int32, (keys, queries), 0)).astype(jnp.float32)
+    return jnp.where((key >= start) & (key <= query), 0.0, MASKED)
+
+
+def by_query(q, k, do, v, bias):
+    scores = dot(q, k, 1, 1) * (SCALE * LOG2E) + bias
+    return scores, dot(do, v, 1, 1)
+
+
+def full_rows(pairs):
+    tops = [jnp.max(s, axis=1, keepdims=True) for s, _ in pairs]
+    raws = [jnp.exp2(s - top) for (s, _), top in zip(pairs, tops)]
+    parts = [1.0 / jnp.sum(raw, axis=1, keepdims=True) for raw in raws]
+    weights = [raw * part for raw, part in zip(raws, parts)]
+    deltas = [jnp.sum(w * dp, axis=1, keepdims=True) for w, (_, dp) in zip(weights, pairs)]
+    grads = [w * (dp - delta) * SCALE for w, (_, dp), delta in zip(weights, pairs, deltas)]
+    return [w.astype(jnp.bfloat16) for w in weights], [g.astype(jnp.bfloat16) for g in grads]
+
+
+def merged_rows(pairs, own):
+    tops = [
+        jnp.maximum(jnp.max(s, axis=0, keepdims=True), log) for (s, _), (log, _) in zip(pairs, own)
+    ]
+    raws = [jnp.exp2(s - top) for (s, _), top in zip(pairs, tops)]
+    own_raws = [jnp.exp2(log - top) for (log, _), top in zip(own, tops)]
+    parts = [
+        1.0 / (jnp.sum(raw, axis=0, keepdims=True) + own_raw)
+        for raw, own_raw in zip(raws, own_raws)
+    ]
+    weights = [raw * part for raw, part in zip(raws, parts)]
+    deltas = [
+        jnp.sum(w * dp, axis=0, keepdims=True) + own_raw * part * own_delta
+        for w, (_, dp), own_raw, part, (_, own_delta) in zip(weights, pairs, own_raws, parts, own)
+    ]
+    grads = [w * (dp - delta) * SCALE for w, (_, dp), delta in zip(weights, pairs, deltas)]
+    return [w.astype(jnp.bfloat16) for w in weights], [g.astype(jnp.bfloat16) for g in grads]
+
+
+def head_columns(width):
+    return [slice(c, c + HEAD_DIM) for c in range(0, width, HEAD_DIM)]
+
+
+def device_first(tok):
+    place = lax.axis_index("seq") * lax.axis_size("head") + lax.axis_index("head")
+    return place * tok
+
+
+def own_kernel(
+    prior, len_ref, q_ref, k_ref, v_ref, do_ref,
+    attn_ref, gq_ref, gk_ref, gv_ref, stat_ref, bias_ref, lead_ref,
+):
+    tok, width = q_ref.shape
+    rest = tok - prior
+    columns = head_columns(width)
+    heads = len(columns)
+
+    @pl.when(pl.program_id(0) == 0)
+    def _():
+        first = device_first(tok)
+        lengths = len_ref[...].astype(jnp.float32)
+        bias_ref[...] = bias_by_query(lengths, first + prior, rest, first, tok)
+        lead_ref[...] = bias_by_key(lengths, first, prior, first, prior)
+
+    bias, lead = bias_ref[...], lead_ref[...]
+    late = slice(prior, tok)
+    early = slice(0, prior)
+    pairs = [
+        by_query(q_ref[late, c], k_ref[:, c], do_ref[late, c], v_ref[:, c], bias) for c in columns
+    ]
+    leads = [
+        by_query(k_ref[early, c], q_ref[early, c], v_ref[early, c], do_ref[early, c], lead)
+        for c in columns
+    ]
+    weights, grads = full_rows(pairs)
+    for c, w, g in zip(columns, weights, grads):
+        attn_ref[:, c] = dot(w, v_ref[:, c], 1, 0).astype(jnp.bfloat16)
+        gq_ref[:, c] = dot(g, k_ref[:, c], 1, 0).astype(jnp.bfloat16)
+        gk_ref[:, c] = dot(g, q_ref[late, c], 0, 0)
+        gv_ref[:, c] = dot(w, do_ref[late, c], 0, 0)
+    tops = [jnp.max(s, axis=0, keepdims=True) for s, _ in leads]
+    raws = [jnp.exp2(s - top) for (s, _), top in zip(leads, tops)]
+    totals = [jnp.sum(raw, axis=0, keepdims=True) for raw in raws]
+    sums = [jnp.sum(raw * dp, axis=0, keepdims=True) for raw, (_, dp) in zip(raws, leads)]
+    for h in range(heads):
+        stat_ref[0, h : h + 1, :] = tops[h] + jnp.log2(totals[h])
+        stat_ref[0, heads + h : heads + h + 1, :] = sums[h] / totals[h]
+
+
+def edge_kernel(
+    prior, len_ref, q_ref, k_ref, v_ref, do_ref, before_ref, after_ref, stat_ref,
+    gk_part_ref, gv_part_ref, *refs,
+):
+    attn_ref, gq_ref, gk_ref, gv_ref, bias_ref, tail_ref = refs[-6:]
+    tok, width = k_ref.shape
+    columns = head_columns(width)
+    heads = len(columns)
+
+    @pl.when(pl.program_id(0) == 0)
+    def _():
+        first = device_first(tok)
+        lengths = len_ref[...].astype(jnp.float32)
+        bias_ref[...] = bias_by_query(lengths, first, prior, first - prior, 2 * prior)
+        tail_ref[...] = bias_by_key(lengths, first + tok, prior, first + tok - prior, prior)
+
+    bias, tail = bias_ref[...], tail_ref[...]
+    early, late = slice(0, prior), slice(tok - prior, tok)
+    second = slice(prior, 2 * prior)
+    keys = [jnp.concatenate([before_ref[early, c], k_ref[early, c]], axis=0) for c in columns]
+    values = [jnp.concatenate([before_ref[second, c], v_ref[early, c]], axis=0) for c in columns]
+    leads = [
+        by_query(q_ref[:, c], k, do_ref[:, c], v, bias) for c, k, v in zip(columns, keys, values)
+    ]
+    tails = [
+        by_query(k_ref[late, c], after_ref[early, c], v_ref[late, c], after_ref[second, c], tail)
+        for c in columns
+    ]
+    own = [
+        (stat_ref[0, h : h + 1, :], stat_ref[0, heads + h : heads + h + 1, :])
+        for h in range(heads)
+    ]
+    weights, grads = full_rows(leads)
+    tail_weights, tail_grads = merged_rows(tails, own)
+    for c, w, g, k, v in zip(columns, weights, grads, keys, values):
+        attn_ref[:, c] = dot(w, v, 1, 0).astype(jnp.bfloat16)
+        gq_ref[:, c] = dot(g, k, 1, 0).astype(jnp.bfloat16)
+        gk = gk_part_ref[early, c] + dot(g[:, second], q_ref[:, c], 0, 0)
+        gv = gv_part_ref[early, c] + dot(w[:, second], do_ref[:, c], 0, 0)
+        gk_ref[early, c] = gk.astype(jnp.bfloat16)
+        gv_ref[early, c] = gv.astype(jnp.bfloat16)
+    for c, w, g in zip(columns, tail_weights, tail_grads):
+        gk = gk_part_ref[late, c] + dot(g, after_ref[early, c], 1, 0)
+        gv = gv_part_ref[late, c] + dot(w, after_ref[second, c], 1, 0)
+        gk_ref[late, c] = gk.astype(jnp.bfloat16)
+        gv_ref[late, c] = gv.astype(jnp.bfloat16)
+
+
+def neighbour(value, by):
+    peers = lax.axis_size("seq") * lax.axis_size("head")
+    pairs = [(i, i + by) for i in range(peers) if 0 <= i + by < peers]
+    return lax.ppermute(value, ("seq", "head"), pairs)
+
+
+def cost(heads, queries, keys, products, moved):
+    return pl.CostEstimate(
+        flops=2 * heads * queries * keys * HEAD_DIM * products,
+        bytes_accessed=moved,
+        transcendentals=heads * queries * keys,
+    )
+
+
+def halo_shards(query_in, key_in, value_in, grad_out, module_lengths):
+    tok, width = query_in.shape
+    prior = tok * lax.axis_size("head") // 8
+    heads = width // HEAD_DIM
+    step = min(width, 4 * HEAD_DIM)
+    groups = width // step
+    per = step // HEAD_DIM
+    lengths = module_lengths.reshape(1, -1)
+    len_spec = pl.BlockSpec(lengths.shape, lambda g: (0, 0))
+    keep = pl.BlockSpec(memory_space=pl.ANY)
+    full16 = jax.ShapeDtypeStruct((tok, width), jnp.bfloat16)
+    full32 = jax.ShapeDtypeStruct((tok, width), jnp.float32)
+
+    def rows(count, at, base=0):
+        return pl.BlockSpec((count, step), lambda g: (at, g + base))
+
+    def stats(base=0):
+        return pl.BlockSpec((1, 2 * per, prior), lambda g: (g + base, 0, 0))
+
+    def halos(cols, after=None):
+        k, v = key_in[tok - prior :, cols], value_in[tok - prior :, cols]
+        q, do = query_in[:prior, cols], grad_out[:prior, cols]
+        if after is not None:
+            k, v, q, do, _ = lax.optimization_barrier((k, v, q, do, after))
+        return neighbour(jnp.concatenate([k, v]), 1), neighbour(jnp.concatenate([q, do]), -1)
+
+    cuts = [0, groups // 2, groups] if groups > 1 else [0, groups]
+    spans = list(zip(cuts[:-1], cuts[1:]))
+    moved = [halos(slice(spans[0][0] * step, spans[0][1] * step))]
+
+    attn, gq, gk_part, gv_part, stat = pl.pallas_call(
+        functools.partial(own_kernel, prior),
+        grid=(groups,),
+        in_specs=[len_spec, rows(tok, 0), rows(tok, 0), rows(tok, 0), rows(tok, 0)],
+        out_specs=[
+            rows(prior, tok // prior - 1), rows(prior, tok // prior - 1),
+            rows(tok, 0), rows(tok, 0), stats(),
+        ],
+        out_shape=[
+            full16, full16, full32, full32,
+            jax.ShapeDtypeStruct((groups, 2 * per, prior), jnp.float32),
+        ],
+        scratch_shapes=[
+            pltpu.VMEM((tok - prior, tok), jnp.float32),
+            pltpu.VMEM((prior, prior), jnp.float32),
+        ],
+        cost_estimate=cost(heads, tok, tok, 4, 24 * tok * width),
+        name="own_block",
+    )(lengths, query_in, key_in, value_in, grad_out)
+    stat_after = neighbour(stat, -1)
+    for low, high in spans[1:]:
+        moved.append(halos(slice(low * step, high * step), stat))
+
+    outs = [attn, gq]
+    for (low, high), (before, after) in zip(spans, moved):
+        outs = pl.pallas_call(
+            functools.partial(edge_kernel, prior),
+            grid=(high - low,),
+            in_specs=[
+                len_spec, rows(prior, 0, low), rows(tok, 0, low), rows(tok, 0, low),
+                rows(prior, 0, low), rows(2 * prior, 0), rows(2 * prior, 0), stats(low),
+                rows(tok, 0, low), rows(tok, 0, low), *[keep] * len(outs),
+            ],
+            out_specs=[
+                rows(prior, 0, low), rows(prior, 0, low), rows(tok, 0, low), rows(tok, 0, low),
+            ],
+            out_shape=[full16] * 4,
+            scratch_shapes=[
+                pltpu.VMEM((prior, 2 * prior), jnp.float32),
+                pltpu.VMEM((prior, prior), jnp.float32),
+            ],
+            input_output_aliases={10 + i: i for i in range(len(outs))},
+            cost_estimate=cost(
+                (high - low) * per, prior, 2 * prior, 7, 20 * tok * step * (high - low)
+            ),
+            name="edges",
+        )(
+            lengths, query_in, key_in, value_in, grad_out, before, after, stat_after,
+            gk_part, gv_part, *outs,
+        )
+    return tuple(outs)
+
+
+def shards(query_in, key_in, value_in, grad_out, module_lengths):
+    tok = query_in.shape[0]
+    prior = tok * lax.axis_size("head") // 8
+    plan = halo_shards if 2 * prior <= tok else gathered_shards
+    return plan(query_in, key_in, value_in, grad_out, module_lengths)
+
+
 def solution(mesh):
     placed = (
         P(("seq", "head"), None),

time: 124 us -> 42.6 us (0.34)
  waiting for transfers between devices: 41.2 us -> 9.05 us
  starting transfers between devices: 38.2 us -> 14.9 us
  matrix products: 18.3 us -> 0 us
  local copies, waits for them, and re-layouts: 19.7 us -> 2.85 us
  Pallas kernels: 0 us -> 14.3 us
  other arithmetic: 4.94 us -> 0.08 us
    all_to_all x8 -> x0, waiting for transfers between devices: 37.3 us -> none  [the longest x1 7.04 us: shards(): lax.all_to_all(grad_q, 'head', split_axis=0, concat_axis=1, tiled=True)]
    all_to_all x8 -> x0, starting transfers between devices: 30.1 us -> none  [the longest x1 5.16 us: shards(): lax.all_to_all(query_in, 'head', split_axis=1, concat_axis=0, tiled=True)]
    dot_general x24 -> x0, matrix products: 18.3 us -> none  [the longest x4 4.63 us: one_block(): jnp.einsum('qk,kd->qd', weight_bf, value_block, preferred_element_type=jn...]
    pallas_call x0 -> x3, Pallas kernels: none -> 14.3 us  [the longest x2 8.61 us: halo_shards(): pl.pallas_call(functools.partial(edge_kernel, prior), grid=(high - low,),...]
    all_to_all x13 -> x0, local copies, waits for them, and re-layouts: 7.9 us -> none  [the longest x1 1.94 us: shards(): lax.all_to_all(query_in, 'head', split_axis=1, concat_axis=0, tiled=True)]
    unnamed x25 -> x16, local copies, waits for them, and re-layouts: 8.82 us -> 1.63 us
    ppermute x4 -> x5, starting transfers between devices: 8.1 us -> 14.9 us  [neighbour(): return lax.ppermute(value, ('seq', 'head'), pairs)]
    ppermute x4 -> x5, waiting for transfers between devices: 3.9 us -> 9.05 us  [neighbour(): return lax.ppermute(value, ('seq', 'head'), pairs)]
  transfers between devices with their start and end apart: 12 -> 5, of which waited for: 9 -> 1; matrix products, arithmetic and copies ran while one was open for 9% -> 0% of each run, Pallas kernels for 0% -> 24%
where the time goes in v2:
time: 42.6 us; the launch traced here: 42.1 us
  starting transfers between devices  14.9 us (35%)
  Pallas kernels  14.3 us (34%)
  waiting for transfers between devices  9.05 us (21%)
  local copies, waits for them, and re-layouts  2.85 us (7%)
  between operations  0.81 us (2%)
    ppermute x5, starting transfers between devices, neighbour(): return lax.ppermute(value, ('seq', 'head'), pairs)  14.9 us
    ppermute x5, waiting for transfers between devices, neighbour(): return lax.ppermute(value, ('seq', 'head'), pairs)  9.05 us
    pallas_call x2, Pallas kernels, halo_shards(): pl.pallas_call(functools.partial(edge_kernel, prior), grid=(high - low,),...  8.61 us
    pallas_call x1, Pallas kernels, halo_shards(): pl.pallas_call(functools.partial(own_kernel, prior), grid=(groups,), in_s...  5.73 us
    unnamed x16, local copies, waits for them, and re-layouts  1.63 us
    slice x1, local copies, waits for them, and re-layouts, halos(): q, do = (query_in[:prior, cols], grad_out[:prior, cols])  1.19 us
  transfers between devices with their start and end apart: 5, of which 1 were waited for; matrix products, arithmetic and copies ran while one was open for 0% of the time, Pallas kernels for 24%

profile of v2, /device:TPU:0, one launch (start us, length us, event | category | flops | bytes accessed | tf_op | source)
XLA Modules:
  0.0 42.1 jit_solution(18196378877138511101)
XLA Ops:
  0.6 0.0 copy-start.1
  0.6 1.2 %fusion = (bf16[64,1024]{1,0:T(8,128)(2,1)S(1)}, bf16[64,1024]{1,0:T(8,128)(2,1)S(1)}, bf16[64,1024]{1,0:T(8,128)(2,1)S(1)}, bf16[64,1024]{1,0:T(8,128)(2,1)S(1)}) fusion(bf16[128,2048]{1,0:T(8,128)(2,1)} %q_ref.5, bf16[128,2048]{1,0:T(8,128)(2,1)} %do_ref.5), kind=kLoop, calls=%fused_computation.4 | loop fusion | bytes 1048576 | tf_op jit(solution)/shard_map/slice | solution.py:348
  1.8 0.0 copy-start
  1.9 1.4 %collective-permute-start.4 = (bf16[128,1024]{1,0:T(8,128)(2,1)S(1)}, bf16[128,1024]{1,0:T(8,128)(2,1)S(1)}, u32[]{:S(2)}, u32[]{:S(2)}) collective-permute-start(bf16[128,1024]{1,0:T(8,128)(2,1)S(1)} %pad_maximum_fusion.3), channel_id=1, source_target_pairs={{1,0},{2,1},{3,2},{4,3},{5,4},{6,5},{7,6},{8,7},{9,8},{10,9},{11,1... | collective-permute-start | bytes 786440 | tf_op jit(solution)/shard_map/ppermute | solution.py:316
  3.3 0.0 copy-done.1
  3.3 0.0 copy-done
  3.4 5.5 %collective-permute-start.3 = (bf16[128,1024]{1,0:T(8,128)(2,1)S(1)}, bf16[128,1024]{1,0:T(8,128)(2,1)S(1)}, u32[]{:S(2)}, u32[]{:S(2)}) collective-permute-start(bf16[128,1024]{1,0:T(8,128)(2,1)S(1)} %pad_maximum_fusion.2), channel_id=1, source_target_pairs={{0,1},{1,2},{2,3},{3,4},{4,5},{5,6},{6,7},{7,8},{8,9},{9,10},{10,1... | collective-permute-start | bytes 786440 | tf_op jit(solution)/shard_map/ppermute | solution.py:316
  8.9 5.7 %own_block.1 = (bf16[128,2048]{1,0:T(8,128)(2,1)}, bf16[128,2048]{1,0:T(8,128)(2,1)}, f32[128,2048]{1,0:T(8,128)}, f32[128,2048]{1,0:T(8,128)}, f32[4,8,64]{2,1,0:T(8,128)}) custom-call(s32[1,128]{1,0:T(1,128)} %bitcast.1, bf16[128,2048]{1,0:T(8,128)(2,1)} %q_ref.5, bf16[128,2048]{1,0:T(8,128)(2,1)} %k_ref.5, bf16[128,2048]{1,0:T(8,128)(2,1)} %v_ref.5, ...), custom_call_target="tpu_custom_call" | custom-call | flops 268435456 | bytes 6291456 | tf_op jit(solution)/shard_map/own_block/pallas_call | solution.py:357
  14.6 0.0 copy-start.7
  14.7 1.3 %collective-permute-start.1 = (bf16[128,1024]{1,0:T(8,128)(2,1)S(1)}, bf16[128,1024]{1,0:T(8,128)(2,1)S(1)}, u32[]{:S(2)}, u32[]{:S(2)}) collective-permute-start(bf16[128,1024]{1,0:T(8,128)(2,1)S(1)} %pad_maximum_fusion.1), channel_id=1, source_target_pairs={{1,0},{2,1},{3,2},{4,3},{5,4},{6,5},{7,6},{8,7},{9,8},{10,9},{11,1... | collective-permute-start | bytes 786440 | tf_op jit(solution)/shard_map/ppermute | solution.py:316
  16.0 5.4 %collective-permute-start = (bf16[128,1024]{1,0:T(8,128)(2,1)S(1)}, bf16[128,1024]{1,0:T(8,128)(2,1)S(1)}, u32[]{:S(2)}, u32[]{:S(2)}) collective-permute-start(bf16[128,1024]{1,0:T(8,128)(2,1)S(1)} %pad_maximum_fusion), channel_id=1, source_target_pairs={{0,1},{1,2},{2,3},{3,4},{4,5},{5,6},{6,7},{7,8},{8,9},{9,10},{10,1... | collective-permute-start | bytes 786440 | tf_op jit(solution)/shard_map/ppermute | solution.py:316
  21.4 0.0 copy-done.7
  21.4 1.3 %collective-permute-start.2 = (f32[4,8,64]{2,1,0:T(8,128)S(1)}, f32[4,8,64]{2,1,0:T(8,128)S(1)}, u32[]{:S(2)}, u32[]{:S(2)}) collective-permute-start(f32[4,8,64]{2,1,0:T(8,128)S(1)} %copy-done.7), channel_id=1, source_target_pairs={{1,0},{2,1},{3,2},{4,3},{5,4},{6,5},{7,6},{8,7},{9,8},{10,9},{11,1... | collective-permute-start | bytes 24584 | tf_op jit(solution)/shard_map/ppermute | solution.py:316
  22.8 9.0 %collective-permute-done.2.stat_ref = f32[4,8,64]{2,1,0:T(8,128)S(1)} collective-permute-done((f32[4,8,64]{2,1,0:T(8,128)S(1)}, f32[4,8,64]{2,1,0:T(8,128)S(1)}, u32[]{:S(2)}, u32[]{:S(2)}) %collective-permute-start.2) | collective-permute-done | bytes 8224 | tf_op jit(solution)/shard_map/ppermute | solution.py:316
  31.8 0.0 copy-start.6
  31.8 0.0 collective-permute-done.4.after_ref
  31.8 0.0 copy-start.2
  31.8 0.0 collective-permute-done.3.before_ref
  31.8 0.0 copy-start.4
  31.8 0.6 %copy-done.6 = f32[4,8,64]{2,1,0:T(8,128)} copy-done((f32[4,8,64]{2,1,0:T(8,128)}, f32[4,8,64]{2,1,0:T(8,128)S(1)}, u32[]{:S(2)}) %copy-start.6) | copy-done | bytes 8216
  32.4 0.1 copy-done.2
  32.5 0.1 copy-done.4
  32.6 4.3 %edges.2 = (bf16[128,2048]{1,0:T(8,128)(2,1)}, bf16[128,2048]{1,0:T(8,128)(2,1)}, bf16[128,2048]{1,0:T(8,128)(2,1)}, bf16[128,2048]{1,0:T(8,128)(2,1)}) custom-call(s32[1,128]{1,0:T(1,128)} %bitcast.2, bf16[128,2048]{1,0:T(8,128)(2,1)} %q_ref.5, bf16[128,2048]{1,0:T(8,128)(2,1)} %k_ref.5, ...), custom_call_target="tpu_custom_call", output_to_operand_aliasing={{0}: (10, {}), {1}: (11, {})} | custom-call | flops 117440512 | bytes 2621440 | tf_op jit(solution)/shard_map/edges/pallas_call | solution.py:382
  36.9 0.0 collective-permute-done.1.after_ref
  36.9 0.0 copy-start.3
  36.9 0.0 collective-permute-done.before_ref
  37.0 0.0 copy-start.5
  37.0 0.7 %copy-done.3 = bf16[128,1024]{1,0:T(8,128)(2,1)} copy-done((bf16[128,1024]{1,0:T(8,128)(2,1)}, bf16[128,1024]{1,0:T(8,128)(2,1)S(1)}, u32[]{:S(2)}) %copy-start.3) | copy-done | bytes 262168
  37.6 0.1 copy-done.5
  37.8 4.3 %edges.3 = (bf16[128,2048]{1,0:T(8,128)(2,1)}, bf16[128,2048]{1,0:T(8,128)(2,1)}, bf16[128,2048]{1,0:T(8,128)(2,1)}, bf16[128,2048]{1,0:T(8,128)(2,1)}) custom-call(s32[1,128]{1,0:T(1,128)} %bitcast.3, bf16[128,2048]{1,0:T(8,128)(2,1)} %q_ref.5, ...), custom_call_target="tpu_custom_call", output_to_operand_aliasing={{0}: (10, {}), {1}: (11, {}), {2}: (12, {}), {3}: (13, {})} | custom-call | flops 117440512 | bytes 2621440 | tf_op jit(solution)/shard_map/edges/pallas_call | solution.py:382
  (5 shorter events, 0.1 us)
Async XLA Ops:
  0.6 2.7 %copy-start.1 = (bf16[128,2048]{1,0:T(8,128)(2,1)S(1)}, bf16[128,2048]{1,0:T(8,128)(2,1)}, u32[]{:S(2)}) copy-start(bf16[128,2048]{1,0:T(8,128)(2,1)} %v_ref.5) | copy-start | bytes 1572868
  1.8 1.5 %copy-start = (bf16[128,2048]{1,0:T(8,128)(2,1)S(1)}, bf16[128,2048]{1,0:T(8,128)(2,1)}, u32[]{:S(2)}) copy-start(bf16[128,2048]{1,0:T(8,128)(2,1)} %k_ref.5) | copy-start | bytes 1572868
  1.9 29.9 %collective-permute-start.4 = (bf16[128,1024]{1,0:T(8,128)(2,1)S(1)}, bf16[128,1024]{1,0:T(8,128)(2,1)S(1)}, u32[]{:S(2)}, u32[]{:S(2)}) collective-permute-start(bf16[128,1024]{1,0:T(8,128)(2,1)S(1)} %pad_maximum_fusion.3), channel_id=1, source_target_pairs={{1,0},{2,1},{3,2},{4,3},{5,4},{6,5},{7,6},{8,7},{9,8},{10,9},{11,1... | collective-permute-start | bytes 786440 | tf_op jit(solution)/shard_map/ppermute | solution.py:316
  3.4 28.4 %collective-permute-start.3 = (bf16[128,1024]{1,0:T(8,128)(2,1)S(1)}, bf16[128,1024]{1,0:T(8,128)(2,1)S(1)}, u32[]{:S(2)}, u32[]{:S(2)}) collective-permute-start(bf16[128,1024]{1,0:T(8,128)(2,1)S(1)} %pad_maximum_fusion.2), channel_id=1, source_target_pairs={{0,1},{1,2},{2,3},{3,4},{4,5},{5,6},{6,7},{7,8},{8,9},{9,10},{10,1... | collective-permute-start | bytes 786440 | tf_op jit(solution)/shard_map/ppermute | solution.py:316
  14.6 6.8 %copy-start.7 = (f32[4,8,64]{2,1,0:T(8,128)S(1)}, f32[4,8,64]{2,1,0:T(8,128)}, u32[]{:S(2)}) copy-start(f32[4,8,64]{2,1,0:T(8,128)} %get-tuple-element.17) | copy-start | bytes 24580
  14.7 22.3 %collective-permute-start.1 = (bf16[128,1024]{1,0:T(8,128)(2,1)S(1)}, bf16[128,1024]{1,0:T(8,128)(2,1)S(1)}, u32[]{:S(2)}, u32[]{:S(2)}) collective-permute-start(bf16[128,1024]{1,0:T(8,128)(2,1)S(1)} %pad_maximum_fusion.1), channel_id=1, source_target_pairs={{1,0},{2,1},{3,2},{4,3},{5,4},{6,5},{7,6},{8,7},{9,8},{10,9},{11,1... | collective-permute-start | bytes 786440 | tf_op jit(solution)/shard_map/ppermute | solution.py:316
  16.0 21.0 %collective-permute-start = (bf16[128,1024]{1,0:T(8,128)(2,1)S(1)}, bf16[128,1024]{1,0:T(8,128)(2,1)S(1)}, u32[]{:S(2)}, u32[]{:S(2)}) collective-permute-start(bf16[128,1024]{1,0:T(8,128)(2,1)S(1)} %pad_maximum_fusion), channel_id=1, source_target_pairs={{0,1},{1,2},{2,3},{3,4},{4,5},{5,6},{6,7},{7,8},{8,9},{9,10},{10,1... | collective-permute-start | bytes 786440 | tf_op jit(solution)/shard_map/ppermute | solution.py:316
  21.4 10.3 %collective-permute-start.2 = (f32[4,8,64]{2,1,0:T(8,128)S(1)}, f32[4,8,64]{2,1,0:T(8,128)S(1)}, u32[]{:S(2)}, u32[]{:S(2)}) collective-permute-start(f32[4,8,64]{2,1,0:T(8,128)S(1)} %copy-done.7), channel_id=1, source_target_pairs={{1,0},{2,1},{3,2},{4,3},{5,4},{6,5},{7,6},{8,7},{9,8},{10,9},{11,1... | collective-permute-start | bytes 24584 | tf_op jit(solution)/shard_map/ppermute | solution.py:316
  31.8 0.6 %copy-start.6 = (f32[4,8,64]{2,1,0:T(8,128)}, f32[4,8,64]{2,1,0:T(8,128)S(1)}, u32[]{:S(2)}) copy-start(f32[4,8,64]{2,1,0:T(8,128)S(1)} %collective-permute-done.2.stat_ref) | copy-start | bytes 24580
  31.8 0.7 %copy-start.2 = (bf16[128,1024]{1,0:T(8,128)(2,1)}, bf16[128,1024]{1,0:T(8,128)(2,1)S(1)}, u32[]{:S(2)}) copy-start(bf16[128,1024]{1,0:T(8,128)(2,1)S(1)} %collective-permute-done.4.after_ref) | copy-start | bytes 786436
  31.8 0.8 %copy-start.4 = (bf16[128,1024]{1,0:T(8,128)(2,1)}, bf16[128,1024]{1,0:T(8,128)(2,1)S(1)}, u32[]{:S(2)}) copy-start(bf16[128,1024]{1,0:T(8,128)(2,1)S(1)} %collective-permute-done.3.before_ref) | copy-start | bytes 786436
  36.9 0.7 %copy-start.3 = (bf16[128,1024]{1,0:T(8,128)(2,1)}, bf16[128,1024]{1,0:T(8,128)(2,1)S(1)}, u32[]{:S(2)}) copy-start(bf16[128,1024]{1,0:T(8,128)(2,1)S(1)} %collective-permute-done.1.after_ref) | copy-start | bytes 786436
  37.0 0.8 %copy-start.5 = (bf16[128,1024]{1,0:T(8,128)(2,1)}, bf16[128,1024]{1,0:T(8,128)(2,1)S(1)}, u32[]{:S(2)}) copy-start(bf16[128,1024]{1,0:T(8,128)(2,1)S(1)} %collective-permute-done.before_ref) | copy-start | bytes 786436

commit v3 on v2

--- a/solution.py
+++ b/solution.py
@@ -263,10 +263,10 @@
 
 
 def edge_kernel(
-    prior, len_ref, q_ref, k_ref, v_ref, do_ref, before_ref, after_ref, stat_ref,
+    prior, odd_ref, len_ref, q_ref, k_ref, v_ref, do_ref, even_pair_ref, odd_pair_ref, stat_ref,
     gk_part_ref, gv_part_ref, *refs,
 ):
-    attn_ref, gq_ref, gk_ref, gv_ref, bias_ref, tail_ref = refs[-6:]
+    attn_ref, gq_ref, gk_ref, gv_ref, bias_ref, tail_ref, before_ref, after_ref = refs[-8:]
     tok, width = k_ref.shape
     columns = head_columns(width)
     heads = len(columns)
@@ -278,6 +278,9 @@
         bias_ref[...] = bias_by_query(lengths, first, prior, first - prior, 2 * prior)
         tail_ref[...] = bias_by_key(lengths, first + tok, prior, first + tok - prior, prior)
 
+    odd = odd_ref[0] == 1
+    before_ref[...] = jnp.where(odd, even_pair_ref[0], odd_pair_ref[0])
+    after_ref[...] = jnp.where(odd, odd_pair_ref[0], even_pair_ref[0])
     bias, tail = bias_ref[...], tail_ref[...]
     early, late = slice(0, prior), slice(tok - prior, tok)
     second = slice(prior, 2 * prior)
@@ -332,27 +335,28 @@
     groups = width // step
     per = step // HEAD_DIM
     lengths = module_lengths.reshape(1, -1)
-    len_spec = pl.BlockSpec(lengths.shape, lambda g: (0, 0))
+    len_spec = pl.BlockSpec(lengths.shape, lambda g, *_: (0, 0))
     keep = pl.BlockSpec(memory_space=pl.ANY)
     full16 = jax.ShapeDtypeStruct((tok, width), jnp.bfloat16)
     full32 = jax.ShapeDtypeStruct((tok, width), jnp.float32)
 
-    def rows(count, at, base=0):
-        return pl.BlockSpec((count, step), lambda g: (at, g + base))
-
-    def stats(base=0):
-        return pl.BlockSpec((1, 2 * per, prior), lambda g: (g + base, 0, 0))
-
-    def halos(cols, after=None):
-        k, v = key_in[tok - prior :, cols], value_in[tok - prior :, cols]
-        q, do = query_in[:prior, cols], grad_out[:prior, cols]
-        if after is not None:
-            k, v, q, do, _ = lax.optimization_barrier((k, v, q, do, after))
-        return neighbour(jnp.concatenate([k, v]), 1), neighbour(jnp.concatenate([q, do]), -1)
-
-    cuts = [0, groups // 2, groups] if groups > 1 else [0, groups]
-    spans = list(zip(cuts[:-1], cuts[1:]))
-    moved = [halos(slice(spans[0][0] * step, spans[0][1] * step))]
+    def rows(count, at):
+        return pl.BlockSpec((count, step), lambda g, *_: (at, g))
+
+    stats = pl.BlockSpec((1, 2 * per, prior), lambda g, *_: (g, 0, 0))
+
+    peers = lax.axis_size("seq") * lax.axis_size("head")
+    odd = lax.axis_index("head") % 2
+    late_kv = jnp.concatenate([key_in[tok - prior :], value_in[tok - prior :]])
+    early_qd = jnp.concatenate([query_in[:prior], grad_out[:prior]])
+    even_pairs = [[i, i + 1] for i in range(0, peers, 2)]
+    odd_pairs = [[i, (i + 1) % peers] for i in range(1, peers, 2)]
+    even_gather = lax.all_gather(
+        jnp.where(odd == 0, late_kv, early_qd), ("seq", "head"), axis_index_groups=even_pairs
+    )
+    odd_gather = lax.all_gather(
+        jnp.where(odd == 0, early_qd, late_kv), ("seq", "head"), axis_index_groups=odd_pairs
+    )
 
     attn, gq, gk_part, gv_part, stat = pl.pallas_call(
         functools.partial(own_kernel, prior),
@@ -360,7 +364,7 @@
         in_specs=[len_spec, rows(tok, 0), rows(tok, 0), rows(tok, 0), rows(tok, 0)],
         out_specs=[
             rows(prior, tok // prior - 1), rows(prior, tok // prior - 1),
-            rows(tok, 0), rows(tok, 0), stats(),
+            rows(tok, 0), rows(tok, 0), stats,
         ],
         out_shape=[
             full16, full16, full32, full32,
@@ -374,37 +378,34 @@
         name="own_block",
     )(lengths, query_in, key_in, value_in, grad_out)
     stat_after = neighbour(stat, -1)
-    for low, high in spans[1:]:
-        moved.append(halos(slice(low * step, high * step), stat))
-
-    outs = [attn, gq]
-    for (low, high), (before, after) in zip(spans, moved):
-        outs = pl.pallas_call(
-            functools.partial(edge_kernel, prior),
-            grid=(high - low,),
+
+    return pl.pallas_call(
+        functools.partial(edge_kernel, prior),
+        grid_spec=pltpu.PrefetchScalarGridSpec(
+            num_scalar_prefetch=1,
+            grid=(groups,),
             in_specs=[
-                len_spec, rows(prior, 0, low), rows(tok, 0, low), rows(tok, 0, low),
-                rows(prior, 0, low), rows(2 * prior, 0), rows(2 * prior, 0), stats(low),
-                rows(tok, 0, low), rows(tok, 0, low), *[keep] * len(outs),
+                len_spec, rows(prior, 0), rows(tok, 0), rows(tok, 0), rows(prior, 0),
+                pl.BlockSpec((1, 2 * prior, step), lambda g, odd: (1 - odd[0], 0, g)),
+                pl.BlockSpec((1, 2 * prior, step), lambda g, odd: (odd[0], 0, g)),
+                stats, rows(tok, 0), rows(tok, 0), keep, keep,
             ],
-            out_specs=[
-                rows(prior, 0, low), rows(prior, 0, low), rows(tok, 0, low), rows(tok, 0, low),
-            ],
-            out_shape=[full16] * 4,
+            out_specs=[rows(prior, 0), rows(prior, 0), rows(tok, 0), rows(tok, 0)],
             scratch_shapes=[
                 pltpu.VMEM((prior, 2 * prior), jnp.float32),
                 pltpu.VMEM((prior, prior), jnp.float32),
+                pltpu.VMEM((2 * prior, step), jnp.bfloat16),
+                pltpu.VMEM((2 * prior, step), jnp.bfloat16),
             ],
-            input_output_aliases={10 + i: i for i in range(len(outs))},
-            cost_estimate=cost(
-                (high - low) * per, prior, 2 * prior, 7, 20 * tok * step * (high - low)
-            ),
-            name="edges",
-        )(
-            lengths, query_in, key_in, value_in, grad_out, before, after, stat_after,
-            gk_part, gv_part, *outs,
-        )
-    return tuple(outs)
+        ),
+        out_shape=[full16] * 4,
+        input_output_aliases={11: 0, 12: 1},
+        cost_estimate=cost(heads, prior, 2 * prior, 7, 20 * tok * width),
+        name="edges",
+    )(
+        odd.astype(jnp.int32).reshape(1), lengths, query_in, key_in, value_in, grad_out,
+        even_gather, odd_gather, stat_after, gk_part, gv_part, attn, gq,
+    )
 
 
 def shards(query_in, key_in, value_in, grad_out, module_lengths):

time: 42.6 us -> 71.9 us (1.69)
  waiting for transfers between devices: 9.05 us -> 41 us
  starting transfers between devices: 14.9 us -> 1.37 us
  between operations: 0.81 us -> 14.1 us
  Pallas kernels: 14.3 us -> 12.5 us
  local copies, waits for them, and re-layouts: 2.85 us -> 1.39 us
  other arithmetic: 0.08 us -> 1.21 us
    all_gather x0 -> x2, waiting for transfers between devices: none -> 34.7 us  [the longest x1 25.7 us: halo_shards(): lax.all_gather(jnp.where(odd == 0, late_kv, early_qd), ('seq', 'head'), a...]
    ppermute x5 -> x1, starting transfers between devices: 14.9 us -> 1.29 us  [neighbour(): return lax.ppermute(value, ('seq', 'head'), pairs)]
    ppermute x5 -> x1, waiting for transfers between devices: 9.05 us -> 5.63 us  [neighbour(): return lax.ppermute(value, ('seq', 'head'), pairs)]
    pallas_call x2 -> x1, Pallas kernels: 8.61 us -> 6.81 us  [halo_shards(): pl.pallas_call(functools.partial(edge_kernel, prior), grid_spec=pltpu.Pre...]
    unnamed x16 -> x6, local copies, waits for them, and re-layouts: 1.63 us -> 0.19 us
    slice x2 -> x0, local copies, waits for them, and re-layouts: 1.23 us -> none  [the longest x1 1.19 us: halos(): q, do = (query_in[:prior, cols], grad_out[:prior, cols])]
    select_n x0 -> x1, other arithmetic: none -> 1.21 us  [halo_shards(): jnp.where(odd == 0, early_qd, late_kv)]
    concatenate x0 -> x2, local copies, waits for them, and re-layouts: none -> 1.19 us  [the longest x1 1.15 us: halo_shards(): early_qd = jnp.concatenate([query_in[:prior], grad_out[:prior]])]
  transfers between devices with their start and end apart: 5 -> 3, of which waited for: 1 -> 3; matrix products, arithmetic and copies ran while one was open for 0% -> 0% of each run, Pallas kernels for 24% -> 8%
where the time goes in v3:
time: 71.9 us; the launch traced here: 71.6 us
  waiting for transfers between devices  41 us (57%)
  between operations  14.1 us (20%)
  Pallas kernels  12.5 us (17%)
  local copies, waits for them, and re-layouts  1.39 us (2%)
  starting transfers between devices  1.37 us (2%)
  other arithmetic  1.21 us (2%)
    all_gather x1, waiting for transfers between devices, halo_shards(): lax.all_gather(jnp.where(odd == 0, late_kv, early_qd), ('seq', 'head'), a...  25.7 us
    all_gather x1, waiting for transfers between devices, halo_shards(): lax.all_gather(jnp.where(odd == 0, early_qd, late_kv), ('seq', 'head'), a...  8.98 us
    pallas_call x1, Pallas kernels, halo_shards(): pl.pallas_call(functools.partial(edge_kernel, prior), grid_spec=pltpu.Pre...  6.81 us
    pallas_call x1, Pallas kernels, halo_shards(): pl.pallas_call(functools.partial(own_kernel, prior), grid=(groups,), in_s...  5.72 us
    ppermute x1, waiting for transfers between devices, neighbour(): return lax.ppermute(value, ('seq', 'head'), pairs)  5.63 us
  transfers between devices with their start and end apart: 3, of which 3 were waited for; matrix products, arithmetic and copies ran while one was open for 0% of the time, Pallas kernels for 8%

profile of v3, /device:TPU:0, one launch (start us, length us, event | category | flops | bytes accessed | tf_op | source)
XLA Modules:
  0.0 71.6 jit_solution(17450833344236318641)
XLA Ops:
  7.2 0.0 all-gather.5.cloned.1.call-start
  7.2 0.0 copy-start
  7.2 0.0 copy-start.1
  7.2 1.2 %slice_bitcast_fusion = (bf16[1,64,2048]{2,1,0:T(8,128)(2,1)S(1)}, bf16[1,64,2048]{2,1,0:T(8,128)(2,1)S(1)}) fusion(bf16[128,2048]{1,0:T(8,128)(2,1)} %do_ref.3, bf16[128,2048]{1,0:T(8,128)(2,1)} %q_ref.3), kind=kLoop, calls=%fused_computation.4 | loop fusion | bytes 1048576 | tf_op jit(solution)/shard_map/concatenate | solution.py:351
  8.4 0.0 copy-done
  8.4 0.2 copy-done.1
  8.6 1.2 %broadcast_select_fusion = (bf16[1,128,2048]{2,1,0:T(8,128)(2,1)}, bf16[1,128,2048]{2,1,0:T(8,128)(2,1)}) fusion(pred[]{:T(512)S(6)} %eq.6, bf16[1,64,2048]{2,1,0:T(8,128)(2,1)S(1)} %get-tuple-element.16, bf16[1,64,2048]{2,1,0:T(8,128)(2,1)S(1)} %get-tuple-element.17, bf16[1,64,2048]{2,1,0:T(8,128)(2,1)S(1)} %get-tuple-element.18, ...), kind=kLoop, calls=%fused_computation.2 | loop fusion | flops 2621440 | bytes 2097153 | tf_op jit(solution)/shard_map/jit(_where)/select_n | solution.py:358
  9.8 0.0 all-gather.5.cloned.1.call-update
  9.9 0.0 all-gather.3.cloned.1.call-start
  9.9 0.7 all-gather.3.cloned.1.call-update
  10.6 5.7 %own_block.1 = (bf16[128,2048]{1,0:T(8,128)(2,1)}, bf16[128,2048]{1,0:T(8,128)(2,1)}, f32[128,2048]{1,0:T(8,128)}, f32[128,2048]{1,0:T(8,128)}, f32[4,8,64]{2,1,0:T(8,128)}) custom-call(s32[1,128]{1,0:T(1,128)} %bitcast.10, bf16[128,2048]{1,0:T(8,128)(2,1)} %q_ref.3, bf16[128,2048]{1,0:T(8,128)(2,1)} %k_ref.3, bf16[128,2048]{1,0:T(8,128)(2,1)} %v_ref.3, ...), custom_call_target="tpu_custom_call" | custom-call | flops 268435456 | bytes 6291456 | tf_op jit(solution)/shard_map/own_block/pallas_call | solution.py:361
  16.3 1.3 %collective-permute-start = (f32[4,8,64]{2,1,0:T(8,128)}, f32[4,8,64]{2,1,0:T(8,128)S(1)}, u32[]{:S(2)}, u32[]{:S(2)}) collective-permute-start(f32[4,8,64]{2,1,0:T(8,128)} %get-tuple-element.9), channel_id=1, source_target_pairs={{1,0},{2,1},{3,2},{4,3},{5,4},{6,5},{7,6},{8,7},{9,8},{10,9},{11,1... | collective-permute-start | bytes 24584 | tf_op jit(solution)/shard_map/ppermute | solution.py:319
  17.6 5.6 %collective-permute-done.stat_ref = f32[4,8,64]{2,1,0:T(8,128)S(1)} collective-permute-done((f32[4,8,64]{2,1,0:T(8,128)}, f32[4,8,64]{2,1,0:T(8,128)S(1)}, u32[]{:S(2)}, u32[]{:S(2)}) %collective-permute-start) | collective-permute-done | bytes 8224 | tf_op jit(solution)/shard_map/ppermute | solution.py:319
  23.3 0.0 copy-start.2
  23.3 9.0 %all-gather.5.cloned.1.call-done.odd_pair_ref = bf16[2,128,2048]{2,1,0:T(8,128)(2,1)} async-done(((bf16[1,128,2048]{2,1,0:T(8,128)(2,1)}), bf16[2,128,2048]{2,1,0:T(8,128)(2,1)}) %all-gather.5.cloned.1.call-update) | async-done | bytes 1048592 | tf_op jit(solution)/shard_map/all_gather | solution.py:357
  32.3 25.7 %all-gather.3.cloned.1.call-done.even_pair_ref = bf16[2,128,2048]{2,1,0:T(8,128)(2,1)} async-done(((bf16[1,128,2048]{2,1,0:T(8,128)(2,1)}), bf16[2,128,2048]{2,1,0:T(8,128)(2,1)}) %all-gather.3.cloned.1.call-update) | async-done | bytes 1048592 | tf_op jit(solution)/shard_map/all_gather | solution.py:354
  58.0 0.0 copy-done.2
  58.0 6.8 %edges.1 = (bf16[128,2048]{1,0:T(8,128)(2,1)}, bf16[128,2048]{1,0:T(8,128)(2,1)}, bf16[128,2048]{1,0:T(8,128)(2,1)}, bf16[128,2048]{1,0:T(8,128)(2,1)}) custom-call(s32[1]{0:T(128)} %bitcast.odd_ref, s32[1,128]{1,0:T(1,128)} %bitcast.11, bf16[128,2048]{1,0:T(8,128)(2,1)} %q_ref.3, ...), custom_call_target="tpu_custom_call", output_to_operand_aliasing={{0}: (11, {}), {1}: (12, {})} | custom-call | flops 234881024 | bytes 5242880 | tf_op jit(solution)/shard_map/edges/pallas_call | solution.py:382
  (1 shorter events, 0.0 us)
Async XLA Ops:
  7.2 25.1 %all-gather.5.cloned.1.call-start = ((), (), s32[]{:S(2)}) async-start(), calls=%async_computation.1 | async-start | bytes 1572864 | tf_op jit(solution)/shard_map/all_gather | solution.py:357
  7.2 1.2 %copy-start = (bf16[128,2048]{1,0:T(8,128)(2,1)S(1)}, bf16[128,2048]{1,0:T(8,128)(2,1)}, u32[]{:S(2)}) copy-start(bf16[128,2048]{1,0:T(8,128)(2,1)} %k_ref.3) | copy-start | bytes 1572868
  7.2 1.3 %copy-start.1 = (bf16[128,2048]{1,0:T(8,128)(2,1)S(1)}, bf16[128,2048]{1,0:T(8,128)(2,1)}, u32[]{:S(2)}) copy-start(bf16[128,2048]{1,0:T(8,128)(2,1)} %v_ref.3) | copy-start | bytes 1572868
  9.9 48.1 %all-gather.3.cloned.1.call-start = ((), (), s32[]{:S(2)}) async-start(), calls=%async_computation | async-start | bytes 1572864 | tf_op jit(solution)/shard_map/all_gather | solution.py:354
  16.3 6.9 %collective-permute-start = (f32[4,8,64]{2,1,0:T(8,128)}, f32[4,8,64]{2,1,0:T(8,128)S(1)}, u32[]{:S(2)}, u32[]{:S(2)}) collective-permute-start(f32[4,8,64]{2,1,0:T(8,128)} %get-tuple-element.9), channel_id=1, source_target_pairs={{1,0},{2,1},{3,2},{4,3},{5,4},{6,5},{7,6},{8,7},{9,8},{10,9},{11,1... | collective-permute-start | bytes 24584 | tf_op jit(solution)/shard_map/ppermute | solution.py:319
  23.3 34.7 %copy-start.2 = (f32[4,8,64]{2,1,0:T(8,128)}, f32[4,8,64]{2,1,0:T(8,128)S(1)}, u32[]{:S(2)}) copy-start(f32[4,8,64]{2,1,0:T(8,128)S(1)} %collective-permute-done.stat_ref) | copy-start | bytes 24580
Sparse Core Ops, SparseCore 0:
  10.1 22.0 all-gather.4
  34.4 23.5 all-gather.2

commit v4 on v2

--- a/solution.py
+++ b/solution.py
@@ -12,6 +12,7 @@
 SCALE = HEAD_DIM ** (-0.5)
 LOG2E = math.log2(math.e)
 MASKED = -1e30
+STAT_ROWS = 16
 
 
 def shifted(value, axis, by):
@@ -221,93 +222,121 @@
     return place * tok
 
 
+def split_bf16(value, terms):
+    parts = []
+    for _ in range(terms):
+        part = value.astype(jnp.bfloat16)
+        parts.append(part.astype(jnp.float32))
+        value = value - parts[-1]
+    return parts
+
+
+def first_kernel(tok, prior, len_ref, q_ref, k_ref, v_ref, do_ref, out_ref, bias_ref):
+    columns = head_columns(q_ref.shape[1])
+
+    @pl.when(pl.program_id(0) == 0)
+    def _():
+        first = device_first(tok)
+        lengths = len_ref[...].astype(jnp.float32)
+        bias_ref[...] = bias_by_key(lengths, first, prior, first, prior)
+
+    out_ref[:prior, :] = q_ref[...]
+    out_ref[prior : 2 * prior, :] = do_ref[...]
+    bias = bias_ref[...]
+    pairs = [by_query(k_ref[:, c], q_ref[:, c], v_ref[:, c], do_ref[:, c], bias) for c in columns]
+    tops = [jnp.max(s, axis=0, keepdims=True) for s, _ in pairs]
+    raws = [jnp.exp2(s - top) for (s, _), top in zip(pairs, tops)]
+    totals = [jnp.sum(raw, axis=0, keepdims=True) for raw in raws]
+    sums = [jnp.sum(raw * dp, axis=0, keepdims=True) for raw, (_, dp) in zip(raws, pairs)]
+    for c, top, total, summed in zip(columns, tops, totals, sums):
+        rows = split_bf16(top + jnp.log2(total), 3) + split_bf16(summed / total, 2)
+        rows.append(jnp.zeros((STAT_ROWS - len(rows), prior), jnp.float32))
+        block = jnp.concatenate(rows, axis=0)
+        block = jnp.concatenate([block, jnp.zeros_like(block)], axis=1)
+        out_ref[2 * prior :, c] = block.astype(jnp.bfloat16)
+
+
 def own_kernel(
-    prior, len_ref, q_ref, k_ref, v_ref, do_ref,
-    attn_ref, gq_ref, gk_ref, gv_ref, stat_ref, bias_ref, lead_ref,
+    prior, len_ref, q_ref, k_ref, v_ref, do_ref, attn_ref, gq_ref, gk_ref, gv_ref, bias_ref
 ):
-    tok, width = q_ref.shape
+    tok, width = k_ref.shape
     rest = tok - prior
     columns = head_columns(width)
-    heads = len(columns)
 
     @pl.when(pl.program_id(0) == 0)
     def _():
         first = device_first(tok)
         lengths = len_ref[...].astype(jnp.float32)
         bias_ref[...] = bias_by_query(lengths, first + prior, rest, first, tok)
-        lead_ref[...] = bias_by_key(lengths, first, prior, first, prior)
-
-    bias, lead = bias_ref[...], lead_ref[...]
-    late = slice(prior, tok)
-    early = slice(0, prior)
-    pairs = [
-        by_query(q_ref[late, c], k_ref[:, c], do_ref[late, c], v_ref[:, c], bias) for c in columns
-    ]
-    leads = [
-        by_query(k_ref[early, c], q_ref[early, c], v_ref[early, c], do_ref[early, c], lead)
-        for c in columns
-    ]
+
+    bias = bias_ref[...]
+    pairs = [by_query(q_ref[:, c], k_ref[:, c], do_ref[:, c], v_ref[:, c], bias) for c in columns]
     weights, grads = full_rows(pairs)
     for c, w, g in zip(columns, weights, grads):
         attn_ref[:, c] = dot(w, v_ref[:, c], 1, 0).astype(jnp.bfloat16)
         gq_ref[:, c] = dot(g, k_ref[:, c], 1, 0).astype(jnp.bfloat16)
-        gk_ref[:, c] = dot(g, q_ref[late, c], 0, 0)
-        gv_ref[:, c] = dot(w, do_ref[late, c], 0, 0)
-    tops = [jnp.max(s, axis=0, keepdims=True) for s, _ in leads]
-    raws = [jnp.exp2(s - top) for (s, _), top in zip(leads, tops)]
-    totals = [jnp.sum(raw, axis=0, keepdims=True) for raw in raws]
-    sums = [jnp.sum(raw * dp, axis=0, keepdims=True) for raw, (_, dp) in zip(raws, leads)]
-    for h in range(heads):
-        stat_ref[0, h : h + 1, :] = tops[h] + jnp.log2(totals[h])
-        stat_ref[0, heads + h : heads + h + 1, :] = sums[h] / totals[h]
-
-
-def edge_kernel(
-    prior, len_ref, q_ref, k_ref, v_ref, do_ref, before_ref, after_ref, stat_ref,
-    gk_part_ref, gv_part_ref, *refs,
+        gk_ref[:, c] = dot(g, q_ref[:, c], 0, 0)
+        gv_ref[:, c] = dot(w, do_ref[:, c], 0, 0)
+
+
+def lead_kernel(
+    prior, len_ref, q_ref, k_ref, v_ref, do_ref, before_ref, gk_part_ref, gv_part_ref,
+    attn_in, gq_in, attn_ref, gq_ref, gk_ref, gv_ref, bias_ref,
 ):
-    attn_ref, gq_ref, gk_ref, gv_ref, bias_ref, tail_ref = refs[-6:]
-    tok, width = k_ref.shape
-    columns = head_columns(width)
-    heads = len(columns)
+    columns = head_columns(q_ref.shape[1])
 
     @pl.when(pl.program_id(0) == 0)
     def _():
-        first = device_first(tok)
+        first = device_first(attn_in.shape[0])
         lengths = len_ref[...].astype(jnp.float32)
         bias_ref[...] = bias_by_query(lengths, first, prior, first - prior, 2 * prior)
-        tail_ref[...] = bias_by_key(lengths, first + tok, prior, first + tok - prior, prior)
-
-    bias, tail = bias_ref[...], tail_ref[...]
-    early, late = slice(0, prior), slice(tok - prior, tok)
-    second = slice(prior, 2 * prior)
-    keys = [jnp.concatenate([before_ref[early, c], k_ref[early, c]], axis=0) for c in columns]
-    values = [jnp.concatenate([before_ref[second, c], v_ref[early, c]], axis=0) for c in columns]
-    leads = [
+
+    bias = bias_ref[...]
+    early, late = slice(0, prior), slice(prior, 2 * prior)
+    keys = [jnp.concatenate([before_ref[early, c], k_ref[:, c]], axis=0) for c in columns]
+    values = [jnp.concatenate([before_ref[late, c], v_ref[:, c]], axis=0) for c in columns]
+    pairs = [
         by_query(q_ref[:, c], k, do_ref[:, c], v, bias) for c, k, v in zip(columns, keys, values)
     ]
-    tails = [
-        by_query(k_ref[late, c], after_ref[early, c], v_ref[late, c], after_ref[second, c], tail)
-        for c in columns
-    ]
-    own = [
-        (stat_ref[0, h : h + 1, :], stat_ref[0, heads + h : heads + h + 1, :])
-        for h in range(heads)
-    ]
-    weights, grads = full_rows(leads)
-    tail_weights, tail_grads = merged_rows(tails, own)
+    weights, grads = full_rows(pairs)
     for c, w, g, k, v in zip(columns, weights, grads, keys, values):
         attn_ref[:, c] = dot(w, v, 1, 0).astype(jnp.bfloat16)
         gq_ref[:, c] = dot(g, k, 1, 0).astype(jnp.bfloat16)
-        gk = gk_part_ref[early, c] + dot(g[:, second], q_ref[:, c], 0, 0)
-        gv = gv_part_ref[early, c] + dot(w[:, second], do_ref[:, c], 0, 0)
-        gk_ref[early, c] = gk.astype(jnp.bfloat16)
-        gv_ref[early, c] = gv.astype(jnp.bfloat16)
-    for c, w, g in zip(columns, tail_weights, tail_grads):
-        gk = gk_part_ref[late, c] + dot(g, after_ref[early, c], 1, 0)
-        gv = gv_part_ref[late, c] + dot(w, after_ref[second, c], 1, 0)
-        gk_ref[late, c] = gk.astype(jnp.bfloat16)
-        gv_ref[late, c] = gv.astype(jnp.bfloat16)
+        gk = gk_part_ref[:, c] + dot(g[:, late], q_ref[:, c], 0, 0)
+        gv = gv_part_ref[:, c] + dot(w[:, late], do_ref[:, c], 0, 0)
+        gk_ref[:, c] = gk.astype(jnp.bfloat16)
+        gv_ref[:, c] = gv.astype(jnp.bfloat16)
+
+
+def tail_kernel(
+    prior, len_ref, k_ref, v_ref, after_ref, gk_part_ref, gv_part_ref,
+    gk_in, gv_in, gk_ref, gv_ref, bias_ref,
+):
+    columns = head_columns(k_ref.shape[1])
+
+    @pl.when(pl.program_id(0) == 0)
+    def _():
+        tok = gk_in.shape[0]
+        first = device_first(tok)
+        lengths = len_ref[...].astype(jnp.float32)
+        bias_ref[...] = bias_by_key(lengths, first + tok, prior, first + tok - prior, prior)
+
+    bias = bias_ref[...]
+    early, late = slice(0, prior), slice(prior, 2 * prior)
+    pairs = [
+        by_query(k_ref[:, c], after_ref[early, c], v_ref[:, c], after_ref[late, c], bias)
+        for c in columns
+    ]
+    own = []
+    for c in columns:
+        stat = after_ref[2 * prior :, c].astype(jnp.float32)[:, :prior]
+        own.append((stat[0:1] + stat[1:2] + stat[2:3], stat[3:4] + stat[4:5]))
+    weights, grads = merged_rows(pairs, own)
+    for c, w, g in zip(columns, weights, grads):
+        gk = gk_part_ref[:, c] + dot(g, after_ref[early, c], 1, 0)
+        gv = gv_part_ref[:, c] + dot(w, after_ref[late, c], 1, 0)
+        gk_ref[:, c] = gk.astype(jnp.bfloat16)
+        gv_ref[:, c] = gv.astype(jnp.bfloat16)
 
 
 def neighbour(value, by):
@@ -336,75 +365,59 @@
     keep = pl.BlockSpec(memory_space=pl.ANY)
     full16 = jax.ShapeDtypeStruct((tok, width), jnp.bfloat16)
     full32 = jax.ShapeDtypeStruct((tok, width), jnp.float32)
-
-    def rows(count, at, base=0):
+    late_at = tok // prior - 1
+
+    def rows(count, at=0, base=0):
         return pl.BlockSpec((count, step), lambda g: (at, g + base))
 
-    def stats(base=0):
-        return pl.BlockSpec((1, 2 * per, prior), lambda g: (g + base, 0, 0))
-
-    def halos(cols, after=None):
-        k, v = key_in[tok - prior :, cols], value_in[tok - prior :, cols]
-        q, do = query_in[:prior, cols], grad_out[:prior, cols]
-        if after is not None:
-            k, v, q, do, _ = lax.optimization_barrier((k, v, q, do, after))
-        return neighbour(jnp.concatenate([k, v]), 1), neighbour(jnp.concatenate([q, do]), -1)
+    def call(kernel, name, grid, ins, outs, shapes, bias, products, moved, aliases=None):
+        return pl.pallas_call(
+            functools.partial(kernel, prior),
+            grid=(grid,),
+            in_specs=[len_spec, *ins],
+            out_specs=outs,
+            out_shape=shapes,
+            scratch_shapes=[pltpu.VMEM(bias, jnp.float32)],
+            input_output_aliases=aliases or {},
+            cost_estimate=cost(grid * per, *bias, products, moved * grid * step),
+            name=name,
+        )
+
+    before = neighbour(jnp.concatenate([key_in[tok - prior :], value_in[tok - prior :]]), 1)
 
     cuts = [0, groups // 2, groups] if groups > 1 else [0, groups]
     spans = list(zip(cuts[:-1], cuts[1:]))
-    moved = [halos(slice(spans[0][0] * step, spans[0][1] * step))]
-
-    attn, gq, gk_part, gv_part, stat = pl.pallas_call(
-        functools.partial(own_kernel, prior),
-        grid=(groups,),
-        in_specs=[len_spec, rows(tok, 0), rows(tok, 0), rows(tok, 0), rows(tok, 0)],
-        out_specs=[
-            rows(prior, tok // prior - 1), rows(prior, tok // prior - 1),
-            rows(tok, 0), rows(tok, 0), stats(),
-        ],
-        out_shape=[
-            full16, full16, full32, full32,
-            jax.ShapeDtypeStruct((groups, 2 * per, prior), jnp.float32),
-        ],
-        scratch_shapes=[
-            pltpu.VMEM((tok - prior, tok), jnp.float32),
-            pltpu.VMEM((prior, prior), jnp.float32),
-        ],
-        cost_estimate=cost(heads, tok, tok, 4, 24 * tok * width),
-        name="own_block",
+    sent = 2 * prior + STAT_ROWS
+    afters = []
+    for low, high in spans:
+        packed = call(
+            functools.partial(first_kernel, tok), "first_rows", high - low, [rows(prior, 0, low)] * 4, rows(sent),
+            jax.ShapeDtypeStruct((sent, (high - low) * step), jnp.bfloat16), (prior, prior), 2,
+            12 * prior,
+        )(lengths, query_in, key_in, value_in, grad_out)
+        afters.append(neighbour(packed, -1))
+
+    attn, gq, gk_part, gv_part = call(
+        own_kernel, "own_block", groups,
+        [rows(prior, late_at), rows(tok), rows(tok), rows(prior, late_at)],
+        [rows(prior, late_at), rows(prior, late_at), rows(tok), rows(tok)],
+        [full16, full16, full32, full32], (tok - prior, tok), 6, 18 * tok,
     )(lengths, query_in, key_in, value_in, grad_out)
-    stat_after = neighbour(stat, -1)
-    for low, high in spans[1:]:
-        moved.append(halos(slice(low * step, high * step), stat))
-
-    outs = [attn, gq]
-    for (low, high), (before, after) in zip(spans, moved):
-        outs = pl.pallas_call(
-            functools.partial(edge_kernel, prior),
-            grid=(high - low,),
-            in_specs=[
-                len_spec, rows(prior, 0, low), rows(tok, 0, low), rows(tok, 0, low),
-                rows(prior, 0, low), rows(2 * prior, 0), rows(2 * prior, 0), stats(low),
-                rows(tok, 0, low), rows(tok, 0, low), *[keep] * len(outs),
-            ],
-            out_specs=[
-                rows(prior, 0, low), rows(prior, 0, low), rows(tok, 0, low), rows(tok, 0, low),
-            ],
-            out_shape=[full16] * 4,
-            scratch_shapes=[
-                pltpu.VMEM((prior, 2 * prior), jnp.float32),
-                pltpu.VMEM((prior, prior), jnp.float32),
-            ],
-            input_output_aliases={10 + i: i for i in range(len(outs))},
-            cost_estimate=cost(
-                (high - low) * per, prior, 2 * prior, 7, 20 * tok * step * (high - low)
-            ),
-            name="edges",
-        )(
-            lengths, query_in, key_in, value_in, grad_out, before, after, stat_after,
-            gk_part, gv_part, *outs,
-        )
-    return tuple(outs)
+
+    attn, gq, gk, gv = call(
+        lead_kernel, "lead_rows", groups,
+        [rows(prior)] * 4 + [rows(2 * prior), rows(prior), rows(prior), keep, keep],
+        [rows(prior)] * 4, [full16] * 4, (prior, 2 * prior), 5, 14 * tok, {8: 0, 9: 1},
+    )(lengths, query_in, key_in, value_in, grad_out, before, gk_part, gv_part, attn, gq)
+
+    for (low, high), after in zip(spans, afters):
+        late = rows(prior, late_at, low)
+        gk, gv = call(
+            tail_kernel, "tail_keys", high - low,
+            [late, late, rows(sent), late, late, keep, keep],
+            [late, late], [full16] * 2, (prior, prior), 4, 10 * tok, {6: 0, 7: 1},
+        )(lengths, key_in, value_in, after, gk_part, gv_part, gk, gv)
+    return (attn, gq, gk, gv)
 
 
 def shards(query_in, key_in, value_in, grad_out, module_lengths):

time: 42.6 us -> 39.5 us (0.927)
  starting transfers between devices: 14.9 us -> 7.44 us
  Pallas kernels: 14.3 us -> 21.7 us
  waiting for transfers between devices: 9.05 us -> 5.95 us
    ppermute x5 -> x3, starting transfers between devices: 14.9 us -> 7.44 us  [neighbour(): return lax.ppermute(value, ('seq', 'head'), pairs)]
    pallas_call x3 -> x6, Pallas kernels: 14.3 us -> 21.7 us  [the longest x1 6.23 us: halo_shards(): call(lead_kernel, 'lead_rows', groups, [rows(prior)] * 4 + [rows(2 * prio...]
    ppermute x5 -> x3, waiting for transfers between devices: 9.05 us -> 5.95 us  [neighbour(): return lax.ppermute(value, ('seq', 'head'), pairs)]
    unnamed x16 -> x6, local copies, waits for them, and re-layouts: 1.63 us -> 2.21 us
    slice x2 -> x4, local copies, waits for them, and re-layouts: 1.23 us -> 1.02 us  [the longest x2 0.93 us: halo_shards(): key_in[tok - prior:]]
  transfers between devices with their start and end apart: 5 -> 3, of which waited for: 1 -> 1; matrix products, arithmetic and copies ran while one was open for 0% -> 0% of each run, Pallas kernels for 24% -> 49%
where the time goes in v4:
time: 39.5 us; the launch traced here: 39 us
  Pallas kernels  21.7 us (55%)
  starting transfers between devices  7.44 us (19%)
  waiting for transfers between devices  5.95 us (15%)
  local copies, waits for them, and re-layouts  3.23 us (8%)
  between operations  0.71 us (2%)
    ppermute x3, starting transfers between devices, neighbour(): return lax.ppermute(value, ('seq', 'head'), pairs)  7.44 us
    pallas_call x1, Pallas kernels, halo_shards(): call(lead_kernel, 'lead_rows', groups, [rows(prior)] * 4 + [rows(2 * prio...  6.23 us
    ppermute x3, waiting for transfers between devices, neighbour(): return lax.ppermute(value, ('seq', 'head'), pairs)  5.95 us
    pallas_call x1, Pallas kernels, halo_shards(): call(own_kernel, 'own_block', groups, [rows(prior, late_at), rows(tok), r...  5.54 us
    pallas_call x2, Pallas kernels, halo_shards(): call(tail_kernel, 'tail_keys', high - low, [late, late, rows(sent), late,...  5.36 us
    pallas_call x2, Pallas kernels, halo_shards(): call(functools.partial(first_kernel, tok), 'first_rows', high - low, [row...  4.54 us
    unnamed x6, local copies, waits for them, and re-layouts  2.21 us
    slice x2, local copies, waits for them, and re-layouts, halo_shards(): key_in[tok - prior:]  0.93 us
  transfers between devices with their start and end apart: 3, of which 1 were waited for; matrix products, arithmetic and copies ran while one was open for 0% of the time, Pallas kernels for 49%

profile of v4, /device:TPU:0, one launch (start us, length us, event | category | flops | bytes accessed | tf_op | source)
XLA Modules:
  0.0 39.0 jit_solution(11379442751583291374)
XLA Ops:
  0.6 0.0 slice-start
  0.6 0.0 slice-start.1
  0.7 0.9 %slice-done = bf16[64,2048]{1,0:T(8,128)(2,1)S(1)} async-done(((bf16[128,2048]{1,0:T(8,128)(2,1)}), bf16[64,2048]{1,0:T(8,128)(2,1)S(1)}, s32[]{:S(2)}) %slice-start) | async-done | bytes 262168 | tf_op jit(solution)/shard_map/slice | solution.py:386
  1.6 0.1 slice-done.1
  1.7 4.9 %collective-permute-start = (bf16[128,2048]{1,0:T(8,128)(2,1)S(1)}, bf16[128,2048]{1,0:T(8,128)(2,1)S(1)}, u32[]{:S(2)}, u32[]{:S(2)}) collective-permute-start(bf16[128,2048]{1,0:T(8,128)(2,1)S(1)} %pad_maximum_fusion), channel_id=1, source_target_pairs={{0,1},{1,2},{2,3},{3,4},{4,5},{5,6},{6,7},{7,8},{8,9},{9,10},{10,1... | collective-permute-start | bytes 1572872 | tf_op jit(solution)/shard_map/ppermute | solution.py:345
  6.6 2.3 %first_rows.3 = bf16[144,1024]{1,0:T(8,128)(2,1)} custom-call(s32[1,128]{1,0:T(1,128)} %bitcast.1, bf16[128,2048]{1,0:T(8,128)(2,1)} %q_ref.7, bf16[128,2048]{1,0:T(8,128)(2,1)} %k_ref.11, bf16[128,2048]{1,0:T(8,128)(2,1)} %v_ref.11, bf16[128,2048]{1,0:T(8,128)(2,1)} %do_ref.7), custom_call_target="tpu_custom_call" | custom-call | flops 16777216 | bytes 786432 | tf_op jit(solution)/shard_map/first_rows/pallas_call | solution.py:393
  8.9 1.3 %collective-permute-start.2 = (bf16[144,1024]{1,0:T(8,128)(2,1)}, bf16[144,1024]{1,0:T(8,128)(2,1)S(1)}, u32[]{:S(2)}, u32[]{:S(2)}) collective-permute-start(bf16[144,1024]{1,0:T(8,128)(2,1)} %first_rows.3), channel_id=1, source_target_pairs={{1,0},{2,1},{3,2},{4,3},{5,4},{6,5},{7,6},{8,7},{9,8},{10,9},{11,1... | collective-permute-start | bytes 884744 | tf_op jit(solution)/shard_map/ppermute | solution.py:345
  10.1 2.3 %first_rows.2 = bf16[144,1024]{1,0:T(8,128)(2,1)} custom-call(s32[1,128]{1,0:T(1,128)} %bitcast.2, bf16[128,2048]{1,0:T(8,128)(2,1)} %q_ref.7, bf16[128,2048]{1,0:T(8,128)(2,1)} %k_ref.11, bf16[128,2048]{1,0:T(8,128)(2,1)} %v_ref.11, bf16[128,2048]{1,0:T(8,128)(2,1)} %do_ref.7), custom_call_target="tpu_custom_call" | custom-call | flops 16777216 | bytes 786432 | tf_op jit(solution)/shard_map/first_rows/pallas_call | solution.py:393
  12.4 1.3 %collective-permute-start.1 = (bf16[144,1024]{1,0:T(8,128)(2,1)}, bf16[144,1024]{1,0:T(8,128)(2,1)S(1)}, u32[]{:S(2)}, u32[]{:S(2)}) collective-permute-start(bf16[144,1024]{1,0:T(8,128)(2,1)} %first_rows.2), channel_id=1, source_target_pairs={{1,0},{2,1},{3,2},{4,3},{5,4},{6,5},{7,6},{8,7},{9,8},{10,9},{11,1... | collective-permute-start | bytes 884744 | tf_op jit(solution)/shard_map/ppermute | solution.py:345
  13.7 5.5 %own_block.1 = (bf16[128,2048]{1,0:T(8,128)(2,1)}, bf16[128,2048]{1,0:T(8,128)(2,1)}, f32[128,2048]{1,0:T(8,128)}, f32[128,2048]{1,0:T(8,128)}) custom-call(s32[1,128]{1,0:T(1,128)} %bitcast.3, bf16[128,2048]{1,0:T(8,128)(2,1)} %q_ref.7, bf16[128,2048]{1,0:T(8,128)(2,1)} %k_ref.11, bf16[128,2048]{1,0:T(8,128)(2,1)} %v_ref.11, bf16[128,2048]{1,0:T(8,128)(2,1)} %do_ref.7), custom_call_target="tpu_custom_call" | custom-call | flops 201326592 | bytes 4718592 | tf_op jit(solution)/shard_map/own_block/pallas_call | solution.py:400
  19.3 5.9 %collective-permute-done.before_ref = bf16[128,2048]{1,0:T(8,128)(2,1)S(1)} collective-permute-done((bf16[128,2048]{1,0:T(8,128)(2,1)S(1)}, bf16[128,2048]{1,0:T(8,128)(2,1)S(1)}, u32[]{:S(2)}, u32[]{:S(2)}) %collective-permute-start) | collective-permute-done | bytes 524320 | tf_op jit(solution)/shard_map/ppermute | solution.py:345
  25.2 0.0 copy-start
  25.2 0.8 %copy-done = bf16[128,2048]{1,0:T(8,128)(2,1)} copy-done((bf16[128,2048]{1,0:T(8,128)(2,1)}, bf16[128,2048]{1,0:T(8,128)(2,1)S(1)}, u32[]{:S(2)}) %copy-start) | copy-done | bytes 524312
  26.0 6.2 %lead_rows.1 = (bf16[128,2048]{1,0:T(8,128)(2,1)}, bf16[128,2048]{1,0:T(8,128)(2,1)}, bf16[128,2048]{1,0:T(8,128)(2,1)}, bf16[128,2048]{1,0:T(8,128)(2,1)}) custom-call(s32[1,128]{1,0:T(1,128)} %bitcast.4, bf16[128,2048]{1,0:T(8,128)(2,1)} %q_ref.7, bf16[128,2048]{1,0:T(8,128)(2,1)} %k_ref.11, ...), custom_call_target="tpu_custom_call", output_to_operand_aliasing={{0}: (8, {}), {1}: (9, {})} | custom-call | flops 167772160 | bytes 3670016 | tf_op jit(solution)/shard_map/lead_rows/pallas_call | solution.py:407
  32.2 0.0 collective-permute-done.2.after_ref
  32.2 0.0 copy-start.2
  32.3 0.7 %copy-done.2 = bf16[144,1024]{1,0:T(8,128)(2,1)} copy-done((bf16[144,1024]{1,0:T(8,128)(2,1)}, bf16[144,1024]{1,0:T(8,128)(2,1)S(1)}, u32[]{:S(2)}) %copy-start.2) | copy-done | bytes 294936
  33.0 2.7 %tail_keys.2 = (bf16[128,2048]{1,0:T(8,128)(2,1)}, bf16[128,2048]{1,0:T(8,128)(2,1)}) custom-call(s32[1,128]{1,0:T(1,128)} %bitcast.5, bf16[128,2048]{1,0:T(8,128)(2,1)} %k_ref.11, bf16[128,2048]{1,0:T(8,128)(2,1)} %v_ref.11, bf16[144,1024]{1,0:T(8,128)(2,1)} %copy-done.2, ...), custom_call_target="tpu_custom_call", output_to_operand_aliasing={{0}: (6, {}), {1}: (7, {})} | custom-call | flops 33554432 | bytes 1310720 | tf_op jit(solution)/shard_map/tail_keys/pallas_call | solution.py:415
  35.6 0.0 collective-permute-done.1.after_ref
  35.6 0.0 copy-start.1
  35.6 0.7 %copy-done.1 = bf16[144,1024]{1,0:T(8,128)(2,1)} copy-done((bf16[144,1024]{1,0:T(8,128)(2,1)}, bf16[144,1024]{1,0:T(8,128)(2,1)S(1)}, u32[]{:S(2)}) %copy-start.1) | copy-done | bytes 294936
  36.3 2.7 %tail_keys.3 = (bf16[128,2048]{1,0:T(8,128)(2,1)}, bf16[128,2048]{1,0:T(8,128)(2,1)}) custom-call(s32[1,128]{1,0:T(1,128)} %bitcast.6, bf16[128,2048]{1,0:T(8,128)(2,1)} %k_ref.11, bf16[128,2048]{1,0:T(8,128)(2,1)} %v_ref.11, bf16[144,1024]{1,0:T(8,128)(2,1)} %copy-done.1, ...), custom_call_target="tpu_custom_call", output_to_operand_aliasing={{0}: (6, {}), {1}: (7, {})} | custom-call | flops 33554432 | bytes 1310720 | tf_op jit(solution)/shard_map/tail_keys/pallas_call | solution.py:415
  (1 shorter events, 0.0 us)
Async XLA Ops:
  0.6 1.0 %slice-start = ((bf16[128,2048]{1,0:T(8,128)(2,1)}), bf16[64,2048]{1,0:T(8,128)(2,1)S(1)}, s32[]{:S(2)}) async-start(bf16[128,2048]{1,0:T(8,128)(2,1)} %k_ref.11), calls=%async_computation | async-start | bytes 524288 | tf_op jit(solution)/shard_map/slice | solution.py:386
  0.6 1.0 %slice-start.1 = ((bf16[128,2048]{1,0:T(8,128)(2,1)}), bf16[64,2048]{1,0:T(8,128)(2,1)S(1)}, s32[]{:S(2)}) async-start(bf16[128,2048]{1,0:T(8,128)(2,1)} %v_ref.11), calls=%async_computation.1 | async-start | bytes 524288 | tf_op jit(solution)/shard_map/slice | solution.py:386
  1.7 23.5 %collective-permute-start = (bf16[128,2048]{1,0:T(8,128)(2,1)S(1)}, bf16[128,2048]{1,0:T(8,128)(2,1)S(1)}, u32[]{:S(2)}, u32[]{:S(2)}) collective-permute-start(bf16[128,2048]{1,0:T(8,128)(2,1)S(1)} %pad_maximum_fusion), channel_id=1, source_target_pairs={{0,1},{1,2},{2,3},{3,4},{4,5},{5,6},{6,7},{7,8},{8,9},{9,10},{10,1... | collective-permute-start | bytes 1572872 | tf_op jit(solution)/shard_map/ppermute | solution.py:345
  8.9 23.4 %collective-permute-start.2 = (bf16[144,1024]{1,0:T(8,128)(2,1)}, bf16[144,1024]{1,0:T(8,128)(2,1)S(1)}, u32[]{:S(2)}, u32[]{:S(2)}) collective-permute-start(bf16[144,1024]{1,0:T(8,128)(2,1)} %first_rows.3), channel_id=1, source_target_pairs={{1,0},{2,1},{3,2},{4,3},{5,4},{6,5},{7,6},{8,7},{9,8},{10,9},{11,1... | collective-permute-start | bytes 884744 | tf_op jit(solution)/shard_map/ppermute | solution.py:345
  12.4 23.2 %collective-permute-start.1 = (bf16[144,1024]{1,0:T(8,128)(2,1)}, bf16[144,1024]{1,0:T(8,128)(2,1)S(1)}, u32[]{:S(2)}, u32[]{:S(2)}) collective-permute-start(bf16[144,1024]{1,0:T(8,128)(2,1)} %first_rows.2), channel_id=1, source_target_pairs={{1,0},{2,1},{3,2},{4,3},{5,4},{6,5},{7,6},{8,7},{9,8},{10,9},{11,1... | collective-permute-start | bytes 884744 | tf_op jit(solution)/shard_map/ppermute | solution.py:345
  25.2 0.8 %copy-start = (bf16[128,2048]{1,0:T(8,128)(2,1)}, bf16[128,2048]{1,0:T(8,128)(2,1)S(1)}, u32[]{:S(2)}) copy-start(bf16[128,2048]{1,0:T(8,128)(2,1)S(1)} %collective-permute-done.before_ref) | copy-start | bytes 1572868
  32.2 0.7 %copy-start.2 = (bf16[144,1024]{1,0:T(8,128)(2,1)}, bf16[144,1024]{1,0:T(8,128)(2,1)S(1)}, u32[]{:S(2)}) copy-start(bf16[144,1024]{1,0:T(8,128)(2,1)S(1)} %collective-permute-done.2.after_ref) | copy-start | bytes 884740
  35.6 0.7 %copy-start.1 = (bf16[144,1024]{1,0:T(8,128)(2,1)}, bf16[144,1024]{1,0:T(8,128)(2,1)S(1)}, u32[]{:S(2)}) copy-start(bf16[144,1024]{1,0:T(8,128)(2,1)S(1)} %collective-permute-done.1.after_ref) | copy-start | bytes 884740

commit v5 on v4

--- a/solution.py
+++ b/solution.py
@@ -231,66 +231,63 @@
     return parts
 
 
-def first_kernel(tok, prior, len_ref, q_ref, k_ref, v_ref, do_ref, out_ref, bias_ref):
-    columns = head_columns(q_ref.shape[1])
+def own_kernel(
+    prior, len_ref, q_ref, k_ref, v_ref, do_ref, attn_ref, gq_ref, gk_ref, gv_ref,
+    lead_bias_ref, tail_bias_ref, *refs,
+):
+    *packed_refs, bias_ref, first_bias_ref = refs
+    tok, width = k_ref.shape
+    columns = head_columns(width)
+    early, late = slice(0, prior), slice(tok - prior, tok)
 
     @pl.when(pl.program_id(0) == 0)
     def _():
         first = device_first(tok)
         lengths = len_ref[...].astype(jnp.float32)
-        bias_ref[...] = bias_by_key(lengths, first, prior, first, prior)
-
-    out_ref[:prior, :] = q_ref[...]
-    out_ref[prior : 2 * prior, :] = do_ref[...]
-    bias = bias_ref[...]
-    pairs = [by_query(k_ref[:, c], q_ref[:, c], v_ref[:, c], do_ref[:, c], bias) for c in columns]
-    tops = [jnp.max(s, axis=0, keepdims=True) for s, _ in pairs]
-    raws = [jnp.exp2(s - top) for (s, _), top in zip(pairs, tops)]
-    totals = [jnp.sum(raw, axis=0, keepdims=True) for raw in raws]
-    sums = [jnp.sum(raw * dp, axis=0, keepdims=True) for raw, (_, dp) in zip(raws, pairs)]
-    for c, top, total, summed in zip(columns, tops, totals, sums):
-        rows = split_bf16(top + jnp.log2(total), 3) + split_bf16(summed / total, 2)
-        rows.append(jnp.zeros((STAT_ROWS - len(rows), prior), jnp.float32))
-        block = jnp.concatenate(rows, axis=0)
-        block = jnp.concatenate([block, jnp.zeros_like(block)], axis=1)
-        out_ref[2 * prior :, c] = block.astype(jnp.bfloat16)
-
-
-def own_kernel(
-    prior, len_ref, q_ref, k_ref, v_ref, do_ref, attn_ref, gq_ref, gk_ref, gv_ref, bias_ref
-):
-    tok, width = k_ref.shape
-    rest = tok - prior
-    columns = head_columns(width)
-
-    @pl.when(pl.program_id(0) == 0)
-    def _():
-        first = device_first(tok)
-        lengths = len_ref[...].astype(jnp.float32)
-        bias_ref[...] = bias_by_query(lengths, first + prior, rest, first, tok)
-
-    bias = bias_ref[...]
-    pairs = [by_query(q_ref[:, c], k_ref[:, c], do_ref[:, c], v_ref[:, c], bias) for c in columns]
+        bias_ref[...] = bias_by_query(lengths, first + prior, tok - prior, first, tok)
+        first_bias_ref[...] = bias_by_key(lengths, first, prior, first, prior)
+        lead_bias_ref[...] = bias_by_query(lengths, first, prior, first - prior, 2 * prior)
+        tail_bias_ref[...] = bias_by_key(lengths, first + tok, prior, first + tok - prior, prior)
+
+    bias, first_bias = bias_ref[...], first_bias_ref[...]
+    pairs = [
+        by_query(q_ref[late, c], k_ref[:, c], do_ref[late, c], v_ref[:, c], bias) for c in columns
+    ]
+    firsts = [
+        by_query(k_ref[early, c], q_ref[early, c], v_ref[early, c], do_ref[early, c], first_bias)
+        for c in columns
+    ]
     weights, grads = full_rows(pairs)
     for c, w, g in zip(columns, weights, grads):
         attn_ref[:, c] = dot(w, v_ref[:, c], 1, 0).astype(jnp.bfloat16)
         gq_ref[:, c] = dot(g, k_ref[:, c], 1, 0).astype(jnp.bfloat16)
-        gk_ref[:, c] = dot(g, q_ref[:, c], 0, 0)
-        gv_ref[:, c] = dot(w, do_ref[:, c], 0, 0)
+        gk_ref[:, c] = dot(g, q_ref[late, c], 0, 0)
+        gv_ref[:, c] = dot(w, do_ref[late, c], 0, 0)
+    tops = [jnp.max(s, axis=0, keepdims=True) for s, _ in firsts]
+    raws = [jnp.exp2(s - top) for (s, _), top in zip(firsts, tops)]
+    totals = [jnp.sum(raw, axis=0, keepdims=True) for raw in raws]
+    sums = [jnp.sum(raw * dp, axis=0, keepdims=True) for raw, (_, dp) in zip(raws, firsts)]
+    blocks = []
+    for top, total, summed in zip(tops, totals, sums):
+        rows = split_bf16(top + jnp.log2(total), 3) + split_bf16(summed / total, 2)
+        rows.append(jnp.zeros((STAT_ROWS - len(rows), prior), jnp.float32))
+        block = jnp.concatenate(rows, axis=0)
+        blocks.append(jnp.concatenate([block, jnp.zeros_like(block)], axis=1).astype(jnp.bfloat16))
+    for at, packed_ref in enumerate(packed_refs):
+
+        @pl.when(pl.program_id(0) == at)
+        def _(packed_ref=packed_ref):
+            packed_ref[early, :] = q_ref[early, :]
+            packed_ref[prior : 2 * prior, :] = do_ref[early, :]
+            for c, block in zip(columns, blocks):
+                packed_ref[2 * prior :, c] = block
 
 
 def lead_kernel(
-    prior, len_ref, q_ref, k_ref, v_ref, do_ref, before_ref, gk_part_ref, gv_part_ref,
-    attn_in, gq_in, attn_ref, gq_ref, gk_ref, gv_ref, bias_ref,
+    prior, bias_ref, q_ref, k_ref, v_ref, do_ref, before_ref, gk_part_ref, gv_part_ref,
+    attn_in, gq_in, attn_ref, gq_ref, gk_ref, gv_ref,
 ):
     columns = head_columns(q_ref.shape[1])
-
-    @pl.when(pl.program_id(0) == 0)
-    def _():
-        first = device_first(attn_in.shape[0])
-        lengths = len_ref[...].astype(jnp.float32)
-        bias_ref[...] = bias_by_query(lengths, first, prior, first - prior, 2 * prior)
-
     bias = bias_ref[...]
     early, late = slice(0, prior), slice(prior, 2 * prior)
     keys = [jnp.concatenate([before_ref[early, c], k_ref[:, c]], axis=0) for c in columns]
@@ -309,18 +306,10 @@
 
 
 def tail_kernel(
-    prior, len_ref, k_ref, v_ref, after_ref, gk_part_ref, gv_part_ref,
-    gk_in, gv_in, gk_ref, gv_ref, bias_ref,
+    prior, bias_ref, k_ref, v_ref, after_ref, gk_part_ref, gv_part_ref,
+    gk_in, gv_in, gk_ref, gv_ref,
 ):
     columns = head_columns(k_ref.shape[1])
-
-    @pl.when(pl.program_id(0) == 0)
-    def _():
-        tok = gk_in.shape[0]
-        first = device_first(tok)
-        lengths = len_ref[...].astype(jnp.float32)
-        bias_ref[...] = bias_by_key(lengths, first + tok, prior, first + tok - prior, prior)
-
     bias = bias_ref[...]
     early, late = slice(0, prior), slice(prior, 2 * prior)
     pairs = [
@@ -356,67 +345,69 @@
 def halo_shards(query_in, key_in, value_in, grad_out, module_lengths):
     tok, width = query_in.shape
     prior = tok * lax.axis_size("head") // 8
-    heads = width // HEAD_DIM
-    step = min(width, 4 * HEAD_DIM)
+    step = math.gcd(width, 8 * HEAD_DIM)
     groups = width // step
     per = step // HEAD_DIM
+    late_at = tok // prior - 1
+    sent = 2 * prior + STAT_ROWS
     lengths = module_lengths.reshape(1, -1)
-    len_spec = pl.BlockSpec(lengths.shape, lambda g: (0, 0))
     keep = pl.BlockSpec(memory_space=pl.ANY)
     full16 = jax.ShapeDtypeStruct((tok, width), jnp.bfloat16)
     full32 = jax.ShapeDtypeStruct((tok, width), jnp.float32)
-    late_at = tok // prior - 1
+    packed = jax.ShapeDtypeStruct((sent, step), jnp.bfloat16)
+    lead_shape, tail_shape = (prior, 2 * prior), (prior, prior)
 
     def rows(count, at=0, base=0):
         return pl.BlockSpec((count, step), lambda g: (at, g + base))
 
-    def call(kernel, name, grid, ins, outs, shapes, bias, products, moved, aliases=None):
+    def fixed(*shape):
+        return pl.BlockSpec(shape, lambda g: (0, 0))
+
+    def call(kernel, name, grid, ins, outs, shapes, work, moved, aliases=None, scratch=()):
         return pl.pallas_call(
             functools.partial(kernel, prior),
             grid=(grid,),
-            in_specs=[len_spec, *ins],
+            in_specs=ins,
             out_specs=outs,
             out_shape=shapes,
-            scratch_shapes=[pltpu.VMEM(bias, jnp.float32)],
+            scratch_shapes=scratch,
             input_output_aliases=aliases or {},
-            cost_estimate=cost(grid * per, *bias, products, moved * grid * step),
+            cost_estimate=cost(grid * per, *work, moved * grid * step),
+            compiler_params=pltpu.CompilerParams(vmem_limit_bytes=16 * 2**20),
             name=name,
         )
 
     before = neighbour(jnp.concatenate([key_in[tok - prior :], value_in[tok - prior :]]), 1)
 
-    cuts = [0, groups // 2, groups] if groups > 1 else [0, groups]
-    spans = list(zip(cuts[:-1], cuts[1:]))
-    sent = 2 * prior + STAT_ROWS
-    afters = []
-    for low, high in spans:
-        packed = call(
-            functools.partial(first_kernel, tok), "first_rows", high - low, [rows(prior, 0, low)] * 4, rows(sent),
-            jax.ShapeDtypeStruct((sent, (high - low) * step), jnp.bfloat16), (prior, prior), 2,
-            12 * prior,
-        )(lengths, query_in, key_in, value_in, grad_out)
-        afters.append(neighbour(packed, -1))
-
-    attn, gq, gk_part, gv_part = call(
+    attn, gq, gk_part, gv_part, lead_bias, tail_bias, *parts = call(
         own_kernel, "own_block", groups,
-        [rows(prior, late_at), rows(tok), rows(tok), rows(prior, late_at)],
-        [rows(prior, late_at), rows(prior, late_at), rows(tok), rows(tok)],
-        [full16, full16, full32, full32], (tok - prior, tok), 6, 18 * tok,
+        [fixed(*lengths.shape), rows(tok), rows(tok), rows(tok), rows(tok)],
+        [rows(prior, late_at), rows(prior, late_at), rows(tok), rows(tok)]
+        + [fixed(*lead_shape), fixed(*tail_shape)] + [fixed(sent, step)] * groups,
+        [full16, full16, full32, full32]
+        + [jax.ShapeDtypeStruct(shape, jnp.float32) for shape in (lead_shape, tail_shape)]
+        + [packed] * groups,
+        (tok, tok, 4), 22 * tok,
+        scratch=[
+            pltpu.VMEM((tok - prior, tok), jnp.float32), pltpu.VMEM((prior, prior), jnp.float32)
+        ],
     )(lengths, query_in, key_in, value_in, grad_out)
+    afters = [neighbour(part, -1) for part in parts]
 
     attn, gq, gk, gv = call(
         lead_kernel, "lead_rows", groups,
-        [rows(prior)] * 4 + [rows(2 * prior), rows(prior), rows(prior), keep, keep],
-        [rows(prior)] * 4, [full16] * 4, (prior, 2 * prior), 5, 14 * tok, {8: 0, 9: 1},
-    )(lengths, query_in, key_in, value_in, grad_out, before, gk_part, gv_part, attn, gq)
-
-    for (low, high), after in zip(spans, afters):
-        late = rows(prior, late_at, low)
+        [fixed(*lead_shape)] + [rows(prior)] * 4 + [rows(2 * prior), rows(prior), rows(prior)]
+        + [keep, keep],
+        [rows(prior)] * 4, [full16] * 4, (prior, 2 * prior, 5), 14 * tok, {8: 0, 9: 1},
+    )(lead_bias, query_in, key_in, value_in, grad_out, before, gk_part, gv_part, attn, gq)
+
+    for at, after in enumerate(afters):
+        late = rows(prior, late_at, at)
         gk, gv = call(
-            tail_kernel, "tail_keys", high - low,
-            [late, late, rows(sent), late, late, keep, keep],
-            [late, late], [full16] * 2, (prior, prior), 4, 10 * tok, {6: 0, 7: 1},
-        )(lengths, key_in, value_in, after, gk_part, gv_part, gk, gv)
+            tail_kernel, "tail_keys", 1,
+            [fixed(*tail_shape), late, late, rows(sent), late, late, keep, keep],
+            [late, late], [full16] * 2, (prior, prior, 4), 10 * tok, {6: 0, 7: 1},
+        )(tail_bias, key_in, value_in, after, gk_part, gv_part, gk, gv)
     return (attn, gq, gk, gv)
 
 

time: 39.5 us -> 34 us (0.86)
  Pallas kernels: 21.7 us -> 10.1 us
  waiting for transfers between devices: 5.95 us -> 13.1 us
  local copies, waits for them, and re-layouts: 3.23 us -> 2.22 us
    pallas_call x6 -> x4, Pallas kernels: 21.7 us -> 10.1 us  [the longest x1 4.25 us: halo_shards(): call(lead_kernel, 'lead_rows', groups, [fixed(*lead_shape)] + [rows(prior...]
    ppermute x3, waiting for transfers between devices: 5.95 us -> 13.1 us  [neighbour(): return lax.ppermute(value, ('seq', 'head'), pairs)]
    unnamed x6 -> x10, local copies, waits for them, and re-layouts: 2.21 us -> 1.05 us
  transfers between devices with their start and end apart: 3 -> 3, of which waited for: 1 -> 2; matrix products, arithmetic and copies ran while one was open for 0% -> 0% of each run, Pallas kernels for 49% -> 27%
where the time goes in v5:
time: 34 us; the launch traced here: 33.8 us
  waiting for transfers between devices  13.1 us (39%)
  Pallas kernels  10.1 us (30%)
  starting transfers between devices  7.58 us (22%)
  local copies, waits for them, and re-layouts  2.22 us (7%)
  between operations  0.74 us (2%)
    ppermute x3, waiting for transfers between devices, neighbour(): return lax.ppermute(value, ('seq', 'head'), pairs)  13.1 us
    ppermute x3, starting transfers between devices, neighbour(): return lax.ppermute(value, ('seq', 'head'), pairs)  7.58 us
    pallas_call x1, Pallas kernels, halo_shards(): call(lead_kernel, 'lead_rows', groups, [fixed(*lead_shape)] + [rows(prior...  4.25 us
    pallas_call x1, Pallas kernels, halo_shards(): call(own_kernel, 'own_block', groups, [fixed(*lengths.shape), rows(tok),...  3.55 us
    pallas_call x2, Pallas kernels, halo_shards(): call(tail_kernel, 'tail_keys', 1, [fixed(*tail_shape), late, late, rows(s...  2.33 us
    slice x2, local copies, waits for them, and re-layouts, halo_shards(): key_in[tok - prior:]  1.08 us
    unnamed x10, local copies, waits for them, and re-layouts  1.05 us
  transfers between devices with their start and end apart: 3, of which 2 were waited for; matrix products, arithmetic and copies ran while one was open for 0% of the time, Pallas kernels for 27%

profile of v5, /device:TPU:0, one launch (start us, length us, event | category | flops | bytes accessed | tf_op | source)
XLA Modules:
  0.0 33.8 jit_solution(15288341469190677281)
XLA Ops:
  0.6 0.0 copy-start.2
  0.6 0.0 slice-start
  0.7 0.0 slice-start.1
  0.7 1.1 %slice-done = bf16[64,2048]{1,0:T(8,128)(2,1)S(1)} async-done(((bf16[128,2048]{1,0:T(8,128)(2,1)}), bf16[64,2048]{1,0:T(8,128)(2,1)S(1)}, s32[]{:S(2)}) %slice-start) | async-done | bytes 262168 | tf_op jit(solution)/shard_map/slice | solution.py:380
  1.7 0.1 slice-done.1
  1.8 0.0 copy-start
  1.8 0.0 copy-start.1
  1.9 0.0 copy-start.4
  1.9 5.0 %collective-permute-start = (bf16[128,2048]{1,0:T(8,128)(2,1)S(1)}, bf16[128,2048]{1,0:T(8,128)(2,1)S(1)}, u32[]{:S(2)}, u32[]{:S(2)}) collective-permute-start(bf16[128,2048]{1,0:T(8,128)(2,1)S(1)} %pad_maximum_fusion), channel_id=1, source_target_pairs={{0,1},{1,2},{2,3},{3,4},{4,5},{5,6},{6,7},{7,8},{8,9},{9,10},{10,1... | collective-permute-start | bytes 1572872 | tf_op jit(solution)/shard_map/ppermute | solution.py:334
  6.9 0.0 copy-done.2
  6.9 0.0 copy-done
  6.9 0.0 copy-done.1
  6.9 0.0 copy-done.4
  6.9 0.0 copy-start.3
  6.9 1.0 %copy-done.3 = bf16[128,2048]{1,0:T(8,128)(2,1)S(1)} copy-done((bf16[128,2048]{1,0:T(8,128)(2,1)S(1)}, bf16[128,2048]{1,0:T(8,128)(2,1)}, u32[]{:S(2)}) %copy-start.3) | copy-done | bytes 524312
  8.0 3.5 %own_block.1 = (bf16[128,2048]{1,0:T(8,128)(2,1)}, bf16[128,2048]{1,0:T(8,128)(2,1)}, f32[128,2048]{1,0:T(8,128)S(1)}, f32[128,2048]{1,0:T(8,128)S(1)}, f32[64,1...) custom-call(s32[1,128]{1,0:T(1,128)S(1)} %bitcast.1, ...), custom_call_target="tpu_custom_call" | custom-call | flops 268435456 | bytes 5767168 | tf_op jit(solution)/shard_map/own_block/pallas_call | solution.py:382
  11.5 1.3 %collective-permute-start.2 = (bf16[144,1024]{1,0:T(8,128)(2,1)S(1)}, bf16[144,1024]{1,0:T(8,128)(2,1)S(1)}, u32[]{:S(2)}, u32[]{:S(2)}) collective-permute-start(bf16[144,1024]{1,0:T(8,128)(2,1)S(1)} %get-tuple-element.29), channel_id=1, source_target_pairs={{1,0},{2,1},{3,2},{4,3},{5,4},{6,5},{7,6},{8,7},{9,8},{10,9},{11,1... | collective-permute-start | bytes 884744 | tf_op jit(solution)/shard_map/ppermute | solution.py:334
  12.8 1.3 %collective-permute-start.1 = (bf16[144,1024]{1,0:T(8,128)(2,1)S(1)}, bf16[144,1024]{1,0:T(8,128)(2,1)S(1)}, u32[]{:S(2)}, u32[]{:S(2)}) collective-permute-start(bf16[144,1024]{1,0:T(8,128)(2,1)S(1)} %get-tuple-element.28), channel_id=1, source_target_pairs={{1,0},{2,1},{3,2},{4,3},{5,4},{6,5},{7,6},{8,7},{9,8},{10,9},{11,1... | collective-permute-start | bytes 884744 | tf_op jit(solution)/shard_map/ppermute | solution.py:334
  14.1 11.4 %collective-permute-done.before_ref = bf16[128,2048]{1,0:T(8,128)(2,1)S(1)} collective-permute-done((bf16[128,2048]{1,0:T(8,128)(2,1)S(1)}, bf16[128,2048]{1,0:T(8,128)(2,1)S(1)}, u32[]{:S(2)}, u32[]{:S(2)}) %collective-permute-start) | collective-permute-done | bytes 524320 | tf_op jit(solution)/shard_map/ppermute | solution.py:334
  25.5 4.3 %lead_rows.1 = (bf16[128,2048]{1,0:T(8,128)(2,1)}, bf16[128,2048]{1,0:T(8,128)(2,1)}, bf16[128,2048]{1,0:T(8,128)(2,1)}, bf16[128,2048]{1,0:T(8,128)(2,1)}) custom-call(f32[64,128]{1,0:T(8,128)S(1)} %get-tuple-element.20.bias_ref, bf16[128,2048]{1,0:T(8,128)(2,1)S(1)} %copy-done.2, ...), custom_call_target="tpu_custom_call", output_to_operand_aliasing={{0}: (8, {}), {1}: (9, {})} | custom-call | flops 167772160 | bytes 3670016 | tf_op jit(solution)/shard_map/lead_rows/pallas_call | solution.py:397
  29.7 0.0 collective-permute-done.2.after_ref
  29.8 1.2 %tail_keys.2 = (bf16[128,2048]{1,0:T(8,128)(2,1)}, bf16[128,2048]{1,0:T(8,128)(2,1)}) custom-call(f32[64,64]{1,0:T(8,128)S(1)} %get-tuple-element.27.bias_ref, bf16[128,2048]{1,0:T(8,128)(2,1)S(1)} %copy-done, bf16[128,2048]{1,0:T(8,128)(2,1)S(1)} %copy-done.1, ...), custom_call_target="tpu_custom_call", output_to_operand_aliasing={{0}: (6, {}), {1}: (7, {})} | custom-call | flops 33554432 | bytes 1310720 | tf_op jit(solution)/shard_map/tail_keys/pallas_call | solution.py:406
  30.9 1.7 %collective-permute-done.1.after_ref = bf16[144,1024]{1,0:T(8,128)(2,1)S(1)} collective-permute-done((bf16[144,1024]{1,0:T(8,128)(2,1)S(1)}, bf16[144,1024]{1,0:T(8,128)(2,1)S(1)}, u32[]{:S(2)}, u32[]{:S(2)}) %collective-permute-start.1) | collective-permute-done | bytes 294944 | tf_op jit(solution)/shard_map/ppermute | solution.py:334
  32.6 1.2 %tail_keys.3 = (bf16[128,2048]{1,0:T(8,128)(2,1)}, bf16[128,2048]{1,0:T(8,128)(2,1)}) custom-call(f32[64,64]{1,0:T(8,128)S(1)} %get-tuple-element.27.bias_ref, bf16[128,2048]{1,0:T(8,128)(2,1)S(1)} %copy-done, bf16[128,2048]{1,0:T(8,128)(2,1)S(1)} %copy-done.1, ...), custom_call_target="tpu_custom_call", output_to_operand_aliasing={{0}: (6, {}), {1}: (7, {})} | custom-call | flops 33554432 | bytes 1310720 | tf_op jit(solution)/shard_map/tail_keys/pallas_call | solution.py:406
  (1 shorter events, 0.0 us)
Async XLA Ops:
  0.6 6.3 %copy-start.2 = (bf16[128,2048]{1,0:T(8,128)(2,1)S(1)}, bf16[128,2048]{1,0:T(8,128)(2,1)}, u32[]{:S(2)}) copy-start(bf16[128,2048]{1,0:T(8,128)(2,1)} %q_ref.3) | copy-start | bytes 1572868
  0.6 1.1 %slice-start = ((bf16[128,2048]{1,0:T(8,128)(2,1)}), bf16[64,2048]{1,0:T(8,128)(2,1)S(1)}, s32[]{:S(2)}) async-start(bf16[128,2048]{1,0:T(8,128)(2,1)} %k_ref.7), calls=%async_computation | async-start | bytes 524288 | tf_op jit(solution)/shard_map/slice | solution.py:380
  0.7 1.2 %slice-start.1 = ((bf16[128,2048]{1,0:T(8,128)(2,1)}), bf16[64,2048]{1,0:T(8,128)(2,1)S(1)}, s32[]{:S(2)}) async-start(bf16[128,2048]{1,0:T(8,128)(2,1)} %v_ref.7), calls=%async_computation.1 | async-start | bytes 524288 | tf_op jit(solution)/shard_map/slice | solution.py:380
  1.8 5.1 %copy-start = (bf16[128,2048]{1,0:T(8,128)(2,1)S(1)}, bf16[128,2048]{1,0:T(8,128)(2,1)}, u32[]{:S(2)}) copy-start(bf16[128,2048]{1,0:T(8,128)(2,1)} %k_ref.7) | copy-start | bytes 1572868
  1.8 5.1 %copy-start.1 = (bf16[128,2048]{1,0:T(8,128)(2,1)S(1)}, bf16[128,2048]{1,0:T(8,128)(2,1)}, u32[]{:S(2)}) copy-start(bf16[128,2048]{1,0:T(8,128)(2,1)} %v_ref.7) | copy-start | bytes 1572868
  1.9 5.1 %copy-start.4 = (s32[128]{0:T(128)S(1)}, s32[128]{0:T(128)}, u32[]{:S(2)}) copy-start(s32[128]{0:T(128)} %param.9) | copy-start | bytes 1540
  1.9 23.6 %collective-permute-start = (bf16[128,2048]{1,0:T(8,128)(2,1)S(1)}, bf16[128,2048]{1,0:T(8,128)(2,1)S(1)}, u32[]{:S(2)}, u32[]{:S(2)}) collective-permute-start(bf16[128,2048]{1,0:T(8,128)(2,1)S(1)} %pad_maximum_fusion), channel_id=1, source_target_pairs={{0,1},{1,2},{2,3},{3,4},{4,5},{5,6},{6,7},{7,8},{8,9},{9,10},{10,1... | collective-permute-start | bytes 1572872 | tf_op jit(solution)/shard_map/ppermute | solution.py:334
  6.9 1.0 %copy-start.3 = (bf16[128,2048]{1,0:T(8,128)(2,1)S(1)}, bf16[128,2048]{1,0:T(8,128)(2,1)}, u32[]{:S(2)}) copy-start(bf16[128,2048]{1,0:T(8,128)(2,1)} %do_ref.3) | copy-start | bytes 1572868
  11.5 18.2 %collective-permute-start.2 = (bf16[144,1024]{1,0:T(8,128)(2,1)S(1)}, bf16[144,1024]{1,0:T(8,128)(2,1)S(1)}, u32[]{:S(2)}, u32[]{:S(2)}) collective-permute-start(bf16[144,1024]{1,0:T(8,128)(2,1)S(1)} %get-tuple-element.29), channel_id=1, source_target_pairs={{1,0},{2,1},{3,2},{4,3},{5,4},{6,5},{7,6},{8,7},{9,8},{10,9},{11,1... | collective-permute-start | bytes 884744 | tf_op jit(solution)/shard_map/ppermute | solution.py:334
  12.8 19.8 %collective-permute-start.1 = (bf16[144,1024]{1,0:T(8,128)(2,1)S(1)}, bf16[144,1024]{1,0:T(8,128)(2,1)S(1)}, u32[]{:S(2)}, u32[]{:S(2)}) collective-permute-start(bf16[144,1024]{1,0:T(8,128)(2,1)S(1)} %get-tuple-element.28), channel_id=1, source_target_pairs={{1,0},{2,1},{3,2},{4,3},{5,4},{6,5},{7,6},{8,7},{9,8},{10,9},{11,1... | collective-permute-start | bytes 884744 | tf_op jit(solution)/shard_map/ppermute | solution.py:334

commit v6 on v5

--- a/solution.py
+++ b/solution.py
@@ -12,7 +12,6 @@
 SCALE = HEAD_DIM ** (-0.5)
 LOG2E = math.log2(math.e)
 MASKED = -1e30
-STAT_ROWS = 16
 
 
 def shifted(value, axis, by):
@@ -222,13 +221,36 @@
     return place * tok
 
 
-def split_bf16(value, terms):
-    parts = []
-    for _ in range(terms):
-        part = value.astype(jnp.bfloat16)
-        parts.append(part.astype(jnp.float32))
-        value = value - parts[-1]
-    return parts
+def split_bf16(row):
+    high = row.astype(jnp.bfloat16)
+    low = (row - high.astype(jnp.float32)).astype(jnp.bfloat16)
+    return jnp.concatenate([high, low], axis=1)
+
+
+def joined(pair):
+    pair = pair.astype(jnp.float32)
+    half = pair.shape[1] // 2
+    return pair[:, :half] + pair[:, half:]
+
+
+def pack_kernel(prior, k_ref, v_ref, *refs):
+    *packed_refs, sem = refs
+    last = pl.ds(k_ref.shape[0] - prior, prior)
+    copies = []
+    for at, packed_ref in enumerate(packed_refs):
+        width = packed_ref.shape[1]
+        for half, ref in enumerate((k_ref, v_ref)):
+            copies.append(
+                pltpu.make_async_copy(
+                    ref.at[last, pl.ds(at * width, width)],
+                    packed_ref.at[pl.ds(half * prior, prior), :],
+                    sem.at[2 * at + half],
+                )
+            )
+    for copy in copies:
+        copy.start()
+    for copy in copies:
+        copy.wait()
 
 
 def own_kernel(
@@ -267,26 +289,22 @@
     raws = [jnp.exp2(s - top) for (s, _), top in zip(firsts, tops)]
     totals = [jnp.sum(raw, axis=0, keepdims=True) for raw in raws]
     sums = [jnp.sum(raw * dp, axis=0, keepdims=True) for raw, (_, dp) in zip(raws, firsts)]
-    blocks = []
-    for top, total, summed in zip(tops, totals, sums):
-        rows = split_bf16(top + jnp.log2(total), 3) + split_bf16(summed / total, 2)
-        rows.append(jnp.zeros((STAT_ROWS - len(rows), prior), jnp.float32))
-        block = jnp.concatenate(rows, axis=0)
-        blocks.append(jnp.concatenate([block, jnp.zeros_like(block)], axis=1).astype(jnp.bfloat16))
+    logs = [split_bf16(top + jnp.log2(total)) for top, total in zip(tops, totals)]
+    deltas = [split_bf16(summed / total) for summed, total in zip(sums, totals)]
+    spare = lax.broadcasted_iota(jnp.int32, (prior, 1), 0) == prior - 1
     for at, packed_ref in enumerate(packed_refs):
 
         @pl.when(pl.program_id(0) == at)
         def _(packed_ref=packed_ref):
-            packed_ref[early, :] = q_ref[early, :]
-            packed_ref[prior : 2 * prior, :] = do_ref[early, :]
-            for c, block in zip(columns, blocks):
-                packed_ref[2 * prior :, c] = block
+            for c, log, delta in zip(columns, logs, deltas):
+                packed_ref[early, c] = jnp.where(spare, log, q_ref[early, c])
+                packed_ref[prior : 2 * prior, c] = jnp.where(spare, delta, do_ref[early, c])
 
 
 def lead_kernel(
-    prior, bias_ref, q_ref, k_ref, v_ref, do_ref, before_ref, gk_part_ref, gv_part_ref,
-    attn_in, gq_in, attn_ref, gq_ref, gk_ref, gv_ref,
+    prior, bias_ref, q_ref, k_ref, v_ref, do_ref, before_ref, gk_part_ref, gv_part_ref, *refs
 ):
+    attn_ref, gq_ref, gk_ref, gv_ref = refs[-4:]
     columns = head_columns(q_ref.shape[1])
     bias = bias_ref[...]
     early, late = slice(0, prior), slice(prior, 2 * prior)
@@ -316,10 +334,13 @@
         by_query(k_ref[:, c], after_ref[early, c], v_ref[:, c], after_ref[late, c], bias)
         for c in columns
     ]
-    own = []
-    for c in columns:
-        stat = after_ref[2 * prior :, c].astype(jnp.float32)[:, :prior]
-        own.append((stat[0:1] + stat[1:2] + stat[2:3], stat[3:4] + stat[4:5]))
+    own = [
+        (
+            joined(after_ref[prior - 1 : prior, c]),
+            joined(after_ref[2 * prior - 1 : 2 * prior, c]),
+        )
+        for c in columns
+    ]
     weights, grads = merged_rows(pairs, own)
     for c, w, g in zip(columns, weights, grads):
         gk = gk_part_ref[:, c] + dot(g, after_ref[early, c], 1, 0)
@@ -349,7 +370,7 @@
     groups = width // step
     per = step // HEAD_DIM
     late_at = tok // prior - 1
-    sent = 2 * prior + STAT_ROWS
+    sent = 2 * prior
     lengths = module_lengths.reshape(1, -1)
     keep = pl.BlockSpec(memory_space=pl.ANY)
     full16 = jax.ShapeDtypeStruct((tok, width), jnp.bfloat16)
@@ -377,7 +398,15 @@
             name=name,
         )
 
-    before = neighbour(jnp.concatenate([key_in[tok - prior :], value_in[tok - prior :]]), 1)
+    befores = pl.pallas_call(
+        functools.partial(pack_kernel, prior),
+        in_specs=[pl.BlockSpec(memory_space=pltpu.HBM)] * 2,
+        out_specs=[keep] * groups,
+        out_shape=[packed] * groups,
+        scratch_shapes=[pltpu.SemaphoreType.DMA((2 * groups,))],
+        name="pack_late",
+    )(key_in, value_in)
+    befores = [neighbour(part, 1) for part in befores]
 
     attn, gq, gk_part, gv_part, lead_bias, tail_bias, *parts = call(
         own_kernel, "own_block", groups,
@@ -392,14 +421,19 @@
             pltpu.VMEM((tok - prior, tok), jnp.float32), pltpu.VMEM((prior, prior), jnp.float32)
         ],
     )(lengths, query_in, key_in, value_in, grad_out)
-    afters = [neighbour(part, -1) for part in parts]
-
-    attn, gq, gk, gv = call(
-        lead_kernel, "lead_rows", groups,
-        [fixed(*lead_shape)] + [rows(prior)] * 4 + [rows(2 * prior), rows(prior), rows(prior)]
-        + [keep, keep],
-        [rows(prior)] * 4, [full16] * 4, (prior, 2 * prior, 5), 14 * tok, {8: 0, 9: 1},
-    )(lead_bias, query_in, key_in, value_in, grad_out, before, gk_part, gv_part, attn, gq)
+    outs = [attn, gq]
+    afters = []
+    for at, (part, before) in enumerate(zip(parts, befores)):
+        part, before = lax.optimization_barrier((part, before))
+        afters.append(neighbour(part, -1))
+        outs = call(
+            lead_kernel, "lead_rows", 1,
+            [fixed(*lead_shape)] + [rows(prior, 0, at)] * 4
+            + [rows(sent), rows(prior, 0, at), rows(prior, 0, at)] + [keep] * len(outs),
+            [rows(prior, 0, at)] * 4, [full16] * 4, (prior, 2 * prior, 5), 14 * tok,
+            {8 + i: i for i in range(len(outs))},
+        )(lead_bias, query_in, key_in, value_in, grad_out, before, gk_part, gv_part, *outs)
+    attn, gq, gk, gv = outs
 
     for at, after in enumerate(afters):
         late = rows(prior, late_at, at)

time: 34 us -> 48.5 us (1.43)
  Pallas kernels: 10.1 us -> 27.7 us
  waiting for transfers between devices: 13.1 us -> 6.9 us
  starting transfers between devices: 7.58 us -> 10.8 us
    pallas_call x1 -> x3, Pallas kernels: 4.25 us -> 21.8 us  [the longest x1 17 us: halo_shards(): pl.pallas_call(functools.partial(pack_kernel, prior), in_specs=[pl.BlockS...]
    ppermute x3 -> x4, waiting for transfers between devices: 13.1 us -> 6.9 us  [neighbour(): return lax.ppermute(value, ('seq', 'head'), pairs)]
    ppermute x3 -> x4, starting transfers between devices: 7.58 us -> 10.8 us  [neighbour(): return lax.ppermute(value, ('seq', 'head'), pairs)]
    slice x4 -> x0, local copies, waits for them, and re-layouts: 1.16 us -> none  [the longest x2 1.08 us: halo_shards(): key_in[tok - prior:]]
    unnamed x10, local copies, waits for them, and re-layouts: 1.05 us -> 2.09 us
  transfers between devices with their start and end apart: 3 -> 4, of which waited for: 2 -> 3; matrix products, arithmetic and copies ran while one was open for 0% -> 0% of each run, Pallas kernels for 27% -> 20%
where the time goes in v6:
time: 48.5 us; the launch traced here: 48.3 us
  Pallas kernels  27.7 us (57%)
  starting transfers between devices  10.8 us (22%)
  waiting for transfers between devices  6.9 us (14%)
  local copies, waits for them, and re-layouts  2.09 us (4%)
  between operations  0.73 us (2%)
    pallas_call x1, Pallas kernels, halo_shards(): pl.pallas_call(functools.partial(pack_kernel, prior), in_specs=[pl.BlockS...  17 us
    ppermute x4, starting transfers between devices, neighbour(): return lax.ppermute(value, ('seq', 'head'), pairs)  10.8 us
    ppermute x4, waiting for transfers between devices, neighbour(): return lax.ppermute(value, ('seq', 'head'), pairs)  6.9 us
    pallas_call x2, Pallas kernels, halo_shards(): call(lead_kernel, 'lead_rows', 1, [fixed(*lead_shape)] + [rows(prior, 0,...  4.74 us
    pallas_call x1, Pallas kernels, halo_shards(): call(own_kernel, 'own_block', groups, [fixed(*lengths.shape), rows(tok),...  3.61 us
    pallas_call x2, Pallas kernels, halo_shards(): call(tail_kernel, 'tail_keys', 1, [fixed(*tail_shape), late, late, rows(s...  2.33 us
    unnamed x10, local copies, waits for them, and re-layouts  2.09 us
  transfers between devices with their start and end apart: 4, of which 3 were waited for; matrix products, arithmetic and copies ran while one was open for 0% of the time, Pallas kernels for 20%

profile of v6, /device:TPU:0, one launch (start us, length us, event | category | flops | bytes accessed | tf_op | source)
XLA Modules:
  0.0 48.3 jit_solution(8161033991341040307)
XLA Ops:
  0.6 0.0 copy-start.1
  0.6 0.0 copy-start
  0.7 17.0 %pack_late.1 = (bf16[128,1024]{1,0:T(8,128)(2,1)}, bf16[128,1024]{1,0:T(8,128)(2,1)}) custom-call(bf16[128,2048]{1,0:T(8,128)(2,1)} %k_ref.11, bf16[128,2048]{1,0:T(8,128)(2,1)} %v_ref.11), custom_call_target="tpu_custom_call" | custom-call | tf_op jit(solution)/shard_map/pack_late/pallas_call | solution.py:401
  17.7 4.9 %collective-permute-start.1 = (bf16[128,1024]{1,0:T(8,128)(2,1)}, bf16[128,1024]{1,0:T(8,128)(2,1)S(1)}, u32[]{:S(2)}, u32[]{:S(2)}) collective-permute-start(bf16[128,1024]{1,0:T(8,128)(2,1)} %get-tuple-element.37), channel_id=1, source_target_pairs={{0,1},{1,2},{2,3},{3,4},{4,5},{5,6},{6,7},{7,8},{8,9},{9,10},{10,1... | collective-permute-start | bytes 786440 | tf_op jit(solution)/shard_map/ppermute | solution.py:355
  22.5 0.0 copy-start.4
  22.6 3.4 %collective-permute-start = (bf16[128,1024]{1,0:T(8,128)(2,1)}, bf16[128,1024]{1,0:T(8,128)(2,1)S(1)}, u32[]{:S(2)}, u32[]{:S(2)}) collective-permute-start(bf16[128,1024]{1,0:T(8,128)(2,1)} %get-tuple-element.32), channel_id=1, source_target_pairs={{0,1},{1,2},{2,3},{3,4},{4,5},{5,6},{6,7},{7,8},{8,9},{9,10},{10,1... | collective-permute-start | bytes 786440 | tf_op jit(solution)/shard_map/ppermute | solution.py:355
  26.0 0.0 copy-done.1
  26.0 0.0 copy-done
  26.0 0.0 copy-done.4
  26.0 0.0 copy-start.2
  26.0 1.0 %copy-done.2 = bf16[128,2048]{1,0:T(8,128)(2,1)S(1)} copy-done((bf16[128,2048]{1,0:T(8,128)(2,1)S(1)}, bf16[128,2048]{1,0:T(8,128)(2,1)}, u32[]{:S(2)}) %copy-start.2) | copy-done | bytes 524312
  27.0 0.0 copy-start.3
  27.0 1.0 %copy-done.3 = bf16[128,2048]{1,0:T(8,128)(2,1)S(1)} copy-done((bf16[128,2048]{1,0:T(8,128)(2,1)S(1)}, bf16[128,2048]{1,0:T(8,128)(2,1)}, u32[]{:S(2)}) %copy-start.3) | copy-done | bytes 524312
  28.1 3.6 %own_block.1 = (bf16[128,2048]{1,0:T(8,128)(2,1)}, bf16[128,2048]{1,0:T(8,128)(2,1)}, f32[128,2048]{1,0:T(8,128)S(1)}, f32[128,2048]{1,0:T(8,128)S(1)}, f32[64,1...) custom-call(s32[1,128]{1,0:T(1,128)S(1)} %bitcast.1, ...), custom_call_target="tpu_custom_call" | custom-call | flops 268435456 | bytes 5767168 | tf_op jit(solution)/shard_map/own_block/pallas_call | solution.py:411
  31.7 0.0 collective-permute-done.1.before_ref
  31.7 1.3 %collective-permute-start.3 = (bf16[128,1024]{1,0:T(8,128)(2,1)S(1)}, bf16[128,1024]{1,0:T(8,128)(2,1)S(1)}, u32[]{:S(2)}, u32[]{:S(2)}) collective-permute-start(bf16[128,1024]{1,0:T(8,128)(2,1)S(1)} %get-tuple-element.49), channel_id=1, source_target_pairs={{1,0},{2,1},{3,2},{4,3},{5,4},{6,5},{7,6},{8,7},{9,8},{10,9},{11,1... | collective-permute-start | bytes 786440 | tf_op jit(solution)/shard_map/ppermute | solution.py:355
  33.0 1.0 %collective-permute-done.before_ref = bf16[128,1024]{1,0:T(8,128)(2,1)S(1)} collective-permute-done((bf16[128,1024]{1,0:T(8,128)(2,1)}, bf16[128,1024]{1,0:T(8,128)(2,1)S(1)}, u32[]{:S(2)}, u32[]{:S(2)}) %collective-permute-start) | collective-permute-done | bytes 262176 | tf_op jit(solution)/shard_map/ppermute | solution.py:355
  34.0 1.3 %collective-permute-start.2 = (bf16[128,1024]{1,0:T(8,128)(2,1)S(1)}, bf16[128,1024]{1,0:T(8,128)(2,1)S(1)}, u32[]{:S(2)}, u32[]{:S(2)}) collective-permute-start(bf16[128,1024]{1,0:T(8,128)(2,1)S(1)} %get-tuple-element.48), channel_id=1, source_target_pairs={{1,0},{2,1},{3,2},{4,3},{5,4},{6,5},{7,6},{8,7},{9,8},{10,9},{11,1... | collective-permute-start | bytes 786440 | tf_op jit(solution)/shard_map/ppermute | solution.py:355
  35.3 2.4 %lead_rows.2 = (bf16[128,2048]{1,0:T(8,128)(2,1)}, bf16[128,2048]{1,0:T(8,128)(2,1)}, bf16[128,2048]{1,0:T(8,128)(2,1)}, bf16[128,2048]{1,0:T(8,128)(2,1)}) custom-call(f32[64,128]{1,0:T(8,128)S(1)} %get-tuple-element.30.bias_ref, bf16[128,2048]{1,0:T(8,128)(2,1)S(1)} %copy-done.2, ...), custom_call_target="tpu_custom_call", output_to_operand_aliasing={{0}: (8, {}), {1}: (9, {})} | custom-call | flops 83886080 | bytes 1835008 | tf_op jit(solution)/shard_map/lead_rows/pallas_call | solution.py:429
  37.7 2.4 %lead_rows.3 = (bf16[128,2048]{1,0:T(8,128)(2,1)}, bf16[128,2048]{1,0:T(8,128)(2,1)}, bf16[128,2048]{1,0:T(8,128)(2,1)}, bf16[128,2048]{1,0:T(8,128)(2,1)}) custom-call(f32[64,128]{1,0:T(8,128)S(1)} %get-tuple-element.30.bias_ref, bf16[128,2048]{1,0:T(8,128)(2,1)S(1)} %copy-done.2, ...), custom_call_target="tpu_custom_call", output_to_operand_aliasing={{0}: (8, {}), {1}: (9, {}), {2}: (10, {}), {3}: (11, {})} | custom-call | flops 83886080 | bytes 1835008 | tf_op jit(solution)/shard_map/lead_rows/pallas_call | solution.py:429
  40.0 2.8 %collective-permute-done.3.after_ref = bf16[128,1024]{1,0:T(8,128)(2,1)S(1)} collective-permute-done((bf16[128,1024]{1,0:T(8,128)(2,1)S(1)}, bf16[128,1024]{1,0:T(8,128)(2,1)S(1)}, u32[]{:S(2)}, u32[]{:S(2)}) %collective-permute-start.3) | collective-permute-done | bytes 262176 | tf_op jit(solution)/shard_map/ppermute | solution.py:355
  42.8 1.2 %tail_keys.2 = (bf16[128,2048]{1,0:T(8,128)(2,1)}, bf16[128,2048]{1,0:T(8,128)(2,1)}) custom-call(f32[64,64]{1,0:T(8,128)S(1)} %get-tuple-element.47.bias_ref, bf16[128,2048]{1,0:T(8,128)(2,1)S(1)} %copy-done, bf16[128,2048]{1,0:T(8,128)(2,1)S(1)} %copy-done.1, ...), custom_call_target="tpu_custom_call", output_to_operand_aliasing={{0}: (6, {}), {1}: (7, {})} | custom-call | flops 33554432 | bytes 1310720 | tf_op jit(solution)/shard_map/tail_keys/pallas_call | solution.py:440
  44.0 3.1 %collective-permute-done.2.after_ref = bf16[128,1024]{1,0:T(8,128)(2,1)S(1)} collective-permute-done((bf16[128,1024]{1,0:T(8,128)(2,1)S(1)}, bf16[128,1024]{1,0:T(8,128)(2,1)S(1)}, u32[]{:S(2)}, u32[]{:S(2)}) %collective-permute-start.2) | collective-permute-done | bytes 262176 | tf_op jit(solution)/shard_map/ppermute | solution.py:355
  47.1 1.2 %tail_keys.3 = (bf16[128,2048]{1,0:T(8,128)(2,1)}, bf16[128,2048]{1,0:T(8,128)(2,1)}) custom-call(f32[64,64]{1,0:T(8,128)S(1)} %get-tuple-element.47.bias_ref, bf16[128,2048]{1,0:T(8,128)(2,1)S(1)} %copy-done, bf16[128,2048]{1,0:T(8,128)(2,1)S(1)} %copy-done.1, ...), custom_call_target="tpu_custom_call", output_to_operand_aliasing={{0}: (6, {}), {1}: (7, {})} | custom-call | flops 33554432 | bytes 1310720 | tf_op jit(solution)/shard_map/tail_keys/pallas_call | solution.py:440
Async XLA Ops:
  0.6 25.3 %copy-start.1 = (bf16[128,2048]{1,0:T(8,128)(2,1)S(1)}, bf16[128,2048]{1,0:T(8,128)(2,1)}, u32[]{:S(2)}) copy-start(bf16[128,2048]{1,0:T(8,128)(2,1)} %v_ref.11) | copy-start | bytes 1572868
  0.6 25.3 %copy-start = (bf16[128,2048]{1,0:T(8,128)(2,1)S(1)}, bf16[128,2048]{1,0:T(8,128)(2,1)}, u32[]{:S(2)}) copy-start(bf16[128,2048]{1,0:T(8,128)(2,1)} %k_ref.11) | copy-start | bytes 1572868
  17.7 14.0 %collective-permute-start.1 = (bf16[128,1024]{1,0:T(8,128)(2,1)}, bf16[128,1024]{1,0:T(8,128)(2,1)S(1)}, u32[]{:S(2)}, u32[]{:S(2)}) collective-permute-start(bf16[128,1024]{1,0:T(8,128)(2,1)} %get-tuple-element.37), channel_id=1, source_target_pairs={{0,1},{1,2},{2,3},{3,4},{4,5},{5,6},{6,7},{7,8},{8,9},{9,10},{10,1... | collective-permute-start | bytes 786440 | tf_op jit(solution)/shard_map/ppermute | solution.py:355
  22.5 3.4 %copy-start.4 = (s32[128]{0:T(128)S(1)}, s32[128]{0:T(128)}, u32[]{:S(2)}) copy-start(s32[128]{0:T(128)} %param.9) | copy-start | bytes 1540
  22.6 11.5 %collective-permute-start = (bf16[128,1024]{1,0:T(8,128)(2,1)}, bf16[128,1024]{1,0:T(8,128)(2,1)S(1)}, u32[]{:S(2)}, u32[]{:S(2)}) collective-permute-start(bf16[128,1024]{1,0:T(8,128)(2,1)} %get-tuple-element.32), channel_id=1, source_target_pairs={{0,1},{1,2},{2,3},{3,4},{4,5},{5,6},{6,7},{7,8},{8,9},{9,10},{10,1... | collective-permute-start | bytes 786440 | tf_op jit(solution)/shard_map/ppermute | solution.py:355
  26.0 1.0 %copy-start.2 = (bf16[128,2048]{1,0:T(8,128)(2,1)S(1)}, bf16[128,2048]{1,0:T(8,128)(2,1)}, u32[]{:S(2)}) copy-start(bf16[128,2048]{1,0:T(8,128)(2,1)} %q_ref.5) | copy-start | bytes 1572868
  27.0 1.0 %copy-start.3 = (bf16[128,2048]{1,0:T(8,128)(2,1)S(1)}, bf16[128,2048]{1,0:T(8,128)(2,1)}, u32[]{:S(2)}) copy-start(bf16[128,2048]{1,0:T(8,128)(2,1)} %do_ref.5) | copy-start | bytes 1572868
  31.7 11.1 %collective-permute-start.3 = (bf16[128,1024]{1,0:T(8,128)(2,1)S(1)}, bf16[128,1024]{1,0:T(8,128)(2,1)S(1)}, u32[]{:S(2)}, u32[]{:S(2)}) collective-permute-start(bf16[128,1024]{1,0:T(8,128)(2,1)S(1)} %get-tuple-element.49), channel_id=1, source_target_pairs={{1,0},{2,1},{3,2},{4,3},{5,4},{6,5},{7,6},{8,7},{9,8},{10,9},{11,1... | collective-permute-start | bytes 786440 | tf_op jit(solution)/shard_map/ppermute | solution.py:355
  34.0 13.1 %collective-permute-start.2 = (bf16[128,1024]{1,0:T(8,128)(2,1)S(1)}, bf16[128,1024]{1,0:T(8,128)(2,1)S(1)}, u32[]{:S(2)}, u32[]{:S(2)}) collective-permute-start(bf16[128,1024]{1,0:T(8,128)(2,1)S(1)} %get-tuple-element.48), channel_id=1, source_target_pairs={{1,0},{2,1},{3,2},{4,3},{5,4},{6,5},{7,6},{8,7},{9,8},{10,9},{11,1... | collective-permute-start | bytes 786440 | tf_op jit(solution)/shard_map/ppermute | solution.py:355

commit v7 on v6

--- a/solution.py
+++ b/solution.py
@@ -233,26 +233,6 @@
     return pair[:, :half] + pair[:, half:]
 
 
-def pack_kernel(prior, k_ref, v_ref, *refs):
-    *packed_refs, sem = refs
-    last = pl.ds(k_ref.shape[0] - prior, prior)
-    copies = []
-    for at, packed_ref in enumerate(packed_refs):
-        width = packed_ref.shape[1]
-        for half, ref in enumerate((k_ref, v_ref)):
-            copies.append(
-                pltpu.make_async_copy(
-                    ref.at[last, pl.ds(at * width, width)],
-                    packed_ref.at[pl.ds(half * prior, prior), :],
-                    sem.at[2 * at + half],
-                )
-            )
-    for copy in copies:
-        copy.start()
-    for copy in copies:
-        copy.wait()
-
-
 def own_kernel(
     prior, len_ref, q_ref, k_ref, v_ref, do_ref, attn_ref, gq_ref, gk_ref, gv_ref,
     lead_bias_ref, tail_bias_ref, *refs,
@@ -384,7 +364,7 @@
     def fixed(*shape):
         return pl.BlockSpec(shape, lambda g: (0, 0))
 
-    def call(kernel, name, grid, ins, outs, shapes, work, moved, aliases=None, scratch=()):
+    def call(kernel, name, grid, ins, outs, shapes, work, moved, aliases=None, scratch=(), room=16):
         return pl.pallas_call(
             functools.partial(kernel, prior),
             grid=(grid,),
@@ -394,19 +374,15 @@
             scratch_shapes=scratch,
             input_output_aliases=aliases or {},
             cost_estimate=cost(grid * per, *work, moved * grid * step),
-            compiler_params=pltpu.CompilerParams(vmem_limit_bytes=16 * 2**20),
+            compiler_params=pltpu.CompilerParams(vmem_limit_bytes=room * 2**20),
             name=name,
         )
 
-    befores = pl.pallas_call(
-        functools.partial(pack_kernel, prior),
-        in_specs=[pl.BlockSpec(memory_space=pltpu.HBM)] * 2,
-        out_specs=[keep] * groups,
-        out_shape=[packed] * groups,
-        scratch_shapes=[pltpu.SemaphoreType.DMA((2 * groups,))],
-        name="pack_late",
-    )(key_in, value_in)
-    befores = [neighbour(part, 1) for part in befores]
+    befores = []
+    for at in range(groups):
+        cols = slice(at * step, (at + 1) * step)
+        late_kv = [key_in[tok - prior :, cols], value_in[tok - prior :, cols]]
+        befores.append(neighbour(jnp.concatenate(late_kv), 1))
 
     attn, gq, gk_part, gv_part, lead_bias, tail_bias, *parts = call(
         own_kernel, "own_block", groups,
@@ -420,6 +396,7 @@
         scratch=[
             pltpu.VMEM((tok - prior, tok), jnp.float32), pltpu.VMEM((prior, prior), jnp.float32)
         ],
+        room=56,
     )(lengths, query_in, key_in, value_in, grad_out)
     outs = [attn, gq]
     afters = []

time: 48.5 us -> 33.5 us (0.69)
  the two profiles are of different devices: /device:TPU:0 before, /device:TPU:1 now
where the time goes in v7:
time: 33.5 us; the launch traced here: 33.2 us
  starting transfers between devices  15.6 us (47%)
  Pallas kernels  12.3 us (37%)
  local copies, waits for them, and re-layouts  4.37 us (13%)
  between operations  0.8 us (2%)
    ppermute x4, starting transfers between devices, neighbour(): return lax.ppermute(value, ('seq', 'head'), pairs)  15.6 us
    pallas_call x1, Pallas kernels, halo_shards(): call(own_kernel, 'own_block', groups, [fixed(*lengths.shape), rows(tok),...  5.27 us
    pallas_call x2, Pallas kernels, halo_shards(): call(lead_kernel, 'lead_rows', 1, [fixed(*lead_shape)] + [rows(prior, 0,...  4.74 us
    unnamed x20, local copies, waits for them, and re-layouts  3.24 us
    pallas_call x2, Pallas kernels, halo_shards(): call(tail_kernel, 'tail_keys', 1, [fixed(*tail_shape), late, late, rows(s...  2.34 us
    slice x1, local copies, waits for them, and re-layouts, halo_shards(): late_kv = [key_in[tok - prior:, cols], value_in[tok - prior:, cols]]  1.13 us
  transfers between devices with their start and end apart: 4, of which 0 were waited for; matrix products, arithmetic and copies ran while one was open for 0% of the time, Pallas kernels for 34%

profile of v7, /device:TPU:1, one launch (start us, length us, event | category | flops | bytes accessed | tf_op | source)
XLA Modules:
  0.0 33.2 jit_solution(8983770549078117097)
XLA Ops:
  0.6 1.1 %fusion = (bf16[64,1024]{1,0:T(8,128)(2,1)S(1)}, bf16[64,1024]{1,0:T(8,128)(2,1)S(1)}, bf16[64,1024]{1,0:T(8,128)(2,1)S(1)}, bf16[64,1024]{1,0:T(8,128)(2,1)S(1)}) fusion(bf16[128,2048]{1,0:T(8,128)(2,1)} %k_ref.9, bf16[128,2048]{1,0:T(8,128)(2,1)} %v_ref.9), kind=kLoop, calls=%fused_computation.2 | loop fusion | bytes 1048576 | tf_op jit(solution)/shard_map/slice | solution.py:384
  1.8 3.9 %collective-permute-start.1 = (bf16[128,1024]{1,0:T(8,128)(2,1)S(1)}, bf16[128,1024]{1,0:T(8,128)(2,1)S(1)}, u32[]{:S(2)}, u32[]{:S(2)}) collective-permute-start(bf16[128,1024]{1,0:T(8,128)(2,1)S(1)} %pad_maximum_fusion.1), channel_id=1, source_target_pairs={{0,1},{1,2},{2,3},{3,4},{4,5},{5,6},{6,7},{7,8},{8,9},{9,10},{10,1... | collective-permute-start | bytes 786440 | tf_op jit(solution)/shard_map/ppermute | solution.py:335
  5.8 3.1 %collective-permute-start = (bf16[128,1024]{1,0:T(8,128)(2,1)S(1)}, bf16[128,1024]{1,0:T(8,128)(2,1)S(1)}, u32[]{:S(2)}, u32[]{:S(2)}) collective-permute-start(bf16[128,1024]{1,0:T(8,128)(2,1)S(1)} %pad_maximum_fusion), channel_id=1, source_target_pairs={{0,1},{1,2},{2,3},{3,4},{4,5},{5,6},{6,7},{7,8},{8,9},{9,10},{10,1... | collective-permute-start | bytes 786440 | tf_op jit(solution)/shard_map/ppermute | solution.py:335
  8.9 0.0 copy-start.4
  8.9 0.0 copy-start.5
  8.9 0.0 copy-start.6
  8.9 0.0 copy-start.7
  9.0 5.3 %own_block.1 = (bf16[128,2048]{1,0:T(8,128)(2,1)}, bf16[128,2048]{1,0:T(8,128)(2,1)}, f32[128,2048]{1,0:T(8,128)}, f32[128,2048]{1,0:T(8,128)}, f32[64,128]{1,0:...) custom-call(s32[1,128]{1,0:T(1,128)} %bitcast.1, bf16[128,2048]{1,0:T(8,128)(2,1)} %q_ref.5, ...), custom_call_target="tpu_custom_call" | custom-call | flops 268435456 | bytes 5767168 | tf_op jit(solution)/shard_map/own_block/pallas_call | solution.py:387
  14.2 0.0 collective-permute-done.1.before_ref
  14.2 4.1 %collective-permute-start.3 = (bf16[128,1024]{1,0:T(8,128)(2,1)}, bf16[128,1024]{1,0:T(8,128)(2,1)S(1)}, u32[]{:S(2)}, u32[]{:S(2)}) collective-permute-start(bf16[128,1024]{1,0:T(8,128)(2,1)} %get-tuple-element.45), channel_id=1, source_target_pairs={{1,0},{2,1},{3,2},{4,3},{5,4},{6,5},{7,6},{8,7},{9,8},{10,9},{11,1... | collective-permute-start | bytes 786440 | tf_op jit(solution)/shard_map/ppermute | solution.py:335
  18.3 0.0 collective-permute-done.before_ref
  18.4 4.5 %collective-permute-start.2 = (bf16[128,1024]{1,0:T(8,128)(2,1)}, bf16[128,1024]{1,0:T(8,128)(2,1)S(1)}, u32[]{:S(2)}, u32[]{:S(2)}) collective-permute-start(bf16[128,1024]{1,0:T(8,128)(2,1)} %get-tuple-element.44), channel_id=1, source_target_pairs={{1,0},{2,1},{3,2},{4,3},{5,4},{6,5},{7,6},{8,7},{9,8},{10,9},{11,1... | collective-permute-start | bytes 786440 | tf_op jit(solution)/shard_map/ppermute | solution.py:335
  22.8 0.0 copy-done.4
  22.8 0.0 copy-done.5
  22.8 0.0 copy-done.6
  22.8 0.0 copy-done.7
  22.9 0.0 copy-start
  22.9 1.2 %copy-done = f32[128,2048]{1,0:T(8,128)S(1)} copy-done((f32[128,2048]{1,0:T(8,128)S(1)}, f32[128,2048]{1,0:T(8,128)}, u32[]{:S(2)}) %copy-start) | copy-done | bytes 1048600
  24.1 0.0 copy-start.2
  24.1 1.2 %copy-done.2 = f32[128,2048]{1,0:T(8,128)S(1)} copy-done((f32[128,2048]{1,0:T(8,128)S(1)}, f32[128,2048]{1,0:T(8,128)}, u32[]{:S(2)}) %copy-start.2) | copy-done | bytes 1048600
  25.3 0.0 copy-start.9
  25.3 0.8 %copy-done.9 = f32[64,128]{1,0:T(8,128)S(1)} copy-done((f32[64,128]{1,0:T(8,128)S(1)}, f32[64,128]{1,0:T(8,128)}, u32[]{:S(2)}) %copy-start.9) | copy-done | bytes 32792
  26.1 2.4 %lead_rows.2 = (bf16[128,2048]{1,0:T(8,128)(2,1)}, bf16[128,2048]{1,0:T(8,128)(2,1)}, bf16[128,2048]{1,0:T(8,128)(2,1)}, bf16[128,2048]{1,0:T(8,128)(2,1)}) custom-call(f32[64,128]{1,0:T(8,128)S(1)} %copy-done.9, bf16[128,2048]{1,0:T(8,128)(2,1)S(1)} %copy-done.6, bf16[128,2048]{1,0:T(8,128)(2,1)S(1)} %copy-done.4, ...), custom_call_target="tpu_custom_call", output_to_operand_aliasing={{0}: (8, {}), {1}: (9, {})} | custom-call | flops 83886080 | bytes 1835008 | tf_op jit(solution)/shard_map/lead_rows/pallas_call | solution.py:406
  28.4 0.0 copy-start.1
  28.4 0.0 copy-start.3
  28.4 0.0 copy-start.8
  28.4 2.4 %lead_rows.3 = (bf16[128,2048]{1,0:T(8,128)(2,1)}, bf16[128,2048]{1,0:T(8,128)(2,1)}, bf16[128,2048]{1,0:T(8,128)(2,1)}, bf16[128,2048]{1,0:T(8,128)(2,1)}) custom-call(f32[64,128]{1,0:T(8,128)S(1)} %copy-done.9, bf16[128,2048]{1,0:T(8,128)(2,1)S(1)} %copy-done.6, ...), custom_call_target="tpu_custom_call", output_to_operand_aliasing={{0}: (8, {}), {1}: (9, {}), {2}: (10, {}), {3}: (11, {})} | custom-call | flops 83886080 | bytes 1835008 | tf_op jit(solution)/shard_map/lead_rows/pallas_call | solution.py:406
  30.8 0.0 collective-permute-done.3.after_ref
  30.8 0.0 copy-done.1
  30.8 0.0 copy-done.3
  30.8 0.0 copy-done.8
  30.8 1.2 %tail_keys.2 = (bf16[128,2048]{1,0:T(8,128)(2,1)}, bf16[128,2048]{1,0:T(8,128)(2,1)}) custom-call(f32[64,64]{1,0:T(8,128)S(1)} %copy-done.8, bf16[128,2048]{1,0:T(8,128)(2,1)S(1)} %copy-done.4, bf16[128,2048]{1,0:T(8,128)(2,1)S(1)} %copy-done.5, ...), custom_call_target="tpu_custom_call", output_to_operand_aliasing={{0}: (6, {}), {1}: (7, {})} | custom-call | flops 33554432 | bytes 1310720 | tf_op jit(solution)/shard_map/tail_keys/pallas_call | solution.py:417
  32.0 0.0 collective-permute-done.2.after_ref
  32.0 1.2 %tail_keys.3 = (bf16[128,2048]{1,0:T(8,128)(2,1)}, bf16[128,2048]{1,0:T(8,128)(2,1)}) custom-call(f32[64,64]{1,0:T(8,128)S(1)} %copy-done.8, bf16[128,2048]{1,0:T(8,128)(2,1)S(1)} %copy-done.4, bf16[128,2048]{1,0:T(8,128)(2,1)S(1)} %copy-done.5, ...), custom_call_target="tpu_custom_call", output_to_operand_aliasing={{0}: (6, {}), {1}: (7, {})} | custom-call | flops 33554432 | bytes 1310720 | tf_op jit(solution)/shard_map/tail_keys/pallas_call | solution.py:417
  (2 shorter events, 0.0 us)
Async XLA Ops:
  1.8 12.4 %collective-permute-start.1 = (bf16[128,1024]{1,0:T(8,128)(2,1)S(1)}, bf16[128,1024]{1,0:T(8,128)(2,1)S(1)}, u32[]{:S(2)}, u32[]{:S(2)}) collective-permute-start(bf16[128,1024]{1,0:T(8,128)(2,1)S(1)} %pad_maximum_fusion.1), channel_id=1, source_target_pairs={{0,1},{1,2},{2,3},{3,4},{4,5},{5,6},{6,7},{7,8},{8,9},{9,10},{10,1... | collective-permute-start | bytes 786440 | tf_op jit(solution)/shard_map/ppermute | solution.py:335
  5.8 12.6 %collective-permute-start = (bf16[128,1024]{1,0:T(8,128)(2,1)S(1)}, bf16[128,1024]{1,0:T(8,128)(2,1)S(1)}, u32[]{:S(2)}, u32[]{:S(2)}) collective-permute-start(bf16[128,1024]{1,0:T(8,128)(2,1)S(1)} %pad_maximum_fusion), channel_id=1, source_target_pairs={{0,1},{1,2},{2,3},{3,4},{4,5},{5,6},{6,7},{7,8},{8,9},{9,10},{10,1... | collective-permute-start | bytes 786440 | tf_op jit(solution)/shard_map/ppermute | solution.py:335
  8.9 13.9 %copy-start.4 = (bf16[128,2048]{1,0:T(8,128)(2,1)S(1)}, bf16[128,2048]{1,0:T(8,128)(2,1)}, u32[]{:S(2)}) copy-start(bf16[128,2048]{1,0:T(8,128)(2,1)} %k_ref.9) | copy-start | bytes 1572868
  8.9 13.9 %copy-start.5 = (bf16[128,2048]{1,0:T(8,128)(2,1)S(1)}, bf16[128,2048]{1,0:T(8,128)(2,1)}, u32[]{:S(2)}) copy-start(bf16[128,2048]{1,0:T(8,128)(2,1)} %v_ref.9) | copy-start | bytes 1572868
  8.9 13.9 %copy-start.6 = (bf16[128,2048]{1,0:T(8,128)(2,1)S(1)}, bf16[128,2048]{1,0:T(8,128)(2,1)}, u32[]{:S(2)}) copy-start(bf16[128,2048]{1,0:T(8,128)(2,1)} %q_ref.5) | copy-start | bytes 1572868
  8.9 13.9 %copy-start.7 = (bf16[128,2048]{1,0:T(8,128)(2,1)S(1)}, bf16[128,2048]{1,0:T(8,128)(2,1)}, u32[]{:S(2)}) copy-start(bf16[128,2048]{1,0:T(8,128)(2,1)} %do_ref.5) | copy-start | bytes 1572868
  14.2 16.6 %collective-permute-start.3 = (bf16[128,1024]{1,0:T(8,128)(2,1)}, bf16[128,1024]{1,0:T(8,128)(2,1)S(1)}, u32[]{:S(2)}, u32[]{:S(2)}) collective-permute-start(bf16[128,1024]{1,0:T(8,128)(2,1)} %get-tuple-element.45), channel_id=1, source_target_pairs={{1,0},{2,1},{3,2},{4,3},{5,4},{6,5},{7,6},{8,7},{9,8},{10,9},{11,1... | collective-permute-start | bytes 786440 | tf_op jit(solution)/shard_map/ppermute | solution.py:335
  18.4 13.7 %collective-permute-start.2 = (bf16[128,1024]{1,0:T(8,128)(2,1)}, bf16[128,1024]{1,0:T(8,128)(2,1)S(1)}, u32[]{:S(2)}, u32[]{:S(2)}) collective-permute-start(bf16[128,1024]{1,0:T(8,128)(2,1)} %get-tuple-element.44), channel_id=1, source_target_pairs={{1,0},{2,1},{3,2},{4,3},{5,4},{6,5},{7,6},{8,7},{9,8},{10,9},{11,1... | collective-permute-start | bytes 786440 | tf_op jit(solution)/shard_map/ppermute | solution.py:335
  22.9 1.2 %copy-start = (f32[128,2048]{1,0:T(8,128)S(1)}, f32[128,2048]{1,0:T(8,128)}, u32[]{:S(2)}) copy-start(f32[128,2048]{1,0:T(8,128)} %get-tuple-element.31.gk_part_ref) | copy-start | bytes 3145732
  24.1 1.2 %copy-start.2 = (f32[128,2048]{1,0:T(8,128)S(1)}, f32[128,2048]{1,0:T(8,128)}, u32[]{:S(2)}) copy-start(f32[128,2048]{1,0:T(8,128)} %get-tuple-element.32.gv_part_ref) | copy-start | bytes 3145732
  25.3 0.8 %copy-start.9 = (f32[64,128]{1,0:T(8,128)S(1)}, f32[64,128]{1,0:T(8,128)}, u32[]{:S(2)}) copy-start(f32[64,128]{1,0:T(8,128)} %get-tuple-element.28.bias_ref) | copy-start | bytes 98308
  28.4 2.4 %copy-start.1 = (f32[128,2048]{1,0:T(8,128)S(1)}, f32[128,2048]{1,0:T(8,128)}, u32[]{:S(2)}) copy-start(f32[128,2048]{1,0:T(8,128)} %get-tuple-element.31.gk_part_ref) | copy-start | bytes 3145732
  28.4 2.4 %copy-start.3 = (f32[128,2048]{1,0:T(8,128)S(1)}, f32[128,2048]{1,0:T(8,128)}, u32[]{:S(2)}) copy-start(f32[128,2048]{1,0:T(8,128)} %get-tuple-element.32.gv_part_ref) | copy-start | bytes 3145732
  28.4 2.4 %copy-start.8 = (f32[64,64]{1,0:T(8,128)S(1)}, f32[64,64]{1,0:T(8,128)}, u32[]{:S(2)}) copy-start(f32[64,64]{1,0:T(8,128)} %get-tuple-element.43.bias_ref) | copy-start | bytes 49156

commit v8 on v7

--- a/solution.py
+++ b/solution.py
@@ -186,30 +186,17 @@
 def full_rows(pairs):
     tops = [jnp.max(s, axis=1, keepdims=True) for s, _ in pairs]
     raws = [jnp.exp2(s - top) for (s, _), top in zip(pairs, tops)]
-    parts = [1.0 / jnp.sum(raw, axis=1, keepdims=True) for raw in raws]
-    weights = [raw * part for raw, part in zip(raws, parts)]
+    totals = [jnp.sum(raw, axis=1, keepdims=True) for raw in raws]
+    weights = [raw * (1.0 / total) for raw, total in zip(raws, totals)]
     deltas = [jnp.sum(w * dp, axis=1, keepdims=True) for w, (_, dp) in zip(weights, pairs)]
     grads = [w * (dp - delta) * SCALE for w, (_, dp), delta in zip(weights, pairs, deltas)]
-    return [w.astype(jnp.bfloat16) for w in weights], [g.astype(jnp.bfloat16) for g in grads]
-
-
-def merged_rows(pairs, own):
-    tops = [
-        jnp.maximum(jnp.max(s, axis=0, keepdims=True), log) for (s, _), (log, _) in zip(pairs, own)
-    ]
-    raws = [jnp.exp2(s - top) for (s, _), top in zip(pairs, tops)]
-    own_raws = [jnp.exp2(log - top) for (log, _), top in zip(own, tops)]
-    parts = [
-        1.0 / (jnp.sum(raw, axis=0, keepdims=True) + own_raw)
-        for raw, own_raw in zip(raws, own_raws)
-    ]
-    weights = [raw * part for raw, part in zip(raws, parts)]
-    deltas = [
-        jnp.sum(w * dp, axis=0, keepdims=True) + own_raw * part * own_delta
-        for w, (_, dp), own_raw, part, (_, own_delta) in zip(weights, pairs, own_raws, parts, own)
-    ]
-    grads = [w * (dp - delta) * SCALE for w, (_, dp), delta in zip(weights, pairs, deltas)]
-    return [w.astype(jnp.bfloat16) for w in weights], [g.astype(jnp.bfloat16) for g in grads]
+    logs = [top + jnp.log2(total) for top, total in zip(tops, totals)]
+    return (
+        [w.astype(jnp.bfloat16) for w in weights],
+        [g.astype(jnp.bfloat16) for g in grads],
+        logs,
+        deltas,
+    )
 
 
 def head_columns(width):
@@ -221,86 +208,88 @@
     return place * tok
 
 
+def as_rows(columns):
+    count = columns[0].shape[0]
+    lane = lax.broadcasted_iota(jnp.int32, (count, HEAD_DIM), 1)
+    table = jnp.zeros((count, HEAD_DIM), jnp.float32)
+    for at, column in enumerate(columns):
+        table = jnp.where(lane == at, column, table)
+    fill = jnp.zeros((HEAD_DIM - count, HEAD_DIM), jnp.float32)
+    table = jnp.transpose(jnp.concatenate([table, fill], axis=0))
+    return [table[at : at + 1, :count] for at in range(len(columns))]
+
+
 def split_bf16(row):
-    high = row.astype(jnp.bfloat16)
-    low = (row - high.astype(jnp.float32)).astype(jnp.bfloat16)
-    return jnp.concatenate([high, low], axis=1)
-
-
-def joined(pair):
-    pair = pair.astype(jnp.float32)
-    half = pair.shape[1] // 2
-    return pair[:, :half] + pair[:, half:]
+    parts = []
+    for _ in range(3):
+        part = row.astype(jnp.bfloat16)
+        parts.append(part)
+        row = row - part.astype(jnp.float32)
+    return jnp.concatenate([*parts, jnp.zeros_like(parts[0])], axis=1)
+
+
+def joined(parts):
+    parts = parts.astype(jnp.float32)
+    count = parts.shape[1] // 4
+    return parts[:, :count] + parts[:, count : 2 * count] + parts[:, 2 * count : 3 * count]
 
 
 def own_kernel(
     prior, len_ref, q_ref, k_ref, v_ref, do_ref, attn_ref, gq_ref, gk_ref, gv_ref,
-    lead_bias_ref, tail_bias_ref, *refs,
+    lead_bias_ref, tail_bias_ref, bias_ref,
 ):
-    *packed_refs, bias_ref, first_bias_ref = refs
     tok, width = k_ref.shape
     columns = head_columns(width)
-    early, late = slice(0, prior), slice(tok - prior, tok)
 
     @pl.when(pl.program_id(0) == 0)
     def _():
         first = device_first(tok)
         lengths = len_ref[...].astype(jnp.float32)
         bias_ref[...] = bias_by_query(lengths, first + prior, tok - prior, first, tok)
-        first_bias_ref[...] = bias_by_key(lengths, first, prior, first, prior)
         lead_bias_ref[...] = bias_by_query(lengths, first, prior, first - prior, 2 * prior)
-        tail_bias_ref[...] = bias_by_key(lengths, first + tok, prior, first + tok - prior, prior)
-
-    bias, first_bias = bias_ref[...], first_bias_ref[...]
-    pairs = [
-        by_query(q_ref[late, c], k_ref[:, c], do_ref[late, c], v_ref[:, c], bias) for c in columns
-    ]
-    firsts = [
-        by_query(k_ref[early, c], q_ref[early, c], v_ref[early, c], do_ref[early, c], first_bias)
-        for c in columns
-    ]
-    weights, grads = full_rows(pairs)
+        tail_bias_ref[...] = bias_by_key(
+            lengths, first + tok, prior // 2, first + tok - prior, prior
+        )
+
+    bias = bias_ref[...]
+    pairs = [by_query(q_ref[:, c], k_ref[:, c], do_ref[:, c], v_ref[:, c], bias) for c in columns]
+    weights, grads, _, _ = full_rows(pairs)
     for c, w, g in zip(columns, weights, grads):
         attn_ref[:, c] = dot(w, v_ref[:, c], 1, 0).astype(jnp.bfloat16)
         gq_ref[:, c] = dot(g, k_ref[:, c], 1, 0).astype(jnp.bfloat16)
-        gk_ref[:, c] = dot(g, q_ref[late, c], 0, 0)
-        gv_ref[:, c] = dot(w, do_ref[late, c], 0, 0)
-    tops = [jnp.max(s, axis=0, keepdims=True) for s, _ in firsts]
-    raws = [jnp.exp2(s - top) for (s, _), top in zip(firsts, tops)]
-    totals = [jnp.sum(raw, axis=0, keepdims=True) for raw in raws]
-    sums = [jnp.sum(raw * dp, axis=0, keepdims=True) for raw, (_, dp) in zip(raws, firsts)]
-    logs = [split_bf16(top + jnp.log2(total)) for top, total in zip(tops, totals)]
-    deltas = [split_bf16(summed / total) for summed, total in zip(sums, totals)]
-    spare = lax.broadcasted_iota(jnp.int32, (prior, 1), 0) == prior - 1
-    for at, packed_ref in enumerate(packed_refs):
-
-        @pl.when(pl.program_id(0) == at)
-        def _(packed_ref=packed_ref):
-            for c, log, delta in zip(columns, logs, deltas):
-                packed_ref[early, c] = jnp.where(spare, log, q_ref[early, c])
-                packed_ref[prior : 2 * prior, c] = jnp.where(spare, delta, do_ref[early, c])
+        gk_ref[:, c] = dot(g, q_ref[:, c], 0, 0)
+        gv_ref[:, c] = dot(w, do_ref[:, c], 0, 0)
 
 
 def lead_kernel(
     prior, bias_ref, q_ref, k_ref, v_ref, do_ref, before_ref, gk_part_ref, gv_part_ref, *refs
 ):
-    attn_ref, gq_ref, gk_ref, gv_ref = refs[-4:]
+    attn_ref, gq_ref, gk_ref, gv_ref, back_ref = refs[-5:]
     columns = head_columns(q_ref.shape[1])
+    half = prior // 2
     bias = bias_ref[...]
+    many = bias_ref[half - 1 : half, prior - 1 : prior] == 0.0
+    spare = lax.broadcasted_iota(jnp.int32, (half, 1), 0) == half - 1
     early, late = slice(0, prior), slice(prior, 2 * prior)
     keys = [jnp.concatenate([before_ref[early, c], k_ref[:, c]], axis=0) for c in columns]
     values = [jnp.concatenate([before_ref[late, c], v_ref[:, c]], axis=0) for c in columns]
     pairs = [
         by_query(q_ref[:, c], k, do_ref[:, c], v, bias) for c, k, v in zip(columns, keys, values)
     ]
-    weights, grads = full_rows(pairs)
-    for c, w, g, k, v in zip(columns, weights, grads, keys, values):
+    weights, grads, logs, deltas = full_rows(pairs)
+    rows = as_rows([column[:half] for column in logs + deltas])
+    logs, deltas = rows[: len(columns)], rows[len(columns) :]
+    for c, w, g, k, v, log, delta in zip(columns, weights, grads, keys, values, logs, deltas):
         attn_ref[:, c] = dot(w, v, 1, 0).astype(jnp.bfloat16)
         gq_ref[:, c] = dot(g, k, 1, 0).astype(jnp.bfloat16)
-        gk = gk_part_ref[:, c] + dot(g[:, late], q_ref[:, c], 0, 0)
-        gv = gv_part_ref[:, c] + dot(w[:, late], do_ref[:, c], 0, 0)
-        gk_ref[:, c] = gk.astype(jnp.bfloat16)
-        gv_ref[:, c] = gv.astype(jnp.bfloat16)
+        gk = dot(g, q_ref[:, c], 0, 0)
+        gv = dot(w, do_ref[:, c], 0, 0)
+        gk_ref[:, c] = (gk_part_ref[:, c] + gk[prior:]).astype(jnp.bfloat16)
+        gv_ref[:, c] = (gv_part_ref[:, c] + gv[prior:]).astype(jnp.bfloat16)
+        few_q = jnp.where(spare, split_bf16(log), q_ref[:half, c])
+        few_do = jnp.where(spare, split_bf16(delta), do_ref[:half, c])
+        back_ref[:half, c] = jnp.where(many, gk[half:prior].astype(jnp.bfloat16), few_q)
+        back_ref[half:, c] = jnp.where(many, gv[half:prior].astype(jnp.bfloat16), few_do)
 
 
 def tail_kernel(
@@ -308,25 +297,30 @@
     gk_in, gv_in, gk_ref, gv_ref,
 ):
     columns = head_columns(k_ref.shape[1])
-    bias = bias_ref[...]
-    early, late = slice(0, prior), slice(prior, 2 * prior)
+    half = prior // 2
+    many = bias_ref[prior - 1 : prior, half - 1 : half] == 0.0
+    bias = jnp.where(many, MASKED, bias_ref[...])
+    first, second = slice(0, half), slice(half, prior)
     pairs = [
-        by_query(k_ref[:, c], after_ref[early, c], v_ref[:, c], after_ref[late, c], bias)
+        by_query(k_ref[:, c], after_ref[first, c], v_ref[:, c], after_ref[second, c], bias)
         for c in columns
     ]
-    own = [
-        (
-            joined(after_ref[prior - 1 : prior, c]),
-            joined(after_ref[2 * prior - 1 : 2 * prior, c]),
-        )
-        for c in columns
+    weights = [
+        jnp.exp2(s - joined(after_ref[half - 1 : half, c])) for (s, _), c in zip(pairs, columns)
     ]
-    weights, grads = merged_rows(pairs, own)
+    grads = [
+        w * (dp - joined(after_ref[prior - 1 : prior, c])) * SCALE
+        for w, (_, dp), c in zip(weights, pairs, columns)
+    ]
     for c, w, g in zip(columns, weights, grads):
-        gk = gk_part_ref[:, c] + dot(g, after_ref[early, c], 1, 0)
-        gv = gv_part_ref[:, c] + dot(w, after_ref[late, c], 1, 0)
-        gk_ref[:, c] = gk.astype(jnp.bfloat16)
-        gv_ref[:, c] = gv.astype(jnp.bfloat16)
+        for out_ref, part_ref, left, rows in (
+            (gk_ref, gk_part_ref, g, first), (gv_ref, gv_part_ref, w, second)
+        ):
+            came = after_ref[rows, c]
+            total = part_ref[:, c] + dot(left.astype(jnp.bfloat16), came, 1, 0)
+            terms = jnp.where(many, came.astype(jnp.float32), 0.0)
+            out_ref[first, c] = total[first].astype(jnp.bfloat16)
+            out_ref[second, c] = (total[second] + terms).astype(jnp.bfloat16)
 
 
 def neighbour(value, by):
@@ -350,13 +344,12 @@
     groups = width // step
     per = step // HEAD_DIM
     late_at = tok // prior - 1
-    sent = 2 * prior
     lengths = module_lengths.reshape(1, -1)
     keep = pl.BlockSpec(memory_space=pl.ANY)
     full16 = jax.ShapeDtypeStruct((tok, width), jnp.bfloat16)
-    full32 = jax.ShapeDtypeStruct((tok, width), jnp.float32)
-    packed = jax.ShapeDtypeStruct((sent, step), jnp.bfloat16)
-    lead_shape, tail_shape = (prior, 2 * prior), (prior, prior)
+    part32 = pltpu.VMEM((tok, width), jnp.float32)
+    back16 = jax.ShapeDtypeStruct((prior, step), jnp.bfloat16)
+    lead_shape, tail_shape = (prior, 2 * prior), (prior, prior // 2)
 
     def rows(count, at=0, base=0):
         return pl.BlockSpec((count, step), lambda g: (at, g + base))
@@ -364,7 +357,7 @@
     def fixed(*shape):
         return pl.BlockSpec(shape, lambda g: (0, 0))
 
-    def call(kernel, name, grid, ins, outs, shapes, work, moved, aliases=None, scratch=(), room=16):
+    def call(kernel, name, grid, ins, outs, shapes, work, moved, aliases=None, scratch=()):
         return pl.pallas_call(
             functools.partial(kernel, prior),
             grid=(grid,),
@@ -374,7 +367,7 @@
             scratch_shapes=scratch,
             input_output_aliases=aliases or {},
             cost_estimate=cost(grid * per, *work, moved * grid * step),
-            compiler_params=pltpu.CompilerParams(vmem_limit_bytes=room * 2**20),
+            compiler_params=pltpu.CompilerParams(vmem_limit_bytes=16 * 2**20),
             name=name,
         )
 
@@ -384,40 +377,40 @@
         late_kv = [key_in[tok - prior :, cols], value_in[tok - prior :, cols]]
         befores.append(neighbour(jnp.concatenate(late_kv), 1))
 
-    attn, gq, gk_part, gv_part, lead_bias, tail_bias, *parts = call(
+    in_hbm = [
+        pltpu.with_memory_space_constraint(value, pltpu.HBM)
+        for value in (query_in, key_in, value_in, grad_out)
+    ]
+    attn, gq, gk_part, gv_part, lead_bias, tail_bias = call(
         own_kernel, "own_block", groups,
-        [fixed(*lengths.shape), rows(tok), rows(tok), rows(tok), rows(tok)],
+        [fixed(*lengths.shape), rows(prior, late_at), rows(tok), rows(tok), rows(prior, late_at)],
         [rows(prior, late_at), rows(prior, late_at), rows(tok), rows(tok)]
-        + [fixed(*lead_shape), fixed(*tail_shape)] + [fixed(sent, step)] * groups,
-        [full16, full16, full32, full32]
-        + [jax.ShapeDtypeStruct(shape, jnp.float32) for shape in (lead_shape, tail_shape)]
-        + [packed] * groups,
-        (tok, tok, 4), 22 * tok,
-        scratch=[
-            pltpu.VMEM((tok - prior, tok), jnp.float32), pltpu.VMEM((prior, prior), jnp.float32)
-        ],
-        room=56,
-    )(lengths, query_in, key_in, value_in, grad_out)
+        + [fixed(*lead_shape), fixed(*tail_shape)],
+        [full16, full16, part32, part32]
+        + [pltpu.VMEM(shape, jnp.float32) for shape in (lead_shape, tail_shape)],
+        (tok - prior, tok, 6), 18 * tok,
+        scratch=[pltpu.VMEM((tok - prior, tok), jnp.float32)],
+    )(lengths, *in_hbm)
+
     outs = [attn, gq]
     afters = []
-    for at, (part, before) in enumerate(zip(parts, befores)):
-        part, before = lax.optimization_barrier((part, before))
-        afters.append(neighbour(part, -1))
-        outs = call(
+    for at, before in enumerate(befores):
+        *outs, back = call(
             lead_kernel, "lead_rows", 1,
             [fixed(*lead_shape)] + [rows(prior, 0, at)] * 4
-            + [rows(sent), rows(prior, 0, at), rows(prior, 0, at)] + [keep] * len(outs),
-            [rows(prior, 0, at)] * 4, [full16] * 4, (prior, 2 * prior, 5), 14 * tok,
-            {8 + i: i for i in range(len(outs))},
+            + [rows(2 * prior), rows(prior, 0, at), rows(prior, 0, at)] + [keep] * len(outs),
+            [rows(prior, 0, at)] * 4 + [rows(prior)], [full16] * 4 + [back16],
+            (prior, 2 * prior, 6), 16 * tok, {8 + i: i for i in range(len(outs))},
         )(lead_bias, query_in, key_in, value_in, grad_out, before, gk_part, gv_part, *outs)
+        afters.append(neighbour(back, -1))
     attn, gq, gk, gv = outs
 
     for at, after in enumerate(afters):
         late = rows(prior, late_at, at)
         gk, gv = call(
             tail_kernel, "tail_keys", 1,
-            [fixed(*tail_shape), late, late, rows(sent), late, late, keep, keep],
-            [late, late], [full16] * 2, (prior, prior, 4), 10 * tok, {6: 0, 7: 1},
+            [fixed(*tail_shape), late, late, rows(prior), late, late, keep, keep],
+            [late, late], [full16] * 2, (prior, prior // 2, 4), 10 * tok, {6: 0, 7: 1},
         )(tail_bias, key_in, value_in, after, gk_part, gv_part, gk, gv)
     return (attn, gq, gk, gv)
 

time: 33.5 us -> 30.4 us (0.907)
  the two profiles are of different devices: /device:TPU:1 before, /device:TPU:25 now
where the time goes in v8:
time: 30.4 us; the launch traced here: 30.1 us
  starting transfers between devices  11 us (36%)
  Pallas kernels  10.3 us (34%)
  waiting for transfers between devices  6.9 us (23%)
  local copies, waits for them, and re-layouts  1.17 us (4%)
  between operations  0.76 us (2%)
    ppermute x4, starting transfers between devices, neighbour(): return lax.ppermute(value, ('seq', 'head'), pairs)  11 us
    ppermute x4, waiting for transfers between devices, neighbour(): return lax.ppermute(value, ('seq', 'head'), pairs)  6.9 us
    pallas_call x1, Pallas kernels, halo_shards(): call(own_kernel, 'own_block', groups, [fixed(*lengths.shape), rows(prior,...  4.35 us
    pallas_call x2, Pallas kernels, halo_shards(): call(lead_kernel, 'lead_rows', 1, [fixed(*lead_shape)] + [rows(prior, 0,...  3.75 us
    pallas_call x2, Pallas kernels, halo_shards(): call(tail_kernel, 'tail_keys', 1, [fixed(*tail_shape), late, late, rows(p...  2.19 us
    slice x1, local copies, waits for them, and re-layouts, halo_shards(): late_kv = [key_in[tok - prior:, cols], value_in[tok - prior:, cols]]  1.13 us
  transfers between devices with their start and end apart: 4, of which 2 were waited for; matrix products, arithmetic and copies ran while one was open for 0% of the time, Pallas kernels for 31%

profile of v8, /device:TPU:25, one launch (start us, length us, event | category | flops | bytes accessed | tf_op | source)
XLA Modules:
  0.0 30.1 jit_solution(4875790524313022777)
XLA Ops:
  0.6 1.1 %fusion = (bf16[64,1024]{1,0:T(8,128)(2,1)S(1)}, bf16[64,1024]{1,0:T(8,128)(2,1)S(1)}, bf16[64,1024]{1,0:T(8,128)(2,1)S(1)}, bf16[64,1024]{1,0:T(8,128)(2,1)S(1)}) fusion(bf16[128,2048]{1,0:T(8,128)(2,1)} %k_ref.9, bf16[128,2048]{1,0:T(8,128)(2,1)} %v_ref.9), kind=kLoop, calls=%fused_computation.2 | loop fusion | bytes 1048576 | tf_op jit(solution)/shard_map/slice | solution.py:377
  1.8 3.1 %collective-permute-start.1 = (bf16[128,1024]{1,0:T(8,128)(2,1)S(1)}, bf16[128,1024]{1,0:T(8,128)(2,1)S(1)}, u32[]{:S(2)}, u32[]{:S(2)}) collective-permute-start(bf16[128,1024]{1,0:T(8,128)(2,1)S(1)} %pad_maximum_fusion.1), channel_id=1, source_target_pairs={{0,1},{1,2},{2,3},{3,4},{4,5},{5,6},{6,7},{7,8},{8,9},{9,10},{10,1... | collective-permute-start | bytes 786440 | tf_op jit(solution)/shard_map/ppermute | solution.py:329
  4.9 0.0 copy-start.4
  5.0 3.1 %collective-permute-start = (bf16[128,1024]{1,0:T(8,128)(2,1)S(1)}, bf16[128,1024]{1,0:T(8,128)(2,1)S(1)}, u32[]{:S(2)}, u32[]{:S(2)}) collective-permute-start(bf16[128,1024]{1,0:T(8,128)(2,1)S(1)} %pad_maximum_fusion), channel_id=1, source_target_pairs={{0,1},{1,2},{2,3},{3,4},{4,5},{5,6},{6,7},{7,8},{8,9},{9,10},{10,1... | collective-permute-start | bytes 786440 | tf_op jit(solution)/shard_map/ppermute | solution.py:329
  8.1 0.0 copy-done.4
  8.1 0.0 copy-start
  8.1 0.0 copy-start.1
  8.1 0.0 copy-start.2
  8.1 0.0 copy-start.3
  8.1 4.3 %own_block.1 = (bf16[128,2048]{1,0:T(8,128)(2,1)}, bf16[128,2048]{1,0:T(8,128)(2,1)}, f32[128,2048]{1,0:T(8,128)S(1)}, f32[128,2048]{1,0:T(8,128)S(1)}, f32[64,128]{1,0:T(8,128)S(1)}, /*index=5*/f32[64,32]{1,0:T(8,128)S(1)}) custom-call(s32[1,128]{1,0:T(1,128)S(1)} %bitcast.1, bf16[128,2048]{1,0:T(8,128)(2,1)} %q_ref.5, bf16[128,2048]{1,0:T(8,128)(2,1)} %k_ref.9, ...), custom_call_target="tpu_custom_call" | custom-call | flops 201326592 | bytes 4718592 | tf_op jit(solution)/shard_map/own_block/pallas_call | solution.py:384
  12.5 3.6 %collective-permute-done.1.before_ref = bf16[128,1024]{1,0:T(8,128)(2,1)S(1)} collective-permute-done((bf16[128,1024]{1,0:T(8,128)(2,1)S(1)}, bf16[128,1024]{1,0:T(8,128)(2,1)S(1)}, u32[]{:S(2)}, u32[]{:S(2)}) %collective-permute-start.1) | collective-permute-done | bytes 262176 | tf_op jit(solution)/shard_map/ppermute | solution.py:329
  16.1 0.0 copy-done
  16.1 0.0 copy-done.1
  16.1 0.0 copy-done.2
  16.1 0.0 copy-done.3
  16.1 1.9 %lead_rows.2 = (bf16[128,2048]{1,0:T(8,128)(2,1)}, bf16[128,2048]{1,0:T(8,128)(2,1)}, bf16[128,2048]{1,0:T(8,128)(2,1)}, bf16[128,2048]{1,0:T(8,128)(2,1)}, bf16[64,1024]{1,0:T(8,128)(2,1)S(1)}) custom-call(f32[64,128]{1,0:T(8,128)S(1)} %get-tuple-element.24.bias_ref, bf16[128,2048]{1,0:T(8,128)(2,1)S(1)} %copy-done.2, ...), custom_call_target="tpu_custom_call", output_to_operand_aliasing={{0}: (8, {}), {1}: (9, {})} | custom-call | flops 100663296 | bytes 2097152 | tf_op jit(solution)/shard_map/lead_rows/pallas_call | solution.py:398
  18.0 1.9 %collective-permute-start.3 = (bf16[64,1024]{1,0:T(8,128)(2,1)S(1)}, bf16[64,1024]{1,0:T(8,128)(2,1)S(1)}, u32[]{:S(2)}, u32[]{:S(2)}) collective-permute-start(bf16[64,1024]{1,0:T(8,128)(2,1)S(1)} %get-tuple-element.37), channel_id=1, source_target_pairs={{1,0},{2,1},{3,2},{4,3},{5,4},{6,5},{7,6},{8,7},{9,8},{10,9},{11,1... | collective-permute-start | bytes 393224 | tf_op jit(solution)/shard_map/ppermute | solution.py:329
  19.9 0.0 collective-permute-done.before_ref
  19.9 1.9 %lead_rows.3 = (bf16[128,2048]{1,0:T(8,128)(2,1)}, bf16[128,2048]{1,0:T(8,128)(2,1)}, bf16[128,2048]{1,0:T(8,128)(2,1)}, bf16[128,2048]{1,0:T(8,128)(2,1)}, bf16[64,1024]{1,0:T(8,128)(2,1)S(1)}) custom-call(f32[64,128]{1,0:T(8,128)S(1)} %get-tuple-element.24.bias_ref, ...), custom_call_target="tpu_custom_call", output_to_operand_aliasing={{0}: (8, {}), {1}: (9, {}), {2}: (10, {}), {3}: (11, {})} | custom-call | flops 100663296 | bytes 2097152 | tf_op jit(solution)/shard_map/lead_rows/pallas_call | solution.py:398
  21.8 2.8 %collective-permute-start.2 = (bf16[64,1024]{1,0:T(8,128)(2,1)S(1)}, bf16[64,1024]{1,0:T(8,128)(2,1)S(1)}, u32[]{:S(2)}, u32[]{:S(2)}) collective-permute-start(bf16[64,1024]{1,0:T(8,128)(2,1)S(1)} %get-tuple-element.36), channel_id=1, source_target_pairs={{1,0},{2,1},{3,2},{4,3},{5,4},{6,5},{7,6},{8,7},{9,8},{10,9},{11,1... | collective-permute-start | bytes 393224 | tf_op jit(solution)/shard_map/ppermute | solution.py:329
  24.6 0.0 collective-permute-done.3.after_ref
  24.6 1.1 %tail_keys.2 = (bf16[128,2048]{1,0:T(8,128)(2,1)}, bf16[128,2048]{1,0:T(8,128)(2,1)}) custom-call(f32[64,32]{1,0:T(8,128)S(1)} %get-tuple-element.35.bias_ref, bf16[128,2048]{1,0:T(8,128)(2,1)S(1)} %copy-done, bf16[128,2048]{1,0:T(8,128)(2,1)S(1)} %copy-done.1, ...), custom_call_target="tpu_custom_call", output_to_operand_aliasing={{0}: (6, {}), {1}: (7, {})} | custom-call | flops 16777216 | bytes 1310720 | tf_op jit(solution)/shard_map/tail_keys/pallas_call | solution.py:410
  25.7 3.3 %collective-permute-done.2.after_ref = bf16[64,1024]{1,0:T(8,128)(2,1)S(1)} collective-permute-done((bf16[64,1024]{1,0:T(8,128)(2,1)S(1)}, bf16[64,1024]{1,0:T(8,128)(2,1)S(1)}, u32[]{:S(2)}, u32[]{:S(2)}) %collective-permute-start.2) | collective-permute-done | bytes 131104 | tf_op jit(solution)/shard_map/ppermute | solution.py:329
  29.0 1.1 %tail_keys.3 = (bf16[128,2048]{1,0:T(8,128)(2,1)}, bf16[128,2048]{1,0:T(8,128)(2,1)}) custom-call(f32[64,32]{1,0:T(8,128)S(1)} %get-tuple-element.35.bias_ref, bf16[128,2048]{1,0:T(8,128)(2,1)S(1)} %copy-done, bf16[128,2048]{1,0:T(8,128)(2,1)S(1)} %copy-done.1, ...), custom_call_target="tpu_custom_call", output_to_operand_aliasing={{0}: (6, {}), {1}: (7, {})} | custom-call | flops 16777216 | bytes 1310720 | tf_op jit(solution)/shard_map/tail_keys/pallas_call | solution.py:410
  (2 shorter events, 0.0 us)
Async XLA Ops:
  1.8 14.3 %collective-permute-start.1 = (bf16[128,1024]{1,0:T(8,128)(2,1)S(1)}, bf16[128,1024]{1,0:T(8,128)(2,1)S(1)}, u32[]{:S(2)}, u32[]{:S(2)}) collective-permute-start(bf16[128,1024]{1,0:T(8,128)(2,1)S(1)} %pad_maximum_fusion.1), channel_id=1, source_target_pairs={{0,1},{1,2},{2,3},{3,4},{4,5},{5,6},{6,7},{7,8},{8,9},{9,10},{10,1... | collective-permute-start | bytes 786440 | tf_op jit(solution)/shard_map/ppermute | solution.py:329
  4.9 3.1 %copy-start.4 = (s32[128]{0:T(128)S(1)}, s32[128]{0:T(128)}, u32[]{:S(2)}) copy-start(s32[128]{0:T(128)} %param.9) | copy-start | bytes 1540
  5.0 15.0 %collective-permute-start = (bf16[128,1024]{1,0:T(8,128)(2,1)S(1)}, bf16[128,1024]{1,0:T(8,128)(2,1)S(1)}, u32[]{:S(2)}, u32[]{:S(2)}) collective-permute-start(bf16[128,1024]{1,0:T(8,128)(2,1)S(1)} %pad_maximum_fusion), channel_id=1, source_target_pairs={{0,1},{1,2},{2,3},{3,4},{4,5},{5,6},{6,7},{7,8},{8,9},{9,10},{10,1... | collective-permute-start | bytes 786440 | tf_op jit(solution)/shard_map/ppermute | solution.py:329
  8.1 8.0 %copy-start = (bf16[128,2048]{1,0:T(8,128)(2,1)S(1)}, bf16[128,2048]{1,0:T(8,128)(2,1)}, u32[]{:S(2)}) copy-start(bf16[128,2048]{1,0:T(8,128)(2,1)} %k_ref.9) | copy-start | bytes 1572868
  8.1 8.0 %copy-start.1 = (bf16[128,2048]{1,0:T(8,128)(2,1)S(1)}, bf16[128,2048]{1,0:T(8,128)(2,1)}, u32[]{:S(2)}) copy-start(bf16[128,2048]{1,0:T(8,128)(2,1)} %v_ref.9) | copy-start | bytes 1572868
  8.1 8.0 %copy-start.2 = (bf16[128,2048]{1,0:T(8,128)(2,1)S(1)}, bf16[128,2048]{1,0:T(8,128)(2,1)}, u32[]{:S(2)}) copy-start(bf16[128,2048]{1,0:T(8,128)(2,1)} %q_ref.5) | copy-start | bytes 1572868
  8.1 8.0 %copy-start.3 = (bf16[128,2048]{1,0:T(8,128)(2,1)S(1)}, bf16[128,2048]{1,0:T(8,128)(2,1)}, u32[]{:S(2)}) copy-start(bf16[128,2048]{1,0:T(8,128)(2,1)} %do_ref.5) | copy-start | bytes 1572868
  18.0 6.6 %collective-permute-start.3 = (bf16[64,1024]{1,0:T(8,128)(2,1)S(1)}, bf16[64,1024]{1,0:T(8,128)(2,1)S(1)}, u32[]{:S(2)}, u32[]{:S(2)}) collective-permute-start(bf16[64,1024]{1,0:T(8,128)(2,1)S(1)} %get-tuple-element.37), channel_id=1, source_target_pairs={{1,0},{2,1},{3,2},{4,3},{5,4},{6,5},{7,6},{8,7},{9,8},{10,9},{11,1... | collective-permute-start | bytes 393224 | tf_op jit(solution)/shard_map/ppermute | solution.py:329
  21.8 7.2 %collective-permute-start.2 = (bf16[64,1024]{1,0:T(8,128)(2,1)S(1)}, bf16[64,1024]{1,0:T(8,128)(2,1)S(1)}, u32[]{:S(2)}, u32[]{:S(2)}) collective-permute-start(bf16[64,1024]{1,0:T(8,128)(2,1)S(1)} %get-tuple-element.36), channel_id=1, source_target_pairs={{1,0},{2,1},{3,2},{4,3},{5,4},{6,5},{7,6},{8,7},{9,8},{10,9},{11,1... | collective-permute-start | bytes 393224 | tf_op jit(solution)/shard_map/ppermute | solution.py:329

commit v9 on v8

--- a/solution.py
+++ b/solution.py
@@ -341,18 +341,21 @@
     tok, width = query_in.shape
     prior = tok * lax.axis_size("head") // 8
     step = math.gcd(width, 8 * HEAD_DIM)
-    groups = width // step
-    per = step // HEAD_DIM
+    cut = width - max(width // 4, HEAD_DIM)
+    spans = [slice(0, cut), slice(cut, width)] if cut else [slice(0, width)]
     late_at = tok // prior - 1
     lengths = module_lengths.reshape(1, -1)
     keep = pl.BlockSpec(memory_space=pl.ANY)
     full16 = jax.ShapeDtypeStruct((tok, width), jnp.bfloat16)
     part32 = pltpu.VMEM((tok, width), jnp.float32)
-    back16 = jax.ShapeDtypeStruct((prior, step), jnp.bfloat16)
     lead_shape, tail_shape = (prior, 2 * prior), (prior, prior // 2)
 
-    def rows(count, at=0, base=0):
-        return pl.BlockSpec((count, step), lambda g: (at, g + base))
+    def rows(count, at=0):
+        return pl.BlockSpec((count, step), lambda g: (at, g))
+
+    def part(span, count, at=0):
+        wide = span.stop - span.start
+        return pl.BlockSpec((count, wide), lambda g: (at, span.start // wide))
 
     def fixed(*shape):
         return pl.BlockSpec(shape, lambda g: (0, 0))
@@ -366,52 +369,64 @@
             out_shape=shapes,
             scratch_shapes=scratch,
             input_output_aliases=aliases or {},
-            cost_estimate=cost(grid * per, *work, moved * grid * step),
+            cost_estimate=cost(*work, moved),
             compiler_params=pltpu.CompilerParams(vmem_limit_bytes=16 * 2**20),
             name=name,
         )
 
-    befores = []
-    for at in range(groups):
-        cols = slice(at * step, (at + 1) * step)
-        late_kv = [key_in[tok - prior :, cols], value_in[tok - prior :, cols]]
-        befores.append(neighbour(jnp.concatenate(late_kv), 1))
+    def before(span, held=None):
+        late_kv = [key_in[tok - prior :, span], value_in[tok - prior :, span]]
+        if held is not None:
+            *late_kv, _ = lax.optimization_barrier((*late_kv, held))
+        return neighbour(jnp.concatenate(late_kv), 1)
+
+    befores = [before(spans[0])]
 
     in_hbm = [
         pltpu.with_memory_space_constraint(value, pltpu.HBM)
         for value in (query_in, key_in, value_in, grad_out)
     ]
     attn, gq, gk_part, gv_part, lead_bias, tail_bias = call(
-        own_kernel, "own_block", groups,
+        own_kernel, "own_block", width // step,
         [fixed(*lengths.shape), rows(prior, late_at), rows(tok), rows(tok), rows(prior, late_at)],
         [rows(prior, late_at), rows(prior, late_at), rows(tok), rows(tok)]
         + [fixed(*lead_shape), fixed(*tail_shape)],
         [full16, full16, part32, part32]
         + [pltpu.VMEM(shape, jnp.float32) for shape in (lead_shape, tail_shape)],
-        (tok - prior, tok, 6), 18 * tok,
+        (width // HEAD_DIM, tok - prior, tok, 6), 18 * tok * width,
         scratch=[pltpu.VMEM((tok - prior, tok), jnp.float32)],
     )(lengths, *in_hbm)
 
+    befores += [before(span, lead_bias) for span in spans[1:]]
+
     outs = [attn, gq]
     afters = []
-    for at, before in enumerate(befores):
+    for span, came in zip(spans, befores):
+        wide = span.stop - span.start
+        early = part(span, prior)
         *outs, back = call(
             lead_kernel, "lead_rows", 1,
-            [fixed(*lead_shape)] + [rows(prior, 0, at)] * 4
-            + [rows(2 * prior), rows(prior, 0, at), rows(prior, 0, at)] + [keep] * len(outs),
-            [rows(prior, 0, at)] * 4 + [rows(prior)], [full16] * 4 + [back16],
-            (prior, 2 * prior, 6), 16 * tok, {8 + i: i for i in range(len(outs))},
-        )(lead_bias, query_in, key_in, value_in, grad_out, before, gk_part, gv_part, *outs)
+            [fixed(*lead_shape)] + [early] * 4
+            + [pl.BlockSpec((2 * prior, wide), lambda g: (0, 0)), early, early]
+            + [keep] * len(outs),
+            [early] * 4 + [pl.BlockSpec((prior, wide), lambda g: (0, 0))],
+            [full16] * 4 + [jax.ShapeDtypeStruct((prior, wide), jnp.bfloat16)],
+            (wide // HEAD_DIM, prior, 2 * prior, 6), 16 * tok * wide,
+            {8 + i: i for i in range(len(outs))},
+        )(lead_bias, query_in, key_in, value_in, grad_out, came, gk_part, gv_part, *outs)
         afters.append(neighbour(back, -1))
     attn, gq, gk, gv = outs
 
-    for at, after in enumerate(afters):
-        late = rows(prior, late_at, at)
+    for span, came in zip(spans, afters):
+        wide = span.stop - span.start
+        late = part(span, prior, late_at)
         gk, gv = call(
             tail_kernel, "tail_keys", 1,
-            [fixed(*tail_shape), late, late, rows(prior), late, late, keep, keep],
-            [late, late], [full16] * 2, (prior, prior // 2, 4), 10 * tok, {6: 0, 7: 1},
-        )(tail_bias, key_in, value_in, after, gk_part, gv_part, gk, gv)
+            [fixed(*tail_shape), late, late, pl.BlockSpec((prior, wide), lambda g: (0, 0))]
+            + [late, late, keep, keep],
+            [late, late], [full16] * 2,
+            (wide // HEAD_DIM, prior, prior // 2, 4), 10 * tok * wide, {6: 0, 7: 1},
+        )(tail_bias, key_in, value_in, came, gk_part, gv_part, gk, gv)
     return (attn, gq, gk, gv)
 
 

time: 30.4 us -> 31.3 us (1.030)
  the two profiles are of different devices: /device:TPU:25 before, /device:TPU:24 now
where the time goes in v9:
time: 31.3 us; the launch traced here: 31 us
  starting transfers between devices  12.7 us (41%)
  Pallas kernels  10.2 us (33%)
  local copies, waits for them, and re-layouts  4.25 us (14%)
  waiting for transfers between devices  3.07 us (10%)
  between operations  0.74 us (2%)
    ppermute x4, starting transfers between devices, neighbour(): return lax.ppermute(value, ('seq', 'head'), pairs)  12.7 us
    pallas_call x1, Pallas kernels, halo_shards(): call(own_kernel, 'own_block', width // step, [fixed(*lengths.shape), rows...  4.35 us
    pallas_call x2, Pallas kernels, halo_shards(): call(lead_kernel, 'lead_rows', 1, [fixed(*lead_shape)] + [early] * 4 + [p...  3.76 us
    slice x4, local copies, waits for them, and re-layouts, before(): late_kv = [key_in[tok - prior:, span], value_in[tok - prior:, span]]  3.58 us
    ppermute x4, waiting for transfers between devices, neighbour(): return lax.ppermute(value, ('seq', 'head'), pairs)  3.07 us
    pallas_call x2, Pallas kernels, halo_shards(): call(tail_kernel, 'tail_keys', 1, [fixed(*tail_shape), late, late, pl.Blo...  2.13 us
    unnamed x10, local copies, waits for them, and re-layouts  0.67 us
  transfers between devices with their start and end apart: 4, of which 2 were waited for; matrix products, arithmetic and copies ran while one was open for 5% of the time, Pallas kernels for 30%

profile of v9, /device:TPU:24, one launch (start us, length us, event | category | flops | bytes accessed | tf_op | source)
XLA Modules:
  0.0 31.0 jit_solution(12402223939052051341)
XLA Ops:
  0.6 0.9 %slice.14 = bf16[64,1536]{1,0:T(8,128)(2,1)S(1)} slice(bf16[128,2048]{1,0:T(8,128)(2,1)} %k_ref.9), slice={[64:128], [0:1536]} | slice | bytes 393216 | tf_op jit(solution)/shard_map/slice | solution.py:378
  1.6 0.9 %slice.15 = bf16[64,1536]{1,0:T(8,128)(2,1)S(1)} slice(bf16[128,2048]{1,0:T(8,128)(2,1)} %v_ref.9), slice={[64:128], [0:1536]} | slice | bytes 393216 | tf_op jit(solution)/shard_map/slice | solution.py:378
  2.6 3.4 %collective-permute-start.1 = (bf16[128,1536]{1,0:T(8,128)(2,1)S(1)}, bf16[128,1536]{1,0:T(8,128)(2,1)S(1)}, u32[]{:S(2)}, u32[]{:S(2)}) collective-permute-start(bf16[128,1536]{1,0:T(8,128)(2,1)S(1)} %pad_maximum_fusion), channel_id=1, source_target_pairs={{0,1},{1,2},{2,3},{3,4},{4,5},{5,6},{6,7},{7,8},{8,9},{9,10},{10,1... | collective-permute-start | bytes 1179656 | tf_op jit(solution)/shard_map/ppermute | solution.py:329
  6.0 0.8 %slice.12 = bf16[64,512]{1,0:T(8,128)(2,1)S(1)} slice(bf16[128,2048]{1,0:T(8,128)(2,1)} %k_ref.9), slice={[64:128], [1536:2048]} | slice | bytes 131072 | tf_op jit(solution)/shard_map/slice | solution.py:378
  6.8 0.8 %slice.13 = bf16[64,512]{1,0:T(8,128)(2,1)S(1)} slice(bf16[128,2048]{1,0:T(8,128)(2,1)} %v_ref.9), slice={[64:128], [1536:2048]} | slice | bytes 131072 | tf_op jit(solution)/shard_map/slice | solution.py:378
  7.7 0.0 copy-start.4
  7.7 0.7 %copy-done.4 = s32[128]{0:T(128)S(1)} copy-done((s32[128]{0:T(128)S(1)}, s32[128]{0:T(128)}, u32[]{:S(2)}) %copy-start.4) | copy-done | bytes 536
  8.3 0.0 copy-start
  8.3 0.0 copy-start.1
  8.3 0.0 copy-start.2
  8.3 0.0 copy-start.3
  8.3 4.4 %own_block.1 = (bf16[128,2048]{1,0:T(8,128)(2,1)}, bf16[128,2048]{1,0:T(8,128)(2,1)}, f32[128,2048]{1,0:T(8,128)S(1)}, f32[128,2048]{1,0:T(8,128)S(1)}, f32[64,128]{1,0:T(8,128)S(1)}, /*index=5*/f32[64,32]{1,0:T(8,128)S(1)}) custom-call(s32[1,128]{1,0:T(1,128)S(1)} %bitcast.1, bf16[128,2048]{1,0:T(8,128)(2,1)} %q_ref.5, bf16[128,2048]{1,0:T(8,128)(2,1)} %k_ref.9, ...), custom_call_target="tpu_custom_call" | custom-call | flops 201326592 | bytes 4718592 | tf_op jit(solution)/shard_map/own_block/pallas_call | solution.py:389
  12.7 3.4 %collective-permute-start = (bf16[128,512]{1,0:T(8,128)(2,1)S(1)}, bf16[128,512]{1,0:T(8,128)(2,1)S(1)}, u32[]{:S(2)}, u32[]{:S(2)}) collective-permute-start(bf16[128,512]{1,0:T(8,128)(2,1)S(1)} %pad_maximum_fusion.1), channel_id=1, source_target_pairs={{0,1},{1,2},{2,3},{3,4},{4,5},{5,6},{6,7},{7,8},{8,9},{9,10},{10,1... | collective-permute-start | bytes 393224 | tf_op jit(solution)/shard_map/ppermute | solution.py:329
  16.1 0.0 collective-permute-done.1.before_ref
  16.1 0.0 copy-done
  16.1 0.0 copy-done.1
  16.1 0.0 copy-done.2
  16.1 0.0 copy-done.3
  16.1 2.3 %lead_rows.2 = (bf16[128,2048]{1,0:T(8,128)(2,1)}, bf16[128,2048]{1,0:T(8,128)(2,1)}, bf16[128,2048]{1,0:T(8,128)(2,1)}, bf16[128,2048]{1,0:T(8,128)(2,1)}, bf16[64,1536]{1,0:T(8,128)(2,1)S(1)}) custom-call(f32[64,128]{1,0:T(8,128)S(1)} %get-tuple-element.26.bias_ref, bf16[128,2048]{1,0:T(8,128)(2,1)S(1)} %copy-done.2, ...), custom_call_target="tpu_custom_call", output_to_operand_aliasing={{0}: (8, {}), {1}: (9, {})} | custom-call | flops 150994944 | bytes 3145728 | tf_op jit(solution)/shard_map/lead_rows/pallas_call | solution.py:407
  18.5 4.0 %collective-permute-start.3 = (bf16[64,1536]{1,0:T(8,128)(2,1)S(1)}, bf16[64,1536]{1,0:T(8,128)(2,1)S(1)}, u32[]{:S(2)}, u32[]{:S(2)}) collective-permute-start(bf16[64,1536]{1,0:T(8,128)(2,1)S(1)} %get-tuple-element.41), channel_id=1, source_target_pairs={{1,0},{2,1},{3,2},{4,3},{5,4},{6,5},{7,6},{8,7},{9,8},{10,9},{11,1... | collective-permute-start | bytes 589832 | tf_op jit(solution)/shard_map/ppermute | solution.py:329
  22.5 0.0 collective-permute-done.before_ref
  22.5 1.4 %lead_rows.3 = (bf16[128,2048]{1,0:T(8,128)(2,1)}, bf16[128,2048]{1,0:T(8,128)(2,1)}, bf16[128,2048]{1,0:T(8,128)(2,1)}, bf16[128,2048]{1,0:T(8,128)(2,1)}, bf16[64,512]{1,0:T(8,128)(2,1)S(1)}) custom-call(f32[64,128]{1,0:T(8,128)S(1)} %get-tuple-element.26.bias_ref, ...), custom_call_target="tpu_custom_call", output_to_operand_aliasing={{0}: (8, {}), {1}: (9, {}), {2}: (10, {}), {3}: (11, {})} | custom-call | flops 50331648 | bytes 1048576 | tf_op jit(solution)/shard_map/lead_rows/pallas_call | solution.py:407
  23.9 1.9 %collective-permute-start.2 = (bf16[64,512]{1,0:T(8,128)(2,1)S(1)}, bf16[64,512]{1,0:T(8,128)(2,1)S(1)}, u32[]{:S(2)}, u32[]{:S(2)}) collective-permute-start(bf16[64,512]{1,0:T(8,128)(2,1)S(1)} %get-tuple-element.40), channel_id=1, source_target_pairs={{1,0},{2,1},{3,2},{4,3},{5,4},{6,5},{7,6},{8,7},{9,8},{10,9},{11,1... | collective-permute-start | bytes 196616 | tf_op jit(solution)/shard_map/ppermute | solution.py:329
  25.8 1.9 %collective-permute-done.3.after_ref = bf16[64,1536]{1,0:T(8,128)(2,1)S(1)} collective-permute-done((bf16[64,1536]{1,0:T(8,128)(2,1)S(1)}, bf16[64,1536]{1,0:T(8,128)(2,1)S(1)}, u32[]{:S(2)}, u32[]{:S(2)}) %collective-permute-start.3) | collective-permute-done | bytes 196640 | tf_op jit(solution)/shard_map/ppermute | solution.py:329
  27.8 1.2 %tail_keys.2 = (bf16[128,2048]{1,0:T(8,128)(2,1)}, bf16[128,2048]{1,0:T(8,128)(2,1)}) custom-call(f32[64,32]{1,0:T(8,128)S(1)} %get-tuple-element.39.bias_ref, bf16[128,2048]{1,0:T(8,128)(2,1)S(1)} %copy-done, bf16[128,2048]{1,0:T(8,128)(2,1)S(1)} %copy-done.1, ...), custom_call_target="tpu_custom_call", output_to_operand_aliasing={{0}: (6, {}), {1}: (7, {})} | custom-call | flops 25165824 | bytes 1966080 | tf_op jit(solution)/shard_map/tail_keys/pallas_call | solution.py:423
  28.9 1.1 %collective-permute-done.2.after_ref = bf16[64,512]{1,0:T(8,128)(2,1)S(1)} collective-permute-done((bf16[64,512]{1,0:T(8,128)(2,1)S(1)}, bf16[64,512]{1,0:T(8,128)(2,1)S(1)}, u32[]{:S(2)}, u32[]{:S(2)}) %collective-permute-start.2) | collective-permute-done | bytes 65568 | tf_op jit(solution)/shard_map/ppermute | solution.py:329
  30.0 1.0 %tail_keys.3 = (bf16[128,2048]{1,0:T(8,128)(2,1)}, bf16[128,2048]{1,0:T(8,128)(2,1)}) custom-call(f32[64,32]{1,0:T(8,128)S(1)} %get-tuple-element.39.bias_ref, bf16[128,2048]{1,0:T(8,128)(2,1)S(1)} %copy-done, bf16[128,2048]{1,0:T(8,128)(2,1)S(1)} %copy-done.1, ...), custom_call_target="tpu_custom_call", output_to_operand_aliasing={{0}: (6, {}), {1}: (7, {})} | custom-call | flops 8388608 | bytes 655360 | tf_op jit(solution)/shard_map/tail_keys/pallas_call | solution.py:423
  (2 shorter events, 0.0 us)
Async XLA Ops:
  2.6 13.5 %collective-permute-start.1 = (bf16[128,1536]{1,0:T(8,128)(2,1)S(1)}, bf16[128,1536]{1,0:T(8,128)(2,1)S(1)}, u32[]{:S(2)}, u32[]{:S(2)}) collective-permute-start(bf16[128,1536]{1,0:T(8,128)(2,1)S(1)} %pad_maximum_fusion), channel_id=1, source_target_pairs={{0,1},{1,2},{2,3},{3,4},{4,5},{5,6},{6,7},{7,8},{8,9},{9,10},{10,1... | collective-permute-start | bytes 1179656 | tf_op jit(solution)/shard_map/ppermute | solution.py:329
  7.7 0.7 %copy-start.4 = (s32[128]{0:T(128)S(1)}, s32[128]{0:T(128)}, u32[]{:S(2)}) copy-start(s32[128]{0:T(128)} %param.9) | copy-start | bytes 1540
  8.3 7.8 %copy-start = (bf16[128,2048]{1,0:T(8,128)(2,1)S(1)}, bf16[128,2048]{1,0:T(8,128)(2,1)}, u32[]{:S(2)}) copy-start(bf16[128,2048]{1,0:T(8,128)(2,1)} %k_ref.9) | copy-start | bytes 1572868
  8.3 7.8 %copy-start.1 = (bf16[128,2048]{1,0:T(8,128)(2,1)S(1)}, bf16[128,2048]{1,0:T(8,128)(2,1)}, u32[]{:S(2)}) copy-start(bf16[128,2048]{1,0:T(8,128)(2,1)} %v_ref.9) | copy-start | bytes 1572868
  8.3 7.8 %copy-start.2 = (bf16[128,2048]{1,0:T(8,128)(2,1)S(1)}, bf16[128,2048]{1,0:T(8,128)(2,1)}, u32[]{:S(2)}) copy-start(bf16[128,2048]{1,0:T(8,128)(2,1)} %q_ref.5) | copy-start | bytes 1572868
  8.3 7.8 %copy-start.3 = (bf16[128,2048]{1,0:T(8,128)(2,1)S(1)}, bf16[128,2048]{1,0:T(8,128)(2,1)}, u32[]{:S(2)}) copy-start(bf16[128,2048]{1,0:T(8,128)(2,1)} %do_ref.5) | copy-start | bytes 1572868
  12.7 9.8 %collective-permute-start = (bf16[128,512]{1,0:T(8,128)(2,1)S(1)}, bf16[128,512]{1,0:T(8,128)(2,1)S(1)}, u32[]{:S(2)}, u32[]{:S(2)}) collective-permute-start(bf16[128,512]{1,0:T(8,128)(2,1)S(1)} %pad_maximum_fusion.1), channel_id=1, source_target_pairs={{0,1},{1,2},{2,3},{3,4},{4,5},{5,6},{6,7},{7,8},{8,9},{9,10},{10,1... | collective-permute-start | bytes 393224 | tf_op jit(solution)/shard_map/ppermute | solution.py:329
  18.5 9.3 %collective-permute-start.3 = (bf16[64,1536]{1,0:T(8,128)(2,1)S(1)}, bf16[64,1536]{1,0:T(8,128)(2,1)S(1)}, u32[]{:S(2)}, u32[]{:S(2)}) collective-permute-start(bf16[64,1536]{1,0:T(8,128)(2,1)S(1)} %get-tuple-element.41), channel_id=1, source_target_pairs={{1,0},{2,1},{3,2},{4,3},{5,4},{6,5},{7,6},{8,7},{9,8},{10,9},{11,1... | collective-permute-start | bytes 589832 | tf_op jit(solution)/shard_map/ppermute | solution.py:329
  23.9 6.1 %collective-permute-start.2 = (bf16[64,512]{1,0:T(8,128)(2,1)S(1)}, bf16[64,512]{1,0:T(8,128)(2,1)S(1)}, u32[]{:S(2)}, u32[]{:S(2)}) collective-permute-start(bf16[64,512]{1,0:T(8,128)(2,1)S(1)} %get-tuple-element.40), channel_id=1, source_target_pairs={{1,0},{2,1},{3,2},{4,3},{5,4},{6,5},{7,6},{8,7},{9,8},{10,9},{11,1... | collective-permute-start | bytes 196616 | tf_op jit(solution)/shard_map/ppermute | solution.py:329

commit v10 on v8

--- a/solution.py
+++ b/solution.py
@@ -234,93 +234,165 @@
     return parts[:, :count] + parts[:, count : 2 * count] + parts[:, 2 * count : 3 * count]
 
 
+def pack_kernel(prior, spans, k_ref, v_ref, *refs):
+    *packed_refs, sems = refs
+    last = pl.ds(k_ref.shape[0] - prior, prior)
+    copies = []
+    for span, packed_ref in zip(spans, packed_refs):
+        for half, ref in enumerate((k_ref, v_ref)):
+            copies.append(
+                pltpu.make_async_copy(
+                    ref.at[last, span],
+                    packed_ref.at[pl.ds(half * prior, prior), :],
+                    sems.at[len(copies)],
+                )
+            )
+    for copy in copies:
+        copy.start()
+    for copy in copies:
+        copy.wait()
+
+
 def own_kernel(
-    prior, len_ref, q_ref, k_ref, v_ref, do_ref, attn_ref, gq_ref, gk_ref, gv_ref,
-    lead_bias_ref, tail_bias_ref, bias_ref,
+    prior, step, len_hbm, q_hbm, k_hbm, v_hbm, do_hbm,
+    q_ref, k_ref, v_ref, do_ref, attn_ref, gq_ref, gk_ref, gv_ref, lead_bias_ref, tail_bias_ref,
+    len_ref, bias_ref, sems, len_sem,
 ):
     tok, width = k_ref.shape
-    columns = head_columns(width)
-
-    @pl.when(pl.program_id(0) == 0)
-    def _():
-        first = device_first(tok)
-        lengths = len_ref[...].astype(jnp.float32)
-        bias_ref[...] = bias_by_query(lengths, first + prior, tok - prior, first, tok)
-        lead_bias_ref[...] = bias_by_query(lengths, first, prior, first - prior, 2 * prior)
-        tail_bias_ref[...] = bias_by_key(
-            lengths, first + tok, prior // 2, first + tok - prior, prior
-        )
-
-    bias = bias_ref[...]
-    pairs = [by_query(q_ref[:, c], k_ref[:, c], do_ref[:, c], v_ref[:, c], bias) for c in columns]
-    weights, grads, _, _ = full_rows(pairs)
-    for c, w, g in zip(columns, weights, grads):
-        attn_ref[:, c] = dot(w, v_ref[:, c], 1, 0).astype(jnp.bfloat16)
-        gq_ref[:, c] = dot(g, k_ref[:, c], 1, 0).astype(jnp.bfloat16)
-        gk_ref[:, c] = dot(g, q_ref[:, c], 0, 0)
-        gv_ref[:, c] = dot(w, do_ref[:, c], 0, 0)
+    pairs = ((k_hbm, k_ref), (v_hbm, v_ref), (q_hbm, q_ref), (do_hbm, do_ref))
+
+    def copies(at):
+        cols = pl.ds(pl.multiple_of(at * step, step), step)
+        return [
+            pltpu.make_async_copy(hbm.at[:, cols], ref.at[:, cols], sems.at[at, n])
+            for n, (hbm, ref) in enumerate(pairs)
+        ]
+
+    len_copy = pltpu.make_async_copy(len_hbm, len_ref, len_sem)
+    len_copy.start()
+    for at in range(width // step):
+        for copy in copies(at):
+            copy.start()
+    len_copy.wait()
+    first = device_first(tok)
+    lengths = len_ref[...].astype(jnp.float32)
+    bias_ref[...] = bias_by_query(lengths, first + prior, tok - prior, first, tok)
+    lead_bias_ref[...] = bias_by_query(lengths, first, prior, first - prior, 2 * prior)
+    tail_bias_ref[...] = bias_by_key(lengths, first + tok, prior // 2, first + tok - prior, prior)
+
+    @pl.loop(0, width // step)
+    def _(at):
+        for copy in copies(at):
+            copy.wait()
+        bias = bias_ref[...]
+        columns = [
+            pl.ds(pl.multiple_of(at * step + c, HEAD_DIM), HEAD_DIM)
+            for c in range(0, step, HEAD_DIM)
+        ]
+        late = slice(prior, tok)
+        pairs = [
+            by_query(q_ref[late, c], k_ref[:, c], do_ref[late, c], v_ref[:, c], bias)
+            for c in columns
+        ]
+        weights, grads, _, _ = full_rows(pairs)
+        for c, w, g in zip(columns, weights, grads):
+            attn_ref[:, c] = dot(w, v_ref[:, c], 1, 0).astype(jnp.bfloat16)
+            gq_ref[:, c] = dot(g, k_ref[:, c], 1, 0).astype(jnp.bfloat16)
+            gk_ref[:, c] = dot(g, q_ref[late, c], 0, 0)
+            gv_ref[:, c] = dot(w, do_ref[late, c], 0, 0)
 
 
 def lead_kernel(
-    prior, bias_ref, q_ref, k_ref, v_ref, do_ref, before_ref, gk_part_ref, gv_part_ref, *refs
+    prior, span, bias_ref, q_ref, k_ref, v_ref, do_ref, before_ref, gk_part_ref, gv_part_ref,
+    attn_ref, gq_ref, gk_ref, gv_ref, back_ref,
 ):
-    attn_ref, gq_ref, gk_ref, gv_ref, back_ref = refs[-5:]
-    columns = head_columns(q_ref.shape[1])
+    places = head_columns(span.stop - span.start)
+    columns = [slice(span.start + c.start, span.start + c.stop) for c in places]
     half = prior // 2
     bias = bias_ref[...]
     many = bias_ref[half - 1 : half, prior - 1 : prior] == 0.0
     spare = lax.broadcasted_iota(jnp.int32, (half, 1), 0) == half - 1
     early, late = slice(0, prior), slice(prior, 2 * prior)
-    keys = [jnp.concatenate([before_ref[early, c], k_ref[:, c]], axis=0) for c in columns]
-    values = [jnp.concatenate([before_ref[late, c], v_ref[:, c]], axis=0) for c in columns]
+    keys = [
+        jnp.concatenate([before_ref[early, p], k_ref[early, c]], axis=0)
+        for p, c in zip(places, columns)
+    ]
+    values = [
+        jnp.concatenate([before_ref[late, p], v_ref[early, c]], axis=0)
+        for p, c in zip(places, columns)
+    ]
     pairs = [
-        by_query(q_ref[:, c], k, do_ref[:, c], v, bias) for c, k, v in zip(columns, keys, values)
+        by_query(q_ref[early, c], k, do_ref[early, c], v, bias)
+        for c, k, v in zip(columns, keys, values)
     ]
     weights, grads, logs, deltas = full_rows(pairs)
     rows = as_rows([column[:half] for column in logs + deltas])
     logs, deltas = rows[: len(columns)], rows[len(columns) :]
-    for c, w, g, k, v, log, delta in zip(columns, weights, grads, keys, values, logs, deltas):
-        attn_ref[:, c] = dot(w, v, 1, 0).astype(jnp.bfloat16)
-        gq_ref[:, c] = dot(g, k, 1, 0).astype(jnp.bfloat16)
-        gk = dot(g, q_ref[:, c], 0, 0)
-        gv = dot(w, do_ref[:, c], 0, 0)
-        gk_ref[:, c] = (gk_part_ref[:, c] + gk[prior:]).astype(jnp.bfloat16)
-        gv_ref[:, c] = (gv_part_ref[:, c] + gv[prior:]).astype(jnp.bfloat16)
-        few_q = jnp.where(spare, split_bf16(log), q_ref[:half, c])
-        few_do = jnp.where(spare, split_bf16(delta), do_ref[:half, c])
-        back_ref[:half, c] = jnp.where(many, gk[half:prior].astype(jnp.bfloat16), few_q)
-        back_ref[half:, c] = jnp.where(many, gv[half:prior].astype(jnp.bfloat16), few_do)
+    for at, (p, c) in enumerate(zip(places, columns)):
+        w, g = weights[at], grads[at]
+        gk = dot(g, q_ref[early, c], 0, 0)
+        gv = dot(w, do_ref[early, c], 0, 0)
+        few_q = jnp.where(spare, split_bf16(logs[at]), q_ref[:half, c])
+        few_do = jnp.where(spare, split_bf16(deltas[at]), do_ref[:half, c])
+        back_ref[:half, p] = jnp.where(many, gk[half:prior].astype(jnp.bfloat16), few_q)
+        back_ref[half:, p] = jnp.where(many, gv[half:prior].astype(jnp.bfloat16), few_do)
+        attn_ref[:, p] = dot(w, values[at], 1, 0).astype(jnp.bfloat16)
+        gq_ref[:, p] = dot(g, keys[at], 1, 0).astype(jnp.bfloat16)
+        gk_ref[:, p] = (gk_part_ref[early, c] + gk[prior:]).astype(jnp.bfloat16)
+        gv_ref[:, p] = (gv_part_ref[early, c] + gv[prior:]).astype(jnp.bfloat16)
 
 
 def tail_kernel(
-    prior, bias_ref, k_ref, v_ref, after_ref, gk_part_ref, gv_part_ref,
-    gk_in, gv_in, gk_ref, gv_ref,
+    prior, span, places, bias_ref, k_ref, v_ref, after_ref, gk_part_ref, gv_part_ref, *refs
 ):
-    columns = head_columns(k_ref.shape[1])
+    outs = 4 if places else 2
+    pieces, refs = refs[: len(places)], refs[len(places) :]
+    *refs, gk_ref, gv_ref, gk_late_ref, gv_late_ref, sems = refs
+    targets = (*refs[-2:], gk_ref, gv_ref) if outs == 4 else ()
+    copies = []
+    for piece, (target, row, col) in zip(pieces, places):
+        rows, cols = pl.ds(row, piece.shape[0]), pl.ds(col, piece.shape[1])
+        copies.append(
+            pltpu.make_async_copy(piece, targets[target].at[rows, cols], sems.at[len(copies)])
+        )
+        copies[-1].start()
+
+    tok = k_ref.shape[0]
+    here = head_columns(span.stop - span.start)
+    columns = [slice(span.start + c.start, span.start + c.stop) for c in here]
     half = prior // 2
     many = bias_ref[prior - 1 : prior, half - 1 : half] == 0.0
     bias = jnp.where(many, MASKED, bias_ref[...])
-    first, second = slice(0, half), slice(half, prior)
+    first, second, last = slice(0, half), slice(half, prior), slice(tok - prior, tok)
     pairs = [
-        by_query(k_ref[:, c], after_ref[first, c], v_ref[:, c], after_ref[second, c], bias)
-        for c in columns
+        by_query(k_ref[last, c], after_ref[first, p], v_ref[last, c], after_ref[second, p], bias)
+        for p, c in zip(here, columns)
     ]
     weights = [
-        jnp.exp2(s - joined(after_ref[half - 1 : half, c])) for (s, _), c in zip(pairs, columns)
+        jnp.exp2(s - joined(after_ref[half - 1 : half, p])) for (s, _), p in zip(pairs, here)
     ]
     grads = [
-        w * (dp - joined(after_ref[prior - 1 : prior, c])) * SCALE
-        for w, (_, dp), c in zip(weights, pairs, columns)
+        w * (dp - joined(after_ref[prior - 1 : prior, p])) * SCALE
+        for w, (_, dp), p in zip(weights, pairs, here)
     ]
-    for c, w, g in zip(columns, weights, grads):
+    for p, c, w, g in zip(here, columns, weights, grads):
         for out_ref, part_ref, left, rows in (
-            (gk_ref, gk_part_ref, g, first), (gv_ref, gv_part_ref, w, second)
+            (gk_late_ref, gk_part_ref, g, first), (gv_late_ref, gv_part_ref, w, second)
         ):
-            came = after_ref[rows, c]
-            total = part_ref[:, c] + dot(left.astype(jnp.bfloat16), came, 1, 0)
+            came = after_ref[rows, p]
+            total = part_ref[last, c] + dot(left.astype(jnp.bfloat16), came, 1, 0)
             terms = jnp.where(many, came.astype(jnp.float32), 0.0)
-            out_ref[first, c] = total[first].astype(jnp.bfloat16)
-            out_ref[second, c] = (total[second] + terms).astype(jnp.bfloat16)
+            out_ref[first, p] = total[first].astype(jnp.bfloat16)
+            out_ref[second, p] = (total[second] + terms).astype(jnp.bfloat16)
+    for late_ref, out_ref in ((gk_late_ref, gk_ref), (gv_late_ref, gv_ref)):
+        copies.append(
+            pltpu.make_async_copy(
+                late_ref, out_ref.at[pl.ds(tok - prior, prior), span], sems.at[len(copies)]
+            )
+        )
+        copies[-1].start()
+    for copy in copies:
+        copy.wait()
 
 
 def neighbour(value, by):
@@ -341,84 +413,96 @@
     tok, width = query_in.shape
     prior = tok * lax.axis_size("head") // 8
     step = math.gcd(width, 8 * HEAD_DIM)
-    groups = width // step
-    per = step // HEAD_DIM
-    late_at = tok // prior - 1
-    lengths = module_lengths.reshape(1, -1)
-    keep = pl.BlockSpec(memory_space=pl.ANY)
+    cut = width - max(width // 4, HEAD_DIM)
+    spans = [slice(0, cut), slice(cut, width)] if cut else [slice(0, width)]
+    wides = [span.stop - span.start for span in spans]
+    anywhere = pl.BlockSpec(memory_space=pl.ANY)
+    near = pl.BlockSpec(memory_space=pltpu.VMEM)
     full16 = jax.ShapeDtypeStruct((tok, width), jnp.bfloat16)
-    part32 = pltpu.VMEM((tok, width), jnp.float32)
-    back16 = jax.ShapeDtypeStruct((prior, step), jnp.bfloat16)
-    lead_shape, tail_shape = (prior, 2 * prior), (prior, prior // 2)
-
-    def rows(count, at=0, base=0):
-        return pl.BlockSpec((count, step), lambda g: (at, g + base))
-
-    def fixed(*shape):
-        return pl.BlockSpec(shape, lambda g: (0, 0))
-
-    def call(kernel, name, grid, ins, outs, shapes, work, moved, aliases=None, scratch=()):
+
+    def near16(rows, columns):
+        return pltpu.VMEM((rows, columns), jnp.bfloat16)
+
+    def near32(rows, columns):
+        return pltpu.VMEM((rows, columns), jnp.float32)
+
+    def in_hbm(*values):
+        return [pltpu.with_memory_space_constraint(value, pltpu.HBM) for value in values]
+
+    def in_vmem(*values):
+        return [pltpu.with_memory_space_constraint(value, pltpu.VMEM) for value in values]
+
+    def call(kernel, name, ins, outs, shapes, scratch, work, moved, aliases=None):
         return pl.pallas_call(
-            functools.partial(kernel, prior),
-            grid=(grid,),
+            kernel,
             in_specs=ins,
             out_specs=outs,
             out_shape=shapes,
             scratch_shapes=scratch,
             input_output_aliases=aliases or {},
-            cost_estimate=cost(grid * per, *work, moved * grid * step),
+            cost_estimate=cost(*work, moved),
             compiler_params=pltpu.CompilerParams(vmem_limit_bytes=16 * 2**20),
             name=name,
         )
 
-    befores = []
-    for at in range(groups):
-        cols = slice(at * step, (at + 1) * step)
-        late_kv = [key_in[tok - prior :, cols], value_in[tok - prior :, cols]]
-        befores.append(neighbour(jnp.concatenate(late_kv), 1))
-
-    in_hbm = [
-        pltpu.with_memory_space_constraint(value, pltpu.HBM)
-        for value in (query_in, key_in, value_in, grad_out)
-    ]
-    attn, gq, gk_part, gv_part, lead_bias, tail_bias = call(
-        own_kernel, "own_block", groups,
-        [fixed(*lengths.shape), rows(prior, late_at), rows(tok), rows(tok), rows(prior, late_at)],
-        [rows(prior, late_at), rows(prior, late_at), rows(tok), rows(tok)]
-        + [fixed(*lead_shape), fixed(*tail_shape)],
-        [full16, full16, part32, part32]
-        + [pltpu.VMEM(shape, jnp.float32) for shape in (lead_shape, tail_shape)],
-        (tok - prior, tok, 6), 18 * tok,
-        scratch=[pltpu.VMEM((tok - prior, tok), jnp.float32)],
-    )(lengths, *in_hbm)
-
-    outs = [attn, gq]
-    afters = []
-    for at, before in enumerate(befores):
-        *outs, back = call(
-            lead_kernel, "lead_rows", 1,
-            [fixed(*lead_shape)] + [rows(prior, 0, at)] * 4
-            + [rows(2 * prior), rows(prior, 0, at), rows(prior, 0, at)] + [keep] * len(outs),
-            [rows(prior, 0, at)] * 4 + [rows(prior)], [full16] * 4 + [back16],
-            (prior, 2 * prior, 6), 16 * tok, {8 + i: i for i in range(len(outs))},
-        )(lead_bias, query_in, key_in, value_in, grad_out, before, gk_part, gv_part, *outs)
+    to_next = call(
+        functools.partial(pack_kernel, prior, spans), "pack_late",
+        [anywhere] * 2, [near] * len(spans), [near16(2 * prior, wide) for wide in wides],
+        [pltpu.SemaphoreType.DMA((2 * len(spans),))], (0, 0, 0, 0), 8 * prior * width,
+    )(*in_hbm(key_in, value_in))
+    befores = [neighbour(to_next[0], 1)]
+
+    q, k, v, do, attn, gq, gk_part, gv_part, lead_bias, tail_bias = call(
+        functools.partial(own_kernel, prior, step), "own_block",
+        [anywhere] * 5, [near] * 10,
+        [near16(tok, width)] * 4 + [near16(tok - prior, width)] * 2 + [near32(tok, width)] * 2
+        + [near32(prior, 2 * prior), near32(prior, prior // 2)],
+        [
+            pltpu.VMEM((1, module_lengths.shape[0]), jnp.int32), near32(tok - prior, tok),
+            pltpu.SemaphoreType.DMA((width // step, 4)), pltpu.SemaphoreType.DMA(()),
+        ],
+        (width // HEAD_DIM, tok - prior, tok, 6), 24 * tok * width,
+    )(*in_hbm(module_lengths.reshape(1, -1), query_in, key_in, value_in, grad_out))
+    for part in to_next[1:]:
+        part, _ = lax.optimization_barrier((part, lead_bias))
+        befores.append(neighbour(part, 1))
+
+    pieces, places, afters = [attn, gq], [(0, prior, 0), (1, prior, 0)], []
+    for span, wide, before in zip(spans, wides, befores):
+        *done, back = call(
+            functools.partial(lead_kernel, prior, span), "lead_rows",
+            [near] * 8, [near] * 5, [near16(prior, wide)] * 5, (),
+            (wide // HEAD_DIM, prior, 2 * prior, 6), 16 * tok * wide,
+        )(*in_vmem(lead_bias, q, k, v, do, before, gk_part, gv_part))
+        pieces += done
+        places += [(target, 0, span.start) for target in range(4)]
         afters.append(neighbour(back, -1))
-    attn, gq, gk, gv = outs
-
-    for at, after in enumerate(afters):
-        late = rows(prior, late_at, at)
-        gk, gv = call(
-            tail_kernel, "tail_keys", 1,
-            [fixed(*tail_shape), late, late, rows(prior), late, late, keep, keep],
-            [late, late], [full16] * 2, (prior, prior // 2, 4), 10 * tok, {6: 0, 7: 1},
-        )(tail_bias, key_in, value_in, after, gk_part, gv_part, gk, gv)
-    return (attn, gq, gk, gv)
+
+    outs = []
+    for span, wide, after in zip(spans, wides, afters):
+        keep = outs[2:]
+        done = call(
+            functools.partial(tail_kernel, prior, span, [] if outs else places), "tail_keys",
+            [near] * 6 + ([anywhere] * 2 if outs else [near] * len(pieces)),
+            [anywhere] * (2 if outs else 4), [full16] * (2 if outs else 4),
+            [
+                near16(prior, wide), near16(prior, wide),
+                pltpu.SemaphoreType.DMA((2 if outs else len(places) + 2,)),
+            ],
+            (wide // HEAD_DIM, prior, prior // 2, 4), 10 * tok * wide,
+            {6: 0, 7: 1} if outs else None,
+        )(
+            *in_vmem(tail_bias, k, v, after, gk_part, gv_part),
+            *(keep if outs else in_vmem(*pieces)),
+        )
+        outs = [*outs[:2], *done]
+    return tuple(outs)
 
 
 def shards(query_in, key_in, value_in, grad_out, module_lengths):
     tok = query_in.shape[0]
     prior = tok * lax.axis_size("head") // 8
-    plan = halo_shards if 2 * prior <= tok else gathered_shards
+    plan = halo_shards if 2 * prior == tok else gathered_shards
     return plan(query_in, key_in, value_in, grad_out, module_lengths)
 
 

time: 30.4 us -> 29.7 us (0.977)
  the two profiles are of different devices: /device:TPU:25 before, /device:TPU:9 now
where the time goes in v10:
time: 29.7 us; the launch traced here: 29.4 us
  starting transfers between devices  12.4 us (42%)
  Pallas kernels  9.52 us (32%)
  waiting for transfers between devices  6.81 us (23%)
  between operations  0.71 us (2%)
    ppermute x4, starting transfers between devices, neighbour(): return lax.ppermute(value, ('seq', 'head'), pairs)  12.4 us
    ppermute x4, waiting for transfers between devices, neighbour(): return lax.ppermute(value, ('seq', 'head'), pairs)  6.81 us
    pallas_call x1, Pallas kernels, halo_shards(): call(functools.partial(own_kernel, prior, step), 'own_block', [anywhere]...  3.69 us
    pallas_call x2, Pallas kernels, halo_shards(): call(functools.partial(tail_kernel, prior, span, [] if outs else places),...  2.48 us
    pallas_call x2, Pallas kernels, halo_shards(): call(functools.partial(lead_kernel, prior, span), 'lead_rows', [near] * 8...  2.25 us
    pallas_call x1, Pallas kernels, halo_shards(): call(functools.partial(pack_kernel, prior, spans), 'pack_late', [anywhere...  1.1 us
  transfers between devices with their start and end apart: 4, of which 2 were waited for; matrix products, arithmetic and copies ran while one was open for 0% of the time, Pallas kernels for 25%

profile of v10, /device:TPU:9, one launch (start us, length us, event | category | flops | bytes accessed | tf_op | source)
XLA Modules:
  0.0 29.4 jit_solution(12103659258967525096)
XLA Ops:
  0.6 1.1 %pack_late.1 = (bf16[128,1536]{1,0:T(8,128)(2,1)S(1)}, bf16[128,512]{1,0:T(8,128)(2,1)S(1)}) custom-call(bf16[128,2048]{1,0:T(8,128)(2,1)} %k_ref.1, bf16[128,2048]{1,0:T(8,128)(2,1)} %v_ref.1), custom_call_target="tpu_custom_call" | custom-call | bytes 1048576 | tf_op jit(solution)/shard_map/pack_late/pallas_call | solution.py:448
  1.7 3.1 %collective-permute-start = (bf16[128,1536]{1,0:T(8,128)(2,1)S(1)}, bf16[128,1536]{1,0:T(8,128)(2,1)S(1)}, u32[]{:S(2)}, u32[]{:S(2)}) collective-permute-start(bf16[128,1536]{1,0:T(8,128)(2,1)S(1)} %get-tuple-element.39), channel_id=1, source_target_pairs={{0,1},{1,2},{2,3},{3,4},{4,5},{5,6},{6,7},{7,8},{8,9},{9,10},{10,1... | collective-permute-start | bytes 1179656 | tf_op jit(solution)/shard_map/ppermute | solution.py:401
  4.9 3.7 %own_block.1 = (bf16[128,2048]{1,0:T(8,128)(2,1)S(1)}, bf16[128,2048]{1,0:T(8,128)(2,1)S(1)}, bf16[128,2048]{1,0:T(8,128)(2,1)S(1)}, bf16[128,2048]{1,0:T(8,128)...) custom-call(s32[1,128]{1,0:T(1,128)} %bitcast.1, ...), custom_call_target="tpu_custom_call" | custom-call | flops 201326592 | bytes 6291456 | tf_op jit(solution)/shard_map/own_block/pallas_call | solution.py:455
  8.6 3.1 %collective-permute-start.2 = (bf16[128,512]{1,0:T(8,128)(2,1)S(1)}, bf16[128,512]{1,0:T(8,128)(2,1)S(1)}, u32[]{:S(2)}, u32[]{:S(2)}) collective-permute-start(bf16[128,512]{1,0:T(8,128)(2,1)S(1)} %get-tuple-element.50), channel_id=1, source_target_pairs={{0,1},{1,2},{2,3},{3,4},{4,5},{5,6},{6,7},{7,8},{8,9},{9,10},{10,1... | collective-permute-start | bytes 393224 | tf_op jit(solution)/shard_map/ppermute | solution.py:401
  11.7 5.8 %collective-permute-done.before_ref = bf16[128,1536]{1,0:T(8,128)(2,1)S(1)} collective-permute-done((bf16[128,1536]{1,0:T(8,128)(2,1)S(1)}, bf16[128,1536]{1,0:T(8,128)(2,1)S(1)}, u32[]{:S(2)}, u32[]{:S(2)}) %collective-permute-start) | collective-permute-done | bytes 393248 | tf_op jit(solution)/shard_map/ppermute | solution.py:401
  17.4 1.5 %lead_rows.2 = (bf16[64,1536]{1,0:T(8,128)(2,1)S(1)}, bf16[64,1536]{1,0:T(8,128)(2,1)S(1)}, bf16[64,1536]{1,0:T(8,128)(2,1)S(1)}, bf16[64,1536]{1,0:T(8,128)(2,1)S(1)}, bf16[64,1536]{1,0:T(8,128)(2,1)S(1)}) custom-call(f32[64,128]{1,0:T(8,128)S(1)} %get-tuple-element.36.bias_ref, bf16[128,2048]{1,0:T(8,128)(2,1)S(1)} %get-tuple-element.37.q_ref, ...), custom_call_target="tpu_custom_call" | custom-call | flops 150994944 | bytes 3145728 | tf_op jit(solution)/shard_map/lead_rows/pallas_call | solution.py:472
  18.9 2.7 %collective-permute-start.1 = (bf16[64,1536]{1,0:T(8,128)(2,1)S(1)}, bf16[64,1536]{1,0:T(8,128)(2,1)S(1)}, u32[]{:S(2)}, u32[]{:S(2)}) collective-permute-start(bf16[64,1536]{1,0:T(8,128)(2,1)S(1)} %get-tuple-element.42), channel_id=1, source_target_pairs={{1,0},{2,1},{3,2},{4,3},{5,4},{6,5},{7,6},{8,7},{9,8},{10,9},{11,1... | collective-permute-start | bytes 589832 | tf_op jit(solution)/shard_map/ppermute | solution.py:401
  21.6 0.0 collective-permute-done.2.before_ref
  21.6 0.8 %lead_rows.3 = (bf16[64,512]{1,0:T(8,128)(2,1)S(1)}, bf16[64,512]{1,0:T(8,128)(2,1)S(1)}, bf16[64,512]{1,0:T(8,128)(2,1)S(1)}, bf16[64,512]{1,0:T(8,128)(2,1)S(1)}, bf16[64,512]{1,0:T(8,128)(2,1)S(1)}) custom-call(f32[64,128]{1,0:T(8,128)S(1)} %get-tuple-element.36.bias_ref, bf16[128,2048]{1,0:T(8,128)(2,1)S(1)} %get-tuple-element.37.q_ref, ...), custom_call_target="tpu_custom_call" | custom-call | flops 50331648 | bytes 1048576 | tf_op jit(solution)/shard_map/lead_rows/pallas_call | solution.py:472
  22.4 3.5 %collective-permute-start.3 = (bf16[64,512]{1,0:T(8,128)(2,1)S(1)}, bf16[64,512]{1,0:T(8,128)(2,1)S(1)}, u32[]{:S(2)}, u32[]{:S(2)}) collective-permute-start(bf16[64,512]{1,0:T(8,128)(2,1)S(1)} %get-tuple-element.57), channel_id=1, source_target_pairs={{1,0},{2,1},{3,2},{4,3},{5,4},{6,5},{7,6},{8,7},{9,8},{10,9},{11,1... | collective-permute-start | bytes 196616 | tf_op jit(solution)/shard_map/ppermute | solution.py:401
  25.9 1.0 %collective-permute-done.1.after_ref = bf16[64,1536]{1,0:T(8,128)(2,1)S(1)} collective-permute-done((bf16[64,1536]{1,0:T(8,128)(2,1)S(1)}, bf16[64,1536]{1,0:T(8,128)(2,1)S(1)}, u32[]{:S(2)}, u32[]{:S(2)}) %collective-permute-start.1) | collective-permute-done | bytes 196640 | tf_op jit(solution)/shard_map/ppermute | solution.py:401
  26.9 1.5 %tail_keys.2 = (bf16[128,2048]{1,0:T(8,128)(2,1)}, bf16[128,2048]{1,0:T(8,128)(2,1)}, bf16[128,2048]{1,0:T(8,128)(2,1)}, bf16[128,2048]{1,0:T(8,128)(2,1)}) custom-call(f32[64,32]{1,0:T(8,128)S(1)} %get-tuple-element.33.bias_ref, bf16[128,2048]{1,0:T(8,128)(2,1)S(1)} %get-tuple-element.34.k_ref, bf16[128,2048]{1,0:T(8,128)(2,1)S(1)} %get-tuple-element.35.v_ref, ...), custom_call_target="tpu_custom_call" | custom-call | flops 25165824 | bytes 1966080 | tf_op jit(solution)/shard_map/tail_keys/pallas_call | solution.py:484
  28.5 0.0 collective-permute-done.3.after_ref
  28.5 1.0 %tail_keys.3 = (bf16[128,2048]{1,0:T(8,128)(2,1)}, bf16[128,2048]{1,0:T(8,128)(2,1)}) custom-call(f32[64,32]{1,0:T(8,128)S(1)} %get-tuple-element.33.bias_ref, bf16[128,2048]{1,0:T(8,128)(2,1)S(1)} %get-tuple-element.34.k_ref, bf16[128,2048]{1,0:T(8,128)(2,1)S(1)} %get-tuple-element.35.v_ref, ...), custom_call_target="tpu_custom_call", output_to_operand_aliasing={{0}: (6, {}), {1}: (7, {})} | custom-call | flops 8388608 | bytes 655360 | tf_op jit(solution)/shard_map/tail_keys/pallas_call | solution.py:484
Async XLA Ops:
  1.7 15.7 %collective-permute-start = (bf16[128,1536]{1,0:T(8,128)(2,1)S(1)}, bf16[128,1536]{1,0:T(8,128)(2,1)S(1)}, u32[]{:S(2)}, u32[]{:S(2)}) collective-permute-start(bf16[128,1536]{1,0:T(8,128)(2,1)S(1)} %get-tuple-element.39), channel_id=1, source_target_pairs={{0,1},{1,2},{2,3},{3,4},{4,5},{5,6},{6,7},{7,8},{8,9},{9,10},{10,1... | collective-permute-start | bytes 1179656 | tf_op jit(solution)/shard_map/ppermute | solution.py:401
  8.6 13.0 %collective-permute-start.2 = (bf16[128,512]{1,0:T(8,128)(2,1)S(1)}, bf16[128,512]{1,0:T(8,128)(2,1)S(1)}, u32[]{:S(2)}, u32[]{:S(2)}) collective-permute-start(bf16[128,512]{1,0:T(8,128)(2,1)S(1)} %get-tuple-element.50), channel_id=1, source_target_pairs={{0,1},{1,2},{2,3},{3,4},{4,5},{5,6},{6,7},{7,8},{8,9},{9,10},{10,1... | collective-permute-start | bytes 393224 | tf_op jit(solution)/shard_map/ppermute | solution.py:401
  18.9 8.0 %collective-permute-start.1 = (bf16[64,1536]{1,0:T(8,128)(2,1)S(1)}, bf16[64,1536]{1,0:T(8,128)(2,1)S(1)}, u32[]{:S(2)}, u32[]{:S(2)}) collective-permute-start(bf16[64,1536]{1,0:T(8,128)(2,1)S(1)} %get-tuple-element.42), channel_id=1, source_target_pairs={{1,0},{2,1},{3,2},{4,3},{5,4},{6,5},{7,6},{8,7},{9,8},{10,9},{11,1... | collective-permute-start | bytes 589832 | tf_op jit(solution)/shard_map/ppermute | solution.py:401
  22.4 6.1 %collective-permute-start.3 = (bf16[64,512]{1,0:T(8,128)(2,1)S(1)}, bf16[64,512]{1,0:T(8,128)(2,1)S(1)}, u32[]{:S(2)}, u32[]{:S(2)}) collective-permute-start(bf16[64,512]{1,0:T(8,128)(2,1)S(1)} %get-tuple-element.57), channel_id=1, source_target_pairs={{1,0},{2,1},{3,2},{4,3},{5,4},{6,5},{7,6},{8,7},{9,8},{10,9},{11,1... | collective-permute-start | bytes 196616 | tf_op jit(solution)/shard_map/ppermute | solution.py:401

commit v11 on v10

--- a/solution.py
+++ b/solution.py
@@ -199,8 +199,27 @@
     )
 
 
-def head_columns(width):
-    return [slice(c, c + HEAD_DIM) for c in range(0, width, HEAD_DIM)]
+def merged_rows(pairs, own):
+    tops = [
+        jnp.maximum(jnp.max(s, axis=0, keepdims=True), log) for (s, _), (log, _) in zip(pairs, own)
+    ]
+    raws = [jnp.exp2(s - top) for (s, _), top in zip(pairs, tops)]
+    own_raws = [jnp.exp2(log - top) for (log, _), top in zip(own, tops)]
+    parts = [
+        1.0 / (jnp.sum(raw, axis=0, keepdims=True) + own_raw)
+        for raw, own_raw in zip(raws, own_raws)
+    ]
+    weights = [raw * part for raw, part in zip(raws, parts)]
+    deltas = [
+        jnp.sum(w * dp, axis=0, keepdims=True) + own_raw * part * own_delta
+        for w, (_, dp), own_raw, part, (_, own_delta) in zip(weights, pairs, own_raws, parts, own)
+    ]
+    grads = [w * (dp - delta) * SCALE for w, (_, dp), delta in zip(weights, pairs, deltas)]
+    return [w.astype(jnp.bfloat16) for w in weights], [g.astype(jnp.bfloat16) for g in grads]
+
+
+def head_columns(low, high):
+    return [slice(c, c + HEAD_DIM) for c in range(low, high, HEAD_DIM)]
 
 
 def device_first(tok):
@@ -234,16 +253,15 @@
     return parts[:, :count] + parts[:, count : 2 * count] + parts[:, 2 * count : 3 * count]
 
 
-def pack_kernel(prior, spans, k_ref, v_ref, *refs):
-    *packed_refs, sems = refs
-    last = pl.ds(k_ref.shape[0] - prior, prior)
+def pack_kernel(prior, k_ref, v_ref, near_ref, far_ref, sems):
+    half, tok = prior // 2, k_ref.shape[0]
     copies = []
-    for span, packed_ref in zip(spans, packed_refs):
-        for half, ref in enumerate((k_ref, v_ref)):
+    for at, packed_ref in enumerate((near_ref, far_ref)):
+        rows = pl.ds(tok - (at + 1) * half, half)
+        for place, ref in enumerate((k_ref, v_ref)):
             copies.append(
                 pltpu.make_async_copy(
-                    ref.at[last, span],
-                    packed_ref.at[pl.ds(half * prior, prior), :],
+                    ref.at[rows, :], packed_ref.at[pl.ds(place * half, half), :],
                     sems.at[len(copies)],
                 )
             )
@@ -255,8 +273,8 @@
 
 def own_kernel(
     prior, step, len_hbm, q_hbm, k_hbm, v_hbm, do_hbm,
-    q_ref, k_ref, v_ref, do_ref, attn_ref, gq_ref, gk_ref, gv_ref, lead_bias_ref, tail_bias_ref,
-    len_ref, bias_ref, sems, len_sem,
+    q_ref, k_ref, v_ref, do_ref, attn_ref, gq_ref, gk_ref, gv_ref,
+    near_bias_ref, lead_bias_ref, tail_bias_ref, len_ref, bias_ref, sems, len_sem,
 ):
     tok, width = k_ref.shape
     pairs = ((k_hbm, k_ref), (v_hbm, v_ref), (q_hbm, q_ref), (do_hbm, do_ref))
@@ -278,6 +296,9 @@
     lengths = len_ref[...].astype(jnp.float32)
     bias_ref[...] = bias_by_query(lengths, first + prior, tok - prior, first, tok)
     lead_bias_ref[...] = bias_by_query(lengths, first, prior, first - prior, 2 * prior)
+    near_bias_ref[...] = bias_by_query(
+        lengths, first, prior, first - prior // 2, prior + prior // 2
+    )
     tail_bias_ref[...] = bias_by_key(lengths, first + tok, prior // 2, first + tok - prior, prior)
 
     @pl.loop(0, width // step)
@@ -302,95 +323,132 @@
             gv_ref[:, c] = dot(w, do_ref[late, c], 0, 0)
 
 
-def lead_kernel(
-    prior, span, bias_ref, q_ref, k_ref, v_ref, do_ref, before_ref, gk_part_ref, gv_part_ref,
-    attn_ref, gq_ref, gk_ref, gv_ref, back_ref,
+def near_kernel(
+    prior, near_bias_ref, lead_bias_ref, q_ref, k_ref, v_ref, do_ref, near_ref, back_ref
 ):
-    places = head_columns(span.stop - span.start)
-    columns = [slice(span.start + c.start, span.start + c.stop) for c in places]
     half = prior // 2
-    bias = bias_ref[...]
-    many = bias_ref[half - 1 : half, prior - 1 : prior] == 0.0
+    far = lead_bias_ref[0:1, half - 1 : half] == 0.0
+    lane = lax.broadcasted_iota(jnp.int32, (1, prior + half), 1)
+    bias = jnp.where(far & (lane < half), MASKED, near_bias_ref[...])
     spare = lax.broadcasted_iota(jnp.int32, (half, 1), 0) == half - 1
-    early, late = slice(0, prior), slice(prior, 2 * prior)
-    keys = [
-        jnp.concatenate([before_ref[early, p], k_ref[early, c]], axis=0)
-        for p, c in zip(places, columns)
-    ]
-    values = [
-        jnp.concatenate([before_ref[late, p], v_ref[early, c]], axis=0)
-        for p, c in zip(places, columns)
-    ]
-    pairs = [
-        by_query(q_ref[early, c], k, do_ref[early, c], v, bias)
-        for c, k, v in zip(columns, keys, values)
-    ]
+    early, first, second = slice(0, prior), slice(0, half), slice(half, prior)
+    columns = head_columns(0, q_ref.shape[1])
+    pairs = []
+    for c in columns:
+        k = jnp.concatenate([near_ref[first, c], k_ref[early, c]], axis=0)
+        v = jnp.concatenate([near_ref[second, c], v_ref[early, c]], axis=0)
+        pairs.append(by_query(q_ref[early, c], k, do_ref[early, c], v, bias))
     weights, grads, logs, deltas = full_rows(pairs)
     rows = as_rows([column[:half] for column in logs + deltas])
-    logs, deltas = rows[: len(columns)], rows[len(columns) :]
-    for at, (p, c) in enumerate(zip(places, columns)):
-        w, g = weights[at], grads[at]
-        gk = dot(g, q_ref[early, c], 0, 0)
-        gv = dot(w, do_ref[early, c], 0, 0)
-        few_q = jnp.where(spare, split_bf16(logs[at]), q_ref[:half, c])
-        few_do = jnp.where(spare, split_bf16(deltas[at]), do_ref[:half, c])
-        back_ref[:half, p] = jnp.where(many, gk[half:prior].astype(jnp.bfloat16), few_q)
-        back_ref[half:, p] = jnp.where(many, gv[half:prior].astype(jnp.bfloat16), few_do)
-        attn_ref[:, p] = dot(w, values[at], 1, 0).astype(jnp.bfloat16)
-        gq_ref[:, p] = dot(g, keys[at], 1, 0).astype(jnp.bfloat16)
-        gk_ref[:, p] = (gk_part_ref[early, c] + gk[prior:]).astype(jnp.bfloat16)
-        gv_ref[:, p] = (gv_part_ref[early, c] + gv[prior:]).astype(jnp.bfloat16)
+    for at, c in enumerate(columns):
+        for row, left, ref, place in (
+            (rows[at], grads[at], q_ref, first),
+            (rows[len(columns) + at], weights[at], do_ref, second),
+        ):
+            terms = dot(left[:, :half], ref[early, c], 0, 0).astype(jnp.bfloat16)
+            here = jnp.where(spare, split_bf16(row), ref[first, c])
+            back_ref[place, c] = jnp.where(far, here, terms)
+
+
+def lead_kernel(
+    prior, step, bias_ref, q_ref, k_ref, v_ref, do_ref, near_ref, far_ref, gk_part_ref, gv_part_ref,
+    attn_late_ref, gq_late_ref, attn_hbm, gq_hbm, gk_hbm, gv_hbm,
+    attn_ref, gq_ref, gk_ref, gv_ref, sems, late_sems,
+):
+    tok, width = q_ref.shape
+    half = prior // 2
+    early, first, second = slice(0, prior), slice(0, half), slice(half, prior)
+    late = pl.ds(prior, tok - prior)
+    late_copies = [
+        pltpu.make_async_copy(attn_late_ref, attn_hbm.at[late, :], late_sems.at[0]),
+        pltpu.make_async_copy(gq_late_ref, gq_hbm.at[late, :], late_sems.at[1]),
+    ]
+    for copy in late_copies:
+        copy.start()
+
+    def copies(at):
+        cols = pl.ds(pl.multiple_of(at * step, step), step)
+        pairs = ((attn_ref, attn_hbm), (gq_ref, gq_hbm), (gk_ref, gk_hbm), (gv_ref, gv_hbm))
+        return [
+            pltpu.make_async_copy(ref.at[:, cols], hbm.at[pl.ds(0, prior), cols], sems.at[at, n])
+            for n, (ref, hbm) in enumerate(pairs)
+        ]
+
+    @pl.loop(0, width // step)
+    def _(at):
+        bias = bias_ref[...]
+        columns = [
+            pl.ds(pl.multiple_of(at * step + c, HEAD_DIM), HEAD_DIM)
+            for c in range(0, step, HEAD_DIM)
+        ]
+        keys = [
+            jnp.concatenate([far_ref[first, c], near_ref[first, c], k_ref[early, c]], axis=0)
+            for c in columns
+        ]
+        values = [
+            jnp.concatenate([far_ref[second, c], near_ref[second, c], v_ref[early, c]], axis=0)
+            for c in columns
+        ]
+        pairs = [
+            by_query(q_ref[early, c], k, do_ref[early, c], v, bias)
+            for c, k, v in zip(columns, keys, values)
+        ]
+        weights, grads, _, _ = full_rows(pairs)
+        for c, w, g, k, v in zip(columns, weights, grads, keys, values):
+            attn_ref[:, c] = dot(w, v, 1, 0).astype(jnp.bfloat16)
+            gq_ref[:, c] = dot(g, k, 1, 0).astype(jnp.bfloat16)
+            gk = dot(g, q_ref[early, c], 0, 0)
+            gv = dot(w, do_ref[early, c], 0, 0)
+            gk_ref[:, c] = (gk_part_ref[early, c] + gk[prior:]).astype(jnp.bfloat16)
+            gv_ref[:, c] = (gv_part_ref[early, c] + gv[prior:]).astype(jnp.bfloat16)
+        for copy in copies(at):
+            copy.start()
+
+    for at in range(width // step):
+        for copy in copies(at):
+            copy.wait()
+    for copy in late_copies:
+        copy.wait()
 
 
 def tail_kernel(
-    prior, span, places, bias_ref, k_ref, v_ref, after_ref, gk_part_ref, gv_part_ref, *refs
+    prior, step, bias_ref, k_ref, v_ref, after_ref, gk_part_ref, gv_part_ref, gk_in, gv_in,
+    gk_hbm, gv_hbm, gk_ref, gv_ref, sems,
 ):
-    outs = 4 if places else 2
-    pieces, refs = refs[: len(places)], refs[len(places) :]
-    *refs, gk_ref, gv_ref, gk_late_ref, gv_late_ref, sems = refs
-    targets = (*refs[-2:], gk_ref, gv_ref) if outs == 4 else ()
+    tok, width = k_ref.shape
+    half = prior // 2
+    far = bias_ref[half - 1 : half, 0:1] == 0.0
+    bias = jnp.where(far, bias_ref[...], MASKED)
+    first, second, last = slice(0, half), slice(half, prior), slice(tok - prior, tok)
     copies = []
-    for piece, (target, row, col) in zip(pieces, places):
-        rows, cols = pl.ds(row, piece.shape[0]), pl.ds(col, piece.shape[1])
-        copies.append(
-            pltpu.make_async_copy(piece, targets[target].at[rows, cols], sems.at[len(copies)])
-        )
-        copies[-1].start()
-
-    tok = k_ref.shape[0]
-    here = head_columns(span.stop - span.start)
-    columns = [slice(span.start + c.start, span.start + c.stop) for c in here]
-    half = prior // 2
-    many = bias_ref[prior - 1 : prior, half - 1 : half] == 0.0
-    bias = jnp.where(many, MASKED, bias_ref[...])
-    first, second, last = slice(0, half), slice(half, prior), slice(tok - prior, tok)
-    pairs = [
-        by_query(k_ref[last, c], after_ref[first, p], v_ref[last, c], after_ref[second, p], bias)
-        for p, c in zip(here, columns)
-    ]
-    weights = [
-        jnp.exp2(s - joined(after_ref[half - 1 : half, p])) for (s, _), p in zip(pairs, here)
-    ]
-    grads = [
-        w * (dp - joined(after_ref[prior - 1 : prior, p])) * SCALE
-        for w, (_, dp), p in zip(weights, pairs, here)
-    ]
-    for p, c, w, g in zip(here, columns, weights, grads):
-        for out_ref, part_ref, left, rows in (
-            (gk_late_ref, gk_part_ref, g, first), (gv_late_ref, gv_part_ref, w, second)
-        ):
-            came = after_ref[rows, p]
-            total = part_ref[last, c] + dot(left.astype(jnp.bfloat16), came, 1, 0)
-            terms = jnp.where(many, came.astype(jnp.float32), 0.0)
-            out_ref[first, p] = total[first].astype(jnp.bfloat16)
-            out_ref[second, p] = (total[second] + terms).astype(jnp.bfloat16)
-    for late_ref, out_ref in ((gk_late_ref, gk_ref), (gv_late_ref, gv_ref)):
-        copies.append(
-            pltpu.make_async_copy(
-                late_ref, out_ref.at[pl.ds(tok - prior, prior), span], sems.at[len(copies)]
+    for low in range(0, width, step):
+        columns = head_columns(low, low + step)
+        pairs = [
+            by_query(k_ref[last, c], after_ref[first, c], v_ref[last, c], after_ref[second, c], bias)
+            for c in columns
+        ]
+        own = [
+            (joined(after_ref[half - 1 : half, c]), joined(after_ref[prior - 1 : prior, c]))
+            for c in columns
+        ]
+        weights, grads = merged_rows(pairs, own)
+        for c, w, g in zip(columns, weights, grads):
+            for out_ref, part_ref, left, rows in (
+                (gk_ref, gk_part_ref, g, first), (gv_ref, gv_part_ref, w, second)
+            ):
+                came = after_ref[rows, c]
+                total = part_ref[last, c] + dot(left, came, 1, 0)
+                terms = jnp.where(far, 0.0, came.astype(jnp.float32))
+                out_ref[first, c] = total[first].astype(jnp.bfloat16)
+                out_ref[second, c] = (total[second] + terms).astype(jnp.bfloat16)
+        cols = pl.ds(low, step)
+        for ref, hbm in ((gk_ref, gk_hbm), (gv_ref, gv_hbm)):
+            copies.append(
+                pltpu.make_async_copy(
+                    ref.at[:, cols], hbm.at[pl.ds(tok - prior, prior), cols], sems.at[len(copies)]
+                )
             )
-        )
-        copies[-1].start()
+            copies[-1].start()
     for copy in copies:
         copy.wait()
 
@@ -413,11 +471,9 @@
     tok, width = query_in.shape
     prior = tok * lax.axis_size("head") // 8
     step = math.gcd(width, 8 * HEAD_DIM)
-    cut = width - max(width // 4, HEAD_DIM)
-    spans = [slice(0, cut), slice(cut, width)] if cut else [slice(0, width)]
-    wides = [span.stop - span.start for span in spans]
+    groups = width // step
     anywhere = pl.BlockSpec(memory_space=pl.ANY)
-    near = pl.BlockSpec(memory_space=pltpu.VMEM)
+    inside = pl.BlockSpec(memory_space=pltpu.VMEM)
     full16 = jax.ShapeDtypeStruct((tok, width), jnp.bfloat16)
 
     def near16(rows, columns):
@@ -445,58 +501,49 @@
             name=name,
         )
 
-    to_next = call(
-        functools.partial(pack_kernel, prior, spans), "pack_late",
-        [anywhere] * 2, [near] * len(spans), [near16(2 * prior, wide) for wide in wides],
-        [pltpu.SemaphoreType.DMA((2 * len(spans),))], (0, 0, 0, 0), 8 * prior * width,
+    near, far = call(
+        functools.partial(pack_kernel, prior), "pack_late",
+        [anywhere] * 2, [inside] * 2, [near16(prior, width)] * 2,
+        [pltpu.SemaphoreType.DMA((4,))], (0, 0, 0, 0), 8 * prior * width,
     )(*in_hbm(key_in, value_in))
-    befores = [neighbour(to_next[0], 1)]
-
-    q, k, v, do, attn, gq, gk_part, gv_part, lead_bias, tail_bias = call(
+    near = neighbour(near, 1)
+
+    q, k, v, do, attn, gq, gk_part, gv_part, near_bias, lead_bias, tail_bias = call(
         functools.partial(own_kernel, prior, step), "own_block",
-        [anywhere] * 5, [near] * 10,
+        [anywhere] * 5, [inside] * 11,
         [near16(tok, width)] * 4 + [near16(tok - prior, width)] * 2 + [near32(tok, width)] * 2
-        + [near32(prior, 2 * prior), near32(prior, prior // 2)],
+        + [near32(prior, prior + prior // 2), near32(prior, 2 * prior), near32(prior, prior // 2)],
         [
             pltpu.VMEM((1, module_lengths.shape[0]), jnp.int32), near32(tok - prior, tok),
-            pltpu.SemaphoreType.DMA((width // step, 4)), pltpu.SemaphoreType.DMA(()),
+            pltpu.SemaphoreType.DMA((groups, 4)), pltpu.SemaphoreType.DMA(()),
         ],
         (width // HEAD_DIM, tok - prior, tok, 6), 24 * tok * width,
     )(*in_hbm(module_lengths.reshape(1, -1), query_in, key_in, value_in, grad_out))
-    for part in to_next[1:]:
-        part, _ = lax.optimization_barrier((part, lead_bias))
-        befores.append(neighbour(part, 1))
-
-    pieces, places, afters = [attn, gq], [(0, prior, 0), (1, prior, 0)], []
-    for span, wide, before in zip(spans, wides, befores):
-        *done, back = call(
-            functools.partial(lead_kernel, prior, span), "lead_rows",
-            [near] * 8, [near] * 5, [near16(prior, wide)] * 5, (),
-            (wide // HEAD_DIM, prior, 2 * prior, 6), 16 * tok * wide,
-        )(*in_vmem(lead_bias, q, k, v, do, before, gk_part, gv_part))
-        pieces += done
-        places += [(target, 0, span.start) for target in range(4)]
-        afters.append(neighbour(back, -1))
-
-    outs = []
-    for span, wide, after in zip(spans, wides, afters):
-        keep = outs[2:]
-        done = call(
-            functools.partial(tail_kernel, prior, span, [] if outs else places), "tail_keys",
-            [near] * 6 + ([anywhere] * 2 if outs else [near] * len(pieces)),
-            [anywhere] * (2 if outs else 4), [full16] * (2 if outs else 4),
-            [
-                near16(prior, wide), near16(prior, wide),
-                pltpu.SemaphoreType.DMA((2 if outs else len(places) + 2,)),
-            ],
-            (wide // HEAD_DIM, prior, prior // 2, 4), 10 * tok * wide,
-            {6: 0, 7: 1} if outs else None,
-        )(
-            *in_vmem(tail_bias, k, v, after, gk_part, gv_part),
-            *(keep if outs else in_vmem(*pieces)),
-        )
-        outs = [*outs[:2], *done]
-    return tuple(outs)
+    far, _ = lax.optimization_barrier((far, lead_bias))
+    far = neighbour(far, 1)
+
+    back = call(
+        functools.partial(near_kernel, prior), "near_terms",
+        [inside] * 7, inside, near16(prior, width), (),
+        (width // HEAD_DIM, prior, prior + prior // 2, 3), 8 * tok * width,
+    )(*in_vmem(near_bias, lead_bias, q, k, v, do, near))
+    back = neighbour(back, -1)
+
+    attn, gq, gk, gv = call(
+        functools.partial(lead_kernel, prior, step), "lead_rows",
+        [inside] * 11, [anywhere] * 4, [full16] * 4,
+        [near16(prior, width)] * 4
+        + [pltpu.SemaphoreType.DMA((groups, 4)), pltpu.SemaphoreType.DMA((2,))],
+        (width // HEAD_DIM, prior, 2 * prior, 6), 20 * tok * width,
+    )(*in_vmem(lead_bias, q, k, v, do, near, far, gk_part, gv_part, attn, gq))
+
+    gk, gv = call(
+        functools.partial(tail_kernel, prior, step), "tail_keys",
+        [inside] * 6 + [anywhere] * 2, [anywhere] * 2, [full16] * 2,
+        [near16(prior, width)] * 2 + [pltpu.SemaphoreType.DMA((2 * groups,))],
+        (width // HEAD_DIM, prior, prior // 2, 4), 10 * tok * width, {6: 0, 7: 1},
+    )(*in_vmem(tail_bias, k, v, back, gk_part, gv_part), gk, gv)
+    return (attn, gq, gk, gv)
 
 
 def shards(query_in, key_in, value_in, grad_out, module_lengths):

time: 29.7 us -> 28.3 us (0.953)
  the two profiles are of different devices: /device:TPU:9 before, /device:TPU:0 now
where the time goes in v11:
time: 28.3 us; the launch traced here: 28.1 us
  Pallas kernels  10.7 us (38%)
  starting transfers between devices  9.55 us (34%)
  waiting for transfers between devices  7.12 us (25%)
  between operations  0.69 us (2%)
    ppermute x3, starting transfers between devices, neighbour(): return lax.ppermute(value, ('seq', 'head'), pairs)  9.55 us
    ppermute x3, waiting for transfers between devices, neighbour(): return lax.ppermute(value, ('seq', 'head'), pairs)  7.12 us
    pallas_call x1, Pallas kernels, halo_shards(): call(functools.partial(own_kernel, prior, step), 'own_block', [anywhere]...  3.69 us
    pallas_call x1, Pallas kernels, halo_shards(): call(functools.partial(lead_kernel, prior, step), 'lead_rows', [inside] *...  3.06 us
    pallas_call x1, Pallas kernels, halo_shards(): call(functools.partial(tail_kernel, prior, step), 'tail_keys', [inside] *...  1.51 us
    pallas_call x1, Pallas kernels, halo_shards(): call(functools.partial(near_kernel, prior), 'near_terms', [inside] * 7, i...  1.32 us
    pallas_call x1, Pallas kernels, halo_shards(): call(functools.partial(pack_kernel, prior), 'pack_late', [anywhere] * 2,...  1.13 us
  transfers between devices with their start and end apart: 3, of which 2 were waited for; matrix products, arithmetic and copies ran while one was open for 0% of the time, Pallas kernels for 29%

profile of v11, /device:TPU:0, one launch (start us, length us, event | category | flops | bytes accessed | tf_op | source)
XLA Modules:
  0.0 28.1 jit_solution(11289269090838795895)
XLA Ops:
  0.6 1.1 %pack_late.1 = (bf16[64,2048]{1,0:T(8,128)(2,1)S(1)}, bf16[64,2048]{1,0:T(8,128)(2,1)S(1)}) custom-call(bf16[128,2048]{1,0:T(8,128)(2,1)} %k_ref.1, bf16[128,2048]{1,0:T(8,128)(2,1)} %v_ref.1), custom_call_target="tpu_custom_call" | custom-call | bytes 1048576 | tf_op jit(solution)/shard_map/pack_late/pallas_call | solution.py:504
  1.8 4.9 %collective-permute-start = (bf16[64,2048]{1,0:T(8,128)(2,1)S(1)}, bf16[64,2048]{1,0:T(8,128)(2,1)S(1)}, u32[]{:S(2)}, u32[]{:S(2)}) collective-permute-start(bf16[64,2048]{1,0:T(8,128)(2,1)S(1)} %get-tuple-element.29), channel_id=1, source_target_pairs={{0,1},{1,2},{2,3},{3,4},{4,5},{5,6},{6,7},{7,8},{8,9},{9,10},{10,1... | collective-permute-start | bytes 786440 | tf_op jit(solution)/shard_map/ppermute | solution.py:459
  6.6 3.7 %own_block.1 = (bf16[128,2048]{1,0:T(8,128)(2,1)S(1)}, bf16[128,2048]{1,0:T(8,128)(2,1)S(1)}, bf16[128,2048]{1,0:T(8,128)(2,1)S(1)}, bf16[128,2048]{1,0:T(8,128)...) custom-call(s32[1,128]{1,0:T(1,128)} %bitcast.1, ...), custom_call_target="tpu_custom_call" | custom-call | flops 201326592 | bytes 6291456 | tf_op jit(solution)/shard_map/own_block/pallas_call | solution.py:511
  10.3 3.4 %collective-permute-start.1 = (bf16[64,2048]{1,0:T(8,128)(2,1)S(1)}, bf16[64,2048]{1,0:T(8,128)(2,1)S(1)}, u32[]{:S(2)}, u32[]{:S(2)}) collective-permute-start(bf16[64,2048]{1,0:T(8,128)(2,1)S(1)} %get-tuple-element.31), channel_id=1, source_target_pairs={{0,1},{1,2},{2,3},{3,4},{4,5},{5,6},{6,7},{7,8},{8,9},{9,10},{10,1... | collective-permute-start | bytes 786440 | tf_op jit(solution)/shard_map/ppermute | solution.py:459
  13.7 0.0 collective-permute-done.near_ref
  13.7 1.3 %near_terms.1 = bf16[64,2048]{1,0:T(8,128)(2,1)S(1)} custom-call(f32[64,96]{1,0:T(8,128)S(1)} %get-tuple-element.39.near_bias_ref, f32[64,128]{1,0:T(8,128)S(1)} %get-tuple-element.24.bias_ref.lead_bias_ref, bf16[128,2048]{1,0:T(8,128)(2,1)S(1)} %get-tuple-element.25.q_ref, bf16[128,2048]{1,0:T(8,128)(2,1)S(1)} %get-tuple-element.26.k_ref, ...), custom_call_target="tpu_custom_call" | custom-call | flops 75497472 | bytes 2097152 | tf_op jit(solution)/shard_map/near_terms/pallas_call | solution.py:525
  15.1 1.3 %collective-permute-start.2 = (bf16[64,2048]{1,0:T(8,128)(2,1)S(1)}, bf16[64,2048]{1,0:T(8,128)(2,1)S(1)}, u32[]{:S(2)}, u32[]{:S(2)}) collective-permute-start(bf16[64,2048]{1,0:T(8,128)(2,1)S(1)} %near_terms.1), channel_id=1, source_target_pairs={{1,0},{2,1},{3,2},{4,3},{5,4},{6,5},{7,6},{8,7},{9,8},{10,9},{11,1... | collective-permute-start | bytes 786440 | tf_op jit(solution)/shard_map/ppermute | solution.py:459
  16.4 2.6 %collective-permute-done.1.far_ref = bf16[64,2048]{1,0:T(8,128)(2,1)S(1)} collective-permute-done((bf16[64,2048]{1,0:T(8,128)(2,1)S(1)}, bf16[64,2048]{1,0:T(8,128)(2,1)S(1)}, u32[]{:S(2)}, u32[]{:S(2)}) %collective-permute-start.1) | collective-permute-done | bytes 262176 | tf_op jit(solution)/shard_map/ppermute | solution.py:459
  19.0 3.1 %lead_rows.1 = (bf16[128,2048]{1,0:T(8,128)(2,1)}, bf16[128,2048]{1,0:T(8,128)(2,1)}, bf16[128,2048]{1,0:T(8,128)(2,1)}, bf16[128,2048]{1,0:T(8,128)(2,1)}) custom-call(f32[64,128]{1,0:T(8,128)S(1)} %get-tuple-element.24.bias_ref.lead_bias_ref, bf16[128,2048]{1,0:T(8,128)(2,1)S(1)} %get-tuple-element.25.q_ref, ...), custom_call_target="tpu_custom_call" | custom-call | flops 201326592 | bytes 5242880 | tf_op jit(solution)/shard_map/lead_rows/pallas_call | solution.py:532
  22.1 4.5 %collective-permute-done.2.after_ref = bf16[64,2048]{1,0:T(8,128)(2,1)S(1)} collective-permute-done((bf16[64,2048]{1,0:T(8,128)(2,1)S(1)}, bf16[64,2048]{1,0:T(8,128)(2,1)S(1)}, u32[]{:S(2)}, u32[]{:S(2)}) %collective-permute-start.2) | collective-permute-done | bytes 262176 | tf_op jit(solution)/shard_map/ppermute | solution.py:459
  26.6 1.5 %tail_keys.1 = (bf16[128,2048]{1,0:T(8,128)(2,1)}, bf16[128,2048]{1,0:T(8,128)(2,1)}) custom-call(f32[64,32]{1,0:T(8,128)S(1)} %get-tuple-element.38.bias_ref, bf16[128,2048]{1,0:T(8,128)(2,1)S(1)} %get-tuple-element.26.k_ref, bf16[128,2048]{1,0:T(8,128)(2,1)S(1)} %get-tuple-element.27.v_ref, ...), custom_call_target="tpu_custom_call", output_to_operand_aliasing={{0}: (6, {}), {1}: (7, {})} | custom-call | flops 33554432 | bytes 2621440 | tf_op jit(solution)/shard_map/tail_keys/pallas_call | solution.py:540
Async XLA Ops:
  1.8 12.0 %collective-permute-start = (bf16[64,2048]{1,0:T(8,128)(2,1)S(1)}, bf16[64,2048]{1,0:T(8,128)(2,1)S(1)}, u32[]{:S(2)}, u32[]{:S(2)}) collective-permute-start(bf16[64,2048]{1,0:T(8,128)(2,1)S(1)} %get-tuple-element.29), channel_id=1, source_target_pairs={{0,1},{1,2},{2,3},{3,4},{4,5},{5,6},{6,7},{7,8},{8,9},{9,10},{10,1... | collective-permute-start | bytes 786440 | tf_op jit(solution)/shard_map/ppermute | solution.py:459
  10.3 8.7 %collective-permute-start.1 = (bf16[64,2048]{1,0:T(8,128)(2,1)S(1)}, bf16[64,2048]{1,0:T(8,128)(2,1)S(1)}, u32[]{:S(2)}, u32[]{:S(2)}) collective-permute-start(bf16[64,2048]{1,0:T(8,128)(2,1)S(1)} %get-tuple-element.31), channel_id=1, source_target_pairs={{0,1},{1,2},{2,3},{3,4},{4,5},{5,6},{6,7},{7,8},{8,9},{9,10},{10,1... | collective-permute-start | bytes 786440 | tf_op jit(solution)/shard_map/ppermute | solution.py:459
  15.1 11.5 %collective-permute-start.2 = (bf16[64,2048]{1,0:T(8,128)(2,1)S(1)}, bf16[64,2048]{1,0:T(8,128)(2,1)S(1)}, u32[]{:S(2)}, u32[]{:S(2)}) collective-permute-start(bf16[64,2048]{1,0:T(8,128)(2,1)S(1)} %near_terms.1), channel_id=1, source_target_pairs={{1,0},{2,1},{3,2},{4,3},{5,4},{6,5},{7,6},{8,7},{9,8},{10,9},{11,1... | collective-permute-start | bytes 786440 | tf_op jit(solution)/shard_map/ppermute | solution.py:459

commit v12 on v11

--- a/solution.py
+++ b/solution.py
@@ -253,64 +253,61 @@
     return parts[:, :count] + parts[:, count : 2 * count] + parts[:, 2 * count : 3 * count]
 
 
-def pack_kernel(prior, k_ref, v_ref, near_ref, far_ref, sems):
+def pack_copies(prior, at, k_ref, v_ref, packed_ref, sems):
     half, tok = prior // 2, k_ref.shape[0]
-    copies = []
-    for at, packed_ref in enumerate((near_ref, far_ref)):
-        rows = pl.ds(tok - (at + 1) * half, half)
-        for place, ref in enumerate((k_ref, v_ref)):
-            copies.append(
-                pltpu.make_async_copy(
-                    ref.at[rows, :], packed_ref.at[pl.ds(place * half, half), :],
-                    sems.at[len(copies)],
-                )
-            )
+    rows = pl.ds(tok - (at + 1) * half, half)
+    return [
+        pltpu.make_async_copy(
+            ref.at[rows, :], packed_ref.at[pl.ds(n * half, half), :], sems.at[n]
+        )
+        for n, ref in enumerate((k_ref, v_ref))
+    ]
+
+
+def pack_kernel(prior, k_ref, v_ref, near_ref, sems):
+    copies = pack_copies(prior, 0, k_ref, v_ref, near_ref, sems)
     for copy in copies:
         copy.start()
     for copy in copies:
         copy.wait()
 
 
-def own_kernel(
-    prior, step, len_hbm, q_hbm, k_hbm, v_hbm, do_hbm,
-    q_ref, k_ref, v_ref, do_ref, attn_ref, gq_ref, gk_ref, gv_ref,
-    near_bias_ref, lead_bias_ref, tail_bias_ref, len_ref, bias_ref, sems, len_sem,
+def ready_kernel(
+    prior, len_hbm, q_hbm, k_hbm, v_hbm, do_hbm, far_ref, q_ref, k_ref, v_ref, do_ref,
+    own_bias_ref, near_bias_ref, lead_bias_ref, tail_bias_ref, len_ref, sems, far_sems, len_sem,
 ):
-    tok, width = k_ref.shape
-    pairs = ((k_hbm, k_ref), (v_hbm, v_ref), (q_hbm, q_ref), (do_hbm, do_ref))
-
-    def copies(at):
-        cols = pl.ds(pl.multiple_of(at * step, step), step)
-        return [
-            pltpu.make_async_copy(hbm.at[:, cols], ref.at[:, cols], sems.at[at, n])
-            for n, (hbm, ref) in enumerate(pairs)
-        ]
-
+    tok, half = k_ref.shape[0], prior // 2
+    pairs = ((q_hbm, q_ref), (k_hbm, k_ref), (v_hbm, v_ref), (do_hbm, do_ref))
+    copies = pack_copies(prior, 1, k_hbm, v_hbm, far_ref, far_sems)
+    copies += [pltpu.make_async_copy(hbm, ref, sems.at[n]) for n, (hbm, ref) in enumerate(pairs)]
     len_copy = pltpu.make_async_copy(len_hbm, len_ref, len_sem)
     len_copy.start()
-    for at in range(width // step):
-        for copy in copies(at):
-            copy.start()
+    for copy in copies:
+        copy.start()
     len_copy.wait()
     first = device_first(tok)
     lengths = len_ref[...].astype(jnp.float32)
-    bias_ref[...] = bias_by_query(lengths, first + prior, tok - prior, first, tok)
+    own_bias_ref[...] = bias_by_query(lengths, first + prior, tok - prior, first, tok)
+    near_bias_ref[...] = bias_by_query(lengths, first, prior, first - half, prior + half)
     lead_bias_ref[...] = bias_by_query(lengths, first, prior, first - prior, 2 * prior)
-    near_bias_ref[...] = bias_by_query(
-        lengths, first, prior, first - prior // 2, prior + prior // 2
-    )
-    tail_bias_ref[...] = bias_by_key(lengths, first + tok, prior // 2, first + tok - prior, prior)
+    tail_bias_ref[...] = bias_by_key(lengths, first + tok, half, first + tok - prior, prior)
+    for copy in copies:
+        copy.wait()
+
+
+def own_kernel(
+    prior, step, bias_ref, q_ref, k_ref, v_ref, do_ref, attn_ref, gq_ref, gk_ref, gv_ref
+):
+    tok, width = k_ref.shape
+    late = slice(prior, tok)
 
     @pl.loop(0, width // step)
     def _(at):
-        for copy in copies(at):
-            copy.wait()
         bias = bias_ref[...]
         columns = [
             pl.ds(pl.multiple_of(at * step + c, HEAD_DIM), HEAD_DIM)
             for c in range(0, step, HEAD_DIM)
         ]
-        late = slice(prior, tok)
         pairs = [
             by_query(q_ref[late, c], k_ref[:, c], do_ref[late, c], v_ref[:, c], bias)
             for c in columns
@@ -501,25 +498,26 @@
             name=name,
         )
 
-    near, far = call(
-        functools.partial(pack_kernel, prior), "pack_late",
-        [anywhere] * 2, [inside] * 2, [near16(prior, width)] * 2,
-        [pltpu.SemaphoreType.DMA((4,))], (0, 0, 0, 0), 8 * prior * width,
+    near = call(
+        functools.partial(pack_kernel, prior), "near_keys",
+        [anywhere] * 2, inside, near16(prior, width),
+        [pltpu.SemaphoreType.DMA((2,))], (0, 0, 0, 0), 4 * prior * width,
     )(*in_hbm(key_in, value_in))
     near = neighbour(near, 1)
 
-    q, k, v, do, attn, gq, gk_part, gv_part, near_bias, lead_bias, tail_bias = call(
-        functools.partial(own_kernel, prior, step), "own_block",
-        [anywhere] * 5, [inside] * 11,
-        [near16(tok, width)] * 4 + [near16(tok - prior, width)] * 2 + [near32(tok, width)] * 2
-        + [near32(prior, prior + prior // 2), near32(prior, 2 * prior), near32(prior, prior // 2)],
+    lengths = module_lengths.reshape(1, -1)
+    far, q, k, v, do, own_bias, near_bias, lead_bias, tail_bias = call(
+        functools.partial(ready_kernel, prior), "operands",
+        [anywhere] * 5, [inside] * 9,
+        [near16(prior, width)] + [near16(tok, width)] * 4
+        + [near32(tok - prior, tok), near32(prior, prior + prior // 2)]
+        + [near32(prior, 2 * prior), near32(prior, prior // 2)],
         [
-            pltpu.VMEM((1, module_lengths.shape[0]), jnp.int32), near32(tok - prior, tok),
-            pltpu.SemaphoreType.DMA((groups, 4)), pltpu.SemaphoreType.DMA(()),
+            pltpu.VMEM(lengths.shape, jnp.int32), pltpu.SemaphoreType.DMA((4,)),
+            pltpu.SemaphoreType.DMA((2,)), pltpu.SemaphoreType.DMA(()),
         ],
-        (width // HEAD_DIM, tok - prior, tok, 6), 24 * tok * width,
-    )(*in_hbm(module_lengths.reshape(1, -1), query_in, key_in, value_in, grad_out))
-    far, _ = lax.optimization_barrier((far, lead_bias))
+        (0, 0, 0, 0), 18 * tok * width,
+    )(*in_hbm(lengths, query_in, key_in, value_in, grad_out))
     far = neighbour(far, 1)
 
     back = call(
@@ -527,7 +525,15 @@
         [inside] * 7, inside, near16(prior, width), (),
         (width // HEAD_DIM, prior, prior + prior // 2, 3), 8 * tok * width,
     )(*in_vmem(near_bias, lead_bias, q, k, v, do, near))
+    own_bias, back = lax.optimization_barrier((own_bias, back))
     back = neighbour(back, -1)
+
+    attn, gq, gk_part, gv_part = call(
+        functools.partial(own_kernel, prior, step), "own_block",
+        [inside] * 5, [inside] * 4,
+        [near16(tok - prior, width)] * 2 + [near32(tok, width)] * 2, (),
+        (width // HEAD_DIM, tok - prior, tok, 6), 18 * tok * width,
+    )(*in_vmem(own_bias, q, k, v, do))
 
     attn, gq, gk, gv = call(
         functools.partial(lead_kernel, prior, step), "lead_rows",

time: 28.3 us -> 26.9 us (0.951)
  waiting for transfers between devices: 7.12 us -> 5.73 us
    ppermute x3, waiting for transfers between devices: 7.12 us -> 5.73 us  [neighbour(): return lax.ppermute(value, ('seq', 'head'), pairs)]
    pallas_call x2 -> x3, Pallas kernels: 4.82 us -> 4.87 us  [the longest x1 2.2 us: halo_shards(): call(functools.partial(own_kernel, prior, step), 'own_block', [inside] *...]
  transfers between devices with their start and end apart: 3 -> 3, of which waited for: 2 -> 3; matrix products, arithmetic and copies ran while one was open for 0% -> 0% of each run, Pallas kernels for 29% -> 31%
where the time goes in v12:
time: 26.9 us; the launch traced here: 26.7 us
  Pallas kernels  10.8 us (40%)
  starting transfers between devices  9.55 us (36%)
  waiting for transfers between devices  5.73 us (21%)
  between operations  0.68 us (3%)
    ppermute x3, starting transfers between devices, neighbour(): return lax.ppermute(value, ('seq', 'head'), pairs)  9.55 us
    ppermute x3, waiting for transfers between devices, neighbour(): return lax.ppermute(value, ('seq', 'head'), pairs)  5.73 us
    pallas_call x1, Pallas kernels, halo_shards(): call(functools.partial(lead_kernel, prior, step), 'lead_rows', [inside] *...  3.06 us
    pallas_call x1, Pallas kernels, halo_shards(): call(functools.partial(own_kernel, prior, step), 'own_block', [inside] *...  2.2 us
    pallas_call x1, Pallas kernels, halo_shards(): call(functools.partial(ready_kernel, prior), 'operands', [anywhere] * 5,...  1.68 us
    pallas_call x1, Pallas kernels, halo_shards(): call(functools.partial(tail_kernel, prior, step), 'tail_keys', [inside] *...  1.51 us
    pallas_call x1, Pallas kernels, halo_shards(): call(functools.partial(near_kernel, prior), 'near_terms', [inside] * 7, i...  1.32 us
    pallas_call x1, Pallas kernels, halo_shards(): call(functools.partial(pack_kernel, prior), 'near_keys', [anywhere] * 2,...  0.99 us
  transfers between devices with their start and end apart: 3, of which 3 were waited for; matrix products, arithmetic and copies ran while one was open for 0% of the time, Pallas kernels for 31%

profile of v12, /device:TPU:0, one launch (start us, length us, event | category | flops | bytes accessed | tf_op | source)
XLA Modules:
  0.0 26.7 jit_solution(18360319411951379802)
XLA Ops:
  0.6 1.0 %near_keys.1 = bf16[64,2048]{1,0:T(8,128)(2,1)S(1)} custom-call(bf16[128,2048]{1,0:T(8,128)(2,1)} %k_ref.1, bf16[128,2048]{1,0:T(8,128)(2,1)} %v_ref.1), custom_call_target="tpu_custom_call" | custom-call | bytes 524288 | tf_op jit(solution)/shard_map/near_keys/pallas_call | solution.py:501
  1.6 4.9 %collective-permute-start = (bf16[64,2048]{1,0:T(8,128)(2,1)S(1)}, bf16[64,2048]{1,0:T(8,128)(2,1)S(1)}, u32[]{:S(2)}, u32[]{:S(2)}) collective-permute-start(bf16[64,2048]{1,0:T(8,128)(2,1)S(1)} %near_keys.1), channel_id=1, source_target_pairs={{0,1},{1,2},{2,3},{3,4},{4,5},{5,6},{6,7},{7,8},{8,9},{9,10},{10,1... | collective-permute-start | bytes 786440 | tf_op jit(solution)/shard_map/ppermute | solution.py:456
  6.5 1.7 %operands.1 = (bf16[64,2048]{1,0:T(8,128)(2,1)S(1)}, bf16[128,2048]{1,0:T(8,128)(2,1)S(1)}, bf16[128,2048]{1,0:T(8,128)(2,1)S(1)}, bf16[128,2048]{1,0:T(8,128)(2...) custom-call(s32[1,128]{1,0:T(1,128)} %bitcast.1, ...), custom_call_target="tpu_custom_call" | custom-call | bytes 4718592 | tf_op jit(solution)/shard_map/operands/pallas_call | solution.py:509
  8.2 3.4 %collective-permute-start.1 = (bf16[64,2048]{1,0:T(8,128)(2,1)S(1)}, bf16[64,2048]{1,0:T(8,128)(2,1)S(1)}, u32[]{:S(2)}, u32[]{:S(2)}) collective-permute-start(bf16[64,2048]{1,0:T(8,128)(2,1)S(1)} %get-tuple-element.30), channel_id=1, source_target_pairs={{0,1},{1,2},{2,3},{3,4},{4,5},{5,6},{6,7},{7,8},{8,9},{9,10},{10,1... | collective-permute-start | bytes 786440 | tf_op jit(solution)/shard_map/ppermute | solution.py:456
  11.6 1.2 %collective-permute-done.near_ref = bf16[64,2048]{1,0:T(8,128)(2,1)S(1)} collective-permute-done((bf16[64,2048]{1,0:T(8,128)(2,1)S(1)}, bf16[64,2048]{1,0:T(8,128)(2,1)S(1)}, u32[]{:S(2)}, u32[]{:S(2)}) %collective-permute-start) | collective-permute-done | bytes 262176 | tf_op jit(solution)/shard_map/ppermute | solution.py:456
  12.8 1.3 %near_terms.1 = bf16[64,2048]{1,0:T(8,128)(2,1)S(1)} custom-call(f32[64,96]{1,0:T(8,128)S(1)} %get-tuple-element.32.near_bias_ref, f32[64,128]{1,0:T(8,128)S(1)} %get-tuple-element.25.lead_bias_ref.bias_ref, bf16[128,2048]{1,0:T(8,128)(2,1)S(1)} %get-tuple-element.26.q_ref, bf16[128,2048]{1,0:T(8,128)(2,1)S(1)} %get-tuple-element.27.k_ref, ...), custom_call_target="tpu_custom_call" | custom-call | flops 75497472 | bytes 2097152 | tf_op jit(solution)/shard_map/near_terms/pallas_call | solution.py:523
  14.1 1.3 %collective-permute-start.2 = (bf16[64,2048]{1,0:T(8,128)(2,1)S(1)}, bf16[64,2048]{1,0:T(8,128)(2,1)S(1)}, u32[]{:S(2)}, u32[]{:S(2)}) collective-permute-start(bf16[64,2048]{1,0:T(8,128)(2,1)S(1)} %near_terms.1), channel_id=1, source_target_pairs={{1,0},{2,1},{3,2},{4,3},{5,4},{6,5},{7,6},{8,7},{9,8},{10,9},{11,1... | collective-permute-start | bytes 786440 | tf_op jit(solution)/shard_map/ppermute | solution.py:456
  15.4 2.2 %own_block.1 = (bf16[64,2048]{1,0:T(8,128)(2,1)S(1)}, bf16[64,2048]{1,0:T(8,128)(2,1)S(1)}, f32[128,2048]{1,0:T(8,128)S(1)}, f32[128,2048]{1,0:T(8,128)S(1)}) custom-call(f32[64,128]{1,0:T(8,128)S(1)} %get-tuple-element.33.bias_ref, bf16[128,2048]{1,0:T(8,128)(2,1)S(1)} %get-tuple-element.26.q_ref, bf16[128,2048]{1,0:T(8,128)(2,1)S(1)} %get-tuple-element.27.k_ref, ...), custom_call_target="tpu_custom_call" | custom-call | flops 201326592 | bytes 4718592 | tf_op jit(solution)/shard_map/own_block/pallas_call | solution.py:531
  17.6 0.1 collective-permute-done.1.far_ref
  17.6 3.1 %lead_rows.1 = (bf16[128,2048]{1,0:T(8,128)(2,1)}, bf16[128,2048]{1,0:T(8,128)(2,1)}, bf16[128,2048]{1,0:T(8,128)(2,1)}, bf16[128,2048]{1,0:T(8,128)(2,1)}) custom-call(f32[64,128]{1,0:T(8,128)S(1)} %get-tuple-element.25.lead_bias_ref.bias_ref, bf16[128,2048]{1,0:T(8,128)(2,1)S(1)} %get-tuple-element.26.q_ref, ...), custom_call_target="tpu_custom_call" | custom-call | flops 201326592 | bytes 5242880 | tf_op jit(solution)/shard_map/lead_rows/pallas_call | solution.py:538
  20.7 4.5 %collective-permute-done.2.after_ref = bf16[64,2048]{1,0:T(8,128)(2,1)S(1)} collective-permute-done((bf16[64,2048]{1,0:T(8,128)(2,1)S(1)}, bf16[64,2048]{1,0:T(8,128)(2,1)S(1)}, u32[]{:S(2)}, u32[]{:S(2)}) %collective-permute-start.2) | collective-permute-done | bytes 262176 | tf_op jit(solution)/shard_map/ppermute | solution.py:456
  25.2 1.5 %tail_keys.1 = (bf16[128,2048]{1,0:T(8,128)(2,1)}, bf16[128,2048]{1,0:T(8,128)(2,1)}) custom-call(f32[64,32]{1,0:T(8,128)S(1)} %get-tuple-element.40.bias_ref, bf16[128,2048]{1,0:T(8,128)(2,1)S(1)} %get-tuple-element.27.k_ref, bf16[128,2048]{1,0:T(8,128)(2,1)S(1)} %get-tuple-element.28.v_ref, ...), custom_call_target="tpu_custom_call", output_to_operand_aliasing={{0}: (6, {}), {1}: (7, {})} | custom-call | flops 33554432 | bytes 2621440 | tf_op jit(solution)/shard_map/tail_keys/pallas_call | solution.py:546
Async XLA Ops:
  1.6 11.1 %collective-permute-start = (bf16[64,2048]{1,0:T(8,128)(2,1)S(1)}, bf16[64,2048]{1,0:T(8,128)(2,1)S(1)}, u32[]{:S(2)}, u32[]{:S(2)}) collective-permute-start(bf16[64,2048]{1,0:T(8,128)(2,1)S(1)} %near_keys.1), channel_id=1, source_target_pairs={{0,1},{1,2},{2,3},{3,4},{4,5},{5,6},{6,7},{7,8},{8,9},{9,10},{10,1... | collective-permute-start | bytes 786440 | tf_op jit(solution)/shard_map/ppermute | solution.py:456
  8.2 9.5 %collective-permute-start.1 = (bf16[64,2048]{1,0:T(8,128)(2,1)S(1)}, bf16[64,2048]{1,0:T(8,128)(2,1)S(1)}, u32[]{:S(2)}, u32[]{:S(2)}) collective-permute-start(bf16[64,2048]{1,0:T(8,128)(2,1)S(1)} %get-tuple-element.30), channel_id=1, source_target_pairs={{0,1},{1,2},{2,3},{3,4},{4,5},{5,6},{6,7},{7,8},{8,9},{9,10},{10,1... | collective-permute-start | bytes 786440 | tf_op jit(solution)/shard_map/ppermute | solution.py:456
  14.1 11.1 %collective-permute-start.2 = (bf16[64,2048]{1,0:T(8,128)(2,1)S(1)}, bf16[64,2048]{1,0:T(8,128)(2,1)S(1)}, u32[]{:S(2)}, u32[]{:S(2)}) collective-permute-start(bf16[64,2048]{1,0:T(8,128)(2,1)S(1)} %near_terms.1), channel_id=1, source_target_pairs={{1,0},{2,1},{3,2},{4,3},{5,4},{6,5},{7,6},{8,7},{9,8},{10,9},{11,1... | collective-permute-start | bytes 786440 | tf_op jit(solution)/shard_map/ppermute | solution.py:456

commit v13 on v12

--- a/solution.py
+++ b/solution.py
@@ -170,11 +170,14 @@
     return jnp.where((key >= start) & (key <= query), 0.0, MASKED)
 
 
-def bias_by_key(lengths_row, first_query, queries, first_key, keys):
+def bias_by_key(lengths_row, first_query, queries, first_key, keys, heads):
     ends = module_ends_col(lengths_row)
-    query = (first_query + lax.broadcasted_iota(jnp.int32, (1, queries), 1)).astype(jnp.float32)
+    lane = lax.broadcasted_iota(jnp.int32, (1, heads * queries), 1)
+    query = (first_query + lane % queries).astype(jnp.float32)
     start = jnp.max(jnp.where(ends <= query, ends, 0.0), axis=0, keepdims=True)
-    key = (first_key + lax.broadcasted_iota(jnp.int32, (keys, queries), 0)).astype(jnp.float32)
+    key = (first_key + lax.broadcasted_iota(jnp.int32, (keys, heads * queries), 0)).astype(
+        jnp.float32
+    )
     return jnp.where((key >= start) & (key <= query), 0.0, MASKED)
 
 
@@ -186,20 +189,13 @@
 def full_rows(pairs):
     tops = [jnp.max(s, axis=1, keepdims=True) for s, _ in pairs]
     raws = [jnp.exp2(s - top) for (s, _), top in zip(pairs, tops)]
-    totals = [jnp.sum(raw, axis=1, keepdims=True) for raw in raws]
-    weights = [raw * (1.0 / total) for raw, total in zip(raws, totals)]
+    weights = [raw * (1.0 / jnp.sum(raw, axis=1, keepdims=True)) for raw in raws]
     deltas = [jnp.sum(w * dp, axis=1, keepdims=True) for w, (_, dp) in zip(weights, pairs)]
     grads = [w * (dp - delta) * SCALE for w, (_, dp), delta in zip(weights, pairs, deltas)]
-    logs = [top + jnp.log2(total) for top, total in zip(tops, totals)]
-    return (
-        [w.astype(jnp.bfloat16) for w in weights],
-        [g.astype(jnp.bfloat16) for g in grads],
-        logs,
-        deltas,
-    )
-
-
-def merged_rows(pairs, own):
+    return [w.astype(jnp.bfloat16) for w in weights], [g.astype(jnp.bfloat16) for g in grads]
+
+
+def merged_columns(pairs, own):
     tops = [
         jnp.maximum(jnp.max(s, axis=0, keepdims=True), log) for (s, _), (log, _) in zip(pairs, own)
     ]
@@ -218,8 +214,22 @@
     return [w.astype(jnp.bfloat16) for w in weights], [g.astype(jnp.bfloat16) for g in grads]
 
 
-def head_columns(low, high):
-    return [slice(c, c + HEAD_DIM) for c in range(low, high, HEAD_DIM)]
+def side_by_side(rows):
+    heads = rows.shape[1] // HEAD_DIM
+    zero = jnp.zeros((rows.shape[0], HEAD_DIM), rows.dtype)
+    blocks = [rows[:, c] for c in head_columns(0, rows.shape[1])]
+    return jnp.concatenate(
+        [
+            jnp.concatenate([blocks[h] if g == h else zero for g in range(heads)], axis=1)
+            for h in range(heads)
+        ],
+        axis=0,
+    )
+
+
+def head_columns(low, high, heads=1):
+    wide = heads * HEAD_DIM
+    return [slice(c, c + wide) for c in range(low, high, wide)]
 
 
 def device_first(tok):
@@ -227,15 +237,18 @@
     return place * tok
 
 
-def as_rows(columns):
-    count = columns[0].shape[0]
-    lane = lax.broadcasted_iota(jnp.int32, (count, HEAD_DIM), 1)
-    table = jnp.zeros((count, HEAD_DIM), jnp.float32)
-    for at, column in enumerate(columns):
-        table = jnp.where(lane == at, column, table)
-    fill = jnp.zeros((HEAD_DIM - count, HEAD_DIM), jnp.float32)
-    table = jnp.transpose(jnp.concatenate([table, fill], axis=0))
-    return [table[at : at + 1, :count] for at in range(len(columns))]
+def fours(rows):
+    table = jnp.concatenate(rows, axis=0)
+    half = table.shape[1] // 4
+    lane = lax.broadcasted_iota(jnp.int32, (1, table.shape[1]), 1)
+    turned = [pltpu.roll(table, turn * half, 1) for turn in (3, 2, 1)]
+    merged = []
+    for at in range(0, len(rows), 2):
+        now, after = slice(at, at + 1), slice(at + 1, at + 2)
+        row = jnp.where(lane < 3 * half, turned[1][after], turned[2][after])
+        row = jnp.where(lane < 2 * half, turned[0][now], row)
+        merged.append(jnp.where(lane < half, table[now], row))
+    return merged
 
 
 def split_bf16(row):
@@ -288,9 +301,9 @@
     first = device_first(tok)
     lengths = len_ref[...].astype(jnp.float32)
     own_bias_ref[...] = bias_by_query(lengths, first + prior, tok - prior, first, tok)
-    near_bias_ref[...] = bias_by_query(lengths, first, prior, first - half, prior + half)
+    near_bias_ref[...] = bias_by_key(lengths, first, prior, first - half, prior + half, 2)
     lead_bias_ref[...] = bias_by_query(lengths, first, prior, first - prior, 2 * prior)
-    tail_bias_ref[...] = bias_by_key(lengths, first + tok, half, first + tok - prior, prior)
+    tail_bias_ref[...] = bias_by_key(lengths, first + tok, half, first + tok - prior, prior, 4)
     for copy in copies:
         copy.wait()
 
@@ -312,7 +325,7 @@
             by_query(q_ref[late, c], k_ref[:, c], do_ref[late, c], v_ref[:, c], bias)
             for c in columns
         ]
-        weights, grads, _, _ = full_rows(pairs)
+        weights, grads = full_rows(pairs)
         for c, w, g in zip(columns, weights, grads):
             attn_ref[:, c] = dot(w, v_ref[:, c], 1, 0).astype(jnp.bfloat16)
             gq_ref[:, c] = dot(g, k_ref[:, c], 1, 0).astype(jnp.bfloat16)
@@ -325,25 +338,36 @@
 ):
     half = prior // 2
     far = lead_bias_ref[0:1, half - 1 : half] == 0.0
-    lane = lax.broadcasted_iota(jnp.int32, (1, prior + half), 1)
-    bias = jnp.where(far & (lane < half), MASKED, near_bias_ref[...])
+    key = lax.broadcasted_iota(jnp.int32, (prior + half, 1), 0)
+    bias = jnp.where(far & (key < half), MASKED, near_bias_ref[...])
     spare = lax.broadcasted_iota(jnp.int32, (half, 1), 0) == half - 1
     early, first, second = slice(0, prior), slice(0, half), slice(half, prior)
-    columns = head_columns(0, q_ref.shape[1])
+    columns = head_columns(0, q_ref.shape[1], 2)
+    queries = [side_by_side(q_ref[early, c]) for c in columns]
+    cotangents = [side_by_side(do_ref[early, c]) for c in columns]
     pairs = []
-    for c in columns:
+    for c, q, do in zip(columns, queries, cotangents):
         k = jnp.concatenate([near_ref[first, c], k_ref[early, c]], axis=0)
         v = jnp.concatenate([near_ref[second, c], v_ref[early, c]], axis=0)
-        pairs.append(by_query(q_ref[early, c], k, do_ref[early, c], v, bias))
-    weights, grads, logs, deltas = full_rows(pairs)
-    rows = as_rows([column[:half] for column in logs + deltas])
-    for at, c in enumerate(columns):
-        for row, left, ref, place in (
-            (rows[at], grads[at], q_ref, first),
-            (rows[len(columns) + at], weights[at], do_ref, second),
+        pairs.append(by_query(k, q, v, do, bias))
+    tops = [jnp.max(s, axis=0, keepdims=True) for s, _ in pairs]
+    raws = [jnp.exp2(s - top) for (s, _), top in zip(pairs, tops)]
+    totals = [jnp.sum(raw, axis=0, keepdims=True) for raw in raws]
+    weights = [raw * (1.0 / total) for raw, total in zip(raws, totals)]
+    deltas = [jnp.sum(w * dp, axis=0, keepdims=True) for w, (_, dp) in zip(weights, pairs)]
+    grads = [
+        w[:half] * (dp[:half] - delta) * SCALE for w, (_, dp), delta in zip(weights, pairs, deltas)
+    ]
+    k_terms = [dot(g.astype(jnp.bfloat16), q, 1, 0) for g, q in zip(grads, queries)]
+    v_terms = [dot(w[:half].astype(jnp.bfloat16), do, 1, 0) for w, do in zip(weights, cotangents)]
+    logs = fours([top + jnp.log2(total) for top, total in zip(tops, totals)])
+    deltas = fours(deltas)
+    for at, c in enumerate(head_columns(0, q_ref.shape[1], 4)):
+        for row, terms, ref, place in (
+            (logs[at], k_terms, q_ref, first), (deltas[at], v_terms, do_ref, second)
         ):
-            terms = dot(left[:, :half], ref[early, c], 0, 0).astype(jnp.bfloat16)
             here = jnp.where(spare, split_bf16(row), ref[first, c])
+            terms = jnp.concatenate(terms[2 * at : 2 * at + 2], axis=1).astype(jnp.bfloat16)
             back_ref[place, c] = jnp.where(far, here, terms)
 
 
@@ -390,7 +414,7 @@
             by_query(q_ref[early, c], k, do_ref[early, c], v, bias)
             for c, k, v in zip(columns, keys, values)
         ]
-        weights, grads, _, _ = full_rows(pairs)
+        weights, grads = full_rows(pairs)
         for c, w, g, k, v in zip(columns, weights, grads, keys, values):
             attn_ref[:, c] = dot(w, v, 1, 0).astype(jnp.bfloat16)
             gq_ref[:, c] = dot(g, k, 1, 0).astype(jnp.bfloat16)
@@ -419,23 +443,24 @@
     first, second, last = slice(0, half), slice(half, prior), slice(tok - prior, tok)
     copies = []
     for low in range(0, width, step):
-        columns = head_columns(low, low + step)
+        columns = head_columns(low, low + step, 4)
+        queries = [side_by_side(after_ref[first, c]) for c in columns]
+        cotangents = [side_by_side(after_ref[second, c]) for c in columns]
         pairs = [
-            by_query(k_ref[last, c], after_ref[first, c], v_ref[last, c], after_ref[second, c], bias)
-            for c in columns
+            by_query(k_ref[last, c], q, v_ref[last, c], do, bias)
+            for c, q, do in zip(columns, queries, cotangents)
         ]
         own = [
             (joined(after_ref[half - 1 : half, c]), joined(after_ref[prior - 1 : prior, c]))
             for c in columns
         ]
-        weights, grads = merged_rows(pairs, own)
-        for c, w, g in zip(columns, weights, grads):
-            for out_ref, part_ref, left, rows in (
-                (gk_ref, gk_part_ref, g, first), (gv_ref, gv_part_ref, w, second)
+        weights, grads = merged_columns(pairs, own)
+        for c, w, g, q, do in zip(columns, weights, grads, queries, cotangents):
+            for out_ref, part_ref, left, right, rows in (
+                (gk_ref, gk_part_ref, g, q, first), (gv_ref, gv_part_ref, w, do, second)
             ):
-                came = after_ref[rows, c]
-                total = part_ref[last, c] + dot(left, came, 1, 0)
-                terms = jnp.where(far, 0.0, came.astype(jnp.float32))
+                total = part_ref[last, c] + dot(left, right, 1, 0)
+                terms = jnp.where(far, 0.0, after_ref[rows, c].astype(jnp.float32))
                 out_ref[first, c] = total[first].astype(jnp.bfloat16)
                 out_ref[second, c] = (total[second] + terms).astype(jnp.bfloat16)
         cols = pl.ds(low, step)
@@ -510,8 +535,8 @@
         functools.partial(ready_kernel, prior), "operands",
         [anywhere] * 5, [inside] * 9,
         [near16(prior, width)] + [near16(tok, width)] * 4
-        + [near32(tok - prior, tok), near32(prior, prior + prior // 2)]
-        + [near32(prior, 2 * prior), near32(prior, prior // 2)],
+        + [near32(tok - prior, tok), near32(prior + prior // 2, 2 * prior)]
+        + [near32(prior, 2 * prior), near32(prior, 2 * prior)],
         [
             pltpu.VMEM(lengths.shape, jnp.int32), pltpu.SemaphoreType.DMA((4,)),
             pltpu.SemaphoreType.DMA((2,)), pltpu.SemaphoreType.DMA(()),

time: 26.9 us -> 27 us (level)
  Pallas kernels: 10.8 us -> 10.2 us
  waiting for transfers between devices: 5.73 us -> 6.31 us
    pallas_call x1, Pallas kernels: 1.32 us -> 0.73 us  [halo_shards(): call(functools.partial(near_kernel, prior), 'near_terms', [inside] * 7, i...]
    ppermute x3, waiting for transfers between devices: 5.73 us -> 6.31 us  [neighbour(): return lax.ppermute(value, ('seq', 'head'), pairs)]
  transfers between devices with their start and end apart: 3 -> 3, of which waited for: 3 -> 3; matrix products, arithmetic and copies ran while one was open for 0% -> 0% of each run, Pallas kernels for 31% -> 29%
where the time goes in v13:
time: 27 us; the launch traced here: 26.8 us
  Pallas kernels  10.2 us (38%)
  starting transfers between devices  9.55 us (35%)
  waiting for transfers between devices  6.31 us (23%)
  between operations  0.68 us (3%)
    ppermute x3, starting transfers between devices, neighbour(): return lax.ppermute(value, ('seq', 'head'), pairs)  9.55 us
    ppermute x3, waiting for transfers between devices, neighbour(): return lax.ppermute(value, ('seq', 'head'), pairs)  6.31 us
    pallas_call x1, Pallas kernels, halo_shards(): call(functools.partial(lead_kernel, prior, step), 'lead_rows', [inside] *...  3.06 us
    pallas_call x1, Pallas kernels, halo_shards(): call(functools.partial(own_kernel, prior, step), 'own_block', [inside] *...  2.2 us
    pallas_call x1, Pallas kernels, halo_shards(): call(functools.partial(ready_kernel, prior), 'operands', [anywhere] * 5,...  1.68 us
    pallas_call x1, Pallas kernels, halo_shards(): call(functools.partial(tail_kernel, prior, step), 'tail_keys', [inside] *...  1.57 us
    pallas_call x1, Pallas kernels, halo_shards(): call(functools.partial(pack_kernel, prior), 'near_keys', [anywhere] * 2,...  0.99 us
    pallas_call x1, Pallas kernels, halo_shards(): call(functools.partial(near_kernel, prior), 'near_terms', [inside] * 7, i...  0.73 us
  transfers between devices with their start and end apart: 3, of which 3 were waited for; matrix products, arithmetic and copies ran while one was open for 0% of the time, Pallas kernels for 29%

profile of v13, /device:TPU:0, one launch (start us, length us, event | category | flops | bytes accessed | tf_op | source)
XLA Modules:
  0.0 26.8 jit_solution(3063742505971648019)
XLA Ops:
  0.6 1.0 %near_keys.1 = bf16[64,2048]{1,0:T(8,128)(2,1)S(1)} custom-call(bf16[128,2048]{1,0:T(8,128)(2,1)} %k_ref.1, bf16[128,2048]{1,0:T(8,128)(2,1)} %v_ref.1), custom_call_target="tpu_custom_call" | custom-call | bytes 524288 | tf_op jit(solution)/shard_map/near_keys/pallas_call | solution.py:526
  1.6 4.9 %collective-permute-start = (bf16[64,2048]{1,0:T(8,128)(2,1)S(1)}, bf16[64,2048]{1,0:T(8,128)(2,1)S(1)}, u32[]{:S(2)}, u32[]{:S(2)}) collective-permute-start(bf16[64,2048]{1,0:T(8,128)(2,1)S(1)} %near_keys.1), channel_id=1, source_target_pairs={{0,1},{1,2},{2,3},{3,4},{4,5},{5,6},{6,7},{7,8},{8,9},{9,10},{10,1... | collective-permute-start | bytes 786440 | tf_op jit(solution)/shard_map/ppermute | solution.py:481
  6.5 1.7 %operands.1 = (bf16[64,2048]{1,0:T(8,128)(2,1)S(1)}, bf16[128,2048]{1,0:T(8,128)(2,1)S(1)}, bf16[128,2048]{1,0:T(8,128)(2,1)S(1)}, bf16[128,2048]{1,0:T(8,128)(2...) custom-call(s32[1,128]{1,0:T(1,128)} %bitcast.1, ...), custom_call_target="tpu_custom_call" | custom-call | bytes 4718592 | tf_op jit(solution)/shard_map/operands/pallas_call | solution.py:534
  8.2 3.4 %collective-permute-start.1 = (bf16[64,2048]{1,0:T(8,128)(2,1)S(1)}, bf16[64,2048]{1,0:T(8,128)(2,1)S(1)}, u32[]{:S(2)}, u32[]{:S(2)}) collective-permute-start(bf16[64,2048]{1,0:T(8,128)(2,1)S(1)} %get-tuple-element.30), channel_id=1, source_target_pairs={{0,1},{1,2},{2,3},{3,4},{4,5},{5,6},{6,7},{7,8},{8,9},{9,10},{10,1... | collective-permute-start | bytes 786440 | tf_op jit(solution)/shard_map/ppermute | solution.py:481
  11.6 1.2 %collective-permute-done.near_ref = bf16[64,2048]{1,0:T(8,128)(2,1)S(1)} collective-permute-done((bf16[64,2048]{1,0:T(8,128)(2,1)S(1)}, bf16[64,2048]{1,0:T(8,128)(2,1)S(1)}, u32[]{:S(2)}, u32[]{:S(2)}) %collective-permute-start) | collective-permute-done | bytes 262176 | tf_op jit(solution)/shard_map/ppermute | solution.py:481
  12.8 0.7 %near_terms.1 = bf16[64,2048]{1,0:T(8,128)(2,1)S(1)} custom-call(f32[96,128]{1,0:T(8,128)S(1)} %get-tuple-element.32.near_bias_ref, f32[64,128]{1,0:T(8,128)S(1)} %get-tuple-element.25.lead_bias_ref.bias_ref, bf16[128,2048]{1,0:T(8,128)(2,1)S(1)} %get-tuple-element.26.q_ref, bf16[128,2048]{1,0:T(8,128)(2,1)S(1)} %get-tuple-element.27.k_ref, ...), custom_call_target="tpu_custom_call" | custom-call | flops 75497472 | bytes 2097152 | tf_op jit(solution)/shard_map/near_terms/pallas_call | solution.py:548
  13.5 1.3 %collective-permute-start.2 = (bf16[64,2048]{1,0:T(8,128)(2,1)S(1)}, bf16[64,2048]{1,0:T(8,128)(2,1)S(1)}, u32[]{:S(2)}, u32[]{:S(2)}) collective-permute-start(bf16[64,2048]{1,0:T(8,128)(2,1)S(1)} %near_terms.1), channel_id=1, source_target_pairs={{1,0},{2,1},{3,2},{4,3},{5,4},{6,5},{7,6},{8,7},{9,8},{10,9},{11,1... | collective-permute-start | bytes 786440 | tf_op jit(solution)/shard_map/ppermute | solution.py:481
  14.8 2.2 %own_block.1 = (bf16[64,2048]{1,0:T(8,128)(2,1)S(1)}, bf16[64,2048]{1,0:T(8,128)(2,1)S(1)}, f32[128,2048]{1,0:T(8,128)S(1)}, f32[128,2048]{1,0:T(8,128)S(1)}) custom-call(f32[64,128]{1,0:T(8,128)S(1)} %get-tuple-element.33.bias_ref, bf16[128,2048]{1,0:T(8,128)(2,1)S(1)} %get-tuple-element.26.q_ref, bf16[128,2048]{1,0:T(8,128)(2,1)S(1)} %get-tuple-element.27.k_ref, ...), custom_call_target="tpu_custom_call" | custom-call | flops 201326592 | bytes 4718592 | tf_op jit(solution)/shard_map/own_block/pallas_call | solution.py:556
  17.0 0.6 %collective-permute-done.1.far_ref = bf16[64,2048]{1,0:T(8,128)(2,1)S(1)} collective-permute-done((bf16[64,2048]{1,0:T(8,128)(2,1)S(1)}, bf16[64,2048]{1,0:T(8,128)(2,1)S(1)}, u32[]{:S(2)}, u32[]{:S(2)}) %collective-permute-start.1) | collective-permute-done | bytes 262176 | tf_op jit(solution)/shard_map/ppermute | solution.py:481
  17.6 3.1 %lead_rows.1 = (bf16[128,2048]{1,0:T(8,128)(2,1)}, bf16[128,2048]{1,0:T(8,128)(2,1)}, bf16[128,2048]{1,0:T(8,128)(2,1)}, bf16[128,2048]{1,0:T(8,128)(2,1)}) custom-call(f32[64,128]{1,0:T(8,128)S(1)} %get-tuple-element.25.lead_bias_ref.bias_ref, bf16[128,2048]{1,0:T(8,128)(2,1)S(1)} %get-tuple-element.26.q_ref, ...), custom_call_target="tpu_custom_call" | custom-call | flops 201326592 | bytes 5242880 | tf_op jit(solution)/shard_map/lead_rows/pallas_call | solution.py:563
  20.7 4.5 %collective-permute-done.2.after_ref = bf16[64,2048]{1,0:T(8,128)(2,1)S(1)} collective-permute-done((bf16[64,2048]{1,0:T(8,128)(2,1)S(1)}, bf16[64,2048]{1,0:T(8,128)(2,1)S(1)}, u32[]{:S(2)}, u32[]{:S(2)}) %collective-permute-start.2) | collective-permute-done | bytes 262176 | tf_op jit(solution)/shard_map/ppermute | solution.py:481
  25.2 1.6 %tail_keys.1 = (bf16[128,2048]{1,0:T(8,128)(2,1)}, bf16[128,2048]{1,0:T(8,128)(2,1)}) custom-call(f32[64,128]{1,0:T(8,128)S(1)} %get-tuple-element.40.bias_ref, bf16[128,2048]{1,0:T(8,128)(2,1)S(1)} %get-tuple-element.27.k_ref, bf16[128,2048]{1,0:T(8,128)(2,1)S(1)} %get-tuple-element.28.v_ref, ...), custom_call_target="tpu_custom_call", output_to_operand_aliasing={{0}: (6, {}), {1}: (7, {})} | custom-call | flops 33554432 | bytes 2621440 | tf_op jit(solution)/shard_map/tail_keys/pallas_call | solution.py:571
Async XLA Ops:
  1.6 11.1 %collective-permute-start = (bf16[64,2048]{1,0:T(8,128)(2,1)S(1)}, bf16[64,2048]{1,0:T(8,128)(2,1)S(1)}, u32[]{:S(2)}, u32[]{:S(2)}) collective-permute-start(bf16[64,2048]{1,0:T(8,128)(2,1)S(1)} %near_keys.1), channel_id=1, source_target_pairs={{0,1},{1,2},{2,3},{3,4},{4,5},{5,6},{6,7},{7,8},{8,9},{9,10},{10,1... | collective-permute-start | bytes 786440 | tf_op jit(solution)/shard_map/ppermute | solution.py:481
  8.2 9.5 %collective-permute-start.1 = (bf16[64,2048]{1,0:T(8,128)(2,1)S(1)}, bf16[64,2048]{1,0:T(8,128)(2,1)S(1)}, u32[]{:S(2)}, u32[]{:S(2)}) collective-permute-start(bf16[64,2048]{1,0:T(8,128)(2,1)S(1)} %get-tuple-element.30), channel_id=1, source_target_pairs={{0,1},{1,2},{2,3},{3,4},{4,5},{5,6},{6,7},{7,8},{8,9},{9,10},{10,1... | collective-permute-start | bytes 786440 | tf_op jit(solution)/shard_map/ppermute | solution.py:481
  13.5 11.7 %collective-permute-start.2 = (bf16[64,2048]{1,0:T(8,128)(2,1)S(1)}, bf16[64,2048]{1,0:T(8,128)(2,1)S(1)}, u32[]{:S(2)}, u32[]{:S(2)}) collective-permute-start(bf16[64,2048]{1,0:T(8,128)(2,1)S(1)} %near_terms.1), channel_id=1, source_target_pairs={{1,0},{2,1},{3,2},{4,3},{5,4},{6,5},{7,6},{8,7},{9,8},{10,9},{11,1... | collective-permute-start | bytes 786440 | tf_op jit(solution)/shard_map/ppermute | solution.py:481

commit v14 on v13

--- a/solution.py
+++ b/solution.py
@@ -277,8 +277,9 @@
     ]
 
 
-def pack_kernel(prior, k_ref, v_ref, near_ref, sems):
-    copies = pack_copies(prior, 0, k_ref, v_ref, near_ref, sems)
+def pack_kernel(prior, k_ref, v_ref, near_ref, far_ref, near_sems, far_sems):
+    copies = pack_copies(prior, 0, k_ref, v_ref, near_ref, near_sems)
+    copies += pack_copies(prior, 1, k_ref, v_ref, far_ref, far_sems)
     for copy in copies:
         copy.start()
     for copy in copies:
@@ -286,13 +287,12 @@
 
 
 def ready_kernel(
-    prior, len_hbm, q_hbm, k_hbm, v_hbm, do_hbm, far_ref, q_ref, k_ref, v_ref, do_ref,
-    own_bias_ref, near_bias_ref, lead_bias_ref, tail_bias_ref, len_ref, sems, far_sems, len_sem,
+    prior, len_hbm, q_hbm, k_hbm, v_hbm, do_hbm, q_ref, k_ref, v_ref, do_ref,
+    own_bias_ref, near_bias_ref, lead_bias_ref, tail_bias_ref, len_ref, sems, len_sem,
 ):
     tok, half = k_ref.shape[0], prior // 2
     pairs = ((q_hbm, q_ref), (k_hbm, k_ref), (v_hbm, v_ref), (do_hbm, do_ref))
-    copies = pack_copies(prior, 1, k_hbm, v_hbm, far_ref, far_sems)
-    copies += [pltpu.make_async_copy(hbm, ref, sems.at[n]) for n, (hbm, ref) in enumerate(pairs)]
+    copies = [pltpu.make_async_copy(hbm, ref, sems.at[n]) for n, (hbm, ref) in enumerate(pairs)]
     len_copy = pltpu.make_async_copy(len_hbm, len_ref, len_sem)
     len_copy.start()
     for copy in copies:
@@ -523,35 +523,26 @@
             name=name,
         )
 
-    near = call(
-        functools.partial(pack_kernel, prior), "near_keys",
-        [anywhere] * 2, inside, near16(prior, width),
-        [pltpu.SemaphoreType.DMA((2,))], (0, 0, 0, 0), 4 * prior * width,
+    near, far = call(
+        functools.partial(pack_kernel, prior), "late_keys",
+        [anywhere] * 2, [inside] * 2, [near16(prior, width)] * 2,
+        [pltpu.SemaphoreType.DMA((2,))] * 2, (0, 0, 0, 0), 8 * prior * width,
     )(*in_hbm(key_in, value_in))
-    near = neighbour(near, 1)
+    near, far = neighbour(near, 1), neighbour(far, 1)
 
     lengths = module_lengths.reshape(1, -1)
-    far, q, k, v, do, own_bias, near_bias, lead_bias, tail_bias = call(
+    q, k, v, do, own_bias, near_bias, lead_bias, tail_bias = call(
         functools.partial(ready_kernel, prior), "operands",
-        [anywhere] * 5, [inside] * 9,
-        [near16(prior, width)] + [near16(tok, width)] * 4
+        [anywhere] * 5, [inside] * 8,
+        [near16(tok, width)] * 4
         + [near32(tok - prior, tok), near32(prior + prior // 2, 2 * prior)]
         + [near32(prior, 2 * prior), near32(prior, 2 * prior)],
         [
             pltpu.VMEM(lengths.shape, jnp.int32), pltpu.SemaphoreType.DMA((4,)),
-            pltpu.SemaphoreType.DMA((2,)), pltpu.SemaphoreType.DMA(()),
+            pltpu.SemaphoreType.DMA(()),
         ],
-        (0, 0, 0, 0), 18 * tok * width,
+        (0, 0, 0, 0), 16 * tok * width,
     )(*in_hbm(lengths, query_in, key_in, value_in, grad_out))
-    far = neighbour(far, 1)
-
-    back = call(
-        functools.partial(near_kernel, prior), "near_terms",
-        [inside] * 7, inside, near16(prior, width), (),
-        (width // HEAD_DIM, prior, prior + prior // 2, 3), 8 * tok * width,
-    )(*in_vmem(near_bias, lead_bias, q, k, v, do, near))
-    own_bias, back = lax.optimization_barrier((own_bias, back))
-    back = neighbour(back, -1)
 
     attn, gq, gk_part, gv_part = call(
         functools.partial(own_kernel, prior, step), "own_block",
@@ -559,6 +550,14 @@
         [near16(tok - prior, width)] * 2 + [near32(tok, width)] * 2, (),
         (width // HEAD_DIM, tok - prior, tok, 6), 18 * tok * width,
     )(*in_vmem(own_bias, q, k, v, do))
+    near_bias, attn = lax.optimization_barrier((near_bias, attn))
+
+    back = call(
+        functools.partial(near_kernel, prior), "near_terms",
+        [inside] * 7, inside, near16(prior, width), (),
+        (width // HEAD_DIM, prior, prior + prior // 2, 3), 8 * tok * width,
+    )(*in_vmem(near_bias, lead_bias, q, k, v, do, near))
+    back = neighbour(back, -1)
 
     attn, gq, gk, gv = call(
         functools.partial(lead_kernel, prior, step), "lead_rows",

time: 27 us -> 27.3 us (1.011)
  transfers between devices with their start and end apart: 3 -> 3, of which waited for: 3 -> 2; matrix products, arithmetic and copies ran while one was open for 0% -> 0% of each run, Pallas kernels for 29% -> 28%
where the time goes in v14:
time: 27.3 us; the launch traced here: 26.9 us
  Pallas kernels  10.3 us (38%)
  starting transfers between devices  9.55 us (35%)
  waiting for transfers between devices  6.4 us (23%)
  between operations  0.69 us (3%)
    ppermute x3, starting transfers between devices, neighbour(): return lax.ppermute(value, ('seq', 'head'), pairs)  9.55 us
    ppermute x3, waiting for transfers between devices, neighbour(): return lax.ppermute(value, ('seq', 'head'), pairs)  6.4 us
    pallas_call x1, Pallas kernels, halo_shards(): call(functools.partial(lead_kernel, prior, step), 'lead_rows', [inside] *...  3.06 us
    pallas_call x1, Pallas kernels, halo_shards(): call(functools.partial(own_kernel, prior, step), 'own_block', [inside] *...  2.2 us
    pallas_call x1, Pallas kernels, halo_shards(): call(functools.partial(ready_kernel, prior), 'operands', [anywhere] * 5,...  1.58 us
    pallas_call x1, Pallas kernels, halo_shards(): call(functools.partial(tail_kernel, prior, step), 'tail_keys', [inside] *...  1.57 us
    pallas_call x1, Pallas kernels, halo_shards(): call(functools.partial(pack_kernel, prior), 'late_keys', [anywhere] * 2,...  1.13 us
    pallas_call x1, Pallas kernels, halo_shards(): call(functools.partial(near_kernel, prior), 'near_terms', [inside] * 7, i...  0.73 us
  transfers between devices with their start and end apart: 3, of which 2 were waited for; matrix products, arithmetic and copies ran while one was open for 0% of the time, Pallas kernels for 28%

profile of v14, /device:TPU:0, one launch (start us, length us, event | category | flops | bytes accessed | tf_op | source)
XLA Modules:
  0.0 26.9 jit_solution(15736016112997293222)
XLA Ops:
  0.6 1.1 %late_keys.1 = (bf16[64,2048]{1,0:T(8,128)(2,1)S(1)}, bf16[64,2048]{1,0:T(8,128)(2,1)S(1)}) custom-call(bf16[128,2048]{1,0:T(8,128)(2,1)} %k_ref.1, bf16[128,2048]{1,0:T(8,128)(2,1)} %v_ref.1), custom_call_target="tpu_custom_call" | custom-call | bytes 1048576 | tf_op jit(solution)/shard_map/late_keys/pallas_call | solution.py:526
  1.8 4.9 %collective-permute-start = (bf16[64,2048]{1,0:T(8,128)(2,1)S(1)}, bf16[64,2048]{1,0:T(8,128)(2,1)S(1)}, u32[]{:S(2)}, u32[]{:S(2)}) collective-permute-start(bf16[64,2048]{1,0:T(8,128)(2,1)S(1)} %get-tuple-element.31), channel_id=1, source_target_pairs={{0,1},{1,2},{2,3},{3,4},{4,5},{5,6},{6,7},{7,8},{8,9},{9,10},{10,1... | collective-permute-start | bytes 786440 | tf_op jit(solution)/shard_map/ppermute | solution.py:481
  6.6 3.4 %collective-permute-start.1 = (bf16[64,2048]{1,0:T(8,128)(2,1)S(1)}, bf16[64,2048]{1,0:T(8,128)(2,1)S(1)}, u32[]{:S(2)}, u32[]{:S(2)}) collective-permute-start(bf16[64,2048]{1,0:T(8,128)(2,1)S(1)} %get-tuple-element.32), channel_id=1, source_target_pairs={{0,1},{1,2},{2,3},{3,4},{4,5},{5,6},{6,7},{7,8},{8,9},{9,10},{10,1... | collective-permute-start | bytes 786440 | tf_op jit(solution)/shard_map/ppermute | solution.py:481
  10.0 1.6 %operands.1 = (bf16[128,2048]{1,0:T(8,128)(2,1)S(1)}, bf16[128,2048]{1,0:T(8,128)(2,1)S(1)}, bf16[128,2048]{1,0:T(8,128)(2,1)S(1)}, bf16[128,2048]{1,0:T(8,128)(...) custom-call(s32[1,128]{1,0:T(1,128)} %bitcast.1, ...), custom_call_target="tpu_custom_call" | custom-call | bytes 4194304 | tf_op jit(solution)/shard_map/operands/pallas_call | solution.py:534
  11.6 2.2 %own_block.1 = (bf16[64,2048]{1,0:T(8,128)(2,1)S(1)}, bf16[64,2048]{1,0:T(8,128)(2,1)S(1)}, f32[128,2048]{1,0:T(8,128)S(1)}, f32[128,2048]{1,0:T(8,128)S(1)}) custom-call(f32[64,128]{1,0:T(8,128)S(1)} %get-tuple-element.33.bias_ref, bf16[128,2048]{1,0:T(8,128)(2,1)S(1)} %get-tuple-element.27.q_ref, bf16[128,2048]{1,0:T(8,128)(2,1)S(1)} %get-tuple-element.28.k_ref, ...), custom_call_target="tpu_custom_call" | custom-call | flops 201326592 | bytes 4718592 | tf_op jit(solution)/shard_map/own_block/pallas_call | solution.py:547
  13.8 0.0 collective-permute-done.near_ref
  13.8 0.7 %near_terms.1 = bf16[64,2048]{1,0:T(8,128)(2,1)S(1)} custom-call(f32[96,128]{1,0:T(8,128)S(1)} %get-tuple-element.43.near_bias_ref, f32[64,128]{1,0:T(8,128)S(1)} %get-tuple-element.26.bias_ref.lead_bias_ref, bf16[128,2048]{1,0:T(8,128)(2,1)S(1)} %get-tuple-element.27.q_ref, bf16[128,2048]{1,0:T(8,128)(2,1)S(1)} %get-tuple-element.28.k_ref, ...), custom_call_target="tpu_custom_call" | custom-call | flops 75497472 | bytes 2097152 | tf_op jit(solution)/shard_map/near_terms/pallas_call | solution.py:555
  14.6 1.3 %collective-permute-start.2 = (bf16[64,2048]{1,0:T(8,128)(2,1)S(1)}, bf16[64,2048]{1,0:T(8,128)(2,1)S(1)}, u32[]{:S(2)}, u32[]{:S(2)}) collective-permute-start(bf16[64,2048]{1,0:T(8,128)(2,1)S(1)} %near_terms.1), channel_id=1, source_target_pairs={{1,0},{2,1},{3,2},{4,3},{5,4},{6,5},{7,6},{8,7},{9,8},{10,9},{11,1... | collective-permute-start | bytes 786440 | tf_op jit(solution)/shard_map/ppermute | solution.py:481
  15.9 1.9 %collective-permute-done.1.far_ref = bf16[64,2048]{1,0:T(8,128)(2,1)S(1)} collective-permute-done((bf16[64,2048]{1,0:T(8,128)(2,1)S(1)}, bf16[64,2048]{1,0:T(8,128)(2,1)S(1)}, u32[]{:S(2)}, u32[]{:S(2)}) %collective-permute-start.1) | collective-permute-done | bytes 262176 | tf_op jit(solution)/shard_map/ppermute | solution.py:481
  17.8 3.1 %lead_rows.1 = (bf16[128,2048]{1,0:T(8,128)(2,1)}, bf16[128,2048]{1,0:T(8,128)(2,1)}, bf16[128,2048]{1,0:T(8,128)(2,1)}, bf16[128,2048]{1,0:T(8,128)(2,1)}) custom-call(f32[64,128]{1,0:T(8,128)S(1)} %get-tuple-element.26.bias_ref.lead_bias_ref, bf16[128,2048]{1,0:T(8,128)(2,1)S(1)} %get-tuple-element.27.q_ref, ...), custom_call_target="tpu_custom_call" | custom-call | flops 201326592 | bytes 5242880 | tf_op jit(solution)/shard_map/lead_rows/pallas_call | solution.py:562
  20.9 4.5 %collective-permute-done.2.after_ref = bf16[64,2048]{1,0:T(8,128)(2,1)S(1)} collective-permute-done((bf16[64,2048]{1,0:T(8,128)(2,1)S(1)}, bf16[64,2048]{1,0:T(8,128)(2,1)S(1)}, u32[]{:S(2)}, u32[]{:S(2)}) %collective-permute-start.2) | collective-permute-done | bytes 262176 | tf_op jit(solution)/shard_map/ppermute | solution.py:481
  25.3 1.6 %tail_keys.1 = (bf16[128,2048]{1,0:T(8,128)(2,1)}, bf16[128,2048]{1,0:T(8,128)(2,1)}) custom-call(f32[64,128]{1,0:T(8,128)S(1)} %get-tuple-element.42.bias_ref, bf16[128,2048]{1,0:T(8,128)(2,1)S(1)} %get-tuple-element.28.k_ref, bf16[128,2048]{1,0:T(8,128)(2,1)S(1)} %get-tuple-element.29.v_ref, ...), custom_call_target="tpu_custom_call", output_to_operand_aliasing={{0}: (6, {}), {1}: (7, {})} | custom-call | flops 33554432 | bytes 2621440 | tf_op jit(solution)/shard_map/tail_keys/pallas_call | solution.py:570
Async XLA Ops:
  1.8 12.1 %collective-permute-start = (bf16[64,2048]{1,0:T(8,128)(2,1)S(1)}, bf16[64,2048]{1,0:T(8,128)(2,1)S(1)}, u32[]{:S(2)}, u32[]{:S(2)}) collective-permute-start(bf16[64,2048]{1,0:T(8,128)(2,1)S(1)} %get-tuple-element.31), channel_id=1, source_target_pairs={{0,1},{1,2},{2,3},{3,4},{4,5},{5,6},{6,7},{7,8},{8,9},{9,10},{10,1... | collective-permute-start | bytes 786440 | tf_op jit(solution)/shard_map/ppermute | solution.py:481
  6.6 11.1 %collective-permute-start.1 = (bf16[64,2048]{1,0:T(8,128)(2,1)S(1)}, bf16[64,2048]{1,0:T(8,128)(2,1)S(1)}, u32[]{:S(2)}, u32[]{:S(2)}) collective-permute-start(bf16[64,2048]{1,0:T(8,128)(2,1)S(1)} %get-tuple-element.32), channel_id=1, source_target_pairs={{0,1},{1,2},{2,3},{3,4},{4,5},{5,6},{6,7},{7,8},{8,9},{9,10},{10,1... | collective-permute-start | bytes 786440 | tf_op jit(solution)/shard_map/ppermute | solution.py:481
  14.6 10.8 %collective-permute-start.2 = (bf16[64,2048]{1,0:T(8,128)(2,1)S(1)}, bf16[64,2048]{1,0:T(8,128)(2,1)S(1)}, u32[]{:S(2)}, u32[]{:S(2)}) collective-permute-start(bf16[64,2048]{1,0:T(8,128)(2,1)S(1)} %near_terms.1), channel_id=1, source_target_pairs={{1,0},{2,1},{3,2},{4,3},{5,4},{6,5},{7,6},{8,7},{9,8},{10,9},{11,1... | collective-permute-start | bytes 786440 | tf_op jit(solution)/shard_map/ppermute | solution.py:481

commit v15 on v13

--- a/solution.py
+++ b/solution.py
@@ -433,7 +433,7 @@
 
 
 def tail_kernel(
-    prior, step, bias_ref, k_ref, v_ref, after_ref, gk_part_ref, gv_part_ref, gk_in, gv_in,
+    prior, bias_ref, k_ref, v_ref, after_ref, gk_part_ref, gv_part_ref, gk_in, gv_in,
     gk_hbm, gv_hbm, gk_ref, gv_ref, sems,
 ):
     tok, width = k_ref.shape
@@ -441,36 +441,34 @@
     far = bias_ref[half - 1 : half, 0:1] == 0.0
     bias = jnp.where(far, bias_ref[...], MASKED)
     first, second, last = slice(0, half), slice(half, prior), slice(tok - prior, tok)
+    columns = head_columns(0, width, 4)
+    queries = [side_by_side(after_ref[first, c]) for c in columns]
+    cotangents = [side_by_side(after_ref[second, c]) for c in columns]
+    pairs = [
+        by_query(k_ref[last, c], q, v_ref[last, c], do, bias)
+        for c, q, do in zip(columns, queries, cotangents)
+    ]
+    own = [
+        (joined(after_ref[half - 1 : half, c]), joined(after_ref[prior - 1 : prior, c]))
+        for c in columns
+    ]
+    weights, grads = merged_columns(pairs, own)
     copies = []
-    for low in range(0, width, step):
-        columns = head_columns(low, low + step, 4)
-        queries = [side_by_side(after_ref[first, c]) for c in columns]
-        cotangents = [side_by_side(after_ref[second, c]) for c in columns]
-        pairs = [
-            by_query(k_ref[last, c], q, v_ref[last, c], do, bias)
-            for c, q, do in zip(columns, queries, cotangents)
-        ]
-        own = [
-            (joined(after_ref[half - 1 : half, c]), joined(after_ref[prior - 1 : prior, c]))
-            for c in columns
-        ]
-        weights, grads = merged_columns(pairs, own)
-        for c, w, g, q, do in zip(columns, weights, grads, queries, cotangents):
-            for out_ref, part_ref, left, right, rows in (
-                (gk_ref, gk_part_ref, g, q, first), (gv_ref, gv_part_ref, w, do, second)
-            ):
-                total = part_ref[last, c] + dot(left, right, 1, 0)
-                terms = jnp.where(far, 0.0, after_ref[rows, c].astype(jnp.float32))
-                out_ref[first, c] = total[first].astype(jnp.bfloat16)
-                out_ref[second, c] = (total[second] + terms).astype(jnp.bfloat16)
-        cols = pl.ds(low, step)
-        for ref, hbm in ((gk_ref, gk_hbm), (gv_ref, gv_hbm)):
-            copies.append(
-                pltpu.make_async_copy(
-                    ref.at[:, cols], hbm.at[pl.ds(tok - prior, prior), cols], sems.at[len(copies)]
-                )
-            )
-            copies[-1].start()
+    for at, (ref, hbm, part_ref, lefts, rights, rows) in enumerate(
+        (
+            (gv_ref, gv_hbm, gv_part_ref, weights, cotangents, second),
+            (gk_ref, gk_hbm, gk_part_ref, grads, queries, first),
+        )
+    ):
+        for c, left, right in zip(columns, lefts, rights):
+            total = part_ref[last, c] + dot(left, right, 1, 0)
+            terms = jnp.where(far, 0.0, after_ref[rows, c].astype(jnp.float32))
+            ref[first, c] = total[first].astype(jnp.bfloat16)
+            ref[second, c] = (total[second] + terms).astype(jnp.bfloat16)
+        copies.append(
+            pltpu.make_async_copy(ref, hbm.at[pl.ds(tok - prior, prior), :], sems.at[at])
+        )
+        copies[-1].start()
     for copy in copies:
         copy.wait()
 
@@ -569,9 +567,9 @@
     )(*in_vmem(lead_bias, q, k, v, do, near, far, gk_part, gv_part, attn, gq))
 
     gk, gv = call(
-        functools.partial(tail_kernel, prior, step), "tail_keys",
+        functools.partial(tail_kernel, prior), "tail_keys",
         [inside] * 6 + [anywhere] * 2, [anywhere] * 2, [full16] * 2,
-        [near16(prior, width)] * 2 + [pltpu.SemaphoreType.DMA((2 * groups,))],
+        [near16(prior, width)] * 2 + [pltpu.SemaphoreType.DMA((2,))],
         (width // HEAD_DIM, prior, prior // 2, 4), 10 * tok * width, {6: 0, 7: 1},
     )(*in_vmem(tail_bias, k, v, back, gk_part, gv_part), gk, gv)
     return (attn, gq, gk, gv)

time: 27 us -> 26.8 us (level)
  no operation moved by 1% of the time
where the time goes in v15:
time: 26.8 us; the launch traced here: 26.6 us
  Pallas kernels  10.1 us (38%)
  starting transfers between devices  9.55 us (36%)
  waiting for transfers between devices  6.31 us (24%)
  between operations  0.68 us (3%)
    ppermute x3, starting transfers between devices, neighbour(): return lax.ppermute(value, ('seq', 'head'), pairs)  9.55 us
    ppermute x3, waiting for transfers between devices, neighbour(): return lax.ppermute(value, ('seq', 'head'), pairs)  6.31 us
    pallas_call x1, Pallas kernels, halo_shards(): call(functools.partial(lead_kernel, prior, step), 'lead_rows', [inside] *...  3.06 us
    pallas_call x1, Pallas kernels, halo_shards(): call(functools.partial(own_kernel, prior, step), 'own_block', [inside] *...  2.2 us
    pallas_call x1, Pallas kernels, halo_shards(): call(functools.partial(ready_kernel, prior), 'operands', [anywhere] * 5,...  1.68 us
    pallas_call x1, Pallas kernels, halo_shards(): call(functools.partial(tail_kernel, prior), 'tail_keys', [inside] * 6 + [...  1.42 us
    pallas_call x1, Pallas kernels, halo_shards(): call(functools.partial(pack_kernel, prior), 'near_keys', [anywhere] * 2,...  0.99 us
    pallas_call x1, Pallas kernels, halo_shards(): call(functools.partial(near_kernel, prior), 'near_terms', [inside] * 7, i...  0.73 us
  transfers between devices with their start and end apart: 3, of which 3 were waited for; matrix products, arithmetic and copies ran while one was open for 0% of the time, Pallas kernels for 29%

profile of v15, /device:TPU:0, one launch (start us, length us, event | category | flops | bytes accessed | tf_op | source)
XLA Modules:
  0.0 26.6 jit_solution(7963963580880261162)
XLA Ops:
  0.6 1.0 %near_keys.1 = bf16[64,2048]{1,0:T(8,128)(2,1)S(1)} custom-call(bf16[128,2048]{1,0:T(8,128)(2,1)} %k_ref.1, bf16[128,2048]{1,0:T(8,128)(2,1)} %v_ref.1), custom_call_target="tpu_custom_call" | custom-call | bytes 524288 | tf_op jit(solution)/shard_map/near_keys/pallas_call | solution.py:524
  1.6 4.9 %collective-permute-start = (bf16[64,2048]{1,0:T(8,128)(2,1)S(1)}, bf16[64,2048]{1,0:T(8,128)(2,1)S(1)}, u32[]{:S(2)}, u32[]{:S(2)}) collective-permute-start(bf16[64,2048]{1,0:T(8,128)(2,1)S(1)} %near_keys.1), channel_id=1, source_target_pairs={{0,1},{1,2},{2,3},{3,4},{4,5},{5,6},{6,7},{7,8},{8,9},{9,10},{10,1... | collective-permute-start | bytes 786440 | tf_op jit(solution)/shard_map/ppermute | solution.py:479
  6.5 1.7 %operands.1 = (bf16[64,2048]{1,0:T(8,128)(2,1)S(1)}, bf16[128,2048]{1,0:T(8,128)(2,1)S(1)}, bf16[128,2048]{1,0:T(8,128)(2,1)S(1)}, bf16[128,2048]{1,0:T(8,128)(2...) custom-call(s32[1,128]{1,0:T(1,128)} %bitcast.1, ...), custom_call_target="tpu_custom_call" | custom-call | bytes 4718592 | tf_op jit(solution)/shard_map/operands/pallas_call | solution.py:532
  8.2 3.4 %collective-permute-start.1 = (bf16[64,2048]{1,0:T(8,128)(2,1)S(1)}, bf16[64,2048]{1,0:T(8,128)(2,1)S(1)}, u32[]{:S(2)}, u32[]{:S(2)}) collective-permute-start(bf16[64,2048]{1,0:T(8,128)(2,1)S(1)} %get-tuple-element.30), channel_id=1, source_target_pairs={{0,1},{1,2},{2,3},{3,4},{4,5},{5,6},{6,7},{7,8},{8,9},{9,10},{10,1... | collective-permute-start | bytes 786440 | tf_op jit(solution)/shard_map/ppermute | solution.py:479
  11.6 1.2 %collective-permute-done.near_ref = bf16[64,2048]{1,0:T(8,128)(2,1)S(1)} collective-permute-done((bf16[64,2048]{1,0:T(8,128)(2,1)S(1)}, bf16[64,2048]{1,0:T(8,128)(2,1)S(1)}, u32[]{:S(2)}, u32[]{:S(2)}) %collective-permute-start) | collective-permute-done | bytes 262176 | tf_op jit(solution)/shard_map/ppermute | solution.py:479
  12.8 0.7 %near_terms.1 = bf16[64,2048]{1,0:T(8,128)(2,1)S(1)} custom-call(f32[96,128]{1,0:T(8,128)S(1)} %get-tuple-element.32.near_bias_ref, f32[64,128]{1,0:T(8,128)S(1)} %get-tuple-element.25.lead_bias_ref.bias_ref, bf16[128,2048]{1,0:T(8,128)(2,1)S(1)} %get-tuple-element.26.q_ref, bf16[128,2048]{1,0:T(8,128)(2,1)S(1)} %get-tuple-element.27.k_ref, ...), custom_call_target="tpu_custom_call" | custom-call | flops 75497472 | bytes 2097152 | tf_op jit(solution)/shard_map/near_terms/pallas_call | solution.py:546
  13.5 1.3 %collective-permute-start.2 = (bf16[64,2048]{1,0:T(8,128)(2,1)S(1)}, bf16[64,2048]{1,0:T(8,128)(2,1)S(1)}, u32[]{:S(2)}, u32[]{:S(2)}) collective-permute-start(bf16[64,2048]{1,0:T(8,128)(2,1)S(1)} %near_terms.1), channel_id=1, source_target_pairs={{1,0},{2,1},{3,2},{4,3},{5,4},{6,5},{7,6},{8,7},{9,8},{10,9},{11,1... | collective-permute-start | bytes 786440 | tf_op jit(solution)/shard_map/ppermute | solution.py:479
  14.8 2.2 %own_block.1 = (bf16[64,2048]{1,0:T(8,128)(2,1)S(1)}, bf16[64,2048]{1,0:T(8,128)(2,1)S(1)}, f32[128,2048]{1,0:T(8,128)S(1)}, f32[128,2048]{1,0:T(8,128)S(1)}) custom-call(f32[64,128]{1,0:T(8,128)S(1)} %get-tuple-element.33.bias_ref, bf16[128,2048]{1,0:T(8,128)(2,1)S(1)} %get-tuple-element.26.q_ref, bf16[128,2048]{1,0:T(8,128)(2,1)S(1)} %get-tuple-element.27.k_ref, ...), custom_call_target="tpu_custom_call" | custom-call | flops 201326592 | bytes 4718592 | tf_op jit(solution)/shard_map/own_block/pallas_call | solution.py:554
  17.0 0.6 %collective-permute-done.1.far_ref = bf16[64,2048]{1,0:T(8,128)(2,1)S(1)} collective-permute-done((bf16[64,2048]{1,0:T(8,128)(2,1)S(1)}, bf16[64,2048]{1,0:T(8,128)(2,1)S(1)}, u32[]{:S(2)}, u32[]{:S(2)}) %collective-permute-start.1) | collective-permute-done | bytes 262176 | tf_op jit(solution)/shard_map/ppermute | solution.py:479
  17.6 3.1 %lead_rows.1 = (bf16[128,2048]{1,0:T(8,128)(2,1)}, bf16[128,2048]{1,0:T(8,128)(2,1)}, bf16[128,2048]{1,0:T(8,128)(2,1)}, bf16[128,2048]{1,0:T(8,128)(2,1)}) custom-call(f32[64,128]{1,0:T(8,128)S(1)} %get-tuple-element.25.lead_bias_ref.bias_ref, bf16[128,2048]{1,0:T(8,128)(2,1)S(1)} %get-tuple-element.26.q_ref, ...), custom_call_target="tpu_custom_call" | custom-call | flops 201326592 | bytes 5242880 | tf_op jit(solution)/shard_map/lead_rows/pallas_call | solution.py:561
  20.7 4.5 %collective-permute-done.2.after_ref = bf16[64,2048]{1,0:T(8,128)(2,1)S(1)} collective-permute-done((bf16[64,2048]{1,0:T(8,128)(2,1)S(1)}, bf16[64,2048]{1,0:T(8,128)(2,1)S(1)}, u32[]{:S(2)}, u32[]{:S(2)}) %collective-permute-start.2) | collective-permute-done | bytes 262176 | tf_op jit(solution)/shard_map/ppermute | solution.py:479
  25.2 1.4 %tail_keys.1 = (bf16[128,2048]{1,0:T(8,128)(2,1)}, bf16[128,2048]{1,0:T(8,128)(2,1)}) custom-call(f32[64,128]{1,0:T(8,128)S(1)} %get-tuple-element.40.bias_ref, bf16[128,2048]{1,0:T(8,128)(2,1)S(1)} %get-tuple-element.27.k_ref, bf16[128,2048]{1,0:T(8,128)(2,1)S(1)} %get-tuple-element.28.v_ref, ...), custom_call_target="tpu_custom_call", output_to_operand_aliasing={{0}: (6, {}), {1}: (7, {})} | custom-call | flops 33554432 | bytes 2621440 | tf_op jit(solution)/shard_map/tail_keys/pallas_call | solution.py:569
Async XLA Ops:
  1.6 11.1 %collective-permute-start = (bf16[64,2048]{1,0:T(8,128)(2,1)S(1)}, bf16[64,2048]{1,0:T(8,128)(2,1)S(1)}, u32[]{:S(2)}, u32[]{:S(2)}) collective-permute-start(bf16[64,2048]{1,0:T(8,128)(2,1)S(1)} %near_keys.1), channel_id=1, source_target_pairs={{0,1},{1,2},{2,3},{3,4},{4,5},{5,6},{6,7},{7,8},{8,9},{9,10},{10,1... | collective-permute-start | bytes 786440 | tf_op jit(solution)/shard_map/ppermute | solution.py:479
  8.2 9.5 %collective-permute-start.1 = (bf16[64,2048]{1,0:T(8,128)(2,1)S(1)}, bf16[64,2048]{1,0:T(8,128)(2,1)S(1)}, u32[]{:S(2)}, u32[]{:S(2)}) collective-permute-start(bf16[64,2048]{1,0:T(8,128)(2,1)S(1)} %get-tuple-element.30), channel_id=1, source_target_pairs={{0,1},{1,2},{2,3},{3,4},{4,5},{5,6},{6,7},{7,8},{8,9},{9,10},{10,1... | collective-permute-start | bytes 786440 | tf_op jit(solution)/shard_map/ppermute | solution.py:479
  13.5 11.7 %collective-permute-start.2 = (bf16[64,2048]{1,0:T(8,128)(2,1)S(1)}, bf16[64,2048]{1,0:T(8,128)(2,1)S(1)}, u32[]{:S(2)}, u32[]{:S(2)}) collective-permute-start(bf16[64,2048]{1,0:T(8,128)(2,1)S(1)} %near_terms.1), channel_id=1, source_target_pairs={{1,0},{2,1},{3,2},{4,3},{5,4},{6,5},{7,6},{8,7},{9,8},{10,9},{11,1... | collective-permute-start | bytes 786440 | tf_op jit(solution)/shard_map/ppermute | solution.py:479

commit v16 on v15

--- a/solution.py
+++ b/solution.py
@@ -147,27 +147,11 @@
     )
 
 
-def module_ends_row(lengths_row):
-    count = lengths_row.shape[1]
-    row = lax.broadcasted_iota(jnp.int32, (count, count), 0)
-    col = lax.broadcasted_iota(jnp.int32, (count, count), 1)
-    lengths_col = jnp.sum(jnp.where(row == col, lengths_row, 0.0), axis=1, keepdims=True)
-    return jnp.sum(jnp.where(row <= col, lengths_col, 0.0), axis=0, keepdims=True)
-
-
 def module_ends_col(lengths_row):
     count = lengths_row.shape[1]
     row = lax.broadcasted_iota(jnp.int32, (count, count), 0)
     col = lax.broadcasted_iota(jnp.int32, (count, count), 1)
     return jnp.sum(jnp.where(col <= row, lengths_row, 0.0), axis=1, keepdims=True)
-
-
-def bias_by_query(lengths_row, first_query, queries, first_key, keys):
-    ends = module_ends_row(lengths_row)
-    query = (first_query + lax.broadcasted_iota(jnp.int32, (queries, 1), 0)).astype(jnp.float32)
-    start = jnp.max(jnp.where(ends <= query, ends, 0.0), axis=1, keepdims=True)
-    key = (first_key + lax.broadcasted_iota(jnp.int32, (queries, keys), 1)).astype(jnp.float32)
-    return jnp.where((key >= start) & (key <= query), 0.0, MASKED)
 
 
 def bias_by_key(lengths_row, first_query, queries, first_key, keys, heads):
@@ -181,18 +165,25 @@
     return jnp.where((key >= start) & (key <= query), 0.0, MASKED)
 
 
-def by_query(q, k, do, v, bias):
-    scores = dot(q, k, 1, 1) * (SCALE * LOG2E) + bias
-    return scores, dot(do, v, 1, 1)
-
-
-def full_rows(pairs):
-    tops = [jnp.max(s, axis=1, keepdims=True) for s, _ in pairs]
+def score_pair(k, q, v, do, bias):
+    return dot(k, q, 1, 1) * (SCALE * LOG2E) + bias, dot(v, do, 1, 1)
+
+
+def softmax_columns(pairs):
+    tops = [jnp.max(s, axis=0, keepdims=True) for s, _ in pairs]
     raws = [jnp.exp2(s - top) for (s, _), top in zip(pairs, tops)]
-    weights = [raw * (1.0 / jnp.sum(raw, axis=1, keepdims=True)) for raw in raws]
-    deltas = [jnp.sum(w * dp, axis=1, keepdims=True) for w, (_, dp) in zip(weights, pairs)]
-    grads = [w * (dp - delta) * SCALE for w, (_, dp), delta in zip(weights, pairs, deltas)]
-    return [w.astype(jnp.bfloat16) for w in weights], [g.astype(jnp.bfloat16) for g in grads]
+    totals = [jnp.sum(raw, axis=0, keepdims=True) for raw in raws]
+    weights = [raw * (1.0 / total) for raw, total in zip(raws, totals)]
+    deltas = [jnp.sum(w * dp, axis=0, keepdims=True) for w, (_, dp) in zip(weights, pairs)]
+    logs = [top + jnp.log2(total) for top, total in zip(tops, totals)]
+    return weights, logs, deltas
+
+
+def score_grads_of(pairs, weights, deltas):
+    return [
+        (w * (dp - delta) * SCALE).astype(jnp.bfloat16)
+        for w, (_, dp), delta in zip(weights, pairs, deltas)
+    ]
 
 
 def merged_columns(pairs, own):
@@ -300,12 +291,22 @@
     len_copy.wait()
     first = device_first(tok)
     lengths = len_ref[...].astype(jnp.float32)
-    own_bias_ref[...] = bias_by_query(lengths, first + prior, tok - prior, first, tok)
+    own_bias_ref[...] = bias_by_key(lengths, first + prior, tok - prior, first, tok, 2)
     near_bias_ref[...] = bias_by_key(lengths, first, prior, first - half, prior + half, 2)
-    lead_bias_ref[...] = bias_by_query(lengths, first, prior, first - prior, 2 * prior)
+    lead_bias_ref[...] = bias_by_key(lengths, first, prior, first - prior, 2 * prior, 2)
     tail_bias_ref[...] = bias_by_key(lengths, first + tok, half, first + tok - prior, prior, 4)
     for copy in copies:
         copy.wait()
+
+
+def own_diagonal(both):
+    rows = both.shape[0] // 2
+    return jnp.concatenate([both[:rows, :HEAD_DIM], both[rows:, HEAD_DIM:]], axis=1)
+
+
+def pair_columns(at, step):
+    wide = 2 * HEAD_DIM
+    return [pl.ds(pl.multiple_of(at * step + c, wide), wide) for c in range(0, step, wide)]
 
 
 def own_kernel(
@@ -317,58 +318,56 @@
     @pl.loop(0, width // step)
     def _(at):
         bias = bias_ref[...]
-        columns = [
-            pl.ds(pl.multiple_of(at * step + c, HEAD_DIM), HEAD_DIM)
-            for c in range(0, step, HEAD_DIM)
+        columns = pair_columns(at, step)
+        queries = [side_by_side(q_ref[late, c]) for c in columns]
+        cotangents = [side_by_side(do_ref[late, c]) for c in columns]
+        pairs = [
+            score_pair(k_ref[:, c], q, v_ref[:, c], do, bias)
+            for c, q, do in zip(columns, queries, cotangents)
         ]
-        pairs = [
-            by_query(q_ref[late, c], k_ref[:, c], do_ref[late, c], v_ref[:, c], bias)
-            for c in columns
-        ]
-        weights, grads = full_rows(pairs)
-        for c, w, g in zip(columns, weights, grads):
-            attn_ref[:, c] = dot(w, v_ref[:, c], 1, 0).astype(jnp.bfloat16)
-            gq_ref[:, c] = dot(g, k_ref[:, c], 1, 0).astype(jnp.bfloat16)
-            gk_ref[:, c] = dot(g, q_ref[late, c], 0, 0)
-            gv_ref[:, c] = dot(w, do_ref[late, c], 0, 0)
+        weights, _, deltas = softmax_columns(pairs)
+        grads = score_grads_of(pairs, weights, deltas)
+        for c, w, g, q, do in zip(columns, weights, grads, queries, cotangents):
+            w = w.astype(jnp.bfloat16)
+            attn_ref[:, c] = own_diagonal(dot(w, v_ref[:, c], 0, 0)).astype(jnp.bfloat16)
+            gq_ref[:, c] = own_diagonal(dot(g, k_ref[:, c], 0, 0)).astype(jnp.bfloat16)
+            gk_ref[:, c] = dot(g, q, 1, 0)
+            gv_ref[:, c] = dot(w, do, 1, 0)
 
 
 def near_kernel(
-    prior, near_bias_ref, lead_bias_ref, q_ref, k_ref, v_ref, do_ref, near_ref, back_ref
+    prior, near_bias_ref, lead_bias_ref, q_ref, k_ref, v_ref, do_ref, near_ref, *back_refs
 ):
-    half = prior // 2
-    far = lead_bias_ref[0:1, half - 1 : half] == 0.0
+    width, half = q_ref.shape[1], prior // 2
+    far = lead_bias_ref[half - 1 : half, 0:1] == 0.0
     key = lax.broadcasted_iota(jnp.int32, (prior + half, 1), 0)
     bias = jnp.where(far & (key < half), MASKED, near_bias_ref[...])
     spare = lax.broadcasted_iota(jnp.int32, (half, 1), 0) == half - 1
     early, first, second = slice(0, prior), slice(0, half), slice(half, prior)
-    columns = head_columns(0, q_ref.shape[1], 2)
+    columns = head_columns(0, width, 2)
     queries = [side_by_side(q_ref[early, c]) for c in columns]
     cotangents = [side_by_side(do_ref[early, c]) for c in columns]
     pairs = []
     for c, q, do in zip(columns, queries, cotangents):
         k = jnp.concatenate([near_ref[first, c], k_ref[early, c]], axis=0)
         v = jnp.concatenate([near_ref[second, c], v_ref[early, c]], axis=0)
-        pairs.append(by_query(k, q, v, do, bias))
-    tops = [jnp.max(s, axis=0, keepdims=True) for s, _ in pairs]
-    raws = [jnp.exp2(s - top) for (s, _), top in zip(pairs, tops)]
-    totals = [jnp.sum(raw, axis=0, keepdims=True) for raw in raws]
-    weights = [raw * (1.0 / total) for raw, total in zip(raws, totals)]
-    deltas = [jnp.sum(w * dp, axis=0, keepdims=True) for w, (_, dp) in zip(weights, pairs)]
-    grads = [
-        w[:half] * (dp[:half] - delta) * SCALE for w, (_, dp), delta in zip(weights, pairs, deltas)
-    ]
-    k_terms = [dot(g.astype(jnp.bfloat16), q, 1, 0) for g, q in zip(grads, queries)]
-    v_terms = [dot(w[:half].astype(jnp.bfloat16), do, 1, 0) for w, do in zip(weights, cotangents)]
-    logs = fours([top + jnp.log2(total) for top, total in zip(tops, totals)])
-    deltas = fours(deltas)
-    for at, c in enumerate(head_columns(0, q_ref.shape[1], 4)):
+        pairs.append(score_pair(k, q, v, do, bias))
+    weights, logs, deltas = softmax_columns(pairs)
+    weights = [w[:half] for w in weights]
+    grads = score_grads_of([(s[:half], dp[:half]) for s, dp in pairs], weights, deltas)
+    k_terms = [dot(g, q, 1, 0) for g, q in zip(grads, queries)]
+    v_terms = [dot(w.astype(jnp.bfloat16), do, 1, 0) for w, do in zip(weights, cotangents)]
+    logs, deltas = fours(logs), fours(deltas)
+    for at, c in enumerate(head_columns(0, width, 4)):
+        back_ref = back_refs[c.start * len(back_refs) // width]
+        low = c.start % back_ref.shape[1]
+        here = slice(low, low + c.stop - c.start)
         for row, terms, ref, place in (
             (logs[at], k_terms, q_ref, first), (deltas[at], v_terms, do_ref, second)
         ):
-            here = jnp.where(spare, split_bf16(row), ref[first, c])
+            rows = jnp.where(spare, split_bf16(row), ref[first, c])
             terms = jnp.concatenate(terms[2 * at : 2 * at + 2], axis=1).astype(jnp.bfloat16)
-            back_ref[place, c] = jnp.where(far, here, terms)
+            back_ref[place, here] = jnp.where(far, rows, terms)
 
 
 def lead_kernel(
@@ -398,10 +397,9 @@
     @pl.loop(0, width // step)
     def _(at):
         bias = bias_ref[...]
-        columns = [
-            pl.ds(pl.multiple_of(at * step + c, HEAD_DIM), HEAD_DIM)
-            for c in range(0, step, HEAD_DIM)
-        ]
+        columns = pair_columns(at, step)
+        queries = [side_by_side(q_ref[early, c]) for c in columns]
+        cotangents = [side_by_side(do_ref[early, c]) for c in columns]
         keys = [
             jnp.concatenate([far_ref[first, c], near_ref[first, c], k_ref[early, c]], axis=0)
             for c in columns
@@ -411,17 +409,19 @@
             for c in columns
         ]
         pairs = [
-            by_query(q_ref[early, c], k, do_ref[early, c], v, bias)
-            for c, k, v in zip(columns, keys, values)
+            score_pair(k, q, v, do, bias)
+            for k, q, v, do in zip(keys, queries, values, cotangents)
         ]
-        weights, grads = full_rows(pairs)
-        for c, w, g, k, v in zip(columns, weights, grads, keys, values):
-            attn_ref[:, c] = dot(w, v, 1, 0).astype(jnp.bfloat16)
-            gq_ref[:, c] = dot(g, k, 1, 0).astype(jnp.bfloat16)
-            gk = dot(g, q_ref[early, c], 0, 0)
-            gv = dot(w, do_ref[early, c], 0, 0)
-            gk_ref[:, c] = (gk_part_ref[early, c] + gk[prior:]).astype(jnp.bfloat16)
-            gv_ref[:, c] = (gv_part_ref[early, c] + gv[prior:]).astype(jnp.bfloat16)
+        weights, _, deltas = softmax_columns(pairs)
+        grads = score_grads_of(pairs, weights, deltas)
+        for n, c in enumerate(columns):
+            w, g = weights[n].astype(jnp.bfloat16), grads[n]
+            attn_ref[:, c] = own_diagonal(dot(w, values[n], 0, 0)).astype(jnp.bfloat16)
+            gq_ref[:, c] = own_diagonal(dot(g, keys[n], 0, 0)).astype(jnp.bfloat16)
+            gk = gk_part_ref[early, c] + dot(g[prior:], queries[n], 1, 0)
+            gv = gv_part_ref[early, c] + dot(w[prior:], cotangents[n], 1, 0)
+            gk_ref[:, c] = gk.astype(jnp.bfloat16)
+            gv_ref[:, c] = gv.astype(jnp.bfloat16)
         for copy in copies(at):
             copy.start()
 
@@ -433,24 +433,25 @@
 
 
 def tail_kernel(
-    prior, bias_ref, k_ref, v_ref, after_ref, gk_part_ref, gv_part_ref, gk_in, gv_in,
+    prior, low, bias_ref, k_ref, v_ref, after_ref, gk_part_ref, gv_part_ref, gk_in, gv_in,
     gk_hbm, gv_hbm, gk_ref, gv_ref, sems,
 ):
-    tok, width = k_ref.shape
+    tok, width = k_ref.shape[0], after_ref.shape[1]
     half = prior // 2
     far = bias_ref[half - 1 : half, 0:1] == 0.0
     bias = jnp.where(far, bias_ref[...], MASKED)
     first, second, last = slice(0, half), slice(half, prior), slice(tok - prior, tok)
-    columns = head_columns(0, width, 4)
-    queries = [side_by_side(after_ref[first, c]) for c in columns]
-    cotangents = [side_by_side(after_ref[second, c]) for c in columns]
+    places = head_columns(0, width, 4)
+    columns = head_columns(low, low + width, 4)
+    queries = [side_by_side(after_ref[first, p]) for p in places]
+    cotangents = [side_by_side(after_ref[second, p]) for p in places]
     pairs = [
-        by_query(k_ref[last, c], q, v_ref[last, c], do, bias)
+        score_pair(k_ref[last, c], q, v_ref[last, c], do, bias)
         for c, q, do in zip(columns, queries, cotangents)
     ]
     own = [
-        (joined(after_ref[half - 1 : half, c]), joined(after_ref[prior - 1 : prior, c]))
-        for c in columns
+        (joined(after_ref[half - 1 : half, p]), joined(after_ref[prior - 1 : prior, p]))
+        for p in places
     ]
     weights, grads = merged_columns(pairs, own)
     copies = []
@@ -460,13 +461,15 @@
             (gk_ref, gk_hbm, gk_part_ref, grads, queries, first),
         )
     ):
-        for c, left, right in zip(columns, lefts, rights):
+        for p, c, left, right in zip(places, columns, lefts, rights):
             total = part_ref[last, c] + dot(left, right, 1, 0)
-            terms = jnp.where(far, 0.0, after_ref[rows, c].astype(jnp.float32))
-            ref[first, c] = total[first].astype(jnp.bfloat16)
-            ref[second, c] = (total[second] + terms).astype(jnp.bfloat16)
+            terms = jnp.where(far, 0.0, after_ref[rows, p].astype(jnp.float32))
+            ref[first, p] = total[first].astype(jnp.bfloat16)
+            ref[second, p] = (total[second] + terms).astype(jnp.bfloat16)
         copies.append(
-            pltpu.make_async_copy(ref, hbm.at[pl.ds(tok - prior, prior), :], sems.at[at])
+            pltpu.make_async_copy(
+                ref, hbm.at[pl.ds(tok - prior, prior), pl.ds(low, width)], sems.at[at]
+            )
         )
         copies[-1].start()
     for copy in copies:
@@ -533,8 +536,8 @@
         functools.partial(ready_kernel, prior), "operands",
         [anywhere] * 5, [inside] * 9,
         [near16(prior, width)] + [near16(tok, width)] * 4
-        + [near32(tok - prior, tok), near32(prior + prior // 2, 2 * prior)]
-        + [near32(prior, 2 * prior), near32(prior, 2 * prior)],
+        + [near32(tok, 2 * prior), near32(prior + prior // 2, 2 * prior)]
+        + [near32(2 * prior, 2 * prior), near32(prior, 2 * prior)],
         [
             pltpu.VMEM(lengths.shape, jnp.int32), pltpu.SemaphoreType.DMA((4,)),
             pltpu.SemaphoreType.DMA((2,)), pltpu.SemaphoreType.DMA(()),
@@ -543,13 +546,13 @@
     )(*in_hbm(lengths, query_in, key_in, value_in, grad_out))
     far = neighbour(far, 1)
 
-    back = call(
+    backs = call(
         functools.partial(near_kernel, prior), "near_terms",
-        [inside] * 7, inside, near16(prior, width), (),
+        [inside] * 7, [inside] * groups, [near16(prior, step)] * groups, (),
         (width // HEAD_DIM, prior, prior + prior // 2, 3), 8 * tok * width,
     )(*in_vmem(near_bias, lead_bias, q, k, v, do, near))
-    own_bias, back = lax.optimization_barrier((own_bias, back))
-    back = neighbour(back, -1)
+    own_bias, *backs = lax.optimization_barrier((own_bias, *backs))
+    backs = [neighbour(back, -1) for back in backs]
 
     attn, gq, gk_part, gv_part = call(
         functools.partial(own_kernel, prior, step), "own_block",
@@ -566,12 +569,13 @@
         (width // HEAD_DIM, prior, 2 * prior, 6), 20 * tok * width,
     )(*in_vmem(lead_bias, q, k, v, do, near, far, gk_part, gv_part, attn, gq))
 
-    gk, gv = call(
-        functools.partial(tail_kernel, prior), "tail_keys",
-        [inside] * 6 + [anywhere] * 2, [anywhere] * 2, [full16] * 2,
-        [near16(prior, width)] * 2 + [pltpu.SemaphoreType.DMA((2,))],
-        (width // HEAD_DIM, prior, prior // 2, 4), 10 * tok * width, {6: 0, 7: 1},
-    )(*in_vmem(tail_bias, k, v, back, gk_part, gv_part), gk, gv)
+    for at, back in enumerate(backs):
+        gk, gv = call(
+            functools.partial(tail_kernel, prior, at * step), "tail_keys",
+            [inside] * 6 + [anywhere] * 2, [anywhere] * 2, [full16] * 2,
+            [near16(prior, step)] * 2 + [pltpu.SemaphoreType.DMA((2,))],
+            (step // HEAD_DIM, prior, prior // 2, 4), 10 * tok * step, {6: 0, 7: 1},
+        )(*in_vmem(tail_bias, k, v, back, gk_part, gv_part), gk, gv)
     return (attn, gq, gk, gv)
 
 

time: 26.8 us -> 28.2 us (1.052)
  the two profiles are of different devices: /device:TPU:0 before, /device:TPU:1 now
where the time goes in v16:
time: 28.2 us; the launch traced here: 27.9 us
  starting transfers between devices  17 us (60%)
  Pallas kernels  9.43 us (33%)
  waiting for transfers between devices  0.75 us (3%)
  between operations  0.72 us (3%)
    ppermute x4, starting transfers between devices, neighbour(): return lax.ppermute(value, ('seq', 'head'), pairs)  17 us
    pallas_call x2, Pallas kernels, halo_shards(): call(functools.partial(tail_kernel, prior, at * step), 'tail_keys', [insi...  2.35 us
    pallas_call x1, Pallas kernels, halo_shards(): call(functools.partial(lead_kernel, prior, step), 'lead_rows', [inside] *...  2.2 us
    pallas_call x1, Pallas kernels, halo_shards(): call(functools.partial(ready_kernel, prior), 'operands', [anywhere] * 5,...  1.68 us
    pallas_call x1, Pallas kernels, halo_shards(): call(functools.partial(own_kernel, prior, step), 'own_block', [inside] *...  1.48 us
    pallas_call x1, Pallas kernels, halo_shards(): call(functools.partial(pack_kernel, prior), 'near_keys', [anywhere] * 2,...  0.99 us
    ppermute x4, waiting for transfers between devices, neighbour(): return lax.ppermute(value, ('seq', 'head'), pairs)  0.75 us
    pallas_call x1, Pallas kernels, halo_shards(): call(functools.partial(near_kernel, prior), 'near_terms', [inside] * 7, [...  0.73 us
  transfers between devices with their start and end apart: 4, of which 1 were waited for; matrix products, arithmetic and copies ran while one was open for 0% of the time, Pallas kernels for 26%

profile of v16, /device:TPU:1, one launch (start us, length us, event | category | flops | bytes accessed | tf_op | source)
XLA Modules:
  0.0 27.9 jit_solution(11258377928847430576)
XLA Ops:
  0.6 1.0 %near_keys.1 = bf16[64,2048]{1,0:T(8,128)(2,1)S(1)} custom-call(bf16[128,2048]{1,0:T(8,128)(2,1)} %k_ref.1, bf16[128,2048]{1,0:T(8,128)(2,1)} %v_ref.1), custom_call_target="tpu_custom_call" | custom-call | bytes 524288 | tf_op jit(solution)/shard_map/near_keys/pallas_call | solution.py:527
  1.6 3.9 %collective-permute-start = (bf16[64,2048]{1,0:T(8,128)(2,1)S(1)}, bf16[64,2048]{1,0:T(8,128)(2,1)S(1)}, u32[]{:S(2)}, u32[]{:S(2)}) collective-permute-start(bf16[64,2048]{1,0:T(8,128)(2,1)S(1)} %near_keys.1), channel_id=1, source_target_pairs={{0,1},{1,2},{2,3},{3,4},{4,5},{5,6},{6,7},{7,8},{8,9},{9,10},{10,1... | collective-permute-start | bytes 786440 | tf_op jit(solution)/shard_map/ppermute | solution.py:482
  5.6 1.7 %operands.1 = (bf16[64,2048]{1,0:T(8,128)(2,1)S(1)}, bf16[128,2048]{1,0:T(8,128)(2,1)S(1)}, bf16[128,2048]{1,0:T(8,128)(2,1)S(1)}, bf16[128,2048]{1,0:T(8,128)(2...) custom-call(s32[1,128]{1,0:T(1,128)} %bitcast.1, ...), custom_call_target="tpu_custom_call" | custom-call | bytes 4718592 | tf_op jit(solution)/shard_map/operands/pallas_call | solution.py:535
  7.3 3.1 %collective-permute-start.1 = (bf16[64,2048]{1,0:T(8,128)(2,1)S(1)}, bf16[64,2048]{1,0:T(8,128)(2,1)S(1)}, u32[]{:S(2)}, u32[]{:S(2)}) collective-permute-start(bf16[64,2048]{1,0:T(8,128)(2,1)S(1)} %get-tuple-element.35), channel_id=1, source_target_pairs={{0,1},{1,2},{2,3},{3,4},{4,5},{5,6},{6,7},{7,8},{8,9},{9,10},{10,1... | collective-permute-start | bytes 786440 | tf_op jit(solution)/shard_map/ppermute | solution.py:482
  10.4 0.7 %collective-permute-done.near_ref = bf16[64,2048]{1,0:T(8,128)(2,1)S(1)} collective-permute-done((bf16[64,2048]{1,0:T(8,128)(2,1)S(1)}, bf16[64,2048]{1,0:T(8,128)(2,1)S(1)}, u32[]{:S(2)}, u32[]{:S(2)}) %collective-permute-start) | collective-permute-done | bytes 262176 | tf_op jit(solution)/shard_map/ppermute | solution.py:482
  11.1 0.7 %near_terms.1 = (bf16[64,1024]{1,0:T(8,128)(2,1)S(1)}, bf16[64,1024]{1,0:T(8,128)(2,1)S(1)}) custom-call(f32[96,128]{1,0:T(8,128)S(1)} %get-tuple-element.37.near_bias_ref, f32[128,128]{1,0:T(8,128)S(1)} %get-tuple-element.30.lead_bias_ref.bias_ref, bf16[128,2048]{1,0:T(8,128)(2,1)S(1)} %get-tuple-element.31.q_ref, ...), custom_call_target="tpu_custom_call" | custom-call | flops 75497472 | bytes 2097152 | tf_op jit(solution)/shard_map/near_terms/pallas_call | solution.py:549
  11.9 6.1 %collective-permute-start.3 = (bf16[64,1024]{1,0:T(8,128)(2,1)S(1)}, bf16[64,1024]{1,0:T(8,128)(2,1)S(1)}, u32[]{:S(2)}, u32[]{:S(2)}) collective-permute-start(bf16[64,1024]{1,0:T(8,128)(2,1)S(1)} %get-tuple-element.49), channel_id=1, source_target_pairs={{1,0},{2,1},{3,2},{4,3},{5,4},{6,5},{7,6},{8,7},{9,8},{10,9},{11,1... | collective-permute-start | bytes 393224 | tf_op jit(solution)/shard_map/ppermute | solution.py:482
  17.9 3.9 %collective-permute-start.2 = (bf16[64,1024]{1,0:T(8,128)(2,1)S(1)}, bf16[64,1024]{1,0:T(8,128)(2,1)S(1)}, u32[]{:S(2)}, u32[]{:S(2)}) collective-permute-start(bf16[64,1024]{1,0:T(8,128)(2,1)S(1)} %get-tuple-element.48), channel_id=1, source_target_pairs={{1,0},{2,1},{3,2},{4,3},{5,4},{6,5},{7,6},{8,7},{9,8},{10,9},{11,1... | collective-permute-start | bytes 393224 | tf_op jit(solution)/shard_map/ppermute | solution.py:482
  21.9 1.5 %own_block.1 = (bf16[64,2048]{1,0:T(8,128)(2,1)S(1)}, bf16[64,2048]{1,0:T(8,128)(2,1)S(1)}, f32[128,2048]{1,0:T(8,128)S(1)}, f32[128,2048]{1,0:T(8,128)S(1)}) custom-call(f32[128,128]{1,0:T(8,128)S(1)} %get-tuple-element.40.bias_ref, bf16[128,2048]{1,0:T(8,128)(2,1)S(1)} %get-tuple-element.31.q_ref, bf16[128,2048]{1,0:T(8,128)(2,1)S(1)} %get-tuple-element.32.k_ref, ...), custom_call_target="tpu_custom_call" | custom-call | flops 201326592 | bytes 4718592 | tf_op jit(solution)/shard_map/own_block/pallas_call | solution.py:557
  23.3 0.0 collective-permute-done.1.far_ref
  23.4 2.2 %lead_rows.1 = (bf16[128,2048]{1,0:T(8,128)(2,1)}, bf16[128,2048]{1,0:T(8,128)(2,1)}, bf16[128,2048]{1,0:T(8,128)(2,1)}, bf16[128,2048]{1,0:T(8,128)(2,1)}) custom-call(f32[128,128]{1,0:T(8,128)S(1)} %get-tuple-element.30.lead_bias_ref.bias_ref, bf16[128,2048]{1,0:T(8,128)(2,1)S(1)} %get-tuple-element.31.q_ref, ...), custom_call_target="tpu_custom_call" | custom-call | flops 201326592 | bytes 5242880 | tf_op jit(solution)/shard_map/lead_rows/pallas_call | solution.py:564
  25.6 0.0 collective-permute-done.3.after_ref
  25.6 1.2 %tail_keys.2 = (bf16[128,2048]{1,0:T(8,128)(2,1)}, bf16[128,2048]{1,0:T(8,128)(2,1)}) custom-call(f32[64,128]{1,0:T(8,128)S(1)} %get-tuple-element.47.bias_ref, bf16[128,2048]{1,0:T(8,128)(2,1)S(1)} %get-tuple-element.32.k_ref, bf16[128,2048]{1,0:T(8,128)(2,1)S(1)} %get-tuple-element.33.v_ref, ...), custom_call_target="tpu_custom_call", output_to_operand_aliasing={{0}: (6, {}), {1}: (7, {})} | custom-call | flops 16777216 | bytes 1310720 | tf_op jit(solution)/shard_map/tail_keys/pallas_call | solution.py:573
  26.8 0.0 collective-permute-done.2.after_ref
  26.8 1.2 %tail_keys.3 = (bf16[128,2048]{1,0:T(8,128)(2,1)}, bf16[128,2048]{1,0:T(8,128)(2,1)}) custom-call(f32[64,128]{1,0:T(8,128)S(1)} %get-tuple-element.47.bias_ref, bf16[128,2048]{1,0:T(8,128)(2,1)S(1)} %get-tuple-element.32.k_ref, bf16[128,2048]{1,0:T(8,128)(2,1)S(1)} %get-tuple-element.33.v_ref, ...), custom_call_target="tpu_custom_call", output_to_operand_aliasing={{0}: (6, {}), {1}: (7, {})} | custom-call | flops 16777216 | bytes 1310720 | tf_op jit(solution)/shard_map/tail_keys/pallas_call | solution.py:573
Async XLA Ops:
  1.6 9.5 %collective-permute-start = (bf16[64,2048]{1,0:T(8,128)(2,1)S(1)}, bf16[64,2048]{1,0:T(8,128)(2,1)S(1)}, u32[]{:S(2)}, u32[]{:S(2)}) collective-permute-start(bf16[64,2048]{1,0:T(8,128)(2,1)S(1)} %near_keys.1), channel_id=1, source_target_pairs={{0,1},{1,2},{2,3},{3,4},{4,5},{5,6},{6,7},{7,8},{8,9},{9,10},{10,1... | collective-permute-start | bytes 786440 | tf_op jit(solution)/shard_map/ppermute | solution.py:482
  7.3 16.1 %collective-permute-start.1 = (bf16[64,2048]{1,0:T(8,128)(2,1)S(1)}, bf16[64,2048]{1,0:T(8,128)(2,1)S(1)}, u32[]{:S(2)}, u32[]{:S(2)}) collective-permute-start(bf16[64,2048]{1,0:T(8,128)(2,1)S(1)} %get-tuple-element.35), channel_id=1, source_target_pairs={{0,1},{1,2},{2,3},{3,4},{4,5},{5,6},{6,7},{7,8},{8,9},{9,10},{10,1... | collective-permute-start | bytes 786440 | tf_op jit(solution)/shard_map/ppermute | solution.py:482
  11.9 13.7 %collective-permute-start.3 = (bf16[64,1024]{1,0:T(8,128)(2,1)S(1)}, bf16[64,1024]{1,0:T(8,128)(2,1)S(1)}, u32[]{:S(2)}, u32[]{:S(2)}) collective-permute-start(bf16[64,1024]{1,0:T(8,128)(2,1)S(1)} %get-tuple-element.49), channel_id=1, source_target_pairs={{1,0},{2,1},{3,2},{4,3},{5,4},{6,5},{7,6},{8,7},{9,8},{10,9},{11,1... | collective-permute-start | bytes 393224 | tf_op jit(solution)/shard_map/ppermute | solution.py:482
  17.9 8.8 %collective-permute-start.2 = (bf16[64,1024]{1,0:T(8,128)(2,1)S(1)}, bf16[64,1024]{1,0:T(8,128)(2,1)S(1)}, u32[]{:S(2)}, u32[]{:S(2)}) collective-permute-start(bf16[64,1024]{1,0:T(8,128)(2,1)S(1)} %get-tuple-element.48), channel_id=1, source_target_pairs={{1,0},{2,1},{3,2},{4,3},{5,4},{6,5},{7,6},{8,7},{9,8},{10,9},{11,1... | collective-permute-start | bytes 393224 | tf_op jit(solution)/shard_map/ppermute | solution.py:482

commit v17 on v16

--- a/solution.py
+++ b/solution.py
@@ -432,26 +432,26 @@
         copy.wait()
 
 
-def tail_kernel(
-    prior, low, bias_ref, k_ref, v_ref, after_ref, gk_part_ref, gv_part_ref, gk_in, gv_in,
-    gk_hbm, gv_hbm, gk_ref, gv_ref, sems,
-):
-    tok, width = k_ref.shape[0], after_ref.shape[1]
+def tail_kernel(prior, bias_ref, k_ref, v_ref, gk_part_ref, gv_part_ref, *refs):
+    *after_refs, _, _, gk_hbm, gv_hbm, gk_ref, gv_ref, sems = refs
+    tok, width = k_ref.shape
     half = prior // 2
     far = bias_ref[half - 1 : half, 0:1] == 0.0
     bias = jnp.where(far, bias_ref[...], MASKED)
     first, second, last = slice(0, half), slice(half, prior), slice(tok - prior, tok)
-    places = head_columns(0, width, 4)
-    columns = head_columns(low, low + width, 4)
-    queries = [side_by_side(after_ref[first, p]) for p in places]
-    cotangents = [side_by_side(after_ref[second, p]) for p in places]
+    columns = head_columns(0, width, 4)
+    afters = [
+        (after_ref, p) for after_ref in after_refs for p in head_columns(0, after_ref.shape[1], 4)
+    ]
+    queries = [side_by_side(after_ref[first, p]) for after_ref, p in afters]
+    cotangents = [side_by_side(after_ref[second, p]) for after_ref, p in afters]
     pairs = [
         score_pair(k_ref[last, c], q, v_ref[last, c], do, bias)
         for c, q, do in zip(columns, queries, cotangents)
     ]
     own = [
         (joined(after_ref[half - 1 : half, p]), joined(after_ref[prior - 1 : prior, p]))
-        for p in places
+        for after_ref, p in afters
     ]
     weights, grads = merged_columns(pairs, own)
     copies = []
@@ -461,15 +461,13 @@
             (gk_ref, gk_hbm, gk_part_ref, grads, queries, first),
         )
     ):
-        for p, c, left, right in zip(places, columns, lefts, rights):
+        for (after_ref, p), c, left, right in zip(afters, columns, lefts, rights):
             total = part_ref[last, c] + dot(left, right, 1, 0)
             terms = jnp.where(far, 0.0, after_ref[rows, p].astype(jnp.float32))
-            ref[first, p] = total[first].astype(jnp.bfloat16)
-            ref[second, p] = (total[second] + terms).astype(jnp.bfloat16)
+            ref[first, c] = total[first].astype(jnp.bfloat16)
+            ref[second, c] = (total[second] + terms).astype(jnp.bfloat16)
         copies.append(
-            pltpu.make_async_copy(
-                ref, hbm.at[pl.ds(tok - prior, prior), pl.ds(low, width)], sems.at[at]
-            )
+            pltpu.make_async_copy(ref, hbm.at[pl.ds(tok - prior, prior), :], sems.at[at])
         )
         copies[-1].start()
     for copy in copies:
@@ -546,20 +544,20 @@
     )(*in_hbm(lengths, query_in, key_in, value_in, grad_out))
     far = neighbour(far, 1)
 
-    backs = call(
-        functools.partial(near_kernel, prior), "near_terms",
-        [inside] * 7, [inside] * groups, [near16(prior, step)] * groups, (),
-        (width // HEAD_DIM, prior, prior + prior // 2, 3), 8 * tok * width,
-    )(*in_vmem(near_bias, lead_bias, q, k, v, do, near))
-    own_bias, *backs = lax.optimization_barrier((own_bias, *backs))
-    backs = [neighbour(back, -1) for back in backs]
-
     attn, gq, gk_part, gv_part = call(
         functools.partial(own_kernel, prior, step), "own_block",
         [inside] * 5, [inside] * 4,
         [near16(tok - prior, width)] * 2 + [near32(tok, width)] * 2, (),
         (width // HEAD_DIM, tok - prior, tok, 6), 18 * tok * width,
     )(*in_vmem(own_bias, q, k, v, do))
+
+    near_bias, attn = lax.optimization_barrier((near_bias, attn))
+    backs = call(
+        functools.partial(near_kernel, prior), "near_terms",
+        [inside] * 7, [inside] * groups, [near16(prior, step)] * groups, (),
+        (width // HEAD_DIM, prior, prior + prior // 2, 3), 8 * tok * width,
+    )(*in_vmem(near_bias, lead_bias, q, k, v, do, near))
+    backs = [neighbour(back, -1) for back in backs]
 
     attn, gq, gk, gv = call(
         functools.partial(lead_kernel, prior, step), "lead_rows",
@@ -569,13 +567,13 @@
         (width // HEAD_DIM, prior, 2 * prior, 6), 20 * tok * width,
     )(*in_vmem(lead_bias, q, k, v, do, near, far, gk_part, gv_part, attn, gq))
 
-    for at, back in enumerate(backs):
-        gk, gv = call(
-            functools.partial(tail_kernel, prior, at * step), "tail_keys",
-            [inside] * 6 + [anywhere] * 2, [anywhere] * 2, [full16] * 2,
-            [near16(prior, step)] * 2 + [pltpu.SemaphoreType.DMA((2,))],
-            (step // HEAD_DIM, prior, prior // 2, 4), 10 * tok * step, {6: 0, 7: 1},
-        )(*in_vmem(tail_bias, k, v, back, gk_part, gv_part), gk, gv)
+    gk, gv = call(
+        functools.partial(tail_kernel, prior), "tail_keys",
+        [inside] * (5 + groups) + [anywhere] * 2, [anywhere] * 2, [full16] * 2,
+        [near16(prior, width)] * 2 + [pltpu.SemaphoreType.DMA((2,))],
+        (width // HEAD_DIM, prior, prior // 2, 4), 10 * tok * width,
+        {5 + groups: 0, 6 + groups: 1},
+    )(*in_vmem(tail_bias, k, v, gk_part, gv_part, *backs), gk, gv)
     return (attn, gq, gk, gv)
 
 

time: 28.2 us -> 26.3 us (0.933)
  the two profiles are of different devices: /device:TPU:1 before, /device:TPU:0 now
where the time goes in v17:
time: 26.3 us; the launch traced here: 26.1 us
  starting transfers between devices  10.8 us (41%)
  Pallas kernels  8.49 us (32%)
  waiting for transfers between devices  6.02 us (23%)
  between operations  0.7 us (3%)
    ppermute x4, starting transfers between devices, neighbour(): return lax.ppermute(value, ('seq', 'head'), pairs)  10.8 us
    ppermute x4, waiting for transfers between devices, neighbour(): return lax.ppermute(value, ('seq', 'head'), pairs)  6.02 us
    pallas_call x1, Pallas kernels, halo_shards(): call(functools.partial(lead_kernel, prior, step), 'lead_rows', [inside] *...  2.2 us
    pallas_call x1, Pallas kernels, halo_shards(): call(functools.partial(ready_kernel, prior), 'operands', [anywhere] * 5,...  1.68 us
    pallas_call x1, Pallas kernels, halo_shards(): call(functools.partial(own_kernel, prior, step), 'own_block', [inside] *...  1.49 us
    pallas_call x1, Pallas kernels, halo_shards(): call(functools.partial(tail_kernel, prior), 'tail_keys', [inside] * (5 +...  1.42 us
    pallas_call x1, Pallas kernels, halo_shards(): call(functools.partial(pack_kernel, prior), 'near_keys', [anywhere] * 2,...  0.99 us
    pallas_call x1, Pallas kernels, halo_shards(): call(functools.partial(near_kernel, prior), 'near_terms', [inside] * 7, [...  0.73 us
  transfers between devices with their start and end apart: 4, of which 3 were waited for; matrix products, arithmetic and copies ran while one was open for 0% of the time, Pallas kernels for 23%

profile of v17, /device:TPU:0, one launch (start us, length us, event | category | flops | bytes accessed | tf_op | source)
XLA Modules:
  0.0 26.1 jit_solution(1438831882792454268)
XLA Ops:
  0.6 1.0 %near_keys.1 = bf16[64,2048]{1,0:T(8,128)(2,1)S(1)} custom-call(bf16[128,2048]{1,0:T(8,128)(2,1)} %k_ref.1, bf16[128,2048]{1,0:T(8,128)(2,1)} %v_ref.1), custom_call_target="tpu_custom_call" | custom-call | bytes 524288 | tf_op jit(solution)/shard_map/near_keys/pallas_call | solution.py:525
  1.6 4.9 %collective-permute-start = (bf16[64,2048]{1,0:T(8,128)(2,1)S(1)}, bf16[64,2048]{1,0:T(8,128)(2,1)S(1)}, u32[]{:S(2)}, u32[]{:S(2)}) collective-permute-start(bf16[64,2048]{1,0:T(8,128)(2,1)S(1)} %near_keys.1), channel_id=1, source_target_pairs={{0,1},{1,2},{2,3},{3,4},{4,5},{5,6},{6,7},{7,8},{8,9},{9,10},{10,1... | collective-permute-start | bytes 786440 | tf_op jit(solution)/shard_map/ppermute | solution.py:480
  6.5 1.7 %operands.1 = (bf16[64,2048]{1,0:T(8,128)(2,1)S(1)}, bf16[128,2048]{1,0:T(8,128)(2,1)S(1)}, bf16[128,2048]{1,0:T(8,128)(2,1)S(1)}, bf16[128,2048]{1,0:T(8,128)(2...) custom-call(s32[1,128]{1,0:T(1,128)} %bitcast.1, ...), custom_call_target="tpu_custom_call" | custom-call | bytes 4718592 | tf_op jit(solution)/shard_map/operands/pallas_call | solution.py:533
  8.2 3.4 %collective-permute-start.1 = (bf16[64,2048]{1,0:T(8,128)(2,1)S(1)}, bf16[64,2048]{1,0:T(8,128)(2,1)S(1)}, u32[]{:S(2)}, u32[]{:S(2)}) collective-permute-start(bf16[64,2048]{1,0:T(8,128)(2,1)S(1)} %get-tuple-element.32), channel_id=1, source_target_pairs={{0,1},{1,2},{2,3},{3,4},{4,5},{5,6},{6,7},{7,8},{8,9},{9,10},{10,1... | collective-permute-start | bytes 786440 | tf_op jit(solution)/shard_map/ppermute | solution.py:480
  11.6 1.5 %own_block.1 = (bf16[64,2048]{1,0:T(8,128)(2,1)S(1)}, bf16[64,2048]{1,0:T(8,128)(2,1)S(1)}, f32[128,2048]{1,0:T(8,128)S(1)}, f32[128,2048]{1,0:T(8,128)S(1)}) custom-call(f32[128,128]{1,0:T(8,128)S(1)} %get-tuple-element.33.bias_ref, bf16[128,2048]{1,0:T(8,128)(2,1)S(1)} %get-tuple-element.28.q_ref, bf16[128,2048]{1,0:T(8,128)(2,1)S(1)} %get-tuple-element.29.k_ref, ...), custom_call_target="tpu_custom_call" | custom-call | flops 201326592 | bytes 4718592 | tf_op jit(solution)/shard_map/own_block/pallas_call | solution.py:547
  13.1 0.0 collective-permute-done.near_ref
  13.1 0.7 %near_terms.1 = (bf16[64,1024]{1,0:T(8,128)(2,1)S(1)}, bf16[64,1024]{1,0:T(8,128)(2,1)S(1)}) custom-call(f32[96,128]{1,0:T(8,128)S(1)} %get-tuple-element.43.near_bias_ref, f32[128,128]{1,0:T(8,128)S(1)} %get-tuple-element.27.bias_ref.lead_bias_ref, bf16[128,2048]{1,0:T(8,128)(2,1)S(1)} %get-tuple-element.28.q_ref, ...), custom_call_target="tpu_custom_call" | custom-call | flops 75497472 | bytes 2097152 | tf_op jit(solution)/shard_map/near_terms/pallas_call | solution.py:555
  13.8 1.3 %collective-permute-start.2 = (bf16[64,1024]{1,0:T(8,128)(2,1)S(1)}, bf16[64,1024]{1,0:T(8,128)(2,1)S(1)}, u32[]{:S(2)}, u32[]{:S(2)}) collective-permute-start(bf16[64,1024]{1,0:T(8,128)(2,1)S(1)} %get-tuple-element.44), channel_id=1, source_target_pairs={{1,0},{2,1},{3,2},{4,3},{5,4},{6,5},{7,6},{8,7},{9,8},{10,9},{11,1... | collective-permute-start | bytes 393224 | tf_op jit(solution)/shard_map/ppermute | solution.py:480
  15.1 1.3 %collective-permute-start.3 = (bf16[64,1024]{1,0:T(8,128)(2,1)S(1)}, bf16[64,1024]{1,0:T(8,128)(2,1)S(1)}, u32[]{:S(2)}, u32[]{:S(2)}) collective-permute-start(bf16[64,1024]{1,0:T(8,128)(2,1)S(1)} %get-tuple-element.45), channel_id=1, source_target_pairs={{1,0},{2,1},{3,2},{4,3},{5,4},{6,5},{7,6},{8,7},{9,8},{10,9},{11,1... | collective-permute-start | bytes 393224 | tf_op jit(solution)/shard_map/ppermute | solution.py:480
  16.4 1.2 %collective-permute-done.1.far_ref = bf16[64,2048]{1,0:T(8,128)(2,1)S(1)} collective-permute-done((bf16[64,2048]{1,0:T(8,128)(2,1)S(1)}, bf16[64,2048]{1,0:T(8,128)(2,1)S(1)}, u32[]{:S(2)}, u32[]{:S(2)}) %collective-permute-start.1) | collective-permute-done | bytes 262176 | tf_op jit(solution)/shard_map/ppermute | solution.py:480
  17.6 2.2 %lead_rows.1 = (bf16[128,2048]{1,0:T(8,128)(2,1)}, bf16[128,2048]{1,0:T(8,128)(2,1)}, bf16[128,2048]{1,0:T(8,128)(2,1)}, bf16[128,2048]{1,0:T(8,128)(2,1)}) custom-call(f32[128,128]{1,0:T(8,128)S(1)} %get-tuple-element.27.bias_ref.lead_bias_ref, bf16[128,2048]{1,0:T(8,128)(2,1)S(1)} %get-tuple-element.28.q_ref, ...), custom_call_target="tpu_custom_call" | custom-call | flops 201326592 | bytes 5242880 | tf_op jit(solution)/shard_map/lead_rows/pallas_call | solution.py:562
  19.8 2.6 %collective-permute-done.2.refs_0_ = bf16[64,1024]{1,0:T(8,128)(2,1)S(1)} collective-permute-done((bf16[64,1024]{1,0:T(8,128)(2,1)S(1)}, bf16[64,1024]{1,0:T(8,128)(2,1)S(1)}, u32[]{:S(2)}, u32[]{:S(2)}) %collective-permute-start.2) | collective-permute-done | bytes 131104 | tf_op jit(solution)/shard_map/ppermute | solution.py:480
  22.4 2.2 %collective-permute-done.3.refs_1_ = bf16[64,1024]{1,0:T(8,128)(2,1)S(1)} collective-permute-done((bf16[64,1024]{1,0:T(8,128)(2,1)S(1)}, bf16[64,1024]{1,0:T(8,128)(2,1)S(1)}, u32[]{:S(2)}, u32[]{:S(2)}) %collective-permute-start.3) | collective-permute-done | bytes 131104 | tf_op jit(solution)/shard_map/ppermute | solution.py:480
  24.6 1.4 %tail_keys.1 = (bf16[128,2048]{1,0:T(8,128)(2,1)}, bf16[128,2048]{1,0:T(8,128)(2,1)}) custom-call(f32[64,128]{1,0:T(8,128)S(1)} %get-tuple-element.42.bias_ref, bf16[128,2048]{1,0:T(8,128)(2,1)S(1)} %get-tuple-element.29.k_ref, bf16[128,2048]{1,0:T(8,128)(2,1)S(1)} %get-tuple-element.30.v_ref, ...), custom_call_target="tpu_custom_call", output_to_operand_aliasing={{0}: (7, {}), {1}: (8, {})} | custom-call | flops 33554432 | bytes 2621440 | tf_op jit(solution)/shard_map/tail_keys/pallas_call | solution.py:570
Async XLA Ops:
  1.6 11.5 %collective-permute-start = (bf16[64,2048]{1,0:T(8,128)(2,1)S(1)}, bf16[64,2048]{1,0:T(8,128)(2,1)S(1)}, u32[]{:S(2)}, u32[]{:S(2)}) collective-permute-start(bf16[64,2048]{1,0:T(8,128)(2,1)S(1)} %near_keys.1), channel_id=1, source_target_pairs={{0,1},{1,2},{2,3},{3,4},{4,5},{5,6},{6,7},{7,8},{8,9},{9,10},{10,1... | collective-permute-start | bytes 786440 | tf_op jit(solution)/shard_map/ppermute | solution.py:480
  8.2 9.5 %collective-permute-start.1 = (bf16[64,2048]{1,0:T(8,128)(2,1)S(1)}, bf16[64,2048]{1,0:T(8,128)(2,1)S(1)}, u32[]{:S(2)}, u32[]{:S(2)}) collective-permute-start(bf16[64,2048]{1,0:T(8,128)(2,1)S(1)} %get-tuple-element.32), channel_id=1, source_target_pairs={{0,1},{1,2},{2,3},{3,4},{4,5},{5,6},{6,7},{7,8},{8,9},{9,10},{10,1... | collective-permute-start | bytes 786440 | tf_op jit(solution)/shard_map/ppermute | solution.py:480
  13.8 8.6 %collective-permute-start.2 = (bf16[64,1024]{1,0:T(8,128)(2,1)S(1)}, bf16[64,1024]{1,0:T(8,128)(2,1)S(1)}, u32[]{:S(2)}, u32[]{:S(2)}) collective-permute-start(bf16[64,1024]{1,0:T(8,128)(2,1)S(1)} %get-tuple-element.44), channel_id=1, source_target_pairs={{1,0},{2,1},{3,2},{4,3},{5,4},{6,5},{7,6},{8,7},{9,8},{10,9},{11,1... | collective-permute-start | bytes 393224 | tf_op jit(solution)/shard_map/ppermute | solution.py:480
  15.1 9.5 %collective-permute-start.3 = (bf16[64,1024]{1,0:T(8,128)(2,1)S(1)}, bf16[64,1024]{1,0:T(8,128)(2,1)S(1)}, u32[]{:S(2)}, u32[]{:S(2)}) collective-permute-start(bf16[64,1024]{1,0:T(8,128)(2,1)S(1)} %get-tuple-element.45), channel_id=1, source_target_pairs={{1,0},{2,1},{3,2},{4,3},{5,4},{6,5},{7,6},{8,7},{9,8},{10,9},{11,1... | collective-permute-start | bytes 393224 | tf_op jit(solution)/shard_map/ppermute | solution.py:480

commit v18 on v17

--- a/solution.py
+++ b/solution.py
@@ -358,10 +358,8 @@
     k_terms = [dot(g, q, 1, 0) for g, q in zip(grads, queries)]
     v_terms = [dot(w.astype(jnp.bfloat16), do, 1, 0) for w, do in zip(weights, cotangents)]
     logs, deltas = fours(logs), fours(deltas)
-    for at, c in enumerate(head_columns(0, width, 4)):
-        back_ref = back_refs[c.start * len(back_refs) // width]
-        low = c.start % back_ref.shape[1]
-        here = slice(low, low + c.stop - c.start)
+    places = [(ref, p) for ref in back_refs for p in head_columns(0, ref.shape[1], 4)]
+    for at, (c, (back_ref, here)) in enumerate(zip(head_columns(0, width, 4), places)):
         for row, terms, ref, place in (
             (logs[at], k_terms, q_ref, first), (deltas[at], v_terms, do_ref, second)
         ):
@@ -493,6 +491,8 @@
     prior = tok * lax.axis_size("head") // 8
     step = math.gcd(width, 8 * HEAD_DIM)
     groups = width // step
+    four = 4 * HEAD_DIM
+    parts = [four, width - four]
     anywhere = pl.BlockSpec(memory_space=pl.ANY)
     inside = pl.BlockSpec(memory_space=pltpu.VMEM)
     full16 = jax.ShapeDtypeStruct((tok, width), jnp.bfloat16)
@@ -554,7 +554,7 @@
     near_bias, attn = lax.optimization_barrier((near_bias, attn))
     backs = call(
         functools.partial(near_kernel, prior), "near_terms",
-        [inside] * 7, [inside] * groups, [near16(prior, step)] * groups, (),
+        [inside] * 7, [inside] * len(parts), [near16(prior, wide) for wide in parts], (),
         (width // HEAD_DIM, prior, prior + prior // 2, 3), 8 * tok * width,
     )(*in_vmem(near_bias, lead_bias, q, k, v, do, near))
     backs = [neighbour(back, -1) for back in backs]
@@ -569,10 +569,10 @@
 
     gk, gv = call(
         functools.partial(tail_kernel, prior), "tail_keys",
-        [inside] * (5 + groups) + [anywhere] * 2, [anywhere] * 2, [full16] * 2,
+        [inside] * (5 + len(parts)) + [anywhere] * 2, [anywhere] * 2, [full16] * 2,
         [near16(prior, width)] * 2 + [pltpu.SemaphoreType.DMA((2,))],
         (width // HEAD_DIM, prior, prior // 2, 4), 10 * tok * width,
-        {5 + groups: 0, 6 + groups: 1},
+        {5 + len(parts): 0, 6 + len(parts): 1},
     )(*in_vmem(tail_bias, k, v, gk_part, gv_part, *backs), gk, gv)
     return (attn, gq, gk, gv)
 

time: 26.3 us -> 26.9 us (1.023)
  waiting for transfers between devices: 6.02 us -> 6.59 us
    ppermute x4, waiting for transfers between devices: 6.02 us -> 6.59 us  [neighbour(): return lax.ppermute(value, ('seq', 'head'), pairs)]
  transfers between devices with their start and end apart: 4 -> 4, of which waited for: 3 -> 2; matrix products, arithmetic and copies ran while one was open for 0% -> 0% of each run, Pallas kernels for 23% -> 23%
where the time goes in v18:
time: 26.9 us; the launch traced here: 26.6 us
  starting transfers between devices  10.8 us (40%)
  Pallas kernels  8.48 us (32%)
  waiting for transfers between devices  6.59 us (24%)
  between operations  0.7 us (3%)
    ppermute x4, starting transfers between devices, neighbour(): return lax.ppermute(value, ('seq', 'head'), pairs)  10.8 us
    ppermute x4, waiting for transfers between devices, neighbour(): return lax.ppermute(value, ('seq', 'head'), pairs)  6.59 us
    pallas_call x1, Pallas kernels, halo_shards(): call(functools.partial(lead_kernel, prior, step), 'lead_rows', [inside] *...  2.2 us
    pallas_call x1, Pallas kernels, halo_shards(): call(functools.partial(ready_kernel, prior), 'operands', [anywhere] * 5,...  1.68 us
    pallas_call x1, Pallas kernels, halo_shards(): call(functools.partial(own_kernel, prior, step), 'own_block', [inside] *...  1.49 us
    pallas_call x1, Pallas kernels, halo_shards(): call(functools.partial(tail_kernel, prior), 'tail_keys', [inside] * (5 +...  1.4 us
    pallas_call x1, Pallas kernels, halo_shards(): call(functools.partial(pack_kernel, prior), 'near_keys', [anywhere] * 2,...  0.99 us
    pallas_call x1, Pallas kernels, halo_shards(): call(functools.partial(near_kernel, prior), 'near_terms', [inside] * 7, [...  0.73 us
  transfers between devices with their start and end apart: 4, of which 2 were waited for; matrix products, arithmetic and copies ran while one was open for 0% of the time, Pallas kernels for 23%

profile of v18, /device:TPU:0, one launch (start us, length us, event | category | flops | bytes accessed | tf_op | source)
XLA Modules:
  0.0 26.6 jit_solution(3323926475277667623)
XLA Ops:
  0.6 1.0 %near_keys.1 = bf16[64,2048]{1,0:T(8,128)(2,1)S(1)} custom-call(bf16[128,2048]{1,0:T(8,128)(2,1)} %k_ref.1, bf16[128,2048]{1,0:T(8,128)(2,1)} %v_ref.1), custom_call_target="tpu_custom_call" | custom-call | bytes 524288 | tf_op jit(solution)/shard_map/near_keys/pallas_call | solution.py:525
  1.6 4.9 %collective-permute-start = (bf16[64,2048]{1,0:T(8,128)(2,1)S(1)}, bf16[64,2048]{1,0:T(8,128)(2,1)S(1)}, u32[]{:S(2)}, u32[]{:S(2)}) collective-permute-start(bf16[64,2048]{1,0:T(8,128)(2,1)S(1)} %near_keys.1), channel_id=1, source_target_pairs={{0,1},{1,2},{2,3},{3,4},{4,5},{5,6},{6,7},{7,8},{8,9},{9,10},{10,1... | collective-permute-start | bytes 786440 | tf_op jit(solution)/shard_map/ppermute | solution.py:478
  6.5 1.7 %operands.1 = (bf16[64,2048]{1,0:T(8,128)(2,1)S(1)}, bf16[128,2048]{1,0:T(8,128)(2,1)S(1)}, bf16[128,2048]{1,0:T(8,128)(2,1)S(1)}, bf16[128,2048]{1,0:T(8,128)(2...) custom-call(s32[1,128]{1,0:T(1,128)} %bitcast.1, ...), custom_call_target="tpu_custom_call" | custom-call | bytes 4718592 | tf_op jit(solution)/shard_map/operands/pallas_call | solution.py:533
  8.2 3.4 %collective-permute-start.1 = (bf16[64,2048]{1,0:T(8,128)(2,1)S(1)}, bf16[64,2048]{1,0:T(8,128)(2,1)S(1)}, u32[]{:S(2)}, u32[]{:S(2)}) collective-permute-start(bf16[64,2048]{1,0:T(8,128)(2,1)S(1)} %get-tuple-element.32), channel_id=1, source_target_pairs={{0,1},{1,2},{2,3},{3,4},{4,5},{5,6},{6,7},{7,8},{8,9},{9,10},{10,1... | collective-permute-start | bytes 786440 | tf_op jit(solution)/shard_map/ppermute | solution.py:478
  11.6 1.5 %own_block.1 = (bf16[64,2048]{1,0:T(8,128)(2,1)S(1)}, bf16[64,2048]{1,0:T(8,128)(2,1)S(1)}, f32[128,2048]{1,0:T(8,128)S(1)}, f32[128,2048]{1,0:T(8,128)S(1)}) custom-call(f32[128,128]{1,0:T(8,128)S(1)} %get-tuple-element.33.bias_ref, bf16[128,2048]{1,0:T(8,128)(2,1)S(1)} %get-tuple-element.28.q_ref, bf16[128,2048]{1,0:T(8,128)(2,1)S(1)} %get-tuple-element.29.k_ref, ...), custom_call_target="tpu_custom_call" | custom-call | flops 201326592 | bytes 4718592 | tf_op jit(solution)/shard_map/own_block/pallas_call | solution.py:547
  13.1 0.0 collective-permute-done.near_ref
  13.1 0.7 %near_terms.1 = (bf16[64,512]{1,0:T(8,128)(2,1)S(1)}, bf16[64,1536]{1,0:T(8,128)(2,1)S(1)}) custom-call(f32[96,128]{1,0:T(8,128)S(1)} %get-tuple-element.43.near_bias_ref, f32[128,128]{1,0:T(8,128)S(1)} %get-tuple-element.27.bias_ref.lead_bias_ref, bf16[128,2048]{1,0:T(8,128)(2,1)S(1)} %get-tuple-element.28.q_ref, ...), custom_call_target="tpu_custom_call" | custom-call | flops 75497472 | bytes 2097152 | tf_op jit(solution)/shard_map/near_terms/pallas_call | solution.py:555
  13.8 1.3 %collective-permute-start.3 = (bf16[64,1536]{1,0:T(8,128)(2,1)S(1)}, bf16[64,1536]{1,0:T(8,128)(2,1)S(1)}, u32[]{:S(2)}, u32[]{:S(2)}) collective-permute-start(bf16[64,1536]{1,0:T(8,128)(2,1)S(1)} %get-tuple-element.45), channel_id=1, source_target_pairs={{1,0},{2,1},{3,2},{4,3},{5,4},{6,5},{7,6},{8,7},{9,8},{10,9},{11,1... | collective-permute-start | bytes 589832 | tf_op jit(solution)/shard_map/ppermute | solution.py:478
  15.1 1.3 %collective-permute-start.2 = (bf16[64,512]{1,0:T(8,128)(2,1)S(1)}, bf16[64,512]{1,0:T(8,128)(2,1)S(1)}, u32[]{:S(2)}, u32[]{:S(2)}) collective-permute-start(bf16[64,512]{1,0:T(8,128)(2,1)S(1)} %get-tuple-element.44), channel_id=1, source_target_pairs={{1,0},{2,1},{3,2},{4,3},{5,4},{6,5},{7,6},{8,7},{9,8},{10,9},{11,1... | collective-permute-start | bytes 196616 | tf_op jit(solution)/shard_map/ppermute | solution.py:478
  16.4 1.2 %collective-permute-done.1.far_ref = bf16[64,2048]{1,0:T(8,128)(2,1)S(1)} collective-permute-done((bf16[64,2048]{1,0:T(8,128)(2,1)S(1)}, bf16[64,2048]{1,0:T(8,128)(2,1)S(1)}, u32[]{:S(2)}, u32[]{:S(2)}) %collective-permute-start.1) | collective-permute-done | bytes 262176 | tf_op jit(solution)/shard_map/ppermute | solution.py:478
  17.6 2.2 %lead_rows.1 = (bf16[128,2048]{1,0:T(8,128)(2,1)}, bf16[128,2048]{1,0:T(8,128)(2,1)}, bf16[128,2048]{1,0:T(8,128)(2,1)}, bf16[128,2048]{1,0:T(8,128)(2,1)}) custom-call(f32[128,128]{1,0:T(8,128)S(1)} %get-tuple-element.27.bias_ref.lead_bias_ref, bf16[128,2048]{1,0:T(8,128)(2,1)S(1)} %get-tuple-element.28.q_ref, ...), custom_call_target="tpu_custom_call" | custom-call | flops 201326592 | bytes 5242880 | tf_op jit(solution)/shard_map/lead_rows/pallas_call | solution.py:562
  19.8 5.4 %collective-permute-done.2.refs_0_ = bf16[64,512]{1,0:T(8,128)(2,1)S(1)} collective-permute-done((bf16[64,512]{1,0:T(8,128)(2,1)S(1)}, bf16[64,512]{1,0:T(8,128)(2,1)S(1)}, u32[]{:S(2)}, u32[]{:S(2)}) %collective-permute-start.2) | collective-permute-done | bytes 65568 | tf_op jit(solution)/shard_map/ppermute | solution.py:478
  25.2 0.0 collective-permute-done.3.refs_1_
  25.2 1.4 %tail_keys.1 = (bf16[128,2048]{1,0:T(8,128)(2,1)}, bf16[128,2048]{1,0:T(8,128)(2,1)}) custom-call(f32[64,128]{1,0:T(8,128)S(1)} %get-tuple-element.42.bias_ref, bf16[128,2048]{1,0:T(8,128)(2,1)S(1)} %get-tuple-element.29.k_ref, bf16[128,2048]{1,0:T(8,128)(2,1)S(1)} %get-tuple-element.30.v_ref, ...), custom_call_target="tpu_custom_call", output_to_operand_aliasing={{0}: (7, {}), {1}: (8, {})} | custom-call | flops 33554432 | bytes 2621440 | tf_op jit(solution)/shard_map/tail_keys/pallas_call | solution.py:570
Async XLA Ops:
  1.6 11.5 %collective-permute-start = (bf16[64,2048]{1,0:T(8,128)(2,1)S(1)}, bf16[64,2048]{1,0:T(8,128)(2,1)S(1)}, u32[]{:S(2)}, u32[]{:S(2)}) collective-permute-start(bf16[64,2048]{1,0:T(8,128)(2,1)S(1)} %near_keys.1), channel_id=1, source_target_pairs={{0,1},{1,2},{2,3},{3,4},{4,5},{5,6},{6,7},{7,8},{8,9},{9,10},{10,1... | collective-permute-start | bytes 786440 | tf_op jit(solution)/shard_map/ppermute | solution.py:478
  8.2 9.5 %collective-permute-start.1 = (bf16[64,2048]{1,0:T(8,128)(2,1)S(1)}, bf16[64,2048]{1,0:T(8,128)(2,1)S(1)}, u32[]{:S(2)}, u32[]{:S(2)}) collective-permute-start(bf16[64,2048]{1,0:T(8,128)(2,1)S(1)} %get-tuple-element.32), channel_id=1, source_target_pairs={{0,1},{1,2},{2,3},{3,4},{4,5},{5,6},{6,7},{7,8},{8,9},{9,10},{10,1... | collective-permute-start | bytes 786440 | tf_op jit(solution)/shard_map/ppermute | solution.py:478
  13.8 11.4 %collective-permute-start.3 = (bf16[64,1536]{1,0:T(8,128)(2,1)S(1)}, bf16[64,1536]{1,0:T(8,128)(2,1)S(1)}, u32[]{:S(2)}, u32[]{:S(2)}) collective-permute-start(bf16[64,1536]{1,0:T(8,128)(2,1)S(1)} %get-tuple-element.45), channel_id=1, source_target_pairs={{1,0},{2,1},{3,2},{4,3},{5,4},{6,5},{7,6},{8,7},{9,8},{10,9},{11,1... | collective-permute-start | bytes 589832 | tf_op jit(solution)/shard_map/ppermute | solution.py:478
  15.1 10.1 %collective-permute-start.2 = (bf16[64,512]{1,0:T(8,128)(2,1)S(1)}, bf16[64,512]{1,0:T(8,128)(2,1)S(1)}, u32[]{:S(2)}, u32[]{:S(2)}) collective-permute-start(bf16[64,512]{1,0:T(8,128)(2,1)S(1)} %get-tuple-element.44), channel_id=1, source_target_pairs={{1,0},{2,1},{3,2},{4,3},{5,4},{6,5},{7,6},{8,7},{9,8},{10,9},{11,1... | collective-permute-start | bytes 196616 | tf_op jit(solution)/shard_map/ppermute | solution.py:478

commit v19 on v17

--- a/solution.py
+++ b/solution.py
@@ -268,8 +268,9 @@
     ]
 
 
-def pack_kernel(prior, k_ref, v_ref, near_ref, sems):
-    copies = pack_copies(prior, 0, k_ref, v_ref, near_ref, sems)
+def pack_kernel(prior, k_ref, v_ref, near_ref, far_ref, near_sems, far_sems):
+    copies = pack_copies(prior, 0, k_ref, v_ref, near_ref, near_sems)
+    copies += pack_copies(prior, 1, k_ref, v_ref, far_ref, far_sems)
     for copy in copies:
         copy.start()
     for copy in copies:
@@ -277,13 +278,12 @@
 
 
 def ready_kernel(
-    prior, len_hbm, q_hbm, k_hbm, v_hbm, do_hbm, far_ref, q_ref, k_ref, v_ref, do_ref,
-    own_bias_ref, near_bias_ref, lead_bias_ref, tail_bias_ref, len_ref, sems, far_sems, len_sem,
+    prior, len_hbm, q_hbm, k_hbm, v_hbm, do_hbm, q_ref, k_ref, v_ref, do_ref,
+    own_bias_ref, near_bias_ref, lead_bias_ref, tail_bias_ref, len_ref, sems, len_sem,
 ):
     tok, half = k_ref.shape[0], prior // 2
     pairs = ((q_hbm, q_ref), (k_hbm, k_ref), (v_hbm, v_ref), (do_hbm, do_ref))
-    copies = pack_copies(prior, 1, k_hbm, v_hbm, far_ref, far_sems)
-    copies += [pltpu.make_async_copy(hbm, ref, sems.at[n]) for n, (hbm, ref) in enumerate(pairs)]
+    copies = [pltpu.make_async_copy(hbm, ref, sems.at[n]) for n, (hbm, ref) in enumerate(pairs)]
     len_copy = pltpu.make_async_copy(len_hbm, len_ref, len_sem)
     len_copy.start()
     for copy in copies:
@@ -522,27 +522,26 @@
             name=name,
         )
 
-    near = call(
-        functools.partial(pack_kernel, prior), "near_keys",
-        [anywhere] * 2, inside, near16(prior, width),
-        [pltpu.SemaphoreType.DMA((2,))], (0, 0, 0, 0), 4 * prior * width,
+    near, far = call(
+        functools.partial(pack_kernel, prior), "late_keys",
+        [anywhere] * 2, [inside] * 2, [near16(prior, width)] * 2,
+        [pltpu.SemaphoreType.DMA((2,))] * 2, (0, 0, 0, 0), 8 * prior * width,
     )(*in_hbm(key_in, value_in))
-    near = neighbour(near, 1)
+    near, far = neighbour(near, 1), neighbour(far, 1)
 
     lengths = module_lengths.reshape(1, -1)
-    far, q, k, v, do, own_bias, near_bias, lead_bias, tail_bias = call(
+    q, k, v, do, own_bias, near_bias, lead_bias, tail_bias = call(
         functools.partial(ready_kernel, prior), "operands",
-        [anywhere] * 5, [inside] * 9,
-        [near16(prior, width)] + [near16(tok, width)] * 4
+        [anywhere] * 5, [inside] * 8,
+        [near16(tok, width)] * 4
         + [near32(tok, 2 * prior), near32(prior + prior // 2, 2 * prior)]
         + [near32(2 * prior, 2 * prior), near32(prior, 2 * prior)],
         [
             pltpu.VMEM(lengths.shape, jnp.int32), pltpu.SemaphoreType.DMA((4,)),
-            pltpu.SemaphoreType.DMA((2,)), pltpu.SemaphoreType.DMA(()),
+            pltpu.SemaphoreType.DMA(()),
         ],
-        (0, 0, 0, 0), 18 * tok * width,
+        (0, 0, 0, 0), 16 * tok * width,
     )(*in_hbm(lengths, query_in, key_in, value_in, grad_out))
-    far = neighbour(far, 1)
 
     attn, gq, gk_part, gv_part = call(
         functools.partial(own_kernel, prior, step), "own_block",

time: 26.3 us -> 27.2 us (1.034)
  the two profiles are of different devices: /device:TPU:0 before, /device:TPU:19 now
where the time goes in v19:
time: 27.2 us; the launch traced here: 27 us
  starting transfers between devices  15.3 us (56%)
  Pallas kernels  8.55 us (31%)
  waiting for transfers between devices  2.46 us (9%)
  between operations  0.72 us (3%)
    ppermute x4, starting transfers between devices, neighbour(): return lax.ppermute(value, ('seq', 'head'), pairs)  15.3 us
    ppermute x4, waiting for transfers between devices, neighbour(): return lax.ppermute(value, ('seq', 'head'), pairs)  2.46 us
    pallas_call x1, Pallas kernels, halo_shards(): call(functools.partial(lead_kernel, prior, step), 'lead_rows', [inside] *...  2.2 us
    pallas_call x1, Pallas kernels, halo_shards(): call(functools.partial(ready_kernel, prior), 'operands', [anywhere] * 5,...  1.58 us
    pallas_call x1, Pallas kernels, halo_shards(): call(functools.partial(own_kernel, prior, step), 'own_block', [inside] *...  1.49 us
    pallas_call x1, Pallas kernels, halo_shards(): call(functools.partial(tail_kernel, prior), 'tail_keys', [inside] * (5 +...  1.42 us
    pallas_call x1, Pallas kernels, halo_shards(): call(functools.partial(pack_kernel, prior), 'late_keys', [anywhere] * 2,...  1.13 us
    pallas_call x1, Pallas kernels, halo_shards(): call(functools.partial(near_kernel, prior), 'near_terms', [inside] * 7, [...  0.73 us
  transfers between devices with their start and end apart: 4, of which 1 were waited for; matrix products, arithmetic and copies ran while one was open for 0% of the time, Pallas kernels for 22%

profile of v19, /device:TPU:19, one launch (start us, length us, event | category | flops | bytes accessed | tf_op | source)
XLA Modules:
  0.0 27.0 jit_solution(6736156178442342357)
XLA Ops:
  0.6 1.1 %late_keys.1 = (bf16[64,2048]{1,0:T(8,128)(2,1)S(1)}, bf16[64,2048]{1,0:T(8,128)(2,1)S(1)}) custom-call(bf16[128,2048]{1,0:T(8,128)(2,1)} %k_ref.1, bf16[128,2048]{1,0:T(8,128)(2,1)} %v_ref.1), custom_call_target="tpu_custom_call" | custom-call | bytes 1048576 | tf_op jit(solution)/shard_map/late_keys/pallas_call | solution.py:525
  1.8 3.1 %collective-permute-start = (bf16[64,2048]{1,0:T(8,128)(2,1)S(1)}, bf16[64,2048]{1,0:T(8,128)(2,1)S(1)}, u32[]{:S(2)}, u32[]{:S(2)}) collective-permute-start(bf16[64,2048]{1,0:T(8,128)(2,1)S(1)} %get-tuple-element.33), channel_id=1, source_target_pairs={{0,1},{1,2},{2,3},{3,4},{4,5},{5,6},{6,7},{7,8},{8,9},{9,10},{10,1... | collective-permute-start | bytes 786440 | tf_op jit(solution)/shard_map/ppermute | solution.py:480
  4.9 3.1 %collective-permute-start.1 = (bf16[64,2048]{1,0:T(8,128)(2,1)S(1)}, bf16[64,2048]{1,0:T(8,128)(2,1)S(1)}, u32[]{:S(2)}, u32[]{:S(2)}) collective-permute-start(bf16[64,2048]{1,0:T(8,128)(2,1)S(1)} %get-tuple-element.34), channel_id=1, source_target_pairs={{0,1},{1,2},{2,3},{3,4},{4,5},{5,6},{6,7},{7,8},{8,9},{9,10},{10,1... | collective-permute-start | bytes 786440 | tf_op jit(solution)/shard_map/ppermute | solution.py:480
  8.0 1.6 %operands.1 = (bf16[128,2048]{1,0:T(8,128)(2,1)S(1)}, bf16[128,2048]{1,0:T(8,128)(2,1)S(1)}, bf16[128,2048]{1,0:T(8,128)(2,1)S(1)}, bf16[128,2048]{1,0:T(8,128)(...) custom-call(s32[1,128]{1,0:T(1,128)} %bitcast.1, ...), custom_call_target="tpu_custom_call" | custom-call | bytes 4194304 | tf_op jit(solution)/shard_map/operands/pallas_call | solution.py:533
  9.6 1.5 %own_block.1 = (bf16[64,2048]{1,0:T(8,128)(2,1)S(1)}, bf16[64,2048]{1,0:T(8,128)(2,1)S(1)}, f32[128,2048]{1,0:T(8,128)S(1)}, f32[128,2048]{1,0:T(8,128)S(1)}) custom-call(f32[128,128]{1,0:T(8,128)S(1)} %get-tuple-element.35.bias_ref, bf16[128,2048]{1,0:T(8,128)(2,1)S(1)} %get-tuple-element.29.q_ref, bf16[128,2048]{1,0:T(8,128)(2,1)S(1)} %get-tuple-element.30.k_ref, ...), custom_call_target="tpu_custom_call" | custom-call | flops 201326592 | bytes 4718592 | tf_op jit(solution)/shard_map/own_block/pallas_call | solution.py:546
  11.1 0.0 collective-permute-done.near_ref
  11.1 0.7 %near_terms.1 = (bf16[64,1024]{1,0:T(8,128)(2,1)S(1)}, bf16[64,1024]{1,0:T(8,128)(2,1)S(1)}) custom-call(f32[96,128]{1,0:T(8,128)S(1)} %get-tuple-element.45.near_bias_ref, f32[128,128]{1,0:T(8,128)S(1)} %get-tuple-element.28.bias_ref.lead_bias_ref, bf16[128,2048]{1,0:T(8,128)(2,1)S(1)} %get-tuple-element.29.q_ref, ...), custom_call_target="tpu_custom_call" | custom-call | flops 75497472 | bytes 2097152 | tf_op jit(solution)/shard_map/near_terms/pallas_call | solution.py:554
  11.8 7.1 %collective-permute-start.2 = (bf16[64,1024]{1,0:T(8,128)(2,1)S(1)}, bf16[64,1024]{1,0:T(8,128)(2,1)S(1)}, u32[]{:S(2)}, u32[]{:S(2)}) collective-permute-start(bf16[64,1024]{1,0:T(8,128)(2,1)S(1)} %get-tuple-element.46), channel_id=1, source_target_pairs={{1,0},{2,1},{3,2},{4,3},{5,4},{6,5},{7,6},{8,7},{9,8},{10,9},{11,1... | collective-permute-start | bytes 393224 | tf_op jit(solution)/shard_map/ppermute | solution.py:480
  19.0 1.9 %collective-permute-start.3 = (bf16[64,1024]{1,0:T(8,128)(2,1)S(1)}, bf16[64,1024]{1,0:T(8,128)(2,1)S(1)}, u32[]{:S(2)}, u32[]{:S(2)}) collective-permute-start(bf16[64,1024]{1,0:T(8,128)(2,1)S(1)} %get-tuple-element.47), channel_id=1, source_target_pairs={{1,0},{2,1},{3,2},{4,3},{5,4},{6,5},{7,6},{8,7},{9,8},{10,9},{11,1... | collective-permute-start | bytes 393224 | tf_op jit(solution)/shard_map/ppermute | solution.py:480
  20.9 0.0 collective-permute-done.1.far_ref
  20.9 2.2 %lead_rows.1 = (bf16[128,2048]{1,0:T(8,128)(2,1)}, bf16[128,2048]{1,0:T(8,128)(2,1)}, bf16[128,2048]{1,0:T(8,128)(2,1)}, bf16[128,2048]{1,0:T(8,128)(2,1)}) custom-call(f32[128,128]{1,0:T(8,128)S(1)} %get-tuple-element.28.bias_ref.lead_bias_ref, bf16[128,2048]{1,0:T(8,128)(2,1)S(1)} %get-tuple-element.29.q_ref, ...), custom_call_target="tpu_custom_call" | custom-call | flops 201326592 | bytes 5242880 | tf_op jit(solution)/shard_map/lead_rows/pallas_call | solution.py:561
  23.1 0.0 collective-permute-done.2.refs_0_
  23.1 2.5 %collective-permute-done.3.refs_1_ = bf16[64,1024]{1,0:T(8,128)(2,1)S(1)} collective-permute-done((bf16[64,1024]{1,0:T(8,128)(2,1)S(1)}, bf16[64,1024]{1,0:T(8,128)(2,1)S(1)}, u32[]{:S(2)}, u32[]{:S(2)}) %collective-permute-start.3) | collective-permute-done | bytes 131104 | tf_op jit(solution)/shard_map/ppermute | solution.py:480
  25.6 1.4 %tail_keys.1 = (bf16[128,2048]{1,0:T(8,128)(2,1)}, bf16[128,2048]{1,0:T(8,128)(2,1)}) custom-call(f32[64,128]{1,0:T(8,128)S(1)} %get-tuple-element.44.bias_ref, bf16[128,2048]{1,0:T(8,128)(2,1)S(1)} %get-tuple-element.30.k_ref, bf16[128,2048]{1,0:T(8,128)(2,1)S(1)} %get-tuple-element.31.v_ref, ...), custom_call_target="tpu_custom_call", output_to_operand_aliasing={{0}: (7, {}), {1}: (8, {})} | custom-call | flops 33554432 | bytes 2621440 | tf_op jit(solution)/shard_map/tail_keys/pallas_call | solution.py:569
Async XLA Ops:
  1.8 9.3 %collective-permute-start = (bf16[64,2048]{1,0:T(8,128)(2,1)S(1)}, bf16[64,2048]{1,0:T(8,128)(2,1)S(1)}, u32[]{:S(2)}, u32[]{:S(2)}) collective-permute-start(bf16[64,2048]{1,0:T(8,128)(2,1)S(1)} %get-tuple-element.33), channel_id=1, source_target_pairs={{0,1},{1,2},{2,3},{3,4},{4,5},{5,6},{6,7},{7,8},{8,9},{9,10},{10,1... | collective-permute-start | bytes 786440 | tf_op jit(solution)/shard_map/ppermute | solution.py:480
  4.9 16.0 %collective-permute-start.1 = (bf16[64,2048]{1,0:T(8,128)(2,1)S(1)}, bf16[64,2048]{1,0:T(8,128)(2,1)S(1)}, u32[]{:S(2)}, u32[]{:S(2)}) collective-permute-start(bf16[64,2048]{1,0:T(8,128)(2,1)S(1)} %get-tuple-element.34), channel_id=1, source_target_pairs={{0,1},{1,2},{2,3},{3,4},{4,5},{5,6},{6,7},{7,8},{8,9},{9,10},{10,1... | collective-permute-start | bytes 786440 | tf_op jit(solution)/shard_map/ppermute | solution.py:480
  11.8 11.3 %collective-permute-start.2 = (bf16[64,1024]{1,0:T(8,128)(2,1)S(1)}, bf16[64,1024]{1,0:T(8,128)(2,1)S(1)}, u32[]{:S(2)}, u32[]{:S(2)}) collective-permute-start(bf16[64,1024]{1,0:T(8,128)(2,1)S(1)} %get-tuple-element.46), channel_id=1, source_target_pairs={{1,0},{2,1},{3,2},{4,3},{5,4},{6,5},{7,6},{8,7},{9,8},{10,9},{11,1... | collective-permute-start | bytes 393224 | tf_op jit(solution)/shard_map/ppermute | solution.py:480
  19.0 6.6 %collective-permute-start.3 = (bf16[64,1024]{1,0:T(8,128)(2,1)S(1)}, bf16[64,1024]{1,0:T(8,128)(2,1)S(1)}, u32[]{:S(2)}, u32[]{:S(2)}) collective-permute-start(bf16[64,1024]{1,0:T(8,128)(2,1)S(1)} %get-tuple-element.47), channel_id=1, source_target_pairs={{1,0},{2,1},{3,2},{4,3},{5,4},{6,5},{7,6},{8,7},{9,8},{10,9},{11,1... | collective-permute-start | bytes 393224 | tf_op jit(solution)/shard_map/ppermute | solution.py:480

commit v20 on v17

--- a/solution.py
+++ b/solution.py
@@ -542,7 +542,6 @@
         ],
         (0, 0, 0, 0), 18 * tok * width,
     )(*in_hbm(lengths, query_in, key_in, value_in, grad_out))
-    far = neighbour(far, 1)
 
     attn, gq, gk_part, gv_part = call(
         functools.partial(own_kernel, prior, step), "own_block",
@@ -551,7 +550,9 @@
         (width // HEAD_DIM, tok - prior, tok, 6), 18 * tok * width,
     )(*in_vmem(own_bias, q, k, v, do))
 
-    near_bias, attn = lax.optimization_barrier((near_bias, attn))
+    far, near_bias, attn = lax.optimization_barrier((far, near_bias, attn))
+    far = neighbour(far, 1)
+
     backs = call(
         functools.partial(near_kernel, prior), "near_terms",
         [inside] * 7, [inside] * groups, [near16(prior, step)] * groups, (),

time: 26.3 us -> 27.5 us (1.046)
  waiting for transfers between devices: 6.02 us -> 7.27 us
    ppermute x4, waiting for transfers between devices: 6.02 us -> 7.27 us  [neighbour(): return lax.ppermute(value, ('seq', 'head'), pairs)]
  transfers between devices with their start and end apart: 4 -> 4, of which waited for: 3 -> 3; matrix products, arithmetic and copies ran while one was open for 0% -> 0% of each run, Pallas kernels for 23% -> 22%
where the time goes in v20:
time: 27.5 us; the launch traced here: 27.3 us
  starting transfers between devices  10.8 us (39%)
  Pallas kernels  8.5 us (31%)
  waiting for transfers between devices  7.27 us (26%)
  between operations  0.7 us (3%)
    ppermute x4, starting transfers between devices, neighbour(): return lax.ppermute(value, ('seq', 'head'), pairs)  10.8 us
    ppermute x4, waiting for transfers between devices, neighbour(): return lax.ppermute(value, ('seq', 'head'), pairs)  7.27 us
    pallas_call x1, Pallas kernels, halo_shards(): call(functools.partial(lead_kernel, prior, step), 'lead_rows', [inside] *...  2.19 us
    pallas_call x1, Pallas kernels, halo_shards(): call(functools.partial(ready_kernel, prior), 'operands', [anywhere] * 5,...  1.68 us
    pallas_call x1, Pallas kernels, halo_shards(): call(functools.partial(own_kernel, prior, step), 'own_block', [inside] *...  1.49 us
    pallas_call x1, Pallas kernels, halo_shards(): call(functools.partial(tail_kernel, prior), 'tail_keys', [inside] * (5 +...  1.42 us
    pallas_call x1, Pallas kernels, halo_shards(): call(functools.partial(pack_kernel, prior), 'near_keys', [anywhere] * 2,...  0.99 us
    pallas_call x1, Pallas kernels, halo_shards(): call(functools.partial(near_kernel, prior), 'near_terms', [inside] * 7, [...  0.73 us
  transfers between devices with their start and end apart: 4, of which 3 were waited for; matrix products, arithmetic and copies ran while one was open for 0% of the time, Pallas kernels for 22%

profile of v20, /device:TPU:0, one launch (start us, length us, event | category | flops | bytes accessed | tf_op | source)
XLA Modules:
  0.0 27.3 jit_solution(2961481846741228371)
XLA Ops:
  0.6 1.0 %near_keys.1 = bf16[64,2048]{1,0:T(8,128)(2,1)S(1)} custom-call(bf16[128,2048]{1,0:T(8,128)(2,1)} %k_ref.1, bf16[128,2048]{1,0:T(8,128)(2,1)} %v_ref.1), custom_call_target="tpu_custom_call" | custom-call | bytes 524288 | tf_op jit(solution)/shard_map/near_keys/pallas_call | solution.py:525
  1.6 4.9 %collective-permute-start = (bf16[64,2048]{1,0:T(8,128)(2,1)S(1)}, bf16[64,2048]{1,0:T(8,128)(2,1)S(1)}, u32[]{:S(2)}, u32[]{:S(2)}) collective-permute-start(bf16[64,2048]{1,0:T(8,128)(2,1)S(1)} %near_keys.1), channel_id=1, source_target_pairs={{0,1},{1,2},{2,3},{3,4},{4,5},{5,6},{6,7},{7,8},{8,9},{9,10},{10,1... | collective-permute-start | bytes 786440 | tf_op jit(solution)/shard_map/ppermute | solution.py:480
  6.5 1.7 %operands.1 = (bf16[64,2048]{1,0:T(8,128)(2,1)S(1)}, bf16[128,2048]{1,0:T(8,128)(2,1)S(1)}, bf16[128,2048]{1,0:T(8,128)(2,1)S(1)}, bf16[128,2048]{1,0:T(8,128)(2...) custom-call(s32[1,128]{1,0:T(1,128)} %bitcast.1, ...), custom_call_target="tpu_custom_call" | custom-call | bytes 4718592 | tf_op jit(solution)/shard_map/operands/pallas_call | solution.py:533
  8.2 1.5 %own_block.1 = (bf16[64,2048]{1,0:T(8,128)(2,1)S(1)}, bf16[64,2048]{1,0:T(8,128)(2,1)S(1)}, f32[128,2048]{1,0:T(8,128)S(1)}, f32[128,2048]{1,0:T(8,128)S(1)}) custom-call(f32[128,128]{1,0:T(8,128)S(1)} %get-tuple-element.35.bias_ref, bf16[128,2048]{1,0:T(8,128)(2,1)S(1)} %get-tuple-element.29.q_ref, bf16[128,2048]{1,0:T(8,128)(2,1)S(1)} %get-tuple-element.30.k_ref, ...), custom_call_target="tpu_custom_call" | custom-call | flops 201326592 | bytes 4718592 | tf_op jit(solution)/shard_map/own_block/pallas_call | solution.py:546
  9.7 3.4 %collective-permute-start.1 = (bf16[64,2048]{1,0:T(8,128)(2,1)S(1)}, bf16[64,2048]{1,0:T(8,128)(2,1)S(1)}, u32[]{:S(2)}, u32[]{:S(2)}) collective-permute-start(bf16[64,2048]{1,0:T(8,128)(2,1)S(1)} %get-tuple-element.37), channel_id=1, source_target_pairs={{0,1},{1,2},{2,3},{3,4},{4,5},{5,6},{6,7},{7,8},{8,9},{9,10},{10,1... | collective-permute-start | bytes 786440 | tf_op jit(solution)/shard_map/ppermute | solution.py:480
  13.1 0.0 collective-permute-done.near_ref
  13.1 0.7 %near_terms.1 = (bf16[64,1024]{1,0:T(8,128)(2,1)S(1)}, bf16[64,1024]{1,0:T(8,128)(2,1)S(1)}) custom-call(f32[96,128]{1,0:T(8,128)S(1)} %get-tuple-element.45.near_bias_ref, f32[128,128]{1,0:T(8,128)S(1)} %get-tuple-element.28.bias_ref.lead_bias_ref, bf16[128,2048]{1,0:T(8,128)(2,1)S(1)} %get-tuple-element.29.q_ref, ...), custom_call_target="tpu_custom_call" | custom-call | flops 75497472 | bytes 2097152 | tf_op jit(solution)/shard_map/near_terms/pallas_call | solution.py:556
  13.8 1.3 %collective-permute-start.2 = (bf16[64,1024]{1,0:T(8,128)(2,1)S(1)}, bf16[64,1024]{1,0:T(8,128)(2,1)S(1)}, u32[]{:S(2)}, u32[]{:S(2)}) collective-permute-start(bf16[64,1024]{1,0:T(8,128)(2,1)S(1)} %get-tuple-element.46), channel_id=1, source_target_pairs={{1,0},{2,1},{3,2},{4,3},{5,4},{6,5},{7,6},{8,7},{9,8},{10,9},{11,1... | collective-permute-start | bytes 393224 | tf_op jit(solution)/shard_map/ppermute | solution.py:480
  15.1 1.3 %collective-permute-start.3 = (bf16[64,1024]{1,0:T(8,128)(2,1)S(1)}, bf16[64,1024]{1,0:T(8,128)(2,1)S(1)}, u32[]{:S(2)}, u32[]{:S(2)}) collective-permute-start(bf16[64,1024]{1,0:T(8,128)(2,1)S(1)} %get-tuple-element.47), channel_id=1, source_target_pairs={{1,0},{2,1},{3,2},{4,3},{5,4},{6,5},{7,6},{8,7},{9,8},{10,9},{11,1... | collective-permute-start | bytes 393224 | tf_op jit(solution)/shard_map/ppermute | solution.py:480
  16.4 1.9 %collective-permute-done.1.far_ref = bf16[64,2048]{1,0:T(8,128)(2,1)S(1)} collective-permute-done((bf16[64,2048]{1,0:T(8,128)(2,1)S(1)}, bf16[64,2048]{1,0:T(8,128)(2,1)S(1)}, u32[]{:S(2)}, u32[]{:S(2)}) %collective-permute-start.1) | collective-permute-done | bytes 262176 | tf_op jit(solution)/shard_map/ppermute | solution.py:480
  18.3 2.2 %lead_rows.1 = (bf16[128,2048]{1,0:T(8,128)(2,1)}, bf16[128,2048]{1,0:T(8,128)(2,1)}, bf16[128,2048]{1,0:T(8,128)(2,1)}, bf16[128,2048]{1,0:T(8,128)(2,1)}) custom-call(f32[128,128]{1,0:T(8,128)S(1)} %get-tuple-element.28.bias_ref.lead_bias_ref, bf16[128,2048]{1,0:T(8,128)(2,1)S(1)} %get-tuple-element.29.q_ref, ...), custom_call_target="tpu_custom_call" | custom-call | flops 201326592 | bytes 5242880 | tf_op jit(solution)/shard_map/lead_rows/pallas_call | solution.py:563
  20.5 2.9 %collective-permute-done.2.refs_0_ = bf16[64,1024]{1,0:T(8,128)(2,1)S(1)} collective-permute-done((bf16[64,1024]{1,0:T(8,128)(2,1)S(1)}, bf16[64,1024]{1,0:T(8,128)(2,1)S(1)}, u32[]{:S(2)}, u32[]{:S(2)}) %collective-permute-start.2) | collective-permute-done | bytes 131104 | tf_op jit(solution)/shard_map/ppermute | solution.py:480
  23.4 2.5 %collective-permute-done.3.refs_1_ = bf16[64,1024]{1,0:T(8,128)(2,1)S(1)} collective-permute-done((bf16[64,1024]{1,0:T(8,128)(2,1)S(1)}, bf16[64,1024]{1,0:T(8,128)(2,1)S(1)}, u32[]{:S(2)}, u32[]{:S(2)}) %collective-permute-start.3) | collective-permute-done | bytes 131104 | tf_op jit(solution)/shard_map/ppermute | solution.py:480
  25.9 1.4 %tail_keys.1 = (bf16[128,2048]{1,0:T(8,128)(2,1)}, bf16[128,2048]{1,0:T(8,128)(2,1)}) custom-call(f32[64,128]{1,0:T(8,128)S(1)} %get-tuple-element.44.bias_ref, bf16[128,2048]{1,0:T(8,128)(2,1)S(1)} %get-tuple-element.30.k_ref, bf16[128,2048]{1,0:T(8,128)(2,1)S(1)} %get-tuple-element.31.v_ref, ...), custom_call_target="tpu_custom_call", output_to_operand_aliasing={{0}: (7, {}), {1}: (8, {})} | custom-call | flops 33554432 | bytes 2621440 | tf_op jit(solution)/shard_map/tail_keys/pallas_call | solution.py:571
Async XLA Ops:
  1.6 11.5 %collective-permute-start = (bf16[64,2048]{1,0:T(8,128)(2,1)S(1)}, bf16[64,2048]{1,0:T(8,128)(2,1)S(1)}, u32[]{:S(2)}, u32[]{:S(2)}) collective-permute-start(bf16[64,2048]{1,0:T(8,128)(2,1)S(1)} %near_keys.1), channel_id=1, source_target_pairs={{0,1},{1,2},{2,3},{3,4},{4,5},{5,6},{6,7},{7,8},{8,9},{9,10},{10,1... | collective-permute-start | bytes 786440 | tf_op jit(solution)/shard_map/ppermute | solution.py:480
  9.7 8.7 %collective-permute-start.1 = (bf16[64,2048]{1,0:T(8,128)(2,1)S(1)}, bf16[64,2048]{1,0:T(8,128)(2,1)S(1)}, u32[]{:S(2)}, u32[]{:S(2)}) collective-permute-start(bf16[64,2048]{1,0:T(8,128)(2,1)S(1)} %get-tuple-element.37), channel_id=1, source_target_pairs={{0,1},{1,2},{2,3},{3,4},{4,5},{5,6},{6,7},{7,8},{8,9},{9,10},{10,1... | collective-permute-start | bytes 786440 | tf_op jit(solution)/shard_map/ppermute | solution.py:480
  13.8 9.6 %collective-permute-start.2 = (bf16[64,1024]{1,0:T(8,128)(2,1)S(1)}, bf16[64,1024]{1,0:T(8,128)(2,1)S(1)}, u32[]{:S(2)}, u32[]{:S(2)}) collective-permute-start(bf16[64,1024]{1,0:T(8,128)(2,1)S(1)} %get-tuple-element.46), channel_id=1, source_target_pairs={{1,0},{2,1},{3,2},{4,3},{5,4},{6,5},{7,6},{8,7},{9,8},{10,9},{11,1... | collective-permute-start | bytes 393224 | tf_op jit(solution)/shard_map/ppermute | solution.py:480
  15.1 10.8 %collective-permute-start.3 = (bf16[64,1024]{1,0:T(8,128)(2,1)S(1)}, bf16[64,1024]{1,0:T(8,128)(2,1)S(1)}, u32[]{:S(2)}, u32[]{:S(2)}) collective-permute-start(bf16[64,1024]{1,0:T(8,128)(2,1)S(1)} %get-tuple-element.47), channel_id=1, source_target_pairs={{1,0},{2,1},{3,2},{4,3},{5,4},{6,5},{7,6},{8,7},{9,8},{10,9},{11,1... | collective-permute-start | bytes 393224 | tf_op jit(solution)/shard_map/ppermute | solution.py:480

commit v21 on v17

--- a/solution.py
+++ b/solution.py
@@ -432,44 +432,68 @@
         copy.wait()
 
 
-def tail_kernel(prior, bias_ref, k_ref, v_ref, gk_part_ref, gv_part_ref, *refs):
-    *after_refs, _, _, gk_hbm, gv_hbm, gk_ref, gv_ref, sems = refs
-    tok, width = k_ref.shape
-    half = prior // 2
+def tail_half(prior, low, bias_ref, k_ref, v_ref, gk_part_ref, gv_part_ref, after_ref):
+    tok, half = k_ref.shape[0], prior // 2
     far = bias_ref[half - 1 : half, 0:1] == 0.0
     bias = jnp.where(far, bias_ref[...], MASKED)
     first, second, last = slice(0, half), slice(half, prior), slice(tok - prior, tok)
-    columns = head_columns(0, width, 4)
-    afters = [
-        (after_ref, p) for after_ref in after_refs for p in head_columns(0, after_ref.shape[1], 4)
-    ]
-    queries = [side_by_side(after_ref[first, p]) for after_ref, p in afters]
-    cotangents = [side_by_side(after_ref[second, p]) for after_ref, p in afters]
+    places = head_columns(0, after_ref.shape[1], 4)
+    columns = head_columns(low, low + after_ref.shape[1], 4)
+    queries = [side_by_side(after_ref[first, p]) for p in places]
+    cotangents = [side_by_side(after_ref[second, p]) for p in places]
     pairs = [
         score_pair(k_ref[last, c], q, v_ref[last, c], do, bias)
         for c, q, do in zip(columns, queries, cotangents)
     ]
     own = [
-        (joined(after_ref[half - 1 : half, p]), joined(after_ref[prior - 1 : prior, p]))
-        for after_ref, p in afters
+        (joined(after_ref[half - 16 : half, p][15:]), joined(after_ref[prior - 16 : prior, p][15:]))
+        for p in places
     ]
     weights, grads = merged_columns(pairs, own)
-    copies = []
-    for at, (ref, hbm, part_ref, lefts, rights, rows) in enumerate(
-        (
-            (gv_ref, gv_hbm, gv_part_ref, weights, cotangents, second),
-            (gk_ref, gk_hbm, gk_part_ref, grads, queries, first),
-        )
-    ):
-        for (after_ref, p), c, left, right in zip(afters, columns, lefts, rights):
+
+    def fill(ref, part_ref, lefts, rights, rows):
+        for p, c, left, right in zip(places, columns, lefts, rights):
             total = part_ref[last, c] + dot(left, right, 1, 0)
             terms = jnp.where(far, 0.0, after_ref[rows, p].astype(jnp.float32))
-            ref[first, c] = total[first].astype(jnp.bfloat16)
-            ref[second, c] = (total[second] + terms).astype(jnp.bfloat16)
-        copies.append(
-            pltpu.make_async_copy(ref, hbm.at[pl.ds(tok - prior, prior), :], sems.at[at])
-        )
+            ref[first, p] = total[first].astype(jnp.bfloat16)
+            ref[second, p] = (total[second] + terms).astype(jnp.bfloat16)
+
+    return (
+        lambda ref: fill(ref, gv_part_ref, weights, cotangents, second),
+        lambda ref: fill(ref, gk_part_ref, grads, queries, first),
+    )
+
+
+def tail_kernel(prior, bias_ref, k_ref, v_ref, gk_part_ref, gv_part_ref, after_ref, gk_ref, gv_ref):
+    fill_gv, fill_gk = tail_half(
+        prior, 0, bias_ref, k_ref, v_ref, gk_part_ref, gv_part_ref, after_ref
+    )
+    fill_gv(gv_ref)
+    fill_gk(gk_ref)
+
+
+def last_kernel(
+    prior, bias_ref, k_ref, v_ref, gk_part_ref, gv_part_ref, after_ref, gk_first_ref, gv_first_ref,
+    gk_in, gv_in, gk_hbm, gv_hbm, gk_ref, gv_ref, sems,
+):
+    rows = pl.ds(k_ref.shape[0] - prior, prior)
+    low = gk_first_ref.shape[1]
+    copies = []
+
+    def send(ref, hbm, start):
+        cols = pl.ds(start, ref.shape[1])
+        copies.append(pltpu.make_async_copy(ref, hbm.at[rows, cols], sems.at[len(copies)]))
         copies[-1].start()
+
+    send(gv_first_ref, gv_hbm, 0)
+    send(gk_first_ref, gk_hbm, 0)
+    fill_gv, fill_gk = tail_half(
+        prior, low, bias_ref, k_ref, v_ref, gk_part_ref, gv_part_ref, after_ref
+    )
+    fill_gv(gv_ref)
+    send(gv_ref, gv_hbm, low)
+    fill_gk(gk_ref)
+    send(gk_ref, gk_hbm, low)
     for copy in copies:
         copy.wait()
 
@@ -554,7 +578,7 @@
     near_bias, attn = lax.optimization_barrier((near_bias, attn))
     backs = call(
         functools.partial(near_kernel, prior), "near_terms",
-        [inside] * 7, [inside] * groups, [near16(prior, step)] * groups, (),
+        [inside] * 7, [inside] * 2, [near16(prior, width // 2)] * 2, (),
         (width // HEAD_DIM, prior, prior + prior // 2, 3), 8 * tok * width,
     )(*in_vmem(near_bias, lead_bias, q, k, v, do, near))
     backs = [neighbour(back, -1) for back in backs]
@@ -567,13 +591,18 @@
         (width // HEAD_DIM, prior, 2 * prior, 6), 20 * tok * width,
     )(*in_vmem(lead_bias, q, k, v, do, near, far, gk_part, gv_part, attn, gq))
 
+    here = in_vmem(tail_bias, k, v, gk_part, gv_part)
+    work = (width // HEAD_DIM // 2, prior, prior // 2, 4)
+    halves = call(
+        functools.partial(tail_kernel, prior), "tail_keys",
+        [inside] * 6, [inside] * 2, [near16(prior, width // 2)] * 2, (), work, 4 * tok * width,
+    )(*here, *in_vmem(backs[0]))
     gk, gv = call(
-        functools.partial(tail_kernel, prior), "tail_keys",
-        [inside] * (5 + groups) + [anywhere] * 2, [anywhere] * 2, [full16] * 2,
-        [near16(prior, width)] * 2 + [pltpu.SemaphoreType.DMA((2,))],
-        (width // HEAD_DIM, prior, prior // 2, 4), 10 * tok * width,
-        {5 + groups: 0, 6 + groups: 1},
-    )(*in_vmem(tail_bias, k, v, gk_part, gv_part, *backs), gk, gv)
+        functools.partial(last_kernel, prior), "last_keys",
+        [inside] * 8 + [anywhere] * 2, [anywhere] * 2, [full16] * 2,
+        [near16(prior, width // 2)] * 2 + [pltpu.SemaphoreType.DMA((4,))],
+        work, 6 * tok * width, {8: 0, 9: 1},
+    )(*here, *in_vmem(backs[1], *halves), gk, gv)
     return (attn, gq, gk, gv)
 
 

time: 26.3 us -> 26.1 us (level)
  waiting for transfers between devices: 6.02 us -> 5.52 us
  Pallas kernels: 8.49 us -> 8.77 us
    ppermute x4, waiting for transfers between devices: 6.02 us -> 5.52 us  [neighbour(): return lax.ppermute(value, ('seq', 'head'), pairs)]
    pallas_call x1 -> x2, Pallas kernels: 1.42 us -> 1.69 us  [the longest x1 1.19 us: halo_shards(): call(functools.partial(last_kernel, prior), 'last_keys', [inside] * 8 + [...]
  transfers between devices with their start and end apart: 4 -> 4, of which waited for: 3 -> 3; matrix products, arithmetic and copies ran while one was open for 0% -> 0% of each run, Pallas kernels for 23% -> 26%
where the time goes in v21:
time: 26.1 us; the launch traced here: 25.8 us
  starting transfers between devices  10.8 us (41%)
  Pallas kernels  8.77 us (34%)
  waiting for transfers between devices  5.52 us (21%)
  between operations  0.71 us (3%)
    ppermute x4, starting transfers between devices, neighbour(): return lax.ppermute(value, ('seq', 'head'), pairs)  10.8 us
    ppermute x4, waiting for transfers between devices, neighbour(): return lax.ppermute(value, ('seq', 'head'), pairs)  5.52 us
    pallas_call x1, Pallas kernels, halo_shards(): call(functools.partial(lead_kernel, prior, step), 'lead_rows', [inside] *...  2.2 us
    pallas_call x1, Pallas kernels, halo_shards(): call(functools.partial(ready_kernel, prior), 'operands', [anywhere] * 5,...  1.68 us
    pallas_call x1, Pallas kernels, halo_shards(): call(functools.partial(own_kernel, prior, step), 'own_block', [inside] *...  1.49 us
    pallas_call x1, Pallas kernels, halo_shards(): call(functools.partial(last_kernel, prior), 'last_keys', [inside] * 8 + [...  1.19 us
    pallas_call x1, Pallas kernels, halo_shards(): call(functools.partial(pack_kernel, prior), 'near_keys', [anywhere] * 2,...  0.99 us
    pallas_call x1, Pallas kernels, halo_shards(): call(functools.partial(near_kernel, prior), 'near_terms', [inside] * 7, [...  0.73 us
  transfers between devices with their start and end apart: 4, of which 3 were waited for; matrix products, arithmetic and copies ran while one was open for 0% of the time, Pallas kernels for 26%

profile of v21, /device:TPU:0, one launch (start us, length us, event | category | flops | bytes accessed | tf_op | source)
XLA Modules:
  0.0 25.8 jit_solution(2649745682123410106)
XLA Ops:
  0.6 1.0 %near_keys.1 = bf16[64,2048]{1,0:T(8,128)(2,1)S(1)} custom-call(bf16[128,2048]{1,0:T(8,128)(2,1)} %k_ref.1, bf16[128,2048]{1,0:T(8,128)(2,1)} %v_ref.1), custom_call_target="tpu_custom_call" | custom-call | bytes 524288 | tf_op jit(solution)/shard_map/near_keys/pallas_call | solution.py:549
  1.6 4.9 %collective-permute-start = (bf16[64,2048]{1,0:T(8,128)(2,1)S(1)}, bf16[64,2048]{1,0:T(8,128)(2,1)S(1)}, u32[]{:S(2)}, u32[]{:S(2)}) collective-permute-start(bf16[64,2048]{1,0:T(8,128)(2,1)S(1)} %near_keys.1), channel_id=1, source_target_pairs={{0,1},{1,2},{2,3},{3,4},{4,5},{5,6},{6,7},{7,8},{8,9},{9,10},{10,1... | collective-permute-start | bytes 786440 | tf_op jit(solution)/shard_map/ppermute | solution.py:504
  6.5 1.7 %operands.1 = (bf16[64,2048]{1,0:T(8,128)(2,1)S(1)}, bf16[128,2048]{1,0:T(8,128)(2,1)S(1)}, bf16[128,2048]{1,0:T(8,128)(2,1)S(1)}, bf16[128,2048]{1,0:T(8,128)(2...) custom-call(s32[1,128]{1,0:T(1,128)} %bitcast.1, ...), custom_call_target="tpu_custom_call" | custom-call | bytes 4718592 | tf_op jit(solution)/shard_map/operands/pallas_call | solution.py:557
  8.2 3.4 %collective-permute-start.1 = (bf16[64,2048]{1,0:T(8,128)(2,1)S(1)}, bf16[64,2048]{1,0:T(8,128)(2,1)S(1)}, u32[]{:S(2)}, u32[]{:S(2)}) collective-permute-start(bf16[64,2048]{1,0:T(8,128)(2,1)S(1)} %get-tuple-element.34), channel_id=1, source_target_pairs={{0,1},{1,2},{2,3},{3,4},{4,5},{5,6},{6,7},{7,8},{8,9},{9,10},{10,1... | collective-permute-start | bytes 786440 | tf_op jit(solution)/shard_map/ppermute | solution.py:504
  11.6 1.5 %own_block.1 = (bf16[64,2048]{1,0:T(8,128)(2,1)S(1)}, bf16[64,2048]{1,0:T(8,128)(2,1)S(1)}, f32[128,2048]{1,0:T(8,128)S(1)}, f32[128,2048]{1,0:T(8,128)S(1)}) custom-call(f32[128,128]{1,0:T(8,128)S(1)} %get-tuple-element.35.bias_ref, bf16[128,2048]{1,0:T(8,128)(2,1)S(1)} %get-tuple-element.30.q_ref, bf16[128,2048]{1,0:T(8,128)(2,1)S(1)} %get-tuple-element.31.k_ref, ...), custom_call_target="tpu_custom_call" | custom-call | flops 201326592 | bytes 4718592 | tf_op jit(solution)/shard_map/own_block/pallas_call | solution.py:571
  13.1 0.0 collective-permute-done.near_ref
  13.1 0.7 %near_terms.1 = (bf16[64,1024]{1,0:T(8,128)(2,1)S(1)}, bf16[64,1024]{1,0:T(8,128)(2,1)S(1)}) custom-call(f32[96,128]{1,0:T(8,128)S(1)} %get-tuple-element.45.near_bias_ref, f32[128,128]{1,0:T(8,128)S(1)} %get-tuple-element.29.bias_ref.lead_bias_ref, bf16[128,2048]{1,0:T(8,128)(2,1)S(1)} %get-tuple-element.30.q_ref, ...), custom_call_target="tpu_custom_call" | custom-call | flops 75497472 | bytes 2097152 | tf_op jit(solution)/shard_map/near_terms/pallas_call | solution.py:579
  13.8 1.3 %collective-permute-start.3 = (bf16[64,1024]{1,0:T(8,128)(2,1)S(1)}, bf16[64,1024]{1,0:T(8,128)(2,1)S(1)}, u32[]{:S(2)}, u32[]{:S(2)}) collective-permute-start(bf16[64,1024]{1,0:T(8,128)(2,1)S(1)} %get-tuple-element.47), channel_id=1, source_target_pairs={{1,0},{2,1},{3,2},{4,3},{5,4},{6,5},{7,6},{8,7},{9,8},{10,9},{11,1... | collective-permute-start | bytes 393224 | tf_op jit(solution)/shard_map/ppermute | solution.py:504
  15.1 1.3 %collective-permute-start.2 = (bf16[64,1024]{1,0:T(8,128)(2,1)S(1)}, bf16[64,1024]{1,0:T(8,128)(2,1)S(1)}, u32[]{:S(2)}, u32[]{:S(2)}) collective-permute-start(bf16[64,1024]{1,0:T(8,128)(2,1)S(1)} %get-tuple-element.46), channel_id=1, source_target_pairs={{1,0},{2,1},{3,2},{4,3},{5,4},{6,5},{7,6},{8,7},{9,8},{10,9},{11,1... | collective-permute-start | bytes 393224 | tf_op jit(solution)/shard_map/ppermute | solution.py:504
  16.4 1.2 %collective-permute-done.1.far_ref = bf16[64,2048]{1,0:T(8,128)(2,1)S(1)} collective-permute-done((bf16[64,2048]{1,0:T(8,128)(2,1)S(1)}, bf16[64,2048]{1,0:T(8,128)(2,1)S(1)}, u32[]{:S(2)}, u32[]{:S(2)}) %collective-permute-start.1) | collective-permute-done | bytes 262176 | tf_op jit(solution)/shard_map/ppermute | solution.py:504
  17.6 2.2 %lead_rows.1 = (bf16[128,2048]{1,0:T(8,128)(2,1)}, bf16[128,2048]{1,0:T(8,128)(2,1)}, bf16[128,2048]{1,0:T(8,128)(2,1)}, bf16[128,2048]{1,0:T(8,128)(2,1)}) custom-call(f32[128,128]{1,0:T(8,128)S(1)} %get-tuple-element.29.bias_ref.lead_bias_ref, bf16[128,2048]{1,0:T(8,128)(2,1)S(1)} %get-tuple-element.30.q_ref, ...), custom_call_target="tpu_custom_call" | custom-call | flops 201326592 | bytes 5242880 | tf_op jit(solution)/shard_map/lead_rows/pallas_call | solution.py:586
  19.8 2.6 %collective-permute-done.3.after_ref = bf16[64,1024]{1,0:T(8,128)(2,1)S(1)} collective-permute-done((bf16[64,1024]{1,0:T(8,128)(2,1)S(1)}, bf16[64,1024]{1,0:T(8,128)(2,1)S(1)}, u32[]{:S(2)}, u32[]{:S(2)}) %collective-permute-start.3) | collective-permute-done | bytes 131104 | tf_op jit(solution)/shard_map/ppermute | solution.py:504
  22.4 0.5 %tail_keys.1 = (bf16[64,1024]{1,0:T(8,128)(2,1)S(1)}, bf16[64,1024]{1,0:T(8,128)(2,1)S(1)}) custom-call(f32[64,128]{1,0:T(8,128)S(1)} %get-tuple-element.44.bias_ref, bf16[128,2048]{1,0:T(8,128)(2,1)S(1)} %get-tuple-element.31.k_ref, bf16[128,2048]{1,0:T(8,128)(2,1)S(1)} %get-tuple-element.32.v_ref, f32[128,2048]{1,0:T(8,128)S(1)} %get-tuple-element.36.gk_part_ref, ...), custom_call_target="tpu_custom_call" | custom-call | flops 16777216 | bytes 1048576 | tf_op jit(solution)/shard_map/tail_keys/pallas_call | solution.py:596
  22.9 1.7 %collective-permute-done.2.after_ref = bf16[64,1024]{1,0:T(8,128)(2,1)S(1)} collective-permute-done((bf16[64,1024]{1,0:T(8,128)(2,1)S(1)}, bf16[64,1024]{1,0:T(8,128)(2,1)S(1)}, u32[]{:S(2)}, u32[]{:S(2)}) %collective-permute-start.2) | collective-permute-done | bytes 131104 | tf_op jit(solution)/shard_map/ppermute | solution.py:504
  24.6 1.2 %last_keys.1 = (bf16[128,2048]{1,0:T(8,128)(2,1)}, bf16[128,2048]{1,0:T(8,128)(2,1)}) custom-call(f32[64,128]{1,0:T(8,128)S(1)} %get-tuple-element.44.bias_ref, bf16[128,2048]{1,0:T(8,128)(2,1)S(1)} %get-tuple-element.31.k_ref, bf16[128,2048]{1,0:T(8,128)(2,1)S(1)} %get-tuple-element.32.v_ref, ...), custom_call_target="tpu_custom_call", output_to_operand_aliasing={{0}: (8, {}), {1}: (9, {})} | custom-call | flops 16777216 | bytes 1572864 | tf_op jit(solution)/shard_map/last_keys/pallas_call | solution.py:600
Async XLA Ops:
  1.6 11.5 %collective-permute-start = (bf16[64,2048]{1,0:T(8,128)(2,1)S(1)}, bf16[64,2048]{1,0:T(8,128)(2,1)S(1)}, u32[]{:S(2)}, u32[]{:S(2)}) collective-permute-start(bf16[64,2048]{1,0:T(8,128)(2,1)S(1)} %near_keys.1), channel_id=1, source_target_pairs={{0,1},{1,2},{2,3},{3,4},{4,5},{5,6},{6,7},{7,8},{8,9},{9,10},{10,1... | collective-permute-start | bytes 786440 | tf_op jit(solution)/shard_map/ppermute | solution.py:504
  8.2 9.5 %collective-permute-start.1 = (bf16[64,2048]{1,0:T(8,128)(2,1)S(1)}, bf16[64,2048]{1,0:T(8,128)(2,1)S(1)}, u32[]{:S(2)}, u32[]{:S(2)}) collective-permute-start(bf16[64,2048]{1,0:T(8,128)(2,1)S(1)} %get-tuple-element.34), channel_id=1, source_target_pairs={{0,1},{1,2},{2,3},{3,4},{4,5},{5,6},{6,7},{7,8},{8,9},{9,10},{10,1... | collective-permute-start | bytes 786440 | tf_op jit(solution)/shard_map/ppermute | solution.py:504
  13.8 8.6 %collective-permute-start.3 = (bf16[64,1024]{1,0:T(8,128)(2,1)S(1)}, bf16[64,1024]{1,0:T(8,128)(2,1)S(1)}, u32[]{:S(2)}, u32[]{:S(2)}) collective-permute-start(bf16[64,1024]{1,0:T(8,128)(2,1)S(1)} %get-tuple-element.47), channel_id=1, source_target_pairs={{1,0},{2,1},{3,2},{4,3},{5,4},{6,5},{7,6},{8,7},{9,8},{10,9},{11,1... | collective-permute-start | bytes 393224 | tf_op jit(solution)/shard_map/ppermute | solution.py:504
  15.1 9.5 %collective-permute-start.2 = (bf16[64,1024]{1,0:T(8,128)(2,1)S(1)}, bf16[64,1024]{1,0:T(8,128)(2,1)S(1)}, u32[]{:S(2)}, u32[]{:S(2)}) collective-permute-start(bf16[64,1024]{1,0:T(8,128)(2,1)S(1)} %get-tuple-element.46), channel_id=1, source_target_pairs={{1,0},{2,1},{3,2},{4,3},{5,4},{6,5},{7,6},{8,7},{9,8},{10,9},{11,1... | collective-permute-start | bytes 393224 | tf_op jit(solution)/shard_map/ppermute | solution.py:504

commit v22 on v21

--- a/solution.py
+++ b/solution.py
@@ -257,19 +257,19 @@
     return parts[:, :count] + parts[:, count : 2 * count] + parts[:, 2 * count : 3 * count]
 
 
-def pack_copies(prior, at, k_ref, v_ref, packed_ref, sems):
+def pack_copies(prior, at, low, k_ref, v_ref, packed_ref, sems):
     half, tok = prior // 2, k_ref.shape[0]
-    rows = pl.ds(tok - (at + 1) * half, half)
+    rows, cols = pl.ds(tok - (at + 1) * half, half), pl.ds(low, packed_ref.shape[1])
     return [
         pltpu.make_async_copy(
-            ref.at[rows, :], packed_ref.at[pl.ds(n * half, half), :], sems.at[n]
+            ref.at[rows, cols], packed_ref.at[pl.ds(n * half, half), :], sems.at[n]
         )
         for n, ref in enumerate((k_ref, v_ref))
     ]
 
 
 def pack_kernel(prior, k_ref, v_ref, near_ref, sems):
-    copies = pack_copies(prior, 0, k_ref, v_ref, near_ref, sems)
+    copies = pack_copies(prior, 0, 0, k_ref, v_ref, near_ref, sems)
     for copy in copies:
         copy.start()
     for copy in copies:
@@ -277,12 +277,14 @@
 
 
 def ready_kernel(
-    prior, len_hbm, q_hbm, k_hbm, v_hbm, do_hbm, far_ref, q_ref, k_ref, v_ref, do_ref,
-    own_bias_ref, near_bias_ref, lead_bias_ref, tail_bias_ref, len_ref, sems, far_sems, len_sem,
+    prior, len_hbm, q_hbm, k_hbm, v_hbm, do_hbm, far_ref, far_late_ref, q_ref, k_ref, v_ref, do_ref,
+    own_bias_ref, near_bias_ref, lead_bias_ref, tail_bias_ref, len_ref, sems, far_sems, far_late_sems,
+    len_sem,
 ):
     tok, half = k_ref.shape[0], prior // 2
     pairs = ((q_hbm, q_ref), (k_hbm, k_ref), (v_hbm, v_ref), (do_hbm, do_ref))
-    copies = pack_copies(prior, 1, k_hbm, v_hbm, far_ref, far_sems)
+    copies = pack_copies(prior, 1, 0, k_hbm, v_hbm, far_ref, far_sems)
+    copies += pack_copies(prior, 1, far_ref.shape[1], k_hbm, v_hbm, far_late_ref, far_late_sems)
     copies += [pltpu.make_async_copy(hbm, ref, sems.at[n]) for n, (hbm, ref) in enumerate(pairs)]
     len_copy = pltpu.make_async_copy(len_hbm, len_ref, len_sem)
     len_copy.start()
@@ -371,8 +373,8 @@
 
 
 def lead_kernel(
-    prior, step, bias_ref, q_ref, k_ref, v_ref, do_ref, near_ref, far_ref, gk_part_ref, gv_part_ref,
-    attn_late_ref, gq_late_ref, attn_hbm, gq_hbm, gk_hbm, gv_hbm,
+    prior, bias_ref, q_ref, k_ref, v_ref, do_ref, near_ref, far_ref, far_late_ref,
+    gk_part_ref, gv_part_ref, attn_late_ref, gq_late_ref, attn_hbm, gq_hbm, gk_hbm, gv_hbm,
     attn_ref, gq_ref, gk_ref, gv_ref, sems, late_sems,
 ):
     tok, width = q_ref.shape
@@ -386,27 +388,29 @@
     for copy in late_copies:
         copy.start()
 
+    step = far_ref.shape[1]
+
     def copies(at):
-        cols = pl.ds(pl.multiple_of(at * step, step), step)
+        cols = pl.ds(at * step, step)
         pairs = ((attn_ref, attn_hbm), (gq_ref, gq_hbm), (gk_ref, gk_hbm), (gv_ref, gv_hbm))
         return [
             pltpu.make_async_copy(ref.at[:, cols], hbm.at[pl.ds(0, prior), cols], sems.at[at, n])
             for n, (ref, hbm) in enumerate(pairs)
         ]
 
-    @pl.loop(0, width // step)
-    def _(at):
-        bias = bias_ref[...]
-        columns = pair_columns(at, step)
+    bias = bias_ref[...]
+    for at, far_part_ref in enumerate((far_ref, far_late_ref)):
+        columns = head_columns(at * step, (at + 1) * step, 2)
+        places = head_columns(0, step, 2)
         queries = [side_by_side(q_ref[early, c]) for c in columns]
         cotangents = [side_by_side(do_ref[early, c]) for c in columns]
         keys = [
-            jnp.concatenate([far_ref[first, c], near_ref[first, c], k_ref[early, c]], axis=0)
-            for c in columns
+            jnp.concatenate([far_part_ref[first, p], near_ref[first, c], k_ref[early, c]], axis=0)
+            for p, c in zip(places, columns)
         ]
         values = [
-            jnp.concatenate([far_ref[second, c], near_ref[second, c], v_ref[early, c]], axis=0)
-            for c in columns
+            jnp.concatenate([far_part_ref[second, p], near_ref[second, c], v_ref[early, c]], axis=0)
+            for p, c in zip(places, columns)
         ]
         pairs = [
             score_pair(k, q, v, do, bias)
@@ -425,7 +429,7 @@
         for copy in copies(at):
             copy.start()
 
-    for at in range(width // step):
+    for at in range(2):
         for copy in copies(at):
             copy.wait()
     for copy in late_copies:
@@ -516,7 +520,6 @@
     tok, width = query_in.shape
     prior = tok * lax.axis_size("head") // 8
     step = math.gcd(width, 8 * HEAD_DIM)
-    groups = width // step
     anywhere = pl.BlockSpec(memory_space=pl.ANY)
     inside = pl.BlockSpec(memory_space=pltpu.VMEM)
     full16 = jax.ShapeDtypeStruct((tok, width), jnp.bfloat16)
@@ -554,15 +557,16 @@
     near = neighbour(near, 1)
 
     lengths = module_lengths.reshape(1, -1)
-    far, q, k, v, do, own_bias, near_bias, lead_bias, tail_bias = call(
+    far, far_late, q, k, v, do, own_bias, near_bias, lead_bias, tail_bias = call(
         functools.partial(ready_kernel, prior), "operands",
-        [anywhere] * 5, [inside] * 9,
-        [near16(prior, width)] + [near16(tok, width)] * 4
+        [anywhere] * 5, [inside] * 10,
+        [near16(prior, width // 2)] * 2 + [near16(tok, width)] * 4
         + [near32(tok, 2 * prior), near32(prior + prior // 2, 2 * prior)]
         + [near32(2 * prior, 2 * prior), near32(prior, 2 * prior)],
         [
             pltpu.VMEM(lengths.shape, jnp.int32), pltpu.SemaphoreType.DMA((4,)),
-            pltpu.SemaphoreType.DMA((2,)), pltpu.SemaphoreType.DMA(()),
+            pltpu.SemaphoreType.DMA((2,)), pltpu.SemaphoreType.DMA((2,)),
+            pltpu.SemaphoreType.DMA(()),
         ],
         (0, 0, 0, 0), 18 * tok * width,
     )(*in_hbm(lengths, query_in, key_in, value_in, grad_out))
@@ -575,7 +579,9 @@
         (width // HEAD_DIM, tok - prior, tok, 6), 18 * tok * width,
     )(*in_vmem(own_bias, q, k, v, do))
 
-    near_bias, attn = lax.optimization_barrier((near_bias, attn))
+    far_late, near_bias, attn = lax.optimization_barrier((far_late, near_bias, attn))
+    far_late = neighbour(far_late, 1)
+
     backs = call(
         functools.partial(near_kernel, prior), "near_terms",
         [inside] * 7, [inside] * 2, [near16(prior, width // 2)] * 2, (),
@@ -584,12 +590,12 @@
     backs = [neighbour(back, -1) for back in backs]
 
     attn, gq, gk, gv = call(
-        functools.partial(lead_kernel, prior, step), "lead_rows",
-        [inside] * 11, [anywhere] * 4, [full16] * 4,
+        functools.partial(lead_kernel, prior), "lead_rows",
+        [inside] * 12, [anywhere] * 4, [full16] * 4,
         [near16(prior, width)] * 4
-        + [pltpu.SemaphoreType.DMA((groups, 4)), pltpu.SemaphoreType.DMA((2,))],
+        + [pltpu.SemaphoreType.DMA((2, 4)), pltpu.SemaphoreType.DMA((2,))],
         (width // HEAD_DIM, prior, 2 * prior, 6), 20 * tok * width,
-    )(*in_vmem(lead_bias, q, k, v, do, near, far, gk_part, gv_part, attn, gq))
+    )(*in_vmem(lead_bias, q, k, v, do, near, far, far_late, gk_part, gv_part, attn, gq))
 
     here = in_vmem(tail_bias, k, v, gk_part, gv_part)
     work = (width // HEAD_DIM // 2, prior, prior // 2, 4)

time: 26.1 us -> 28.4 us (1.088)
  starting transfers between devices: 10.8 us -> 14.2 us
  waiting for transfers between devices: 5.52 us -> 4.54 us
    ppermute x4 -> x5, starting transfers between devices: 10.8 us -> 14.2 us  [neighbour(): return lax.ppermute(value, ('seq', 'head'), pairs)]
    ppermute x4 -> x5, waiting for transfers between devices: 5.52 us -> 4.54 us  [neighbour(): return lax.ppermute(value, ('seq', 'head'), pairs)]
  transfers between devices with their start and end apart: 4 -> 5, of which waited for: 3 -> 2; matrix products, arithmetic and copies ran while one was open for 0% -> 0% of each run, Pallas kernels for 26% -> 23%
where the time goes in v22:
time: 28.4 us; the launch traced here: 28.1 us
  starting transfers between devices  14.2 us (50%)
  Pallas kernels  8.6 us (30%)
  waiting for transfers between devices  4.54 us (16%)
  between operations  0.73 us (3%)
    ppermute x5, starting transfers between devices, neighbour(): return lax.ppermute(value, ('seq', 'head'), pairs)  14.2 us
    ppermute x5, waiting for transfers between devices, neighbour(): return lax.ppermute(value, ('seq', 'head'), pairs)  4.54 us
    pallas_call x1, Pallas kernels, halo_shards(): call(functools.partial(lead_kernel, prior), 'lead_rows', [inside] * 12, [...  2.01 us
    pallas_call x1, Pallas kernels, halo_shards(): call(functools.partial(ready_kernel, prior), 'operands', [anywhere] * 5,...  1.7 us
    pallas_call x1, Pallas kernels, halo_shards(): call(functools.partial(own_kernel, prior, step), 'own_block', [inside] *...  1.49 us
    pallas_call x1, Pallas kernels, halo_shards(): call(functools.partial(last_kernel, prior), 'last_keys', [inside] * 8 + [...  1.19 us
    pallas_call x1, Pallas kernels, halo_shards(): call(functools.partial(pack_kernel, prior), 'near_keys', [anywhere] * 2,...  0.99 us
    pallas_call x1, Pallas kernels, halo_shards(): call(functools.partial(near_kernel, prior), 'near_terms', [inside] * 7, [...  0.73 us
  transfers between devices with their start and end apart: 5, of which 2 were waited for; matrix products, arithmetic and copies ran while one was open for 0% of the time, Pallas kernels for 23%

profile of v22, /device:TPU:0, one launch (start us, length us, event | category | flops | bytes accessed | tf_op | source)
XLA Modules:
  0.0 28.1 jit_solution(7229883716851943931)
XLA Ops:
  0.6 1.0 %near_keys.1 = bf16[64,2048]{1,0:T(8,128)(2,1)S(1)} custom-call(bf16[128,2048]{1,0:T(8,128)(2,1)} %k_ref.1, bf16[128,2048]{1,0:T(8,128)(2,1)} %v_ref.1), custom_call_target="tpu_custom_call" | custom-call | bytes 524288 | tf_op jit(solution)/shard_map/near_keys/pallas_call | solution.py:552
  1.6 4.9 %collective-permute-start = (bf16[64,2048]{1,0:T(8,128)(2,1)S(1)}, bf16[64,2048]{1,0:T(8,128)(2,1)S(1)}, u32[]{:S(2)}, u32[]{:S(2)}) collective-permute-start(bf16[64,2048]{1,0:T(8,128)(2,1)S(1)} %near_keys.1), channel_id=1, source_target_pairs={{0,1},{1,2},{2,3},{3,4},{4,5},{5,6},{6,7},{7,8},{8,9},{9,10},{10,1... | collective-permute-start | bytes 786440 | tf_op jit(solution)/shard_map/ppermute | solution.py:508
  6.5 1.7 %operands.1 = (bf16[64,1024]{1,0:T(8,128)(2,1)S(1)}, bf16[64,1024]{1,0:T(8,128)(2,1)S(1)}, bf16[128,2048]{1,0:T(8,128)(2,1)S(1)}, bf16[128,2048]{1,0:T(8,128)(2,...) custom-call(s32[1,128]{1,0:T(1,128)} %bitcast.1, ...), custom_call_target="tpu_custom_call" | custom-call | bytes 4718592 | tf_op jit(solution)/shard_map/operands/pallas_call | solution.py:560
  8.2 3.4 %collective-permute-start.1 = (bf16[64,1024]{1,0:T(8,128)(2,1)S(1)}, bf16[64,1024]{1,0:T(8,128)(2,1)S(1)}, u32[]{:S(2)}, u32[]{:S(2)}) collective-permute-start(bf16[64,1024]{1,0:T(8,128)(2,1)S(1)} %get-tuple-element.36), channel_id=1, source_target_pairs={{0,1},{1,2},{2,3},{3,4},{4,5},{5,6},{6,7},{7,8},{8,9},{9,10},{10,1... | collective-permute-start | bytes 393224 | tf_op jit(solution)/shard_map/ppermute | solution.py:508
  11.6 1.5 %own_block.1 = (bf16[64,2048]{1,0:T(8,128)(2,1)S(1)}, bf16[64,2048]{1,0:T(8,128)(2,1)S(1)}, f32[128,2048]{1,0:T(8,128)S(1)}, f32[128,2048]{1,0:T(8,128)S(1)}) custom-call(f32[128,128]{1,0:T(8,128)S(1)} %get-tuple-element.39.bias_ref, bf16[128,2048]{1,0:T(8,128)(2,1)S(1)} %get-tuple-element.32.q_ref, bf16[128,2048]{1,0:T(8,128)(2,1)S(1)} %get-tuple-element.33.k_ref, ...), custom_call_target="tpu_custom_call" | custom-call | flops 201326592 | bytes 4718592 | tf_op jit(solution)/shard_map/own_block/pallas_call | solution.py:575
  13.1 3.4 %collective-permute-start.2 = (bf16[64,1024]{1,0:T(8,128)(2,1)S(1)}, bf16[64,1024]{1,0:T(8,128)(2,1)S(1)}, u32[]{:S(2)}, u32[]{:S(2)}) collective-permute-start(bf16[64,1024]{1,0:T(8,128)(2,1)S(1)} %get-tuple-element.41), channel_id=1, source_target_pairs={{0,1},{1,2},{2,3},{3,4},{4,5},{5,6},{6,7},{7,8},{8,9},{9,10},{10,1... | collective-permute-start | bytes 393224 | tf_op jit(solution)/shard_map/ppermute | solution.py:508
  16.5 0.0 collective-permute-done.near_ref
  16.5 0.7 %near_terms.1 = (bf16[64,1024]{1,0:T(8,128)(2,1)S(1)}, bf16[64,1024]{1,0:T(8,128)(2,1)S(1)}) custom-call(f32[96,128]{1,0:T(8,128)S(1)} %get-tuple-element.49.near_bias_ref, f32[128,128]{1,0:T(8,128)S(1)} %get-tuple-element.31.bias_ref.lead_bias_ref, bf16[128,2048]{1,0:T(8,128)(2,1)S(1)} %get-tuple-element.32.q_ref, ...), custom_call_target="tpu_custom_call" | custom-call | flops 75497472 | bytes 2097152 | tf_op jit(solution)/shard_map/near_terms/pallas_call | solution.py:585
  17.2 1.3 %collective-permute-start.4 = (bf16[64,1024]{1,0:T(8,128)(2,1)S(1)}, bf16[64,1024]{1,0:T(8,128)(2,1)S(1)}, u32[]{:S(2)}, u32[]{:S(2)}) collective-permute-start(bf16[64,1024]{1,0:T(8,128)(2,1)S(1)} %get-tuple-element.51), channel_id=1, source_target_pairs={{1,0},{2,1},{3,2},{4,3},{5,4},{6,5},{7,6},{8,7},{9,8},{10,9},{11,1... | collective-permute-start | bytes 393224 | tf_op jit(solution)/shard_map/ppermute | solution.py:508
  18.5 1.3 %collective-permute-start.3 = (bf16[64,1024]{1,0:T(8,128)(2,1)S(1)}, bf16[64,1024]{1,0:T(8,128)(2,1)S(1)}, u32[]{:S(2)}, u32[]{:S(2)}) collective-permute-start(bf16[64,1024]{1,0:T(8,128)(2,1)S(1)} %get-tuple-element.50), channel_id=1, source_target_pairs={{1,0},{2,1},{3,2},{4,3},{5,4},{6,5},{7,6},{8,7},{9,8},{10,9},{11,1... | collective-permute-start | bytes 393224 | tf_op jit(solution)/shard_map/ppermute | solution.py:508
  19.8 0.0 collective-permute-done.1.far_ref
  19.9 0.0 collective-permute-done.2.far_late_ref
  19.9 2.0 %lead_rows.1 = (bf16[128,2048]{1,0:T(8,128)(2,1)}, bf16[128,2048]{1,0:T(8,128)(2,1)}, bf16[128,2048]{1,0:T(8,128)(2,1)}, bf16[128,2048]{1,0:T(8,128)(2,1)}) custom-call(f32[128,128]{1,0:T(8,128)S(1)} %get-tuple-element.31.bias_ref.lead_bias_ref, bf16[128,2048]{1,0:T(8,128)(2,1)S(1)} %get-tuple-element.32.q_ref, ...), custom_call_target="tpu_custom_call" | custom-call | flops 201326592 | bytes 5242880 | tf_op jit(solution)/shard_map/lead_rows/pallas_call | solution.py:592
  21.9 2.2 %collective-permute-done.4.after_ref = bf16[64,1024]{1,0:T(8,128)(2,1)S(1)} collective-permute-done((bf16[64,1024]{1,0:T(8,128)(2,1)S(1)}, bf16[64,1024]{1,0:T(8,128)(2,1)S(1)}, u32[]{:S(2)}, u32[]{:S(2)}) %collective-permute-start.4) | collective-permute-done | bytes 131104 | tf_op jit(solution)/shard_map/ppermute | solution.py:508
  24.1 0.5 %tail_keys.1 = (bf16[64,1024]{1,0:T(8,128)(2,1)S(1)}, bf16[64,1024]{1,0:T(8,128)(2,1)S(1)}) custom-call(f32[64,128]{1,0:T(8,128)S(1)} %get-tuple-element.48.bias_ref, bf16[128,2048]{1,0:T(8,128)(2,1)S(1)} %get-tuple-element.33.k_ref, bf16[128,2048]{1,0:T(8,128)(2,1)S(1)} %get-tuple-element.34.v_ref, f32[128,2048]{1,0:T(8,128)S(1)} %get-tuple-element.42.gk_part_ref, ...), custom_call_target="tpu_custom_call" | custom-call | flops 16777216 | bytes 1048576 | tf_op jit(solution)/shard_map/tail_keys/pallas_call | solution.py:602
  24.6 2.3 %collective-permute-done.3.after_ref = bf16[64,1024]{1,0:T(8,128)(2,1)S(1)} collective-permute-done((bf16[64,1024]{1,0:T(8,128)(2,1)S(1)}, bf16[64,1024]{1,0:T(8,128)(2,1)S(1)}, u32[]{:S(2)}, u32[]{:S(2)}) %collective-permute-start.3) | collective-permute-done | bytes 131104 | tf_op jit(solution)/shard_map/ppermute | solution.py:508
  26.9 1.2 %last_keys.1 = (bf16[128,2048]{1,0:T(8,128)(2,1)}, bf16[128,2048]{1,0:T(8,128)(2,1)}) custom-call(f32[64,128]{1,0:T(8,128)S(1)} %get-tuple-element.48.bias_ref, bf16[128,2048]{1,0:T(8,128)(2,1)S(1)} %get-tuple-element.33.k_ref, bf16[128,2048]{1,0:T(8,128)(2,1)S(1)} %get-tuple-element.34.v_ref, ...), custom_call_target="tpu_custom_call", output_to_operand_aliasing={{0}: (8, {}), {1}: (9, {})} | custom-call | flops 16777216 | bytes 1572864 | tf_op jit(solution)/shard_map/last_keys/pallas_call | solution.py:606
Async XLA Ops:
  1.6 14.9 %collective-permute-start = (bf16[64,2048]{1,0:T(8,128)(2,1)S(1)}, bf16[64,2048]{1,0:T(8,128)(2,1)S(1)}, u32[]{:S(2)}, u32[]{:S(2)}) collective-permute-start(bf16[64,2048]{1,0:T(8,128)(2,1)S(1)} %near_keys.1), channel_id=1, source_target_pairs={{0,1},{1,2},{2,3},{3,4},{4,5},{5,6},{6,7},{7,8},{8,9},{9,10},{10,1... | collective-permute-start | bytes 786440 | tf_op jit(solution)/shard_map/ppermute | solution.py:508
  8.2 11.6 %collective-permute-start.1 = (bf16[64,1024]{1,0:T(8,128)(2,1)S(1)}, bf16[64,1024]{1,0:T(8,128)(2,1)S(1)}, u32[]{:S(2)}, u32[]{:S(2)}) collective-permute-start(bf16[64,1024]{1,0:T(8,128)(2,1)S(1)} %get-tuple-element.36), channel_id=1, source_target_pairs={{0,1},{1,2},{2,3},{3,4},{4,5},{5,6},{6,7},{7,8},{8,9},{9,10},{10,1... | collective-permute-start | bytes 393224 | tf_op jit(solution)/shard_map/ppermute | solution.py:508
  13.1 6.8 %collective-permute-start.2 = (bf16[64,1024]{1,0:T(8,128)(2,1)S(1)}, bf16[64,1024]{1,0:T(8,128)(2,1)S(1)}, u32[]{:S(2)}, u32[]{:S(2)}) collective-permute-start(bf16[64,1024]{1,0:T(8,128)(2,1)S(1)} %get-tuple-element.41), channel_id=1, source_target_pairs={{0,1},{1,2},{2,3},{3,4},{4,5},{5,6},{6,7},{7,8},{8,9},{9,10},{10,1... | collective-permute-start | bytes 393224 | tf_op jit(solution)/shard_map/ppermute | solution.py:508
  17.2 6.9 %collective-permute-start.4 = (bf16[64,1024]{1,0:T(8,128)(2,1)S(1)}, bf16[64,1024]{1,0:T(8,128)(2,1)S(1)}, u32[]{:S(2)}, u32[]{:S(2)}) collective-permute-start(bf16[64,1024]{1,0:T(8,128)(2,1)S(1)} %get-tuple-element.51), channel_id=1, source_target_pairs={{1,0},{2,1},{3,2},{4,3},{5,4},{6,5},{7,6},{8,7},{9,8},{10,9},{11,1... | collective-permute-start | bytes 393224 | tf_op jit(solution)/shard_map/ppermute | solution.py:508
  18.5 8.4 %collective-permute-start.3 = (bf16[64,1024]{1,0:T(8,128)(2,1)S(1)}, bf16[64,1024]{1,0:T(8,128)(2,1)S(1)}, u32[]{:S(2)}, u32[]{:S(2)}) collective-permute-start(bf16[64,1024]{1,0:T(8,128)(2,1)S(1)} %get-tuple-element.50), channel_id=1, source_target_pairs={{1,0},{2,1},{3,2},{4,3},{5,4},{6,5},{7,6},{8,7},{9,8},{10,9},{11,1... | collective-permute-start | bytes 393224 | tf_op jit(solution)/shard_map/ppermute | solution.py:508

commit v23 on v21

--- a/solution.py
+++ b/solution.py
@@ -309,30 +309,31 @@
     return [pl.ds(pl.multiple_of(at * step + c, wide), wide) for c in range(0, step, wide)]
 
 
-def own_kernel(
-    prior, step, bias_ref, q_ref, k_ref, v_ref, do_ref, attn_ref, gq_ref, gk_ref, gv_ref
-):
+def own_kernel(prior, step, odd, bias_ref, q_ref, k_ref, v_ref, do_ref, *refs):
+    attn_ref, gq_ref, gk_ref, gv_ref = refs[-4:]
     tok, width = k_ref.shape
     late = slice(prior, tok)
 
-    @pl.loop(0, width // step)
-    def _(at):
-        bias = bias_ref[...]
-        columns = pair_columns(at, step)
-        queries = [side_by_side(q_ref[late, c]) for c in columns]
-        cotangents = [side_by_side(do_ref[late, c]) for c in columns]
-        pairs = [
-            score_pair(k_ref[:, c], q, v_ref[:, c], do, bias)
-            for c, q, do in zip(columns, queries, cotangents)
-        ]
-        weights, _, deltas = softmax_columns(pairs)
-        grads = score_grads_of(pairs, weights, deltas)
-        for c, w, g, q, do in zip(columns, weights, grads, queries, cotangents):
-            w = w.astype(jnp.bfloat16)
-            attn_ref[:, c] = own_diagonal(dot(w, v_ref[:, c], 0, 0)).astype(jnp.bfloat16)
-            gq_ref[:, c] = own_diagonal(dot(g, k_ref[:, c], 0, 0)).astype(jnp.bfloat16)
-            gk_ref[:, c] = dot(g, q, 1, 0)
-            gv_ref[:, c] = dot(w, do, 1, 0)
+    @pl.when(lax.axis_index("seq") % 2 == odd)
+    def _():
+        @pl.loop(0, width // step)
+        def _(at):
+            bias = bias_ref[...]
+            columns = pair_columns(at, step)
+            queries = [side_by_side(q_ref[late, c]) for c in columns]
+            cotangents = [side_by_side(do_ref[late, c]) for c in columns]
+            pairs = [
+                score_pair(k_ref[:, c], q, v_ref[:, c], do, bias)
+                for c, q, do in zip(columns, queries, cotangents)
+            ]
+            weights, _, deltas = softmax_columns(pairs)
+            grads = score_grads_of(pairs, weights, deltas)
+            for c, w, g, q, do in zip(columns, weights, grads, queries, cotangents):
+                w = w.astype(jnp.bfloat16)
+                attn_ref[:, c] = own_diagonal(dot(w, v_ref[:, c], 0, 0)).astype(jnp.bfloat16)
+                gq_ref[:, c] = own_diagonal(dot(g, k_ref[:, c], 0, 0)).astype(jnp.bfloat16)
+                gk_ref[:, c] = dot(g, q, 1, 0)
+                gv_ref[:, c] = dot(w, do, 1, 0)
 
 
 def near_kernel(
@@ -566,15 +567,20 @@
         ],
         (0, 0, 0, 0), 18 * tok * width,
     )(*in_hbm(lengths, query_in, key_in, value_in, grad_out))
+
+    def own_block(odd, *partial):
+        return call(
+            functools.partial(own_kernel, prior, step, odd), "own_block",
+            [inside] * (5 + len(partial)), [inside] * 4,
+            [near16(tok - prior, width)] * 2 + [near32(tok, width)] * 2, (),
+            (width // HEAD_DIM, tok - prior, tok, 6), 18 * tok * width,
+            {5 + n: n for n in range(len(partial))},
+        )(*in_vmem(own_bias, q, k, v, do, *partial))
+
+    partial = own_block(1)
+    far, partial = lax.optimization_barrier((far, partial))
     far = neighbour(far, 1)
-
-    attn, gq, gk_part, gv_part = call(
-        functools.partial(own_kernel, prior, step), "own_block",
-        [inside] * 5, [inside] * 4,
-        [near16(tok - prior, width)] * 2 + [near32(tok, width)] * 2, (),
-        (width // HEAD_DIM, tok - prior, tok, 6), 18 * tok * width,
-    )(*in_vmem(own_bias, q, k, v, do))
-
+    attn, gq, gk_part, gv_part = own_block(0, *partial)
     near_bias, attn = lax.optimization_barrier((near_bias, attn))
     backs = call(
         functools.partial(near_kernel, prior), "near_terms",

time: 26.1 us -> 27.2 us (1.042)
  waiting for transfers between devices: 5.52 us -> 6.62 us
    ppermute x4, waiting for transfers between devices: 5.52 us -> 6.62 us  [neighbour(): return lax.ppermute(value, ('seq', 'head'), pairs)]
    pallas_call x1 -> x2, Pallas kernels: 1.49 us -> 1.52 us  [own_block(): call(functools.partial(own_kernel, prior, step, odd), 'own_block', [insid...]
  transfers between devices with their start and end apart: 4 -> 4, of which waited for: 3 -> 3; matrix products, arithmetic and copies ran while one was open for 0% -> 0% of each run, Pallas kernels for 26% -> 25%
where the time goes in v23:
time: 27.2 us; the launch traced here: 27 us
  starting transfers between devices  10.8 us (40%)
  Pallas kernels  8.79 us (32%)
  waiting for transfers between devices  6.62 us (24%)
  between operations  0.72 us (3%)
    ppermute x4, starting transfers between devices, neighbour(): return lax.ppermute(value, ('seq', 'head'), pairs)  10.8 us
    ppermute x4, waiting for transfers between devices, neighbour(): return lax.ppermute(value, ('seq', 'head'), pairs)  6.62 us
    pallas_call x1, Pallas kernels, halo_shards(): call(functools.partial(lead_kernel, prior, step), 'lead_rows', [inside] *...  2.19 us
    pallas_call x1, Pallas kernels, halo_shards(): call(functools.partial(ready_kernel, prior), 'operands', [anywhere] * 5,...  1.68 us
    pallas_call x2, Pallas kernels, own_block(): call(functools.partial(own_kernel, prior, step, odd), 'own_block', [insid...  1.52 us
    pallas_call x1, Pallas kernels, halo_shards(): call(functools.partial(last_kernel, prior), 'last_keys', [inside] * 8 + [...  1.18 us
    pallas_call x1, Pallas kernels, halo_shards(): call(functools.partial(pack_kernel, prior), 'near_keys', [anywhere] * 2,...  0.99 us
    pallas_call x1, Pallas kernels, halo_shards(): call(functools.partial(near_kernel, prior), 'near_terms', [inside] * 7, [...  0.73 us
  transfers between devices with their start and end apart: 4, of which 3 were waited for; matrix products, arithmetic and copies ran while one was open for 0% of the time, Pallas kernels for 25%

profile of v23, /device:TPU:0, one launch (start us, length us, event | category | flops | bytes accessed | tf_op | source)
XLA Modules:
  0.0 27.0 jit_solution(7080738622271375190)
XLA Ops:
  0.6 1.0 %near_keys.1 = bf16[64,2048]{1,0:T(8,128)(2,1)S(1)} custom-call(bf16[128,2048]{1,0:T(8,128)(2,1)} %k_ref.1, bf16[128,2048]{1,0:T(8,128)(2,1)} %v_ref.1), custom_call_target="tpu_custom_call" | custom-call | bytes 524288 | tf_op jit(solution)/shard_map/near_keys/pallas_call | solution.py:550
  1.6 4.9 %collective-permute-start = (bf16[64,2048]{1,0:T(8,128)(2,1)S(1)}, bf16[64,2048]{1,0:T(8,128)(2,1)S(1)}, u32[]{:S(2)}, u32[]{:S(2)}) collective-permute-start(bf16[64,2048]{1,0:T(8,128)(2,1)S(1)} %near_keys.1), channel_id=1, source_target_pairs={{0,1},{1,2},{2,3},{3,4},{4,5},{5,6},{6,7},{7,8},{8,9},{9,10},{10,1... | collective-permute-start | bytes 786440 | tf_op jit(solution)/shard_map/ppermute | solution.py:505
  6.5 1.7 %operands.1 = (bf16[64,2048]{1,0:T(8,128)(2,1)S(1)}, bf16[128,2048]{1,0:T(8,128)(2,1)S(1)}, bf16[128,2048]{1,0:T(8,128)(2,1)S(1)}, bf16[128,2048]{1,0:T(8,128)(2...) custom-call(s32[1,128]{1,0:T(1,128)} %bitcast.1, ...), custom_call_target="tpu_custom_call" | custom-call | bytes 4718592 | tf_op jit(solution)/shard_map/operands/pallas_call | solution.py:558
  8.2 3.4 %collective-permute-start.1 = (bf16[64,2048]{1,0:T(8,128)(2,1)S(1)}, bf16[64,2048]{1,0:T(8,128)(2,1)S(1)}, u32[]{:S(2)}, u32[]{:S(2)}) collective-permute-start(bf16[64,2048]{1,0:T(8,128)(2,1)S(1)} %get-tuple-element.49), channel_id=1, source_target_pairs={{0,1},{1,2},{2,3},{3,4},{4,5},{5,6},{6,7},{7,8},{8,9},{9,10},{10,1... | collective-permute-start | bytes 786440 | tf_op jit(solution)/shard_map/ppermute | solution.py:505
  11.6 1.5 %own_block.3 = (bf16[64,2048]{1,0:T(8,128)(2,1)S(1)}, bf16[64,2048]{1,0:T(8,128)(2,1)S(1)}, f32[128,2048]{1,0:T(8,128)S(1)}, f32[128,2048]{1,0:T(8,128)S(1)}) custom-call(f32[128,128]{1,0:T(8,128)S(1)} %get-tuple-element.44.bias_ref, ...), custom_call_target="tpu_custom_call", output_to_operand_aliasing={{0}: (5, {}), {1}: (6, {}), {2}: (7, {}), {3}: (8, {})} | custom-call | flops 201326592 | bytes 4718592 | tf_op jit(solution)/shard_map/own_block/pallas_call | solution.py:572
  13.1 0.0 collective-permute-done.near_ref
  13.1 0.7 %near_terms.1 = (bf16[64,1024]{1,0:T(8,128)(2,1)S(1)}, bf16[64,1024]{1,0:T(8,128)(2,1)S(1)}) custom-call(f32[96,128]{1,0:T(8,128)S(1)} %get-tuple-element.63.near_bias_ref, f32[128,128]{1,0:T(8,128)S(1)} %get-tuple-element.38.bias_ref.lead_bias_ref, bf16[128,2048]{1,0:T(8,128)(2,1)S(1)} %get-tuple-element.39.q_ref, ...), custom_call_target="tpu_custom_call" | custom-call | flops 75497472 | bytes 2097152 | tf_op jit(solution)/shard_map/near_terms/pallas_call | solution.py:585
  13.9 1.3 %collective-permute-start.3 = (bf16[64,1024]{1,0:T(8,128)(2,1)S(1)}, bf16[64,1024]{1,0:T(8,128)(2,1)S(1)}, u32[]{:S(2)}, u32[]{:S(2)}) collective-permute-start(bf16[64,1024]{1,0:T(8,128)(2,1)S(1)} %get-tuple-element.65), channel_id=1, source_target_pairs={{1,0},{2,1},{3,2},{4,3},{5,4},{6,5},{7,6},{8,7},{9,8},{10,9},{11,1... | collective-permute-start | bytes 393224 | tf_op jit(solution)/shard_map/ppermute | solution.py:505
  15.2 1.3 %collective-permute-start.2 = (bf16[64,1024]{1,0:T(8,128)(2,1)S(1)}, bf16[64,1024]{1,0:T(8,128)(2,1)S(1)}, u32[]{:S(2)}, u32[]{:S(2)}) collective-permute-start(bf16[64,1024]{1,0:T(8,128)(2,1)S(1)} %get-tuple-element.64), channel_id=1, source_target_pairs={{1,0},{2,1},{3,2},{4,3},{5,4},{6,5},{7,6},{8,7},{9,8},{10,9},{11,1... | collective-permute-start | bytes 393224 | tf_op jit(solution)/shard_map/ppermute | solution.py:505
  16.5 1.8 %collective-permute-done.1.far_ref = bf16[64,2048]{1,0:T(8,128)(2,1)S(1)} collective-permute-done((bf16[64,2048]{1,0:T(8,128)(2,1)S(1)}, bf16[64,2048]{1,0:T(8,128)(2,1)S(1)}, u32[]{:S(2)}, u32[]{:S(2)}) %collective-permute-start.1) | collective-permute-done | bytes 262176 | tf_op jit(solution)/shard_map/ppermute | solution.py:505
  18.2 2.2 %lead_rows.1 = (bf16[128,2048]{1,0:T(8,128)(2,1)}, bf16[128,2048]{1,0:T(8,128)(2,1)}, bf16[128,2048]{1,0:T(8,128)(2,1)}, bf16[128,2048]{1,0:T(8,128)(2,1)}) custom-call(f32[128,128]{1,0:T(8,128)S(1)} %get-tuple-element.38.bias_ref.lead_bias_ref, bf16[128,2048]{1,0:T(8,128)(2,1)S(1)} %get-tuple-element.39.q_ref, ...), custom_call_target="tpu_custom_call" | custom-call | flops 201326592 | bytes 5242880 | tf_op jit(solution)/shard_map/lead_rows/pallas_call | solution.py:592
  20.4 2.6 %collective-permute-done.3.after_ref = bf16[64,1024]{1,0:T(8,128)(2,1)S(1)} collective-permute-done((bf16[64,1024]{1,0:T(8,128)(2,1)S(1)}, bf16[64,1024]{1,0:T(8,128)(2,1)S(1)}, u32[]{:S(2)}, u32[]{:S(2)}) %collective-permute-start.3) | collective-permute-done | bytes 131104 | tf_op jit(solution)/shard_map/ppermute | solution.py:505
  23.0 0.5 %tail_keys.1 = (bf16[64,1024]{1,0:T(8,128)(2,1)S(1)}, bf16[64,1024]{1,0:T(8,128)(2,1)S(1)}) custom-call(f32[64,128]{1,0:T(8,128)S(1)} %get-tuple-element.62.bias_ref, bf16[128,2048]{1,0:T(8,128)(2,1)S(1)} %get-tuple-element.40.k_ref, bf16[128,2048]{1,0:T(8,128)(2,1)S(1)} %get-tuple-element.41.v_ref, f32[128,2048]{1,0:T(8,128)S(1)} %get-tuple-element.54.gk_part_ref, ...), custom_call_target="tpu_custom_call" | custom-call | flops 16777216 | bytes 1048576 | tf_op jit(solution)/shard_map/tail_keys/pallas_call | solution.py:602
  23.5 2.3 %collective-permute-done.2.after_ref = bf16[64,1024]{1,0:T(8,128)(2,1)S(1)} collective-permute-done((bf16[64,1024]{1,0:T(8,128)(2,1)S(1)}, bf16[64,1024]{1,0:T(8,128)(2,1)S(1)}, u32[]{:S(2)}, u32[]{:S(2)}) %collective-permute-start.2) | collective-permute-done | bytes 131104 | tf_op jit(solution)/shard_map/ppermute | solution.py:505
  25.8 1.2 %last_keys.1 = (bf16[128,2048]{1,0:T(8,128)(2,1)}, bf16[128,2048]{1,0:T(8,128)(2,1)}) custom-call(f32[64,128]{1,0:T(8,128)S(1)} %get-tuple-element.62.bias_ref, bf16[128,2048]{1,0:T(8,128)(2,1)S(1)} %get-tuple-element.40.k_ref, bf16[128,2048]{1,0:T(8,128)(2,1)S(1)} %get-tuple-element.41.v_ref, ...), custom_call_target="tpu_custom_call", output_to_operand_aliasing={{0}: (8, {}), {1}: (9, {})} | custom-call | flops 16777216 | bytes 1572864 | tf_op jit(solution)/shard_map/last_keys/pallas_call | solution.py:606
  (1 shorter events, 0.0 us)
Async XLA Ops:
  1.6 11.5 %collective-permute-start = (bf16[64,2048]{1,0:T(8,128)(2,1)S(1)}, bf16[64,2048]{1,0:T(8,128)(2,1)S(1)}, u32[]{:S(2)}, u32[]{:S(2)}) collective-permute-start(bf16[64,2048]{1,0:T(8,128)(2,1)S(1)} %near_keys.1), channel_id=1, source_target_pairs={{0,1},{1,2},{2,3},{3,4},{4,5},{5,6},{6,7},{7,8},{8,9},{9,10},{10,1... | collective-permute-start | bytes 786440 | tf_op jit(solution)/shard_map/ppermute | solution.py:505
  8.2 10.0 %collective-permute-start.1 = (bf16[64,2048]{1,0:T(8,128)(2,1)S(1)}, bf16[64,2048]{1,0:T(8,128)(2,1)S(1)}, u32[]{:S(2)}, u32[]{:S(2)}) collective-permute-start(bf16[64,2048]{1,0:T(8,128)(2,1)S(1)} %get-tuple-element.49), channel_id=1, source_target_pairs={{0,1},{1,2},{2,3},{3,4},{4,5},{5,6},{6,7},{7,8},{8,9},{9,10},{10,1... | collective-permute-start | bytes 786440 | tf_op jit(solution)/shard_map/ppermute | solution.py:505
  13.9 9.1 %collective-permute-start.3 = (bf16[64,1024]{1,0:T(8,128)(2,1)S(1)}, bf16[64,1024]{1,0:T(8,128)(2,1)S(1)}, u32[]{:S(2)}, u32[]{:S(2)}) collective-permute-start(bf16[64,1024]{1,0:T(8,128)(2,1)S(1)} %get-tuple-element.65), channel_id=1, source_target_pairs={{1,0},{2,1},{3,2},{4,3},{5,4},{6,5},{7,6},{8,7},{9,8},{10,9},{11,1... | collective-permute-start | bytes 393224 | tf_op jit(solution)/shard_map/ppermute | solution.py:505
  15.2 10.6 %collective-permute-start.2 = (bf16[64,1024]{1,0:T(8,128)(2,1)S(1)}, bf16[64,1024]{1,0:T(8,128)(2,1)S(1)}, u32[]{:S(2)}, u32[]{:S(2)}) collective-permute-start(bf16[64,1024]{1,0:T(8,128)(2,1)S(1)} %get-tuple-element.64), channel_id=1, source_target_pairs={{1,0},{2,1},{3,2},{4,3},{5,4},{6,5},{7,6},{8,7},{9,8},{10,9},{11,1... | collective-permute-start | bytes 393224 | tf_op jit(solution)/shard_map/ppermute | solution.py:505

commit v24 on v23

--- a/solution.py
+++ b/solution.py
@@ -577,10 +577,10 @@
             {5 + n: n for n in range(len(partial))},
         )(*in_vmem(own_bias, q, k, v, do, *partial))
 
-    partial = own_block(1)
+    partial = own_block(0)
     far, partial = lax.optimization_barrier((far, partial))
     far = neighbour(far, 1)
-    attn, gq, gk_part, gv_part = own_block(0, *partial)
+    attn, gq, gk_part, gv_part = own_block(1, *partial)
     near_bias, attn = lax.optimization_barrier((near_bias, attn))
     backs = call(
         functools.partial(near_kernel, prior), "near_terms",

time: 27.2 us -> 26.7 us (0.982)
  the two profiles are of different devices: /device:TPU:0 before, /device:TPU:1 now
where the time goes in v24:
time: 26.7 us; the launch traced here: 26.4 us
  starting transfers between devices  16.2 us (61%)
  Pallas kernels  8.81 us (33%)
  between operations  0.73 us (3%)
  waiting for transfers between devices  0.68 us (3%)
    ppermute x4, starting transfers between devices, neighbour(): return lax.ppermute(value, ('seq', 'head'), pairs)  16.2 us
    pallas_call x1, Pallas kernels, halo_shards(): call(functools.partial(lead_kernel, prior, step), 'lead_rows', [inside] *...  2.2 us
    pallas_call x1, Pallas kernels, halo_shards(): call(functools.partial(ready_kernel, prior), 'operands', [anywhere] * 5,...  1.68 us
    pallas_call x2, Pallas kernels, own_block(): call(functools.partial(own_kernel, prior, step, odd), 'own_block', [insid...  1.52 us
    pallas_call x1, Pallas kernels, halo_shards(): call(functools.partial(last_kernel, prior), 'last_keys', [inside] * 8 + [...  1.19 us
    pallas_call x1, Pallas kernels, halo_shards(): call(functools.partial(pack_kernel, prior), 'near_keys', [anywhere] * 2,...  0.99 us
    pallas_call x1, Pallas kernels, halo_shards(): call(functools.partial(near_kernel, prior), 'near_terms', [inside] * 7, [...  0.73 us
    ppermute x4, waiting for transfers between devices, neighbour(): return lax.ppermute(value, ('seq', 'head'), pairs)  0.68 us
  transfers between devices with their start and end apart: 4, of which 1 were waited for; matrix products, arithmetic and copies ran while one was open for 0% of the time, Pallas kernels for 25%

profile of v24, /device:TPU:1, one launch (start us, length us, event | category | flops | bytes accessed | tf_op | source)
XLA Modules:
  0.0 26.4 jit_solution(12890937404124656573)
XLA Ops:
  0.6 1.0 %near_keys.1 = bf16[64,2048]{1,0:T(8,128)(2,1)S(1)} custom-call(bf16[128,2048]{1,0:T(8,128)(2,1)} %k_ref.1, bf16[128,2048]{1,0:T(8,128)(2,1)} %v_ref.1), custom_call_target="tpu_custom_call" | custom-call | bytes 524288 | tf_op jit(solution)/shard_map/near_keys/pallas_call | solution.py:550
  1.6 3.9 %collective-permute-start = (bf16[64,2048]{1,0:T(8,128)(2,1)S(1)}, bf16[64,2048]{1,0:T(8,128)(2,1)S(1)}, u32[]{:S(2)}, u32[]{:S(2)}) collective-permute-start(bf16[64,2048]{1,0:T(8,128)(2,1)S(1)} %near_keys.1), channel_id=1, source_target_pairs={{0,1},{1,2},{2,3},{3,4},{4,5},{5,6},{6,7},{7,8},{8,9},{9,10},{10,1... | collective-permute-start | bytes 786440 | tf_op jit(solution)/shard_map/ppermute | solution.py:505
  5.6 1.7 %operands.1 = (bf16[64,2048]{1,0:T(8,128)(2,1)S(1)}, bf16[128,2048]{1,0:T(8,128)(2,1)S(1)}, bf16[128,2048]{1,0:T(8,128)(2,1)S(1)}, bf16[128,2048]{1,0:T(8,128)(2...) custom-call(s32[1,128]{1,0:T(1,128)} %bitcast.1, ...), custom_call_target="tpu_custom_call" | custom-call | bytes 4718592 | tf_op jit(solution)/shard_map/operands/pallas_call | solution.py:558
  7.3 3.1 %collective-permute-start.1 = (bf16[64,2048]{1,0:T(8,128)(2,1)S(1)}, bf16[64,2048]{1,0:T(8,128)(2,1)S(1)}, u32[]{:S(2)}, u32[]{:S(2)}) collective-permute-start(bf16[64,2048]{1,0:T(8,128)(2,1)S(1)} %get-tuple-element.49), channel_id=1, source_target_pairs={{0,1},{1,2},{2,3},{3,4},{4,5},{5,6},{6,7},{7,8},{8,9},{9,10},{10,1... | collective-permute-start | bytes 786440 | tf_op jit(solution)/shard_map/ppermute | solution.py:505
  10.4 1.5 %own_block.3 = (bf16[64,2048]{1,0:T(8,128)(2,1)S(1)}, bf16[64,2048]{1,0:T(8,128)(2,1)S(1)}, f32[128,2048]{1,0:T(8,128)S(1)}, f32[128,2048]{1,0:T(8,128)S(1)}) custom-call(f32[128,128]{1,0:T(8,128)S(1)} %get-tuple-element.44.bias_ref, ...), custom_call_target="tpu_custom_call", output_to_operand_aliasing={{0}: (5, {}), {1}: (6, {}), {2}: (7, {}), {3}: (8, {})} | custom-call | flops 201326592 | bytes 4718592 | tf_op jit(solution)/shard_map/own_block/pallas_call | solution.py:572
  11.9 0.0 collective-permute-done.near_ref
  11.9 0.7 %near_terms.1 = (bf16[64,1024]{1,0:T(8,128)(2,1)S(1)}, bf16[64,1024]{1,0:T(8,128)(2,1)S(1)}) custom-call(f32[96,128]{1,0:T(8,128)S(1)} %get-tuple-element.63.near_bias_ref, f32[128,128]{1,0:T(8,128)S(1)} %get-tuple-element.38.bias_ref.lead_bias_ref, bf16[128,2048]{1,0:T(8,128)(2,1)S(1)} %get-tuple-element.39.q_ref, ...), custom_call_target="tpu_custom_call" | custom-call | flops 75497472 | bytes 2097152 | tf_op jit(solution)/shard_map/near_terms/pallas_call | solution.py:585
  12.7 5.2 %collective-permute-start.3 = (bf16[64,1024]{1,0:T(8,128)(2,1)S(1)}, bf16[64,1024]{1,0:T(8,128)(2,1)S(1)}, u32[]{:S(2)}, u32[]{:S(2)}) collective-permute-start(bf16[64,1024]{1,0:T(8,128)(2,1)S(1)} %get-tuple-element.65), channel_id=1, source_target_pairs={{1,0},{2,1},{3,2},{4,3},{5,4},{6,5},{7,6},{8,7},{9,8},{10,9},{11,1... | collective-permute-start | bytes 393224 | tf_op jit(solution)/shard_map/ppermute | solution.py:505
  17.9 3.9 %collective-permute-start.2 = (bf16[64,1024]{1,0:T(8,128)(2,1)S(1)}, bf16[64,1024]{1,0:T(8,128)(2,1)S(1)}, u32[]{:S(2)}, u32[]{:S(2)}) collective-permute-start(bf16[64,1024]{1,0:T(8,128)(2,1)S(1)} %get-tuple-element.64), channel_id=1, source_target_pairs={{1,0},{2,1},{3,2},{4,3},{5,4},{6,5},{7,6},{8,7},{9,8},{10,9},{11,1... | collective-permute-start | bytes 393224 | tf_op jit(solution)/shard_map/ppermute | solution.py:505
  21.8 0.0 collective-permute-done.1.far_ref
  21.8 2.2 %lead_rows.1 = (bf16[128,2048]{1,0:T(8,128)(2,1)}, bf16[128,2048]{1,0:T(8,128)(2,1)}, bf16[128,2048]{1,0:T(8,128)(2,1)}, bf16[128,2048]{1,0:T(8,128)(2,1)}) custom-call(f32[128,128]{1,0:T(8,128)S(1)} %get-tuple-element.38.bias_ref.lead_bias_ref, bf16[128,2048]{1,0:T(8,128)(2,1)S(1)} %get-tuple-element.39.q_ref, ...), custom_call_target="tpu_custom_call" | custom-call | flops 201326592 | bytes 5242880 | tf_op jit(solution)/shard_map/lead_rows/pallas_call | solution.py:592
  24.0 0.0 collective-permute-done.3.after_ref
  24.1 0.5 %tail_keys.1 = (bf16[64,1024]{1,0:T(8,128)(2,1)S(1)}, bf16[64,1024]{1,0:T(8,128)(2,1)S(1)}) custom-call(f32[64,128]{1,0:T(8,128)S(1)} %get-tuple-element.62.bias_ref, bf16[128,2048]{1,0:T(8,128)(2,1)S(1)} %get-tuple-element.40.k_ref, bf16[128,2048]{1,0:T(8,128)(2,1)S(1)} %get-tuple-element.41.v_ref, f32[128,2048]{1,0:T(8,128)S(1)} %get-tuple-element.54.gk_part_ref, ...), custom_call_target="tpu_custom_call" | custom-call | flops 16777216 | bytes 1048576 | tf_op jit(solution)/shard_map/tail_keys/pallas_call | solution.py:602
  24.6 0.7 %collective-permute-done.2.after_ref = bf16[64,1024]{1,0:T(8,128)(2,1)S(1)} collective-permute-done((bf16[64,1024]{1,0:T(8,128)(2,1)S(1)}, bf16[64,1024]{1,0:T(8,128)(2,1)S(1)}, u32[]{:S(2)}, u32[]{:S(2)}) %collective-permute-start.2) | collective-permute-done | bytes 131104 | tf_op jit(solution)/shard_map/ppermute | solution.py:505
  25.2 1.2 %last_keys.1 = (bf16[128,2048]{1,0:T(8,128)(2,1)}, bf16[128,2048]{1,0:T(8,128)(2,1)}) custom-call(f32[64,128]{1,0:T(8,128)S(1)} %get-tuple-element.62.bias_ref, bf16[128,2048]{1,0:T(8,128)(2,1)S(1)} %get-tuple-element.40.k_ref, bf16[128,2048]{1,0:T(8,128)(2,1)S(1)} %get-tuple-element.41.v_ref, ...), custom_call_target="tpu_custom_call", output_to_operand_aliasing={{0}: (8, {}), {1}: (9, {})} | custom-call | flops 16777216 | bytes 1572864 | tf_op jit(solution)/shard_map/last_keys/pallas_call | solution.py:606
  (1 shorter events, 0.0 us)
Async XLA Ops:
  1.6 10.3 %collective-permute-start = (bf16[64,2048]{1,0:T(8,128)(2,1)S(1)}, bf16[64,2048]{1,0:T(8,128)(2,1)S(1)}, u32[]{:S(2)}, u32[]{:S(2)}) collective-permute-start(bf16[64,2048]{1,0:T(8,128)(2,1)S(1)} %near_keys.1), channel_id=1, source_target_pairs={{0,1},{1,2},{2,3},{3,4},{4,5},{5,6},{6,7},{7,8},{8,9},{9,10},{10,1... | collective-permute-start | bytes 786440 | tf_op jit(solution)/shard_map/ppermute | solution.py:505
  7.3 14.5 %collective-permute-start.1 = (bf16[64,2048]{1,0:T(8,128)(2,1)S(1)}, bf16[64,2048]{1,0:T(8,128)(2,1)S(1)}, u32[]{:S(2)}, u32[]{:S(2)}) collective-permute-start(bf16[64,2048]{1,0:T(8,128)(2,1)S(1)} %get-tuple-element.49), channel_id=1, source_target_pairs={{0,1},{1,2},{2,3},{3,4},{4,5},{5,6},{6,7},{7,8},{8,9},{9,10},{10,1... | collective-permute-start | bytes 786440 | tf_op jit(solution)/shard_map/ppermute | solution.py:505
  12.7 11.4 %collective-permute-start.3 = (bf16[64,1024]{1,0:T(8,128)(2,1)S(1)}, bf16[64,1024]{1,0:T(8,128)(2,1)S(1)}, u32[]{:S(2)}, u32[]{:S(2)}) collective-permute-start(bf16[64,1024]{1,0:T(8,128)(2,1)S(1)} %get-tuple-element.65), channel_id=1, source_target_pairs={{1,0},{2,1},{3,2},{4,3},{5,4},{6,5},{7,6},{8,7},{9,8},{10,9},{11,1... | collective-permute-start | bytes 393224 | tf_op jit(solution)/shard_map/ppermute | solution.py:505
  17.9 7.3 %collective-permute-start.2 = (bf16[64,1024]{1,0:T(8,128)(2,1)S(1)}, bf16[64,1024]{1,0:T(8,128)(2,1)S(1)}, u32[]{:S(2)}, u32[]{:S(2)}) collective-permute-start(bf16[64,1024]{1,0:T(8,128)(2,1)S(1)} %get-tuple-element.64), channel_id=1, source_target_pairs={{1,0},{2,1},{3,2},{4,3},{5,4},{6,5},{7,6},{8,7},{9,8},{10,9},{11,1... | collective-permute-start | bytes 393224 | tf_op jit(solution)/shard_map/ppermute | solution.py:505

commit v25 on v21

--- a/solution.py
+++ b/solution.py
@@ -257,19 +257,22 @@
     return parts[:, :count] + parts[:, count : 2 * count] + parts[:, 2 * count : 3 * count]
 
 
-def pack_copies(prior, at, k_ref, v_ref, packed_ref, sems):
-    half, tok = prior // 2, k_ref.shape[0]
-    rows = pl.ds(tok - (at + 1) * half, half)
+def pack_copies(prior, at, pieces, k_ref, v_ref, packed_ref, sems):
+    half, (tok, width) = prior // 2, k_ref.shape
+    rows, wide = pl.ds(tok - (at + 1) * half, half), width // pieces
     return [
         pltpu.make_async_copy(
-            ref.at[rows, :], packed_ref.at[pl.ds(n * half, half), :], sems.at[n]
+            ref.at[rows, pl.ds(piece * wide, wide)],
+            packed_ref.at[pl.ds(n * half, half), pl.ds(piece * wide, wide)],
+            sems.at[n, piece],
         )
+        for piece in range(pieces)
         for n, ref in enumerate((k_ref, v_ref))
     ]
 
 
 def pack_kernel(prior, k_ref, v_ref, near_ref, sems):
-    copies = pack_copies(prior, 0, k_ref, v_ref, near_ref, sems)
+    copies = pack_copies(prior, 0, 2, k_ref, v_ref, near_ref, sems)
     for copy in copies:
         copy.start()
     for copy in copies:
@@ -282,7 +285,7 @@
 ):
     tok, half = k_ref.shape[0], prior // 2
     pairs = ((q_hbm, q_ref), (k_hbm, k_ref), (v_hbm, v_ref), (do_hbm, do_ref))
-    copies = pack_copies(prior, 1, k_hbm, v_hbm, far_ref, far_sems)
+    copies = pack_copies(prior, 1, 1, k_hbm, v_hbm, far_ref, far_sems)
     copies += [pltpu.make_async_copy(hbm, ref, sems.at[n]) for n, (hbm, ref) in enumerate(pairs)]
     len_copy = pltpu.make_async_copy(len_hbm, len_ref, len_sem)
     len_copy.start()
@@ -451,16 +454,20 @@
     ]
     weights, grads = merged_columns(pairs, own)
 
-    def fill(ref, part_ref, lefts, rights, rows):
+    def fill(ref, part_ref, lefts, rights, rows, send):
         for p, c, left, right in zip(places, columns, lefts, rights):
             total = part_ref[last, c] + dot(left, right, 1, 0)
             terms = jnp.where(far, 0.0, after_ref[rows, p].astype(jnp.float32))
             ref[first, p] = total[first].astype(jnp.bfloat16)
             ref[second, p] = (total[second] + terms).astype(jnp.bfloat16)
+            send(p, c)
+
+    def unsent(p, c):
+        del p, c
 
     return (
-        lambda ref: fill(ref, gv_part_ref, weights, cotangents, second),
-        lambda ref: fill(ref, gk_part_ref, grads, queries, first),
+        lambda ref, send=unsent: fill(ref, gv_part_ref, weights, cotangents, second, send),
+        lambda ref, send=unsent: fill(ref, gk_part_ref, grads, queries, first, send),
     )
 
 
@@ -480,20 +487,17 @@
     low = gk_first_ref.shape[1]
     copies = []
 
-    def send(ref, hbm, start):
-        cols = pl.ds(start, ref.shape[1])
+    def send(ref, hbm, cols):
         copies.append(pltpu.make_async_copy(ref, hbm.at[rows, cols], sems.at[len(copies)]))
         copies[-1].start()
 
-    send(gv_first_ref, gv_hbm, 0)
-    send(gk_first_ref, gk_hbm, 0)
+    send(gv_first_ref, gv_hbm, pl.ds(0, low))
+    send(gk_first_ref, gk_hbm, pl.ds(0, low))
     fill_gv, fill_gk = tail_half(
         prior, low, bias_ref, k_ref, v_ref, gk_part_ref, gv_part_ref, after_ref
     )
-    fill_gv(gv_ref)
-    send(gv_ref, gv_hbm, low)
-    fill_gk(gk_ref)
-    send(gk_ref, gk_hbm, low)
+    fill_gv(gv_ref, lambda p, c: send(gv_ref.at[:, p], gv_hbm, c))
+    fill_gk(gk_ref, lambda p, c: send(gk_ref.at[:, p], gk_hbm, c))
     for copy in copies:
         copy.wait()
 
@@ -546,10 +550,11 @@
             name=name,
         )
 
+    four = 4 * HEAD_DIM
     near = call(
         functools.partial(pack_kernel, prior), "near_keys",
         [anywhere] * 2, inside, near16(prior, width),
-        [pltpu.SemaphoreType.DMA((2,))], (0, 0, 0, 0), 4 * prior * width,
+        [pltpu.SemaphoreType.DMA((2, 2))], (0, 0, 0, 0), 4 * prior * width,
     )(*in_hbm(key_in, value_in))
     near = neighbour(near, 1)
 
@@ -562,7 +567,7 @@
         + [near32(2 * prior, 2 * prior), near32(prior, 2 * prior)],
         [
             pltpu.VMEM(lengths.shape, jnp.int32), pltpu.SemaphoreType.DMA((4,)),
-            pltpu.SemaphoreType.DMA((2,)), pltpu.SemaphoreType.DMA(()),
+            pltpu.SemaphoreType.DMA((2, 1)), pltpu.SemaphoreType.DMA(()),
         ],
         (0, 0, 0, 0), 18 * tok * width,
     )(*in_hbm(lengths, query_in, key_in, value_in, grad_out))
@@ -600,7 +605,7 @@
     gk, gv = call(
         functools.partial(last_kernel, prior), "last_keys",
         [inside] * 8 + [anywhere] * 2, [anywhere] * 2, [full16] * 2,
-        [near16(prior, width // 2)] * 2 + [pltpu.SemaphoreType.DMA((4,))],
+        [near16(prior, width // 2)] * 2 + [pltpu.SemaphoreType.DMA((2 + width // four,))],
         work, 6 * tok * width, {8: 0, 9: 1},
     )(*here, *in_vmem(backs[1], *halves), gk, gv)
     return (attn, gq, gk, gv)

time: 26.1 us -> 26.1 us (level)
  no operation moved by 1% of the time
where the time goes in v25:
time: 26.1 us; the launch traced here: 25.8 us
  starting transfers between devices  10.8 us (41%)
  Pallas kernels  8.74 us (33%)
  waiting for transfers between devices  5.52 us (21%)
  between operations  0.71 us (3%)
    ppermute x4, starting transfers between devices, neighbour(): return lax.ppermute(value, ('seq', 'head'), pairs)  10.8 us
    ppermute x4, waiting for transfers between devices, neighbour(): return lax.ppermute(value, ('seq', 'head'), pairs)  5.52 us
    pallas_call x1, Pallas kernels, halo_shards(): call(functools.partial(lead_kernel, prior, step), 'lead_rows', [inside] *...  2.2 us
    pallas_call x1, Pallas kernels, halo_shards(): call(functools.partial(ready_kernel, prior), 'operands', [anywhere] * 5,...  1.68 us
    pallas_call x1, Pallas kernels, halo_shards(): call(functools.partial(own_kernel, prior, step), 'own_block', [inside] *...  1.49 us
    pallas_call x1, Pallas kernels, halo_shards(): call(functools.partial(last_kernel, prior), 'last_keys', [inside] * 8 + [...  1.18 us
    pallas_call x1, Pallas kernels, halo_shards(): call(functools.partial(pack_kernel, prior), 'near_keys', [anywhere] * 2,...  0.97 us
    pallas_call x1, Pallas kernels, halo_shards(): call(functools.partial(near_kernel, prior), 'near_terms', [inside] * 7, [...  0.73 us
  transfers between devices with their start and end apart: 4, of which 3 were waited for; matrix products, arithmetic and copies ran while one was open for 0% of the time, Pallas kernels for 26%

profile of v25, /device:TPU:0, one launch (start us, length us, event | category | flops | bytes accessed | tf_op | source)
XLA Modules:
  0.0 25.8 jit_solution(12267232995990030239)
XLA Ops:
  0.6 1.0 %near_keys.1 = bf16[64,2048]{1,0:T(8,128)(2,1)S(1)} custom-call(bf16[128,2048]{1,0:T(8,128)(2,1)} %k_ref.1, bf16[128,2048]{1,0:T(8,128)(2,1)} %v_ref.1), custom_call_target="tpu_custom_call" | custom-call | bytes 524288 | tf_op jit(solution)/shard_map/near_keys/pallas_call | solution.py:554
  1.6 4.9 %collective-permute-start = (bf16[64,2048]{1,0:T(8,128)(2,1)S(1)}, bf16[64,2048]{1,0:T(8,128)(2,1)S(1)}, u32[]{:S(2)}, u32[]{:S(2)}) collective-permute-start(bf16[64,2048]{1,0:T(8,128)(2,1)S(1)} %near_keys.1), channel_id=1, source_target_pairs={{0,1},{1,2},{2,3},{3,4},{4,5},{5,6},{6,7},{7,8},{8,9},{9,10},{10,1... | collective-permute-start | bytes 786440 | tf_op jit(solution)/shard_map/ppermute | solution.py:508
  6.5 1.7 %operands.1 = (bf16[64,2048]{1,0:T(8,128)(2,1)S(1)}, bf16[128,2048]{1,0:T(8,128)(2,1)S(1)}, bf16[128,2048]{1,0:T(8,128)(2,1)S(1)}, bf16[128,2048]{1,0:T(8,128)(2...) custom-call(s32[1,128]{1,0:T(1,128)} %bitcast.1, ...), custom_call_target="tpu_custom_call" | custom-call | bytes 4718592 | tf_op jit(solution)/shard_map/operands/pallas_call | solution.py:562
  8.2 3.4 %collective-permute-start.1 = (bf16[64,2048]{1,0:T(8,128)(2,1)S(1)}, bf16[64,2048]{1,0:T(8,128)(2,1)S(1)}, u32[]{:S(2)}, u32[]{:S(2)}) collective-permute-start(bf16[64,2048]{1,0:T(8,128)(2,1)S(1)} %get-tuple-element.34), channel_id=1, source_target_pairs={{0,1},{1,2},{2,3},{3,4},{4,5},{5,6},{6,7},{7,8},{8,9},{9,10},{10,1... | collective-permute-start | bytes 786440 | tf_op jit(solution)/shard_map/ppermute | solution.py:508
  11.6 1.5 %own_block.1 = (bf16[64,2048]{1,0:T(8,128)(2,1)S(1)}, bf16[64,2048]{1,0:T(8,128)(2,1)S(1)}, f32[128,2048]{1,0:T(8,128)S(1)}, f32[128,2048]{1,0:T(8,128)S(1)}) custom-call(f32[128,128]{1,0:T(8,128)S(1)} %get-tuple-element.35.bias_ref, bf16[128,2048]{1,0:T(8,128)(2,1)S(1)} %get-tuple-element.30.q_ref, bf16[128,2048]{1,0:T(8,128)(2,1)S(1)} %get-tuple-element.31.k_ref, ...), custom_call_target="tpu_custom_call" | custom-call | flops 201326592 | bytes 4718592 | tf_op jit(solution)/shard_map/own_block/pallas_call | solution.py:576
  13.1 0.0 collective-permute-done.near_ref
  13.1 0.7 %near_terms.1 = (bf16[64,1024]{1,0:T(8,128)(2,1)S(1)}, bf16[64,1024]{1,0:T(8,128)(2,1)S(1)}) custom-call(f32[96,128]{1,0:T(8,128)S(1)} %get-tuple-element.45.near_bias_ref, f32[128,128]{1,0:T(8,128)S(1)} %get-tuple-element.29.bias_ref.lead_bias_ref, bf16[128,2048]{1,0:T(8,128)(2,1)S(1)} %get-tuple-element.30.q_ref, ...), custom_call_target="tpu_custom_call" | custom-call | flops 75497472 | bytes 2097152 | tf_op jit(solution)/shard_map/near_terms/pallas_call | solution.py:584
  13.8 1.3 %collective-permute-start.3 = (bf16[64,1024]{1,0:T(8,128)(2,1)S(1)}, bf16[64,1024]{1,0:T(8,128)(2,1)S(1)}, u32[]{:S(2)}, u32[]{:S(2)}) collective-permute-start(bf16[64,1024]{1,0:T(8,128)(2,1)S(1)} %get-tuple-element.47), channel_id=1, source_target_pairs={{1,0},{2,1},{3,2},{4,3},{5,4},{6,5},{7,6},{8,7},{9,8},{10,9},{11,1... | collective-permute-start | bytes 393224 | tf_op jit(solution)/shard_map/ppermute | solution.py:508
  15.1 1.3 %collective-permute-start.2 = (bf16[64,1024]{1,0:T(8,128)(2,1)S(1)}, bf16[64,1024]{1,0:T(8,128)(2,1)S(1)}, u32[]{:S(2)}, u32[]{:S(2)}) collective-permute-start(bf16[64,1024]{1,0:T(8,128)(2,1)S(1)} %get-tuple-element.46), channel_id=1, source_target_pairs={{1,0},{2,1},{3,2},{4,3},{5,4},{6,5},{7,6},{8,7},{9,8},{10,9},{11,1... | collective-permute-start | bytes 393224 | tf_op jit(solution)/shard_map/ppermute | solution.py:508
  16.4 1.2 %collective-permute-done.1.far_ref = bf16[64,2048]{1,0:T(8,128)(2,1)S(1)} collective-permute-done((bf16[64,2048]{1,0:T(8,128)(2,1)S(1)}, bf16[64,2048]{1,0:T(8,128)(2,1)S(1)}, u32[]{:S(2)}, u32[]{:S(2)}) %collective-permute-start.1) | collective-permute-done | bytes 262176 | tf_op jit(solution)/shard_map/ppermute | solution.py:508
  17.6 2.2 %lead_rows.1 = (bf16[128,2048]{1,0:T(8,128)(2,1)}, bf16[128,2048]{1,0:T(8,128)(2,1)}, bf16[128,2048]{1,0:T(8,128)(2,1)}, bf16[128,2048]{1,0:T(8,128)(2,1)}) custom-call(f32[128,128]{1,0:T(8,128)S(1)} %get-tuple-element.29.bias_ref.lead_bias_ref, bf16[128,2048]{1,0:T(8,128)(2,1)S(1)} %get-tuple-element.30.q_ref, ...), custom_call_target="tpu_custom_call" | custom-call | flops 201326592 | bytes 5242880 | tf_op jit(solution)/shard_map/lead_rows/pallas_call | solution.py:591
  19.8 2.6 %collective-permute-done.3.after_ref = bf16[64,1024]{1,0:T(8,128)(2,1)S(1)} collective-permute-done((bf16[64,1024]{1,0:T(8,128)(2,1)S(1)}, bf16[64,1024]{1,0:T(8,128)(2,1)S(1)}, u32[]{:S(2)}, u32[]{:S(2)}) %collective-permute-start.3) | collective-permute-done | bytes 131104 | tf_op jit(solution)/shard_map/ppermute | solution.py:508
  22.4 0.5 %tail_keys.1 = (bf16[64,1024]{1,0:T(8,128)(2,1)S(1)}, bf16[64,1024]{1,0:T(8,128)(2,1)S(1)}) custom-call(f32[64,128]{1,0:T(8,128)S(1)} %get-tuple-element.44.bias_ref, bf16[128,2048]{1,0:T(8,128)(2,1)S(1)} %get-tuple-element.31.k_ref, bf16[128,2048]{1,0:T(8,128)(2,1)S(1)} %get-tuple-element.32.v_ref, f32[128,2048]{1,0:T(8,128)S(1)} %get-tuple-element.36.gk_part_ref, ...), custom_call_target="tpu_custom_call" | custom-call | flops 16777216 | bytes 1048576 | tf_op jit(solution)/shard_map/tail_keys/pallas_call | solution.py:601
  22.9 1.7 %collective-permute-done.2.after_ref = bf16[64,1024]{1,0:T(8,128)(2,1)S(1)} collective-permute-done((bf16[64,1024]{1,0:T(8,128)(2,1)S(1)}, bf16[64,1024]{1,0:T(8,128)(2,1)S(1)}, u32[]{:S(2)}, u32[]{:S(2)}) %collective-permute-start.2) | collective-permute-done | bytes 131104 | tf_op jit(solution)/shard_map/ppermute | solution.py:508
  24.6 1.2 %last_keys.1 = (bf16[128,2048]{1,0:T(8,128)(2,1)}, bf16[128,2048]{1,0:T(8,128)(2,1)}) custom-call(f32[64,128]{1,0:T(8,128)S(1)} %get-tuple-element.44.bias_ref, bf16[128,2048]{1,0:T(8,128)(2,1)S(1)} %get-tuple-element.31.k_ref, bf16[128,2048]{1,0:T(8,128)(2,1)S(1)} %get-tuple-element.32.v_ref, ...), custom_call_target="tpu_custom_call", output_to_operand_aliasing={{0}: (8, {}), {1}: (9, {})} | custom-call | flops 16777216 | bytes 1572864 | tf_op jit(solution)/shard_map/last_keys/pallas_call | solution.py:605
Async XLA Ops:
  1.6 11.5 %collective-permute-start = (bf16[64,2048]{1,0:T(8,128)(2,1)S(1)}, bf16[64,2048]{1,0:T(8,128)(2,1)S(1)}, u32[]{:S(2)}, u32[]{:S(2)}) collective-permute-start(bf16[64,2048]{1,0:T(8,128)(2,1)S(1)} %near_keys.1), channel_id=1, source_target_pairs={{0,1},{1,2},{2,3},{3,4},{4,5},{5,6},{6,7},{7,8},{8,9},{9,10},{10,1... | collective-permute-start | bytes 786440 | tf_op jit(solution)/shard_map/ppermute | solution.py:508
  8.2 9.5 %collective-permute-start.1 = (bf16[64,2048]{1,0:T(8,128)(2,1)S(1)}, bf16[64,2048]{1,0:T(8,128)(2,1)S(1)}, u32[]{:S(2)}, u32[]{:S(2)}) collective-permute-start(bf16[64,2048]{1,0:T(8,128)(2,1)S(1)} %get-tuple-element.34), channel_id=1, source_target_pairs={{0,1},{1,2},{2,3},{3,4},{4,5},{5,6},{6,7},{7,8},{8,9},{9,10},{10,1... | collective-permute-start | bytes 786440 | tf_op jit(solution)/shard_map/ppermute | solution.py:508
  13.8 8.6 %collective-permute-start.3 = (bf16[64,1024]{1,0:T(8,128)(2,1)S(1)}, bf16[64,1024]{1,0:T(8,128)(2,1)S(1)}, u32[]{:S(2)}, u32[]{:S(2)}) collective-permute-start(bf16[64,1024]{1,0:T(8,128)(2,1)S(1)} %get-tuple-element.47), channel_id=1, source_target_pairs={{1,0},{2,1},{3,2},{4,3},{5,4},{6,5},{7,6},{8,7},{9,8},{10,9},{11,1... | collective-permute-start | bytes 393224 | tf_op jit(solution)/shard_map/ppermute | solution.py:508
  15.1 9.5 %collective-permute-start.2 = (bf16[64,1024]{1,0:T(8,128)(2,1)S(1)}, bf16[64,1024]{1,0:T(8,128)(2,1)S(1)}, u32[]{:S(2)}, u32[]{:S(2)}) collective-permute-start(bf16[64,1024]{1,0:T(8,128)(2,1)S(1)} %get-tuple-element.46), channel_id=1, source_target_pairs={{1,0},{2,1},{3,2},{4,3},{5,4},{6,5},{7,6},{8,7},{9,8},{10,9},{11,1... | collective-permute-start | bytes 393224 | tf_op jit(solution)/shard_map/ppermute | solution.py:508

commit v26 on v21

--- a/solution.py
+++ b/solution.py
@@ -268,12 +268,14 @@
     ]
 
 
-def pack_kernel(prior, k_ref, v_ref, near_ref, sems):
-    copies = pack_copies(prior, 0, k_ref, v_ref, near_ref, sems)
-    for copy in copies:
-        copy.start()
-    for copy in copies:
-        copy.wait()
+def pack_kernel(prior, odd, k_ref, v_ref, near_ref, sems):
+    @pl.when(lax.axis_index("head") % 2 == odd)
+    def _():
+        copies = pack_copies(prior, 0, k_ref, v_ref, near_ref, sems)
+        for copy in copies:
+            copy.start()
+        for copy in copies:
+            copy.wait()
 
 
 def ready_kernel(
@@ -335,8 +337,14 @@
             gv_ref[:, c] = dot(w, do, 1, 0)
 
 
+def came(odd_ref, even_ref, rows, cols):
+    to_odd = lax.axis_index("head") % 2 == 1
+    return jnp.where(to_odd, even_ref[rows, cols], odd_ref[rows, cols])
+
+
 def near_kernel(
-    prior, near_bias_ref, lead_bias_ref, q_ref, k_ref, v_ref, do_ref, near_ref, *back_refs
+    prior, near_bias_ref, lead_bias_ref, q_ref, k_ref, v_ref, do_ref, near_odd_ref, near_even_ref,
+    *back_refs,
 ):
     width, half = q_ref.shape[1], prior // 2
     far = lead_bias_ref[half - 1 : half, 0:1] == 0.0
@@ -349,8 +357,8 @@
     cotangents = [side_by_side(do_ref[early, c]) for c in columns]
     pairs = []
     for c, q, do in zip(columns, queries, cotangents):
-        k = jnp.concatenate([near_ref[first, c], k_ref[early, c]], axis=0)
-        v = jnp.concatenate([near_ref[second, c], v_ref[early, c]], axis=0)
+        k = jnp.concatenate([came(near_odd_ref, near_even_ref, first, c), k_ref[early, c]], axis=0)
+        v = jnp.concatenate([came(near_odd_ref, near_even_ref, second, c), v_ref[early, c]], axis=0)
         pairs.append(score_pair(k, q, v, do, bias))
     weights, logs, deltas = softmax_columns(pairs)
     weights = [w[:half] for w in weights]
@@ -371,8 +379,8 @@
 
 
 def lead_kernel(
-    prior, step, bias_ref, q_ref, k_ref, v_ref, do_ref, near_ref, far_ref, gk_part_ref, gv_part_ref,
-    attn_late_ref, gq_late_ref, attn_hbm, gq_hbm, gk_hbm, gv_hbm,
+    prior, step, bias_ref, q_ref, k_ref, v_ref, do_ref, near_odd_ref, near_even_ref, far_ref,
+    gk_part_ref, gv_part_ref, attn_late_ref, gq_late_ref, attn_hbm, gq_hbm, gk_hbm, gv_hbm,
     attn_ref, gq_ref, gk_ref, gv_ref, sems, late_sems,
 ):
     tok, width = q_ref.shape
@@ -401,11 +409,17 @@
         queries = [side_by_side(q_ref[early, c]) for c in columns]
         cotangents = [side_by_side(do_ref[early, c]) for c in columns]
         keys = [
-            jnp.concatenate([far_ref[first, c], near_ref[first, c], k_ref[early, c]], axis=0)
+            jnp.concatenate(
+                [far_ref[first, c], came(near_odd_ref, near_even_ref, first, c), k_ref[early, c]],
+                axis=0,
+            )
             for c in columns
         ]
         values = [
-            jnp.concatenate([far_ref[second, c], near_ref[second, c], v_ref[early, c]], axis=0)
+            jnp.concatenate(
+                [far_ref[second, c], came(near_odd_ref, near_even_ref, second, c), v_ref[early, c]],
+                axis=0,
+            )
             for c in columns
         ]
         pairs = [
@@ -498,9 +512,9 @@
         copy.wait()
 
 
-def neighbour(value, by):
+def neighbour(value, by, sources=(0, 1)):
     peers = lax.axis_size("seq") * lax.axis_size("head")
-    pairs = [(i, i + by) for i in range(peers) if 0 <= i + by < peers]
+    pairs = [(i, i + by) for i in range(peers) if 0 <= i + by < peers and i % 2 in sources]
     return lax.ppermute(value, ("seq", "head"), pairs)
 
 
@@ -546,12 +560,17 @@
             name=name,
         )
 
-    near = call(
-        functools.partial(pack_kernel, prior), "near_keys",
-        [anywhere] * 2, inside, near16(prior, width),
-        [pltpu.SemaphoreType.DMA((2,))], (0, 0, 0, 0), 4 * prior * width,
-    )(*in_hbm(key_in, value_in))
-    near = neighbour(near, 1)
+    nears = [
+        neighbour(
+            call(
+                functools.partial(pack_kernel, prior, odd), "near_keys",
+                [anywhere] * 2, inside, near16(prior, width),
+                [pltpu.SemaphoreType.DMA((2,))], (0, 0, 0, 0), 4 * prior * width,
+            )(*in_hbm(key_in, value_in)),
+            1, (odd,),
+        )
+        for odd in (1, 0)
+    ]
 
     lengths = module_lengths.reshape(1, -1)
     far, q, k, v, do, own_bias, near_bias, lead_bias, tail_bias = call(
@@ -578,18 +597,18 @@
     near_bias, attn = lax.optimization_barrier((near_bias, attn))
     backs = call(
         functools.partial(near_kernel, prior), "near_terms",
-        [inside] * 7, [inside] * 2, [near16(prior, width // 2)] * 2, (),
+        [inside] * 8, [inside] * 2, [near16(prior, width // 2)] * 2, (),
         (width // HEAD_DIM, prior, prior + prior // 2, 3), 8 * tok * width,
-    )(*in_vmem(near_bias, lead_bias, q, k, v, do, near))
+    )(*in_vmem(near_bias, lead_bias, q, k, v, do, *nears))
     backs = [neighbour(back, -1) for back in backs]
 
     attn, gq, gk, gv = call(
         functools.partial(lead_kernel, prior, step), "lead_rows",
-        [inside] * 11, [anywhere] * 4, [full16] * 4,
+        [inside] * 12, [anywhere] * 4, [full16] * 4,
         [near16(prior, width)] * 4
         + [pltpu.SemaphoreType.DMA((groups, 4)), pltpu.SemaphoreType.DMA((2,))],
         (width // HEAD_DIM, prior, 2 * prior, 6), 20 * tok * width,
-    )(*in_vmem(lead_bias, q, k, v, do, near, far, gk_part, gv_part, attn, gq))
+    )(*in_vmem(lead_bias, q, k, v, do, *nears, far, gk_part, gv_part, attn, gq))
 
     here = in_vmem(tail_bias, k, v, gk_part, gv_part)
     work = (width // HEAD_DIM // 2, prior, prior // 2, 4)

time: 26.1 us -> 28.1 us (1.077)
  waiting for transfers between devices: 5.52 us -> 7.04 us
  starting transfers between devices: 10.8 us -> 11.2 us
    ppermute x4 -> x5, waiting for transfers between devices: 5.52 us -> 7.04 us  [neighbour(): return lax.ppermute(value, ('seq', 'head'), pairs)]
    ppermute x4 -> x5, starting transfers between devices: 10.8 us -> 11.2 us  [neighbour(): return lax.ppermute(value, ('seq', 'head'), pairs)]
    pallas_call x2 -> x3, Pallas kernels: 1.72 us -> 1.76 us  [the longest x2 1.03 us: halo_shards(): call(functools.partial(pack_kernel, prior, odd), 'near_keys', [anywhere]...]
  transfers between devices with their start and end apart: 4 -> 5, of which waited for: 3 -> 4; matrix products, arithmetic and copies ran while one was open for 0% -> 0% of each run, Pallas kernels for 26% -> 27%
where the time goes in v26:
time: 28.1 us; the launch traced here: 27.8 us
  starting transfers between devices  11.2 us (40%)
  Pallas kernels  8.81 us (31%)
  waiting for transfers between devices  7.04 us (25%)
  between operations  0.72 us (3%)
    ppermute x5, starting transfers between devices, neighbour(): return lax.ppermute(value, ('seq', 'head'), pairs)  11.2 us
    ppermute x5, waiting for transfers between devices, neighbour(): return lax.ppermute(value, ('seq', 'head'), pairs)  7.04 us
    pallas_call x1, Pallas kernels, halo_shards(): call(functools.partial(lead_kernel, prior, step), 'lead_rows', [inside] *...  2.2 us
    pallas_call x1, Pallas kernels, halo_shards(): call(functools.partial(ready_kernel, prior), 'operands', [anywhere] * 5,...  1.68 us
    pallas_call x1, Pallas kernels, halo_shards(): call(functools.partial(own_kernel, prior, step), 'own_block', [inside] *...  1.49 us
    pallas_call x1, Pallas kernels, halo_shards(): call(functools.partial(last_kernel, prior), 'last_keys', [inside] * 8 + [...  1.19 us
    pallas_call x2, Pallas kernels, halo_shards(): call(functools.partial(pack_kernel, prior, odd), 'near_keys', [anywhere]...  1.03 us
    pallas_call x1, Pallas kernels, halo_shards(): call(functools.partial(near_kernel, prior), 'near_terms', [inside] * 8, [...  0.73 us
  transfers between devices with their start and end apart: 5, of which 4 were waited for; matrix products, arithmetic and copies ran while one was open for 0% of the time, Pallas kernels for 27%

profile of v26, /device:TPU:0, one launch (start us, length us, event | category | flops | bytes accessed | tf_op | source)
XLA Modules:
  0.0 27.8 jit_solution(11138065297061790794)
XLA Ops:
  0.7 0.7 %collective-permute-start = (bf16[64,2048]{1,0:T(8,128)(2,1)S(1)}, bf16[64,2048]{1,0:T(8,128)(2,1)S(1)}, u32[]{:S(2)}, u32[]{:S(2)}) collective-permute-start(bf16[64,2048]{1,0:T(8,128)(2,1)S(1)} %near_keys.2), channel_id=1, source_target_pairs={{1,2},{3,4},{5,6},{7,8},{9,10},{11,12},{13,14},{15,16},{17,18},{19... | collective-permute-start | bytes 786440 | tf_op jit(solution)/shard_map/ppermute | solution.py:518
  1.4 1.0 %near_keys.3 = bf16[64,2048]{1,0:T(8,128)(2,1)S(1)} custom-call(bf16[128,2048]{1,0:T(8,128)(2,1)} %k_ref.3, bf16[128,2048]{1,0:T(8,128)(2,1)} %v_ref.3), custom_call_target="tpu_custom_call" | custom-call | bytes 524288 | tf_op jit(solution)/shard_map/near_keys/pallas_call | solution.py:565
  2.4 6.6 %collective-permute-start.1 = (bf16[64,2048]{1,0:T(8,128)(2,1)S(1)}, bf16[64,2048]{1,0:T(8,128)(2,1)S(1)}, u32[]{:S(2)}, u32[]{:S(2)}) collective-permute-start(bf16[64,2048]{1,0:T(8,128)(2,1)S(1)} %near_keys.3), channel_id=1, source_target_pairs={{0,1},{2,3},{4,5},{6,7},{8,9},{10,11},{12,13},{14,15},{16,17},{18,... | collective-permute-start | bytes 786440 | tf_op jit(solution)/shard_map/ppermute | solution.py:518
  9.0 1.7 %operands.1 = (bf16[64,2048]{1,0:T(8,128)(2,1)S(1)}, bf16[128,2048]{1,0:T(8,128)(2,1)S(1)}, bf16[128,2048]{1,0:T(8,128)(2,1)S(1)}, bf16[128,2048]{1,0:T(8,128)(2...) custom-call(s32[1,128]{1,0:T(1,128)} %bitcast.1, ...), custom_call_target="tpu_custom_call" | custom-call | bytes 4718592 | tf_op jit(solution)/shard_map/operands/pallas_call | solution.py:576
  10.7 1.3 %collective-permute-start.2 = (bf16[64,2048]{1,0:T(8,128)(2,1)S(1)}, bf16[64,2048]{1,0:T(8,128)(2,1)S(1)}, u32[]{:S(2)}, u32[]{:S(2)}) collective-permute-start(bf16[64,2048]{1,0:T(8,128)(2,1)S(1)} %get-tuple-element.34), channel_id=1, source_target_pairs={{0,1},{1,2},{2,3},{3,4},{4,5},{5,6},{6,7},{7,8},{8,9},{9,10},{10,1... | collective-permute-start | bytes 786440 | tf_op jit(solution)/shard_map/ppermute | solution.py:518
  12.0 1.5 %own_block.1 = (bf16[64,2048]{1,0:T(8,128)(2,1)S(1)}, bf16[64,2048]{1,0:T(8,128)(2,1)S(1)}, f32[128,2048]{1,0:T(8,128)S(1)}, f32[128,2048]{1,0:T(8,128)S(1)}) custom-call(f32[128,128]{1,0:T(8,128)S(1)} %get-tuple-element.35.bias_ref, bf16[128,2048]{1,0:T(8,128)(2,1)S(1)} %get-tuple-element.30.q_ref, bf16[128,2048]{1,0:T(8,128)(2,1)S(1)} %get-tuple-element.31.k_ref, ...), custom_call_target="tpu_custom_call" | custom-call | flops 201326592 | bytes 4718592 | tf_op jit(solution)/shard_map/own_block/pallas_call | solution.py:590
  13.5 0.0 collective-permute-done.near_odd_ref
  13.5 2.2 %collective-permute-done.1.near_even_ref = bf16[64,2048]{1,0:T(8,128)(2,1)S(1)} collective-permute-done((bf16[64,2048]{1,0:T(8,128)(2,1)S(1)}, bf16[64,2048]{1,0:T(8,128)(2,1)S(1)}, u32[]{:S(2)}, u32[]{:S(2)}) %collective-permute-start.1) | collective-permute-done | bytes 262176 | tf_op jit(solution)/shard_map/ppermute | solution.py:518
  15.7 0.7 %near_terms.1 = (bf16[64,1024]{1,0:T(8,128)(2,1)S(1)}, bf16[64,1024]{1,0:T(8,128)(2,1)S(1)}) custom-call(f32[96,128]{1,0:T(8,128)S(1)} %get-tuple-element.45.near_bias_ref, f32[128,128]{1,0:T(8,128)S(1)} %get-tuple-element.29.bias_ref.lead_bias_ref, bf16[128,2048]{1,0:T(8,128)(2,1)S(1)} %get-tuple-element.30.q_ref, ...), custom_call_target="tpu_custom_call" | custom-call | flops 75497472 | bytes 2097152 | tf_op jit(solution)/shard_map/near_terms/pallas_call | solution.py:598
  16.5 1.3 %collective-permute-start.4 = (bf16[64,1024]{1,0:T(8,128)(2,1)S(1)}, bf16[64,1024]{1,0:T(8,128)(2,1)S(1)}, u32[]{:S(2)}, u32[]{:S(2)}) collective-permute-start(bf16[64,1024]{1,0:T(8,128)(2,1)S(1)} %get-tuple-element.47), channel_id=1, source_target_pairs={{1,0},{2,1},{3,2},{4,3},{5,4},{6,5},{7,6},{8,7},{9,8},{10,9},{11,1... | collective-permute-start | bytes 393224 | tf_op jit(solution)/shard_map/ppermute | solution.py:518
  17.8 1.3 %collective-permute-start.3 = (bf16[64,1024]{1,0:T(8,128)(2,1)S(1)}, bf16[64,1024]{1,0:T(8,128)(2,1)S(1)}, u32[]{:S(2)}, u32[]{:S(2)}) collective-permute-start(bf16[64,1024]{1,0:T(8,128)(2,1)S(1)} %get-tuple-element.46), channel_id=1, source_target_pairs={{1,0},{2,1},{3,2},{4,3},{5,4},{6,5},{7,6},{8,7},{9,8},{10,9},{11,1... | collective-permute-start | bytes 393224 | tf_op jit(solution)/shard_map/ppermute | solution.py:518
  19.1 0.8 %collective-permute-done.2.far_ref = bf16[64,2048]{1,0:T(8,128)(2,1)S(1)} collective-permute-done((bf16[64,2048]{1,0:T(8,128)(2,1)S(1)}, bf16[64,2048]{1,0:T(8,128)(2,1)S(1)}, u32[]{:S(2)}, u32[]{:S(2)}) %collective-permute-start.2) | collective-permute-done | bytes 262176 | tf_op jit(solution)/shard_map/ppermute | solution.py:518
  19.9 2.2 %lead_rows.1 = (bf16[128,2048]{1,0:T(8,128)(2,1)}, bf16[128,2048]{1,0:T(8,128)(2,1)}, bf16[128,2048]{1,0:T(8,128)(2,1)}, bf16[128,2048]{1,0:T(8,128)(2,1)}) custom-call(f32[128,128]{1,0:T(8,128)S(1)} %get-tuple-element.29.bias_ref.lead_bias_ref, bf16[128,2048]{1,0:T(8,128)(2,1)S(1)} %get-tuple-element.30.q_ref, ...), custom_call_target="tpu_custom_call" | custom-call | flops 201326592 | bytes 5242880 | tf_op jit(solution)/shard_map/lead_rows/pallas_call | solution.py:605
  22.1 2.3 %collective-permute-done.4.after_ref = bf16[64,1024]{1,0:T(8,128)(2,1)S(1)} collective-permute-done((bf16[64,1024]{1,0:T(8,128)(2,1)S(1)}, bf16[64,1024]{1,0:T(8,128)(2,1)S(1)}, u32[]{:S(2)}, u32[]{:S(2)}) %collective-permute-start.4) | collective-permute-done | bytes 131104 | tf_op jit(solution)/shard_map/ppermute | solution.py:518
  24.4 0.5 %tail_keys.1 = (bf16[64,1024]{1,0:T(8,128)(2,1)S(1)}, bf16[64,1024]{1,0:T(8,128)(2,1)S(1)}) custom-call(f32[64,128]{1,0:T(8,128)S(1)} %get-tuple-element.44.bias_ref, bf16[128,2048]{1,0:T(8,128)(2,1)S(1)} %get-tuple-element.31.k_ref, bf16[128,2048]{1,0:T(8,128)(2,1)S(1)} %get-tuple-element.32.v_ref, f32[128,2048]{1,0:T(8,128)S(1)} %get-tuple-element.36.gk_part_ref, ...), custom_call_target="tpu_custom_call" | custom-call | flops 16777216 | bytes 1048576 | tf_op jit(solution)/shard_map/tail_keys/pallas_call | solution.py:615
  24.9 1.7 %collective-permute-done.3.after_ref = bf16[64,1024]{1,0:T(8,128)(2,1)S(1)} collective-permute-done((bf16[64,1024]{1,0:T(8,128)(2,1)S(1)}, bf16[64,1024]{1,0:T(8,128)(2,1)S(1)}, u32[]{:S(2)}, u32[]{:S(2)}) %collective-permute-start.3) | collective-permute-done | bytes 131104 | tf_op jit(solution)/shard_map/ppermute | solution.py:518
  26.6 1.2 %last_keys.1 = (bf16[128,2048]{1,0:T(8,128)(2,1)}, bf16[128,2048]{1,0:T(8,128)(2,1)}) custom-call(f32[64,128]{1,0:T(8,128)S(1)} %get-tuple-element.44.bias_ref, bf16[128,2048]{1,0:T(8,128)(2,1)S(1)} %get-tuple-element.31.k_ref, bf16[128,2048]{1,0:T(8,128)(2,1)S(1)} %get-tuple-element.32.v_ref, ...), custom_call_target="tpu_custom_call", output_to_operand_aliasing={{0}: (8, {}), {1}: (9, {})} | custom-call | flops 16777216 | bytes 1572864 | tf_op jit(solution)/shard_map/last_keys/pallas_call | solution.py:619
  (1 shorter events, 0.0 us)
Async XLA Ops:
  0.7 12.8 %collective-permute-start = (bf16[64,2048]{1,0:T(8,128)(2,1)S(1)}, bf16[64,2048]{1,0:T(8,128)(2,1)S(1)}, u32[]{:S(2)}, u32[]{:S(2)}) collective-permute-start(bf16[64,2048]{1,0:T(8,128)(2,1)S(1)} %near_keys.2), channel_id=1, source_target_pairs={{1,2},{3,4},{5,6},{7,8},{9,10},{11,12},{13,14},{15,16},{17,18},{19... | collective-permute-start | bytes 786440 | tf_op jit(solution)/shard_map/ppermute | solution.py:518
  2.4 13.4 %collective-permute-start.1 = (bf16[64,2048]{1,0:T(8,128)(2,1)S(1)}, bf16[64,2048]{1,0:T(8,128)(2,1)S(1)}, u32[]{:S(2)}, u32[]{:S(2)}) collective-permute-start(bf16[64,2048]{1,0:T(8,128)(2,1)S(1)} %near_keys.3), channel_id=1, source_target_pairs={{0,1},{2,3},{4,5},{6,7},{8,9},{10,11},{12,13},{14,15},{16,17},{18,... | collective-permute-start | bytes 786440 | tf_op jit(solution)/shard_map/ppermute | solution.py:518
  10.7 9.2 %collective-permute-start.2 = (bf16[64,2048]{1,0:T(8,128)(2,1)S(1)}, bf16[64,2048]{1,0:T(8,128)(2,1)S(1)}, u32[]{:S(2)}, u32[]{:S(2)}) collective-permute-start(bf16[64,2048]{1,0:T(8,128)(2,1)S(1)} %get-tuple-element.34), channel_id=1, source_target_pairs={{0,1},{1,2},{2,3},{3,4},{4,5},{5,6},{6,7},{7,8},{8,9},{9,10},{10,1... | collective-permute-start | bytes 786440 | tf_op jit(solution)/shard_map/ppermute | solution.py:518
  16.5 7.9 %collective-permute-start.4 = (bf16[64,1024]{1,0:T(8,128)(2,1)S(1)}, bf16[64,1024]{1,0:T(8,128)(2,1)S(1)}, u32[]{:S(2)}, u32[]{:S(2)}) collective-permute-start(bf16[64,1024]{1,0:T(8,128)(2,1)S(1)} %get-tuple-element.47), channel_id=1, source_target_pairs={{1,0},{2,1},{3,2},{4,3},{5,4},{6,5},{7,6},{8,7},{9,8},{10,9},{11,1... | collective-permute-start | bytes 393224 | tf_op jit(solution)/shard_map/ppermute | solution.py:518
  17.8 8.8 %collective-permute-start.3 = (bf16[64,1024]{1,0:T(8,128)(2,1)S(1)}, bf16[64,1024]{1,0:T(8,128)(2,1)S(1)}, u32[]{:S(2)}, u32[]{:S(2)}) collective-permute-start(bf16[64,1024]{1,0:T(8,128)(2,1)S(1)} %get-tuple-element.46), channel_id=1, source_target_pairs={{1,0},{2,1},{3,2},{4,3},{5,4},{6,5},{7,6},{8,7},{9,8},{10,9},{11,1... | collective-permute-start | bytes 393224 | tf_op jit(solution)/shard_map/ppermute | solution.py:518

commit v27 on v24

--- a/solution.py
+++ b/solution.py
@@ -268,35 +268,41 @@
     ]
 
 
-def pack_kernel(prior, k_ref, v_ref, near_ref, sems):
-    copies = pack_copies(prior, 0, k_ref, v_ref, near_ref, sems)
+def pack_kernel(prior, k_ref, v_ref, near_ref, far_ref, near_sems, far_sems):
+    copies = pack_copies(prior, 0, k_ref, v_ref, near_ref, near_sems)
+    copies += pack_copies(prior, 1, k_ref, v_ref, far_ref, far_sems)
     for copy in copies:
         copy.start()
     for copy in copies:
         copy.wait()
 
 
-def ready_kernel(
-    prior, len_hbm, q_hbm, k_hbm, v_hbm, do_hbm, far_ref, q_ref, k_ref, v_ref, do_ref,
-    own_bias_ref, near_bias_ref, lead_bias_ref, tail_bias_ref, len_ref, sems, far_sems, len_sem,
-):
+def ready_kernel(prior, first_place, len_hbm, q_hbm, k_hbm, v_hbm, do_hbm, *refs):
+    (
+        q_ref, k_ref, v_ref, do_ref, own_bias_ref, near_bias_ref, lead_bias_ref, tail_bias_ref,
+        len_ref, sems, len_sem,
+    ) = refs[-11:]
     tok, half = k_ref.shape[0], prior // 2
     pairs = ((q_hbm, q_ref), (k_hbm, k_ref), (v_hbm, v_ref), (do_hbm, do_ref))
-    copies = pack_copies(prior, 1, k_hbm, v_hbm, far_ref, far_sems)
-    copies += [pltpu.make_async_copy(hbm, ref, sems.at[n]) for n, (hbm, ref) in enumerate(pairs)]
-    len_copy = pltpu.make_async_copy(len_hbm, len_ref, len_sem)
-    len_copy.start()
-    for copy in copies:
-        copy.start()
-    len_copy.wait()
-    first = device_first(tok)
-    lengths = len_ref[...].astype(jnp.float32)
-    own_bias_ref[...] = bias_by_key(lengths, first + prior, tok - prior, first, tok, 2)
-    near_bias_ref[...] = bias_by_key(lengths, first, prior, first - half, prior + half, 2)
-    lead_bias_ref[...] = bias_by_key(lengths, first, prior, first - prior, 2 * prior, 2)
-    tail_bias_ref[...] = bias_by_key(lengths, first + tok, half, first + tok - prior, prior, 4)
-    for copy in copies:
-        copy.wait()
+
+    @pl.when((lax.axis_index("head") == 0) == first_place)
+    def _():
+        copies = [pltpu.make_async_copy(hbm, ref, sems.at[n]) for n, (hbm, ref) in enumerate(pairs)]
+        len_copy = pltpu.make_async_copy(len_hbm, len_ref, len_sem)
+        len_copy.start()
+        for copy in copies:
+            copy.start()
+        len_copy.wait()
+        first = device_first(tok)
+        lengths = len_ref[...].astype(jnp.float32)
+        own_bias_ref[...] = bias_by_key(lengths, first + prior, tok - prior, first, tok, 2)
+        near_bias_ref[...] = bias_by_key(lengths, first, prior, first - half, prior + half, 2)
+        lead_bias_ref[...] = bias_by_key(lengths, first, prior, first - prior, 2 * prior, 2)
+        tail_bias_ref[...] = bias_by_key(
+            lengths, first + tok, half, first + tok - prior, prior, 4
+        )
+        for copy in copies:
+            copy.wait()
 
 
 def own_diagonal(both):
@@ -309,12 +315,12 @@
     return [pl.ds(pl.multiple_of(at * step + c, wide), wide) for c in range(0, step, wide)]
 
 
-def own_kernel(prior, step, odd, bias_ref, q_ref, k_ref, v_ref, do_ref, *refs):
+def own_kernel(prior, step, last_place, bias_ref, q_ref, k_ref, v_ref, do_ref, *refs):
     attn_ref, gq_ref, gk_ref, gv_ref = refs[-4:]
     tok, width = k_ref.shape
     late = slice(prior, tok)
 
-    @pl.when(lax.axis_index("seq") % 2 == odd)
+    @pl.when((lax.axis_index("head") == lax.axis_size("head") - 1) == last_place)
     def _():
         @pl.loop(0, width // step)
         def _(at):
@@ -547,47 +553,50 @@
             name=name,
         )
 
-    near = call(
-        functools.partial(pack_kernel, prior), "near_keys",
-        [anywhere] * 2, inside, near16(prior, width),
-        [pltpu.SemaphoreType.DMA((2,))], (0, 0, 0, 0), 4 * prior * width,
+    near, far = call(
+        functools.partial(pack_kernel, prior), "late_keys",
+        [anywhere] * 2, [inside] * 2, [near16(prior, width)] * 2,
+        [pltpu.SemaphoreType.DMA((2,))] * 2, (0, 0, 0, 0), 8 * prior * width,
     )(*in_hbm(key_in, value_in))
     near = neighbour(near, 1)
 
     lengths = module_lengths.reshape(1, -1)
-    far, q, k, v, do, own_bias, near_bias, lead_bias, tail_bias = call(
-        functools.partial(ready_kernel, prior), "operands",
-        [anywhere] * 5, [inside] * 9,
-        [near16(prior, width)] + [near16(tok, width)] * 4
-        + [near32(tok, 2 * prior), near32(prior + prior // 2, 2 * prior)]
-        + [near32(2 * prior, 2 * prior), near32(prior, 2 * prior)],
-        [
-            pltpu.VMEM(lengths.shape, jnp.int32), pltpu.SemaphoreType.DMA((4,)),
-            pltpu.SemaphoreType.DMA((2,)), pltpu.SemaphoreType.DMA(()),
-        ],
-        (0, 0, 0, 0), 18 * tok * width,
-    )(*in_hbm(lengths, query_in, key_in, value_in, grad_out))
-
-    def own_block(odd, *partial):
+
+    def operands(first_place, *held):
         return call(
-            functools.partial(own_kernel, prior, step, odd), "own_block",
+            functools.partial(ready_kernel, prior, first_place), "operands",
+            [anywhere] * 5 + [inside] * len(held), [inside] * 8,
+            [near16(tok, width)] * 4
+            + [near32(tok, 2 * prior), near32(prior + prior // 2, 2 * prior)]
+            + [near32(2 * prior, 2 * prior), near32(prior, 2 * prior)],
+            [
+                pltpu.VMEM(lengths.shape, jnp.int32), pltpu.SemaphoreType.DMA((4,)),
+                pltpu.SemaphoreType.DMA(()),
+            ],
+            (0, 0, 0, 0), 16 * tok * width, {5 + n: n for n in range(len(held))},
+        )(*in_hbm(lengths, query_in, key_in, value_in, grad_out), *in_vmem(*held))
+
+    def own_block(last_place, *partial):
+        return call(
+            functools.partial(own_kernel, prior, step, last_place), "own_block",
             [inside] * (5 + len(partial)), [inside] * 4,
             [near16(tok - prior, width)] * 2 + [near32(tok, width)] * 2, (),
             (width // HEAD_DIM, tok - prior, tok, 6), 18 * tok * width,
             {5 + n: n for n in range(len(partial))},
         )(*in_vmem(own_bias, q, k, v, do, *partial))
 
-    partial = own_block(0)
-    far, partial = lax.optimization_barrier((far, partial))
+    far, *held = lax.optimization_barrier((far, *operands(True)))
     far = neighbour(far, 1)
-    attn, gq, gk_part, gv_part = own_block(1, *partial)
-    near_bias, attn = lax.optimization_barrier((near_bias, attn))
+    q, k, v, do, own_bias, near_bias, lead_bias, tail_bias = operands(False, *held)
+    near_bias, *partial = lax.optimization_barrier((near_bias, *own_block(False)))
     backs = call(
         functools.partial(near_kernel, prior), "near_terms",
         [inside] * 7, [inside] * 2, [near16(prior, width // 2)] * 2, (),
         (width // HEAD_DIM, prior, prior + prior // 2, 3), 8 * tok * width,
     )(*in_vmem(near_bias, lead_bias, q, k, v, do, near))
+    own_bias, *backs = lax.optimization_barrier((own_bias, *backs))
     backs = [neighbour(back, -1) for back in backs]
+    attn, gq, gk_part, gv_part = own_block(True, *partial)
 
     attn, gq, gk, gv = call(
         functools.partial(lead_kernel, prior, step), "lead_rows",

time: 26.7 us -> 26.6 us (level)
    pallas_call x4 -> x5, Pallas kernels: 4.19 us -> 4.29 us  [the longest x2 1.65 us: operands(): call(functools.partial(ready_kernel, prior, first_place), 'operands', [an...]
where the time goes in v27:
time: 26.6 us; the launch traced here: 26.4 us
  starting transfers between devices  16.2 us (61%)
  Pallas kernels  8.9 us (33%)
  between operations  0.74 us (3%)
  waiting for transfers between devices  0.48 us (2%)
    ppermute x4, starting transfers between devices, neighbour(): return lax.ppermute(value, ('seq', 'head'), pairs)  16.2 us
    pallas_call x1, Pallas kernels, halo_shards(): call(functools.partial(lead_kernel, prior, step), 'lead_rows', [inside] *...  2.2 us
    pallas_call x2, Pallas kernels, operands(): call(functools.partial(ready_kernel, prior, first_place), 'operands', [an...  1.65 us
    pallas_call x2, Pallas kernels, own_block(): call(functools.partial(own_kernel, prior, step, last_place), 'own_block',...  1.51 us
    pallas_call x1, Pallas kernels, halo_shards(): call(functools.partial(last_kernel, prior), 'last_keys', [inside] * 8 + [...  1.19 us
    pallas_call x1, Pallas kernels, halo_shards(): call(functools.partial(pack_kernel, prior), 'late_keys', [anywhere] * 2,...  1.13 us
    pallas_call x1, Pallas kernels, halo_shards(): call(functools.partial(near_kernel, prior), 'near_terms', [inside] * 7, [...  0.73 us
  transfers between devices with their start and end apart: 4, of which 1 were waited for; matrix products, arithmetic and copies ran while one was open for 0% of the time, Pallas kernels for 25%

profile of v27, /device:TPU:1, one launch (start us, length us, event | category | flops | bytes accessed | tf_op | source)
XLA Modules:
  0.0 26.4 jit_solution(3563201000936216828)
XLA Ops:
  0.6 1.1 %late_keys.1 = (bf16[64,2048]{1,0:T(8,128)(2,1)S(1)}, bf16[64,2048]{1,0:T(8,128)(2,1)S(1)}) custom-call(bf16[128,2048]{1,0:T(8,128)(2,1)} %k_hbm.3, bf16[128,2048]{1,0:T(8,128)(2,1)} %v_hbm.3), custom_call_target="tpu_custom_call" | custom-call | bytes 1048576 | tf_op jit(solution)/shard_map/late_keys/pallas_call | solution.py:556
  1.8 3.9 %collective-permute-start = (bf16[64,2048]{1,0:T(8,128)(2,1)S(1)}, bf16[64,2048]{1,0:T(8,128)(2,1)S(1)}, u32[]{:S(2)}, u32[]{:S(2)}) collective-permute-start(bf16[64,2048]{1,0:T(8,128)(2,1)S(1)} %get-tuple-element.79), channel_id=1, source_target_pairs={{0,1},{1,2},{2,3},{3,4},{4,5},{5,6},{6,7},{7,8},{8,9},{9,10},{10,1... | collective-permute-start | bytes 786440 | tf_op jit(solution)/shard_map/ppermute | solution.py:511
  5.7 1.6 %operands.2 = (bf16[128,2048]{1,0:T(8,128)(2,1)S(1)}, bf16[128,2048]{1,0:T(8,128)(2,1)S(1)}, bf16[128,2048]{1,0:T(8,128)(2,1)S(1)}, bf16[128,2048]{1,0:T(8,128)(...) custom-call(s32[1,128]{1,0:T(1,128)} %bitcast.1, ...), custom_call_target="tpu_custom_call" | custom-call | bytes 4194304 | tf_op jit(solution)/shard_map/operands/pallas_call | solution.py:566
  7.3 1.9 %collective-permute-start.1 = (bf16[64,2048]{1,0:T(8,128)(2,1)S(1)}, bf16[64,2048]{1,0:T(8,128)(2,1)S(1)}, u32[]{:S(2)}, u32[]{:S(2)}) collective-permute-start(bf16[64,2048]{1,0:T(8,128)(2,1)S(1)} %get-tuple-element.80), channel_id=1, source_target_pairs={{0,1},{1,2},{2,3},{3,4},{4,5},{5,6},{6,7},{7,8},{8,9},{9,10},{10,1... | collective-permute-start | bytes 786440 | tf_op jit(solution)/shard_map/ppermute | solution.py:511
  9.3 0.1 operands.3
  9.3 1.5 %own_block.2 = (bf16[64,2048]{1,0:T(8,128)(2,1)S(1)}, bf16[64,2048]{1,0:T(8,128)(2,1)S(1)}, f32[128,2048]{1,0:T(8,128)S(1)}, f32[128,2048]{1,0:T(8,128)S(1)}) custom-call(f32[128,128]{1,0:T(8,128)S(1)} %get-tuple-element.90.bias_ref, bf16[128,2048]{1,0:T(8,128)(2,1)S(1)} %get-tuple-element.75.q_ref, bf16[128,2048]{1,0:T(8,128)(2,1)S(1)} %get-tuple-element.76.k_ref, ...), custom_call_target="tpu_custom_call" | custom-call | flops 201326592 | bytes 4718592 | tf_op jit(solution)/shard_map/own_block/pallas_call | solution.py:580
  10.8 0.5 %collective-permute-done.near_ref = bf16[64,2048]{1,0:T(8,128)(2,1)S(1)} collective-permute-done((bf16[64,2048]{1,0:T(8,128)(2,1)S(1)}, bf16[64,2048]{1,0:T(8,128)(2,1)S(1)}, u32[]{:S(2)}, u32[]{:S(2)}) %collective-permute-start) | collective-permute-done | bytes 262176 | tf_op jit(solution)/shard_map/ppermute | solution.py:511
  11.3 0.7 %near_terms.1 = (bf16[64,1024]{1,0:T(8,128)(2,1)S(1)}, bf16[64,1024]{1,0:T(8,128)(2,1)S(1)}) custom-call(f32[96,128]{1,0:T(8,128)S(1)} %get-tuple-element.87.near_bias_ref, f32[128,128]{1,0:T(8,128)S(1)} %get-tuple-element.74.lead_bias_ref.bias_ref, bf16[128,2048]{1,0:T(8,128)(2,1)S(1)} %get-tuple-element.75.q_ref, ...), custom_call_target="tpu_custom_call" | custom-call | flops 75497472 | bytes 2097152 | tf_op jit(solution)/shard_map/near_terms/pallas_call | solution.py:592
  12.0 7.0 %collective-permute-start.3 = (bf16[64,1024]{1,0:T(8,128)(2,1)S(1)}, bf16[64,1024]{1,0:T(8,128)(2,1)S(1)}, u32[]{:S(2)}, u32[]{:S(2)}) collective-permute-start(bf16[64,1024]{1,0:T(8,128)(2,1)S(1)} %get-tuple-element.103), channel_id=1, source_target_pairs={{1,0},{2,1},{3,2},{4,3},{5,4},{6,5},{7,6},{8,7},{9,8},{10,9},{11,1... | collective-permute-start | bytes 393224 | tf_op jit(solution)/shard_map/ppermute | solution.py:511
  19.1 3.3 %collective-permute-start.2 = (bf16[64,1024]{1,0:T(8,128)(2,1)S(1)}, bf16[64,1024]{1,0:T(8,128)(2,1)S(1)}, u32[]{:S(2)}, u32[]{:S(2)}) collective-permute-start(bf16[64,1024]{1,0:T(8,128)(2,1)S(1)} %get-tuple-element.102), channel_id=1, source_target_pairs={{1,0},{2,1},{3,2},{4,3},{5,4},{6,5},{7,6},{8,7},{9,8},{10,9},{11,1... | collective-permute-start | bytes 393224 | tf_op jit(solution)/shard_map/ppermute | solution.py:511
  22.4 0.0 collective-permute-done.1.far_ref
  22.4 2.2 %lead_rows.1 = (bf16[128,2048]{1,0:T(8,128)(2,1)}, bf16[128,2048]{1,0:T(8,128)(2,1)}, bf16[128,2048]{1,0:T(8,128)(2,1)}, bf16[128,2048]{1,0:T(8,128)(2,1)}) custom-call(f32[128,128]{1,0:T(8,128)S(1)} %get-tuple-element.74.lead_bias_ref.bias_ref, bf16[128,2048]{1,0:T(8,128)(2,1)S(1)} %get-tuple-element.75.q_ref, ...), custom_call_target="tpu_custom_call" | custom-call | flops 201326592 | bytes 5242880 | tf_op jit(solution)/shard_map/lead_rows/pallas_call | solution.py:601
  24.7 0.0 collective-permute-done.3.after_ref
  24.7 0.5 %tail_keys.1 = (bf16[64,1024]{1,0:T(8,128)(2,1)S(1)}, bf16[64,1024]{1,0:T(8,128)(2,1)S(1)}) custom-call(f32[64,128]{1,0:T(8,128)S(1)} %get-tuple-element.101.bias_ref, bf16[128,2048]{1,0:T(8,128)(2,1)S(1)} %get-tuple-element.76.k_ref, bf16[128,2048]{1,0:T(8,128)(2,1)S(1)} %get-tuple-element.77.v_ref, f32[128,2048]{1,0:T(8,128)S(1)} %get-tuple-element.95.gk_part_ref, ...), custom_call_target="tpu_custom_call" | custom-call | flops 16777216 | bytes 1048576 | tf_op jit(solution)/shard_map/tail_keys/pallas_call | solution.py:611
  25.2 0.0 collective-permute-done.2.after_ref
  25.2 1.2 %last_keys.1 = (bf16[128,2048]{1,0:T(8,128)(2,1)}, bf16[128,2048]{1,0:T(8,128)(2,1)}) custom-call(f32[64,128]{1,0:T(8,128)S(1)} %get-tuple-element.101.bias_ref, bf16[128,2048]{1,0:T(8,128)(2,1)S(1)} %get-tuple-element.76.k_ref, bf16[128,2048]{1,0:T(8,128)(2,1)S(1)} %get-tuple-element.77.v_ref, ...), custom_call_target="tpu_custom_call", output_to_operand_aliasing={{0}: (8, {}), {1}: (9, {})} | custom-call | flops 16777216 | bytes 1572864 | tf_op jit(solution)/shard_map/last_keys/pallas_call | solution.py:615
  (1 shorter events, 0.0 us)
Async XLA Ops:
  1.8 9.5 %collective-permute-start = (bf16[64,2048]{1,0:T(8,128)(2,1)S(1)}, bf16[64,2048]{1,0:T(8,128)(2,1)S(1)}, u32[]{:S(2)}, u32[]{:S(2)}) collective-permute-start(bf16[64,2048]{1,0:T(8,128)(2,1)S(1)} %get-tuple-element.79), channel_id=1, source_target_pairs={{0,1},{1,2},{2,3},{3,4},{4,5},{5,6},{6,7},{7,8},{8,9},{9,10},{10,1... | collective-permute-start | bytes 786440 | tf_op jit(solution)/shard_map/ppermute | solution.py:511
  7.3 15.1 %collective-permute-start.1 = (bf16[64,2048]{1,0:T(8,128)(2,1)S(1)}, bf16[64,2048]{1,0:T(8,128)(2,1)S(1)}, u32[]{:S(2)}, u32[]{:S(2)}) collective-permute-start(bf16[64,2048]{1,0:T(8,128)(2,1)S(1)} %get-tuple-element.80), channel_id=1, source_target_pairs={{0,1},{1,2},{2,3},{3,4},{4,5},{5,6},{6,7},{7,8},{8,9},{9,10},{10,1... | collective-permute-start | bytes 786440 | tf_op jit(solution)/shard_map/ppermute | solution.py:511
  12.0 12.6 %collective-permute-start.3 = (bf16[64,1024]{1,0:T(8,128)(2,1)S(1)}, bf16[64,1024]{1,0:T(8,128)(2,1)S(1)}, u32[]{:S(2)}, u32[]{:S(2)}) collective-permute-start(bf16[64,1024]{1,0:T(8,128)(2,1)S(1)} %get-tuple-element.103), channel_id=1, source_target_pairs={{1,0},{2,1},{3,2},{4,3},{5,4},{6,5},{7,6},{8,7},{9,8},{10,9},{11,1... | collective-permute-start | bytes 393224 | tf_op jit(solution)/shard_map/ppermute | solution.py:511
  19.1 6.1 %collective-permute-start.2 = (bf16[64,1024]{1,0:T(8,128)(2,1)S(1)}, bf16[64,1024]{1,0:T(8,128)(2,1)S(1)}, u32[]{:S(2)}, u32[]{:S(2)}) collective-permute-start(bf16[64,1024]{1,0:T(8,128)(2,1)S(1)} %get-tuple-element.102), channel_id=1, source_target_pairs={{1,0},{2,1},{3,2},{4,3},{5,4},{6,5},{7,6},{8,7},{9,8},{10,9},{11,1... | collective-permute-start | bytes 393224 | tf_op jit(solution)/shard_map/ppermute | solution.py:511

commit v28 on v27

--- a/solution.py
+++ b/solution.py
@@ -277,7 +277,7 @@
         copy.wait()
 
 
-def ready_kernel(prior, first_place, len_hbm, q_hbm, k_hbm, v_hbm, do_hbm, *refs):
+def ready_kernel(prior, at_end, len_hbm, q_hbm, k_hbm, v_hbm, do_hbm, *refs):
     (
         q_ref, k_ref, v_ref, do_ref, own_bias_ref, near_bias_ref, lead_bias_ref, tail_bias_ref,
         len_ref, sems, len_sem,
@@ -285,7 +285,9 @@
     tok, half = k_ref.shape[0], prior // 2
     pairs = ((q_hbm, q_ref), (k_hbm, k_ref), (v_hbm, v_ref), (do_hbm, do_ref))
 
-    @pl.when((lax.axis_index("head") == 0) == first_place)
+    place, last = lax.axis_index("head"), lax.axis_size("head") - 1
+
+    @pl.when(((place == 0) | (place == last)) == at_end)
     def _():
         copies = [pltpu.make_async_copy(hbm, ref, sems.at[n]) for n, (hbm, ref) in enumerate(pairs)]
         len_copy = pltpu.make_async_copy(len_hbm, len_ref, len_sem)
@@ -315,12 +317,12 @@
     return [pl.ds(pl.multiple_of(at * step + c, wide), wide) for c in range(0, step, wide)]
 
 
-def own_kernel(prior, step, last_place, bias_ref, q_ref, k_ref, v_ref, do_ref, *refs):
+def own_kernel(prior, step, behind, bias_ref, q_ref, k_ref, v_ref, do_ref, *refs):
     attn_ref, gq_ref, gk_ref, gv_ref = refs[-4:]
     tok, width = k_ref.shape
     late = slice(prior, tok)
 
-    @pl.when((lax.axis_index("head") == lax.axis_size("head") - 1) == last_place)
+    @pl.when((lax.axis_index("head") == lax.axis_size("head") - 2) == behind)
     def _():
         @pl.loop(0, width // step)
         def _(at):
@@ -562,9 +564,9 @@
 
     lengths = module_lengths.reshape(1, -1)
 
-    def operands(first_place, *held):
+    def operands(at_end, *held):
         return call(
-            functools.partial(ready_kernel, prior, first_place), "operands",
+            functools.partial(ready_kernel, prior, at_end), "operands",
             [anywhere] * 5 + [inside] * len(held), [inside] * 8,
             [near16(tok, width)] * 4
             + [near32(tok, 2 * prior), near32(prior + prior // 2, 2 * prior)]
@@ -576,9 +578,9 @@
             (0, 0, 0, 0), 16 * tok * width, {5 + n: n for n in range(len(held))},
         )(*in_hbm(lengths, query_in, key_in, value_in, grad_out), *in_vmem(*held))
 
-    def own_block(last_place, *partial):
+    def own_block(behind, *partial):
         return call(
-            functools.partial(own_kernel, prior, step, last_place), "own_block",
+            functools.partial(own_kernel, prior, step, behind), "own_block",
             [inside] * (5 + len(partial)), [inside] * 4,
             [near16(tok - prior, width)] * 2 + [near32(tok, width)] * 2, (),
             (width // HEAD_DIM, tok - prior, tok, 6), 18 * tok * width,

time: 26.6 us -> 26.6 us (level)
  no operation moved by 1% of the time
where the time goes in v28:
time: 26.6 us; the launch traced here: 26.4 us
  starting transfers between devices  16.3 us (61%)
  Pallas kernels  8.93 us (34%)
  between operations  0.74 us (3%)
  waiting for transfers between devices  0.47 us (2%)
    ppermute x4, starting transfers between devices, neighbour(): return lax.ppermute(value, ('seq', 'head'), pairs)  16.3 us
    pallas_call x1, Pallas kernels, halo_shards(): call(functools.partial(lead_kernel, prior, step), 'lead_rows', [inside] *...  2.2 us
    pallas_call x2, Pallas kernels, operands(): call(functools.partial(ready_kernel, prior, at_end), 'operands', [anywher...  1.65 us
    pallas_call x2, Pallas kernels, own_block(): call(functools.partial(own_kernel, prior, step, behind), 'own_block', [in...  1.51 us
    pallas_call x1, Pallas kernels, halo_shards(): call(functools.partial(last_kernel, prior), 'last_keys', [inside] * 8 + [...  1.2 us
    pallas_call x1, Pallas kernels, halo_shards(): call(functools.partial(pack_kernel, prior), 'late_keys', [anywhere] * 2,...  1.13 us
    pallas_call x1, Pallas kernels, halo_shards(): call(functools.partial(near_kernel, prior), 'near_terms', [inside] * 7, [...  0.73 us
  transfers between devices with their start and end apart: 4, of which 1 were waited for; matrix products, arithmetic and copies ran while one was open for 0% of the time, Pallas kernels for 25%

profile of v28, /device:TPU:1, one launch (start us, length us, event | category | flops | bytes accessed | tf_op | source)
XLA Modules:
  0.0 26.4 jit_solution(8386022286748632569)
XLA Ops:
  0.6 1.1 %late_keys.1 = (bf16[64,2048]{1,0:T(8,128)(2,1)S(1)}, bf16[64,2048]{1,0:T(8,128)(2,1)S(1)}) custom-call(bf16[128,2048]{1,0:T(8,128)(2,1)} %k_hbm.3, bf16[128,2048]{1,0:T(8,128)(2,1)} %v_hbm.3), custom_call_target="tpu_custom_call" | custom-call | bytes 1048576 | tf_op jit(solution)/shard_map/late_keys/pallas_call | solution.py:558
  1.8 3.9 %collective-permute-start = (bf16[64,2048]{1,0:T(8,128)(2,1)S(1)}, bf16[64,2048]{1,0:T(8,128)(2,1)S(1)}, u32[]{:S(2)}, u32[]{:S(2)}) collective-permute-start(bf16[64,2048]{1,0:T(8,128)(2,1)S(1)} %get-tuple-element.79), channel_id=1, source_target_pairs={{0,1},{1,2},{2,3},{3,4},{4,5},{5,6},{6,7},{7,8},{8,9},{9,10},{10,1... | collective-permute-start | bytes 786440 | tf_op jit(solution)/shard_map/ppermute | solution.py:513
  5.7 1.6 %operands.2 = (bf16[128,2048]{1,0:T(8,128)(2,1)S(1)}, bf16[128,2048]{1,0:T(8,128)(2,1)S(1)}, bf16[128,2048]{1,0:T(8,128)(2,1)S(1)}, bf16[128,2048]{1,0:T(8,128)(...) custom-call(s32[1,128]{1,0:T(1,128)} %bitcast.1, ...), custom_call_target="tpu_custom_call" | custom-call | bytes 4194304 | tf_op jit(solution)/shard_map/operands/pallas_call | solution.py:568
  7.3 1.9 %collective-permute-start.1 = (bf16[64,2048]{1,0:T(8,128)(2,1)S(1)}, bf16[64,2048]{1,0:T(8,128)(2,1)S(1)}, u32[]{:S(2)}, u32[]{:S(2)}) collective-permute-start(bf16[64,2048]{1,0:T(8,128)(2,1)S(1)} %get-tuple-element.80), channel_id=1, source_target_pairs={{0,1},{1,2},{2,3},{3,4},{4,5},{5,6},{6,7},{7,8},{8,9},{9,10},{10,1... | collective-permute-start | bytes 786440 | tf_op jit(solution)/shard_map/ppermute | solution.py:513
  9.3 0.1 operands.3
  9.3 1.5 %own_block.2 = (bf16[64,2048]{1,0:T(8,128)(2,1)S(1)}, bf16[64,2048]{1,0:T(8,128)(2,1)S(1)}, f32[128,2048]{1,0:T(8,128)S(1)}, f32[128,2048]{1,0:T(8,128)S(1)}) custom-call(f32[128,128]{1,0:T(8,128)S(1)} %get-tuple-element.90.bias_ref, bf16[128,2048]{1,0:T(8,128)(2,1)S(1)} %get-tuple-element.75.q_ref, bf16[128,2048]{1,0:T(8,128)(2,1)S(1)} %get-tuple-element.76.k_ref, ...), custom_call_target="tpu_custom_call" | custom-call | flops 201326592 | bytes 4718592 | tf_op jit(solution)/shard_map/own_block/pallas_call | solution.py:582
  10.8 0.5 %collective-permute-done.near_ref = bf16[64,2048]{1,0:T(8,128)(2,1)S(1)} collective-permute-done((bf16[64,2048]{1,0:T(8,128)(2,1)S(1)}, bf16[64,2048]{1,0:T(8,128)(2,1)S(1)}, u32[]{:S(2)}, u32[]{:S(2)}) %collective-permute-start) | collective-permute-done | bytes 262176 | tf_op jit(solution)/shard_map/ppermute | solution.py:513
  11.3 0.7 %near_terms.1 = (bf16[64,1024]{1,0:T(8,128)(2,1)S(1)}, bf16[64,1024]{1,0:T(8,128)(2,1)S(1)}) custom-call(f32[96,128]{1,0:T(8,128)S(1)} %get-tuple-element.87.near_bias_ref, f32[128,128]{1,0:T(8,128)S(1)} %get-tuple-element.74.lead_bias_ref.bias_ref, bf16[128,2048]{1,0:T(8,128)(2,1)S(1)} %get-tuple-element.75.q_ref, ...), custom_call_target="tpu_custom_call" | custom-call | flops 75497472 | bytes 2097152 | tf_op jit(solution)/shard_map/near_terms/pallas_call | solution.py:594
  12.0 6.2 %collective-permute-start.3 = (bf16[64,1024]{1,0:T(8,128)(2,1)S(1)}, bf16[64,1024]{1,0:T(8,128)(2,1)S(1)}, u32[]{:S(2)}, u32[]{:S(2)}) collective-permute-start(bf16[64,1024]{1,0:T(8,128)(2,1)S(1)} %get-tuple-element.103), channel_id=1, source_target_pairs={{1,0},{2,1},{3,2},{4,3},{5,4},{6,5},{7,6},{8,7},{9,8},{10,9},{11,1... | collective-permute-start | bytes 393224 | tf_op jit(solution)/shard_map/ppermute | solution.py:513
  18.2 4.2 %collective-permute-start.2 = (bf16[64,1024]{1,0:T(8,128)(2,1)S(1)}, bf16[64,1024]{1,0:T(8,128)(2,1)S(1)}, u32[]{:S(2)}, u32[]{:S(2)}) collective-permute-start(bf16[64,1024]{1,0:T(8,128)(2,1)S(1)} %get-tuple-element.102), channel_id=1, source_target_pairs={{1,0},{2,1},{3,2},{4,3},{5,4},{6,5},{7,6},{8,7},{9,8},{10,9},{11,1... | collective-permute-start | bytes 393224 | tf_op jit(solution)/shard_map/ppermute | solution.py:513
  22.4 0.0 collective-permute-done.1.far_ref
  22.5 2.2 %lead_rows.1 = (bf16[128,2048]{1,0:T(8,128)(2,1)}, bf16[128,2048]{1,0:T(8,128)(2,1)}, bf16[128,2048]{1,0:T(8,128)(2,1)}, bf16[128,2048]{1,0:T(8,128)(2,1)}) custom-call(f32[128,128]{1,0:T(8,128)S(1)} %get-tuple-element.74.lead_bias_ref.bias_ref, bf16[128,2048]{1,0:T(8,128)(2,1)S(1)} %get-tuple-element.75.q_ref, ...), custom_call_target="tpu_custom_call" | custom-call | flops 201326592 | bytes 5242880 | tf_op jit(solution)/shard_map/lead_rows/pallas_call | solution.py:603
  24.7 0.0 collective-permute-done.3.after_ref
  24.7 0.5 %tail_keys.1 = (bf16[64,1024]{1,0:T(8,128)(2,1)S(1)}, bf16[64,1024]{1,0:T(8,128)(2,1)S(1)}) custom-call(f32[64,128]{1,0:T(8,128)S(1)} %get-tuple-element.101.bias_ref, bf16[128,2048]{1,0:T(8,128)(2,1)S(1)} %get-tuple-element.76.k_ref, bf16[128,2048]{1,0:T(8,128)(2,1)S(1)} %get-tuple-element.77.v_ref, f32[128,2048]{1,0:T(8,128)S(1)} %get-tuple-element.95.gk_part_ref, ...), custom_call_target="tpu_custom_call" | custom-call | flops 16777216 | bytes 1048576 | tf_op jit(solution)/shard_map/tail_keys/pallas_call | solution.py:613
  25.2 0.0 collective-permute-done.2.after_ref
  25.2 1.2 %last_keys.1 = (bf16[128,2048]{1,0:T(8,128)(2,1)}, bf16[128,2048]{1,0:T(8,128)(2,1)}) custom-call(f32[64,128]{1,0:T(8,128)S(1)} %get-tuple-element.101.bias_ref, bf16[128,2048]{1,0:T(8,128)(2,1)S(1)} %get-tuple-element.76.k_ref, bf16[128,2048]{1,0:T(8,128)(2,1)S(1)} %get-tuple-element.77.v_ref, ...), custom_call_target="tpu_custom_call", output_to_operand_aliasing={{0}: (8, {}), {1}: (9, {})} | custom-call | flops 16777216 | bytes 1572864 | tf_op jit(solution)/shard_map/last_keys/pallas_call | solution.py:617
  (1 shorter events, 0.0 us)
Async XLA Ops:
  1.8 9.5 %collective-permute-start = (bf16[64,2048]{1,0:T(8,128)(2,1)S(1)}, bf16[64,2048]{1,0:T(8,128)(2,1)S(1)}, u32[]{:S(2)}, u32[]{:S(2)}) collective-permute-start(bf16[64,2048]{1,0:T(8,128)(2,1)S(1)} %get-tuple-element.79), channel_id=1, source_target_pairs={{0,1},{1,2},{2,3},{3,4},{4,5},{5,6},{6,7},{7,8},{8,9},{9,10},{10,1... | collective-permute-start | bytes 786440 | tf_op jit(solution)/shard_map/ppermute | solution.py:513
  7.3 15.1 %collective-permute-start.1 = (bf16[64,2048]{1,0:T(8,128)(2,1)S(1)}, bf16[64,2048]{1,0:T(8,128)(2,1)S(1)}, u32[]{:S(2)}, u32[]{:S(2)}) collective-permute-start(bf16[64,2048]{1,0:T(8,128)(2,1)S(1)} %get-tuple-element.80), channel_id=1, source_target_pairs={{0,1},{1,2},{2,3},{3,4},{4,5},{5,6},{6,7},{7,8},{8,9},{9,10},{10,1... | collective-permute-start | bytes 786440 | tf_op jit(solution)/shard_map/ppermute | solution.py:513
  12.0 12.7 %collective-permute-start.3 = (bf16[64,1024]{1,0:T(8,128)(2,1)S(1)}, bf16[64,1024]{1,0:T(8,128)(2,1)S(1)}, u32[]{:S(2)}, u32[]{:S(2)}) collective-permute-start(bf16[64,1024]{1,0:T(8,128)(2,1)S(1)} %get-tuple-element.103), channel_id=1, source_target_pairs={{1,0},{2,1},{3,2},{4,3},{5,4},{6,5},{7,6},{8,7},{9,8},{10,9},{11,1... | collective-permute-start | bytes 393224 | tf_op jit(solution)/shard_map/ppermute | solution.py:513
  18.2 7.0 %collective-permute-start.2 = (bf16[64,1024]{1,0:T(8,128)(2,1)S(1)}, bf16[64,1024]{1,0:T(8,128)(2,1)S(1)}, u32[]{:S(2)}, u32[]{:S(2)}) collective-permute-start(bf16[64,1024]{1,0:T(8,128)(2,1)S(1)} %get-tuple-element.102), channel_id=1, source_target_pairs={{1,0},{2,1},{3,2},{4,3},{5,4},{6,5},{7,6},{8,7},{9,8},{10,9},{11,1... | collective-permute-start | bytes 393224 | tf_op jit(solution)/shard_map/ppermute | solution.py:513

commit v29 on v21

--- a/solution.py
+++ b/solution.py
@@ -268,33 +268,50 @@
     ]
 
 
-def pack_kernel(prior, k_ref, v_ref, near_ref, sems):
-    copies = pack_copies(prior, 0, k_ref, v_ref, near_ref, sems)
-    for copy in copies:
-        copy.start()
-    for copy in copies:
-        copy.wait()
-
-
-def ready_kernel(
-    prior, len_hbm, q_hbm, k_hbm, v_hbm, do_hbm, far_ref, q_ref, k_ref, v_ref, do_ref,
-    own_bias_ref, near_bias_ref, lead_bias_ref, tail_bias_ref, len_ref, sems, far_sems, len_sem,
-):
-    tok, half = k_ref.shape[0], prior // 2
-    pairs = ((q_hbm, q_ref), (k_hbm, k_ref), (v_hbm, v_ref), (do_hbm, do_ref))
-    copies = pack_copies(prior, 1, k_hbm, v_hbm, far_ref, far_sems)
-    copies += [pltpu.make_async_copy(hbm, ref, sems.at[n]) for n, (hbm, ref) in enumerate(pairs)]
-    len_copy = pltpu.make_async_copy(len_hbm, len_ref, len_sem)
-    len_copy.start()
-    for copy in copies:
-        copy.start()
-    len_copy.wait()
-    first = device_first(tok)
+def fill_masks(prior, tok, len_ref, own_bias_ref, near_bias_ref, lead_bias_ref, tail_bias_ref):
+    first, half = device_first(tok), prior // 2
     lengths = len_ref[...].astype(jnp.float32)
     own_bias_ref[...] = bias_by_key(lengths, first + prior, tok - prior, first, tok, 2)
     near_bias_ref[...] = bias_by_key(lengths, first, prior, first - half, prior + half, 2)
     lead_bias_ref[...] = bias_by_key(lengths, first, prior, first - prior, 2 * prior, 2)
     tail_bias_ref[...] = bias_by_key(lengths, first + tok, half, first + tok - prior, prior, 4)
+
+
+def pack_kernel(prior, len_hbm, k_ref, v_ref, near_ref, *refs):
+    *mask_refs, len_ref, sems, len_sem = refs
+    copies = pack_copies(prior, 0, k_ref, v_ref, near_ref, sems)
+    for copy in copies:
+        copy.start()
+
+    @pl.when(lax.axis_index("seq") % 2 == 1)
+    def _():
+        len_copy = pltpu.make_async_copy(len_hbm, len_ref, len_sem)
+        len_copy.start()
+        len_copy.wait()
+        fill_masks(prior, k_ref.shape[0], len_ref, *mask_refs)
+
+    for copy in copies:
+        copy.wait()
+
+
+def ready_kernel(
+    prior, len_hbm, q_hbm, k_hbm, v_hbm, do_hbm, _own, _near, _lead, _tail,
+    far_ref, q_ref, k_ref, v_ref, do_ref, *refs,
+):
+    *mask_refs, len_ref, sems, far_sems, len_sem = refs
+    pairs = ((q_hbm, q_ref), (k_hbm, k_ref), (v_hbm, v_ref), (do_hbm, do_ref))
+    copies = pack_copies(prior, 1, k_hbm, v_hbm, far_ref, far_sems)
+    copies += [pltpu.make_async_copy(hbm, ref, sems.at[n]) for n, (hbm, ref) in enumerate(pairs)]
+    for copy in copies:
+        copy.start()
+
+    @pl.when(lax.axis_index("seq") % 2 == 0)
+    def _():
+        len_copy = pltpu.make_async_copy(len_hbm, len_ref, len_sem)
+        len_copy.start()
+        len_copy.wait()
+        fill_masks(prior, k_ref.shape[0], len_ref, *mask_refs)
+
     for copy in copies:
         copy.wait()
 
@@ -546,26 +563,30 @@
             name=name,
         )
 
-    near = call(
+    lengths = module_lengths.reshape(1, -1)
+    len_row = pltpu.VMEM(lengths.shape, jnp.int32)
+    mask_shapes = [
+        near32(tok, 2 * prior), near32(prior + prior // 2, 2 * prior),
+        near32(2 * prior, 2 * prior), near32(prior, 2 * prior),
+    ]
+    near, *masks = call(
         functools.partial(pack_kernel, prior), "near_keys",
-        [anywhere] * 2, inside, near16(prior, width),
-        [pltpu.SemaphoreType.DMA((2,))], (0, 0, 0, 0), 4 * prior * width,
-    )(*in_hbm(key_in, value_in))
+        [anywhere] * 3, [inside] * 5, [near16(prior, width), *mask_shapes],
+        [len_row, pltpu.SemaphoreType.DMA((2,)), pltpu.SemaphoreType.DMA(())],
+        (0, 0, 0, 0), 4 * prior * width,
+    )(*in_hbm(lengths, key_in, value_in))
     near = neighbour(near, 1)
 
-    lengths = module_lengths.reshape(1, -1)
     far, q, k, v, do, own_bias, near_bias, lead_bias, tail_bias = call(
         functools.partial(ready_kernel, prior), "operands",
-        [anywhere] * 5, [inside] * 9,
-        [near16(prior, width)] + [near16(tok, width)] * 4
-        + [near32(tok, 2 * prior), near32(prior + prior // 2, 2 * prior)]
-        + [near32(2 * prior, 2 * prior), near32(prior, 2 * prior)],
+        [anywhere] * 5 + [inside] * 4, [inside] * 9,
+        [near16(prior, width)] + [near16(tok, width)] * 4 + mask_shapes,
         [
-            pltpu.VMEM(lengths.shape, jnp.int32), pltpu.SemaphoreType.DMA((4,)),
-            pltpu.SemaphoreType.DMA((2,)), pltpu.SemaphoreType.DMA(()),
+            len_row, pltpu.SemaphoreType.DMA((4,)), pltpu.SemaphoreType.DMA((2,)),
+            pltpu.SemaphoreType.DMA(()),
         ],
-        (0, 0, 0, 0), 18 * tok * width,
-    )(*in_hbm(lengths, query_in, key_in, value_in, grad_out))
+        (0, 0, 0, 0), 18 * tok * width, {5: 5, 6: 6, 7: 7, 8: 8},
+    )(*in_hbm(lengths, query_in, key_in, value_in, grad_out), *in_vmem(*masks))
     far = neighbour(far, 1)
 
     attn, gq, gk_part, gv_part = call(

time: 26.1 us -> 26.1 us (level)
  no operation moved by 1% of the time
where the time goes in v29:
time: 26.1 us; the launch traced here: 25.8 us
  starting transfers between devices  10.8 us (41%)
  Pallas kernels  8.77 us (34%)
  waiting for transfers between devices  5.51 us (21%)
  between operations  0.71 us (3%)
    ppermute x4, starting transfers between devices, neighbour(): return lax.ppermute(value, ('seq', 'head'), pairs)  10.8 us
    ppermute x4, waiting for transfers between devices, neighbour(): return lax.ppermute(value, ('seq', 'head'), pairs)  5.51 us
    pallas_call x1, Pallas kernels, halo_shards(): call(functools.partial(lead_kernel, prior, step), 'lead_rows', [inside] *...  2.2 us
    pallas_call x1, Pallas kernels, halo_shards(): call(functools.partial(ready_kernel, prior), 'operands', [anywhere] * 5 +...  1.67 us
    pallas_call x1, Pallas kernels, halo_shards(): call(functools.partial(own_kernel, prior, step), 'own_block', [inside] *...  1.48 us
    pallas_call x1, Pallas kernels, halo_shards(): call(functools.partial(last_kernel, prior), 'last_keys', [inside] * 8 + [...  1.19 us
    pallas_call x1, Pallas kernels, halo_shards(): call(functools.partial(pack_kernel, prior), 'near_keys', [anywhere] * 3,...  1 us
    pallas_call x1, Pallas kernels, halo_shards(): call(functools.partial(near_kernel, prior), 'near_terms', [inside] * 7, [...  0.73 us
  transfers between devices with their start and end apart: 4, of which 3 were waited for; matrix products, arithmetic and copies ran while one was open for 0% of the time, Pallas kernels for 26%

profile of v29, /device:TPU:0, one launch (start us, length us, event | category | flops | bytes accessed | tf_op | source)
XLA Modules:
  0.0 25.8 jit_solution(14117505647431399721)
XLA Ops:
  0.6 1.0 %near_keys.1 = (bf16[64,2048]{1,0:T(8,128)(2,1)S(1)}, f32[128,128]{1,0:T(8,128)S(1)}, f32[96,128]{1,0:T(8,128)S(1)}, f32[128,128]{1,0:T(8,128)S(1)}, f32[64,128]{1,0:T(8,128)S(1)}) custom-call(s32[1,128]{1,0:T(1,128)} %bitcast.1, bf16[128,2048]{1,0:T(8,128)(2,1)} %k_hbm.1, bf16[128,2048]{1,0:T(8,128)(2,1)} %v_hbm.1), custom_call_target="tpu_custom_call" | custom-call | bytes 524288 | tf_op jit(solution)/shard_map/near_keys/pallas_call | solution.py:572
  1.6 4.9 %collective-permute-start = (bf16[64,2048]{1,0:T(8,128)(2,1)S(1)}, bf16[64,2048]{1,0:T(8,128)(2,1)S(1)}, u32[]{:S(2)}, u32[]{:S(2)}) collective-permute-start(bf16[64,2048]{1,0:T(8,128)(2,1)S(1)} %get-tuple-element.43), channel_id=1, source_target_pairs={{0,1},{1,2},{2,3},{3,4},{4,5},{5,6},{6,7},{7,8},{8,9},{9,10},{10,1... | collective-permute-start | bytes 786440 | tf_op jit(solution)/shard_map/ppermute | solution.py:521
  6.5 1.7 %operands.1 = (bf16[64,2048]{1,0:T(8,128)(2,1)S(1)}, bf16[128,2048]{1,0:T(8,128)(2,1)S(1)}, bf16[128,2048]{1,0:T(8,128)(2,1)S(1)}, bf16[128,2048]{1,0:T(8,128)(2...) custom-call(s32[1,128]{1,0:T(1,128)} %bitcast.2, ...), custom_call_target="tpu_custom_call", output_to_operand_aliasing={{5}: (5, {}), {6}: (6, {}), {7}: (7, {}), {8}: (8, {})} | custom-call | bytes 4718592 | tf_op jit(solution)/shard_map/operands/pallas_call | solution.py:580
  8.2 3.4 %collective-permute-start.1 = (bf16[64,2048]{1,0:T(8,128)(2,1)S(1)}, bf16[64,2048]{1,0:T(8,128)(2,1)S(1)}, u32[]{:S(2)}, u32[]{:S(2)}) collective-permute-start(bf16[64,2048]{1,0:T(8,128)(2,1)S(1)} %get-tuple-element.44), channel_id=1, source_target_pairs={{0,1},{1,2},{2,3},{3,4},{4,5},{5,6},{6,7},{7,8},{8,9},{9,10},{10,1... | collective-permute-start | bytes 786440 | tf_op jit(solution)/shard_map/ppermute | solution.py:521
  11.6 1.5 %own_block.1 = (bf16[64,2048]{1,0:T(8,128)(2,1)S(1)}, bf16[64,2048]{1,0:T(8,128)(2,1)S(1)}, f32[128,2048]{1,0:T(8,128)S(1)}, f32[128,2048]{1,0:T(8,128)S(1)}) custom-call(f32[128,128]{1,0:T(8,128)S(1)} %get-tuple-element.45.bias_ref, bf16[128,2048]{1,0:T(8,128)(2,1)S(1)} %get-tuple-element.39.q_ref, bf16[128,2048]{1,0:T(8,128)(2,1)S(1)} %get-tuple-element.40.k_ref, ...), custom_call_target="tpu_custom_call" | custom-call | flops 201326592 | bytes 4718592 | tf_op jit(solution)/shard_map/own_block/pallas_call | solution.py:592
  13.1 0.0 collective-permute-done.near_ref
  13.1 0.7 %near_terms.1 = (bf16[64,1024]{1,0:T(8,128)(2,1)S(1)}, bf16[64,1024]{1,0:T(8,128)(2,1)S(1)}) custom-call(f32[96,128]{1,0:T(8,128)S(1)} %get-tuple-element.55.near_bias_ref, f32[128,128]{1,0:T(8,128)S(1)} %get-tuple-element.38.bias_ref.lead_bias_ref, bf16[128,2048]{1,0:T(8,128)(2,1)S(1)} %get-tuple-element.39.q_ref, ...), custom_call_target="tpu_custom_call" | custom-call | flops 75497472 | bytes 2097152 | tf_op jit(solution)/shard_map/near_terms/pallas_call | solution.py:600
  13.8 1.3 %collective-permute-start.3 = (bf16[64,1024]{1,0:T(8,128)(2,1)S(1)}, bf16[64,1024]{1,0:T(8,128)(2,1)S(1)}, u32[]{:S(2)}, u32[]{:S(2)}) collective-permute-start(bf16[64,1024]{1,0:T(8,128)(2,1)S(1)} %get-tuple-element.57), channel_id=1, source_target_pairs={{1,0},{2,1},{3,2},{4,3},{5,4},{6,5},{7,6},{8,7},{9,8},{10,9},{11,1... | collective-permute-start | bytes 393224 | tf_op jit(solution)/shard_map/ppermute | solution.py:521
  15.1 1.3 %collective-permute-start.2 = (bf16[64,1024]{1,0:T(8,128)(2,1)S(1)}, bf16[64,1024]{1,0:T(8,128)(2,1)S(1)}, u32[]{:S(2)}, u32[]{:S(2)}) collective-permute-start(bf16[64,1024]{1,0:T(8,128)(2,1)S(1)} %get-tuple-element.56), channel_id=1, source_target_pairs={{1,0},{2,1},{3,2},{4,3},{5,4},{6,5},{7,6},{8,7},{9,8},{10,9},{11,1... | collective-permute-start | bytes 393224 | tf_op jit(solution)/shard_map/ppermute | solution.py:521
  16.4 1.2 %collective-permute-done.1.far_ref = bf16[64,2048]{1,0:T(8,128)(2,1)S(1)} collective-permute-done((bf16[64,2048]{1,0:T(8,128)(2,1)S(1)}, bf16[64,2048]{1,0:T(8,128)(2,1)S(1)}, u32[]{:S(2)}, u32[]{:S(2)}) %collective-permute-start.1) | collective-permute-done | bytes 262176 | tf_op jit(solution)/shard_map/ppermute | solution.py:521
  17.7 2.2 %lead_rows.1 = (bf16[128,2048]{1,0:T(8,128)(2,1)}, bf16[128,2048]{1,0:T(8,128)(2,1)}, bf16[128,2048]{1,0:T(8,128)(2,1)}, bf16[128,2048]{1,0:T(8,128)(2,1)}) custom-call(f32[128,128]{1,0:T(8,128)S(1)} %get-tuple-element.38.bias_ref.lead_bias_ref, bf16[128,2048]{1,0:T(8,128)(2,1)S(1)} %get-tuple-element.39.q_ref, ...), custom_call_target="tpu_custom_call" | custom-call | flops 201326592 | bytes 5242880 | tf_op jit(solution)/shard_map/lead_rows/pallas_call | solution.py:607
  19.9 2.5 %collective-permute-done.3.after_ref = bf16[64,1024]{1,0:T(8,128)(2,1)S(1)} collective-permute-done((bf16[64,1024]{1,0:T(8,128)(2,1)S(1)}, bf16[64,1024]{1,0:T(8,128)(2,1)S(1)}, u32[]{:S(2)}, u32[]{:S(2)}) %collective-permute-start.3) | collective-permute-done | bytes 131104 | tf_op jit(solution)/shard_map/ppermute | solution.py:521
  22.4 0.5 %tail_keys.1 = (bf16[64,1024]{1,0:T(8,128)(2,1)S(1)}, bf16[64,1024]{1,0:T(8,128)(2,1)S(1)}) custom-call(f32[64,128]{1,0:T(8,128)S(1)} %get-tuple-element.54.bias_ref, bf16[128,2048]{1,0:T(8,128)(2,1)S(1)} %get-tuple-element.40.k_ref, bf16[128,2048]{1,0:T(8,128)(2,1)S(1)} %get-tuple-element.41.v_ref, f32[128,2048]{1,0:T(8,128)S(1)} %get-tuple-element.46.gk_part_ref, ...), custom_call_target="tpu_custom_call" | custom-call | flops 16777216 | bytes 1048576 | tf_op jit(solution)/shard_map/tail_keys/pallas_call | solution.py:617
  22.9 1.7 %collective-permute-done.2.after_ref = bf16[64,1024]{1,0:T(8,128)(2,1)S(1)} collective-permute-done((bf16[64,1024]{1,0:T(8,128)(2,1)S(1)}, bf16[64,1024]{1,0:T(8,128)(2,1)S(1)}, u32[]{:S(2)}, u32[]{:S(2)}) %collective-permute-start.2) | collective-permute-done | bytes 131104 | tf_op jit(solution)/shard_map/ppermute | solution.py:521
  24.6 1.2 %last_keys.1 = (bf16[128,2048]{1,0:T(8,128)(2,1)}, bf16[128,2048]{1,0:T(8,128)(2,1)}) custom-call(f32[64,128]{1,0:T(8,128)S(1)} %get-tuple-element.54.bias_ref, bf16[128,2048]{1,0:T(8,128)(2,1)S(1)} %get-tuple-element.40.k_ref, bf16[128,2048]{1,0:T(8,128)(2,1)S(1)} %get-tuple-element.41.v_ref, ...), custom_call_target="tpu_custom_call", output_to_operand_aliasing={{0}: (8, {}), {1}: (9, {})} | custom-call | flops 16777216 | bytes 1572864 | tf_op jit(solution)/shard_map/last_keys/pallas_call | solution.py:621
Async XLA Ops:
  1.6 11.4 %collective-permute-start = (bf16[64,2048]{1,0:T(8,128)(2,1)S(1)}, bf16[64,2048]{1,0:T(8,128)(2,1)S(1)}, u32[]{:S(2)}, u32[]{:S(2)}) collective-permute-start(bf16[64,2048]{1,0:T(8,128)(2,1)S(1)} %get-tuple-element.43), channel_id=1, source_target_pairs={{0,1},{1,2},{2,3},{3,4},{4,5},{5,6},{6,7},{7,8},{8,9},{9,10},{10,1... | collective-permute-start | bytes 786440 | tf_op jit(solution)/shard_map/ppermute | solution.py:521
  8.2 9.5 %collective-permute-start.1 = (bf16[64,2048]{1,0:T(8,128)(2,1)S(1)}, bf16[64,2048]{1,0:T(8,128)(2,1)S(1)}, u32[]{:S(2)}, u32[]{:S(2)}) collective-permute-start(bf16[64,2048]{1,0:T(8,128)(2,1)S(1)} %get-tuple-element.44), channel_id=1, source_target_pairs={{0,1},{1,2},{2,3},{3,4},{4,5},{5,6},{6,7},{7,8},{8,9},{9,10},{10,1... | collective-permute-start | bytes 786440 | tf_op jit(solution)/shard_map/ppermute | solution.py:521
  13.8 8.6 %collective-permute-start.3 = (bf16[64,1024]{1,0:T(8,128)(2,1)S(1)}, bf16[64,1024]{1,0:T(8,128)(2,1)S(1)}, u32[]{:S(2)}, u32[]{:S(2)}) collective-permute-start(bf16[64,1024]{1,0:T(8,128)(2,1)S(1)} %get-tuple-element.57), channel_id=1, source_target_pairs={{1,0},{2,1},{3,2},{4,3},{5,4},{6,5},{7,6},{8,7},{9,8},{10,9},{11,1... | collective-permute-start | bytes 393224 | tf_op jit(solution)/shard_map/ppermute | solution.py:521
  15.1 9.5 %collective-permute-start.2 = (bf16[64,1024]{1,0:T(8,128)(2,1)S(1)}, bf16[64,1024]{1,0:T(8,128)(2,1)S(1)}, u32[]{:S(2)}, u32[]{:S(2)}) collective-permute-start(bf16[64,1024]{1,0:T(8,128)(2,1)S(1)} %get-tuple-element.56), channel_id=1, source_target_pairs={{1,0},{2,1},{3,2},{4,3},{5,4},{6,5},{7,6},{8,7},{9,8},{10,9},{11,1... | collective-permute-start | bytes 393224 | tf_op jit(solution)/shard_map/ppermute | solution.py:521

commit v30 on v29

--- a/solution.py
+++ b/solution.py
@@ -283,15 +283,15 @@
     for copy in copies:
         copy.start()
 
+    for copy in copies:
+        copy.wait()
+
     @pl.when(lax.axis_index("seq") % 2 == 1)
     def _():
         len_copy = pltpu.make_async_copy(len_hbm, len_ref, len_sem)
         len_copy.start()
         len_copy.wait()
         fill_masks(prior, k_ref.shape[0], len_ref, *mask_refs)
-
-    for copy in copies:
-        copy.wait()
 
 
 def ready_kernel(

time: 26.1 us -> 27.6 us (1.057)
  the two profiles are of different devices: /device:TPU:0 before, /device:TPU:11 now
where the time goes in v30:
time: 27.6 us; the launch traced here: 27.4 us
  starting transfers between devices  14.7 us (53%)
  Pallas kernels  9.58 us (35%)
  waiting for transfers between devices  2.41 us (9%)
  between operations  0.72 us (3%)
    ppermute x4, starting transfers between devices, neighbour(): return lax.ppermute(value, ('seq', 'head'), pairs)  14.7 us
    ppermute x4, waiting for transfers between devices, neighbour(): return lax.ppermute(value, ('seq', 'head'), pairs)  2.41 us
    pallas_call x1, Pallas kernels, halo_shards(): call(functools.partial(lead_kernel, prior, step), 'lead_rows', [inside] *...  2.2 us
    pallas_call x1, Pallas kernels, halo_shards(): call(functools.partial(pack_kernel, prior), 'near_keys', [anywhere] * 3,...  1.8 us
    pallas_call x1, Pallas kernels, halo_shards(): call(functools.partial(ready_kernel, prior), 'operands', [anywhere] * 5 +...  1.67 us
    pallas_call x1, Pallas kernels, halo_shards(): call(functools.partial(own_kernel, prior, step), 'own_block', [inside] *...  1.49 us
    pallas_call x1, Pallas kernels, halo_shards(): call(functools.partial(last_kernel, prior), 'last_keys', [inside] * 8 + [...  1.2 us
    pallas_call x1, Pallas kernels, halo_shards(): call(functools.partial(near_kernel, prior), 'near_terms', [inside] * 7, [...  0.73 us
  transfers between devices with their start and end apart: 4, of which 2 were waited for; matrix products, arithmetic and copies ran while one was open for 0% of the time, Pallas kernels for 24%

profile of v30, /device:TPU:11, one launch (start us, length us, event | category | flops | bytes accessed | tf_op | source)
XLA Modules:
  0.0 27.4 jit_solution(968818905264713800)
XLA Ops:
  0.6 1.8 %near_keys.1 = (bf16[64,2048]{1,0:T(8,128)(2,1)S(1)}, f32[128,128]{1,0:T(8,128)S(1)}, f32[96,128]{1,0:T(8,128)S(1)}, f32[128,128]{1,0:T(8,128)S(1)}, f32[64,128]{1,0:T(8,128)S(1)}) custom-call(s32[1,128]{1,0:T(1,128)} %bitcast.1, bf16[128,2048]{1,0:T(8,128)(2,1)} %k_hbm.1, bf16[128,2048]{1,0:T(8,128)(2,1)} %v_hbm.1), custom_call_target="tpu_custom_call" | custom-call | bytes 524288 | tf_op jit(solution)/shard_map/near_keys/pallas_call | solution.py:572
  2.4 3.1 %collective-permute-start = (bf16[64,2048]{1,0:T(8,128)(2,1)S(1)}, bf16[64,2048]{1,0:T(8,128)(2,1)S(1)}, u32[]{:S(2)}, u32[]{:S(2)}) collective-permute-start(bf16[64,2048]{1,0:T(8,128)(2,1)S(1)} %get-tuple-element.43), channel_id=1, source_target_pairs={{0,1},{1,2},{2,3},{3,4},{4,5},{5,6},{6,7},{7,8},{8,9},{9,10},{10,1... | collective-permute-start | bytes 786440 | tf_op jit(solution)/shard_map/ppermute | solution.py:521
  5.6 1.7 %operands.1 = (bf16[64,2048]{1,0:T(8,128)(2,1)S(1)}, bf16[128,2048]{1,0:T(8,128)(2,1)S(1)}, bf16[128,2048]{1,0:T(8,128)(2,1)S(1)}, bf16[128,2048]{1,0:T(8,128)(2...) custom-call(s32[1,128]{1,0:T(1,128)} %bitcast.2, ...), custom_call_target="tpu_custom_call", output_to_operand_aliasing={{5}: (5, {}), {6}: (6, {}), {7}: (7, {}), {8}: (8, {})} | custom-call | bytes 4718592 | tf_op jit(solution)/shard_map/operands/pallas_call | solution.py:580
  7.2 3.1 %collective-permute-start.1 = (bf16[64,2048]{1,0:T(8,128)(2,1)S(1)}, bf16[64,2048]{1,0:T(8,128)(2,1)S(1)}, u32[]{:S(2)}, u32[]{:S(2)}) collective-permute-start(bf16[64,2048]{1,0:T(8,128)(2,1)S(1)} %get-tuple-element.44), channel_id=1, source_target_pairs={{0,1},{1,2},{2,3},{3,4},{4,5},{5,6},{6,7},{7,8},{8,9},{9,10},{10,1... | collective-permute-start | bytes 786440 | tf_op jit(solution)/shard_map/ppermute | solution.py:521
  10.4 1.5 %own_block.1 = (bf16[64,2048]{1,0:T(8,128)(2,1)S(1)}, bf16[64,2048]{1,0:T(8,128)(2,1)S(1)}, f32[128,2048]{1,0:T(8,128)S(1)}, f32[128,2048]{1,0:T(8,128)S(1)}) custom-call(f32[128,128]{1,0:T(8,128)S(1)} %get-tuple-element.45.bias_ref, bf16[128,2048]{1,0:T(8,128)(2,1)S(1)} %get-tuple-element.39.q_ref, bf16[128,2048]{1,0:T(8,128)(2,1)S(1)} %get-tuple-element.40.k_ref, ...), custom_call_target="tpu_custom_call" | custom-call | flops 201326592 | bytes 4718592 | tf_op jit(solution)/shard_map/own_block/pallas_call | solution.py:592
  11.9 0.5 %collective-permute-done.near_ref = bf16[64,2048]{1,0:T(8,128)(2,1)S(1)} collective-permute-done((bf16[64,2048]{1,0:T(8,128)(2,1)S(1)}, bf16[64,2048]{1,0:T(8,128)(2,1)S(1)}, u32[]{:S(2)}, u32[]{:S(2)}) %collective-permute-start) | collective-permute-done | bytes 262176 | tf_op jit(solution)/shard_map/ppermute | solution.py:521
  12.3 0.7 %near_terms.1 = (bf16[64,1024]{1,0:T(8,128)(2,1)S(1)}, bf16[64,1024]{1,0:T(8,128)(2,1)S(1)}) custom-call(f32[96,128]{1,0:T(8,128)S(1)} %get-tuple-element.55.near_bias_ref, f32[128,128]{1,0:T(8,128)S(1)} %get-tuple-element.38.bias_ref.lead_bias_ref, bf16[128,2048]{1,0:T(8,128)(2,1)S(1)} %get-tuple-element.39.q_ref, ...), custom_call_target="tpu_custom_call" | custom-call | flops 75497472 | bytes 2097152 | tf_op jit(solution)/shard_map/near_terms/pallas_call | solution.py:600
  13.0 6.5 %collective-permute-start.3 = (bf16[64,1024]{1,0:T(8,128)(2,1)S(1)}, bf16[64,1024]{1,0:T(8,128)(2,1)S(1)}, u32[]{:S(2)}, u32[]{:S(2)}) collective-permute-start(bf16[64,1024]{1,0:T(8,128)(2,1)S(1)} %get-tuple-element.57), channel_id=1, source_target_pairs={{1,0},{2,1},{3,2},{4,3},{5,4},{6,5},{7,6},{8,7},{9,8},{10,9},{11,1... | collective-permute-start | bytes 393224 | tf_op jit(solution)/shard_map/ppermute | solution.py:521
  19.5 1.9 %collective-permute-start.2 = (bf16[64,1024]{1,0:T(8,128)(2,1)S(1)}, bf16[64,1024]{1,0:T(8,128)(2,1)S(1)}, u32[]{:S(2)}, u32[]{:S(2)}) collective-permute-start(bf16[64,1024]{1,0:T(8,128)(2,1)S(1)} %get-tuple-element.56), channel_id=1, source_target_pairs={{1,0},{2,1},{3,2},{4,3},{5,4},{6,5},{7,6},{8,7},{9,8},{10,9},{11,1... | collective-permute-start | bytes 393224 | tf_op jit(solution)/shard_map/ppermute | solution.py:521
  21.5 0.0 collective-permute-done.1.far_ref
  21.5 2.2 %lead_rows.1 = (bf16[128,2048]{1,0:T(8,128)(2,1)}, bf16[128,2048]{1,0:T(8,128)(2,1)}, bf16[128,2048]{1,0:T(8,128)(2,1)}, bf16[128,2048]{1,0:T(8,128)(2,1)}) custom-call(f32[128,128]{1,0:T(8,128)S(1)} %get-tuple-element.38.bias_ref.lead_bias_ref, bf16[128,2048]{1,0:T(8,128)(2,1)S(1)} %get-tuple-element.39.q_ref, ...), custom_call_target="tpu_custom_call" | custom-call | flops 201326592 | bytes 5242880 | tf_op jit(solution)/shard_map/lead_rows/pallas_call | solution.py:607
  23.7 0.0 collective-permute-done.3.after_ref
  23.7 0.5 %tail_keys.1 = (bf16[64,1024]{1,0:T(8,128)(2,1)S(1)}, bf16[64,1024]{1,0:T(8,128)(2,1)S(1)}) custom-call(f32[64,128]{1,0:T(8,128)S(1)} %get-tuple-element.54.bias_ref, bf16[128,2048]{1,0:T(8,128)(2,1)S(1)} %get-tuple-element.40.k_ref, bf16[128,2048]{1,0:T(8,128)(2,1)S(1)} %get-tuple-element.41.v_ref, f32[128,2048]{1,0:T(8,128)S(1)} %get-tuple-element.46.gk_part_ref, ...), custom_call_target="tpu_custom_call" | custom-call | flops 16777216 | bytes 1048576 | tf_op jit(solution)/shard_map/tail_keys/pallas_call | solution.py:617
  24.2 1.9 %collective-permute-done.2.after_ref = bf16[64,1024]{1,0:T(8,128)(2,1)S(1)} collective-permute-done((bf16[64,1024]{1,0:T(8,128)(2,1)S(1)}, bf16[64,1024]{1,0:T(8,128)(2,1)S(1)}, u32[]{:S(2)}, u32[]{:S(2)}) %collective-permute-start.2) | collective-permute-done | bytes 131104 | tf_op jit(solution)/shard_map/ppermute | solution.py:521
  26.2 1.2 %last_keys.1 = (bf16[128,2048]{1,0:T(8,128)(2,1)}, bf16[128,2048]{1,0:T(8,128)(2,1)}) custom-call(f32[64,128]{1,0:T(8,128)S(1)} %get-tuple-element.54.bias_ref, bf16[128,2048]{1,0:T(8,128)(2,1)S(1)} %get-tuple-element.40.k_ref, bf16[128,2048]{1,0:T(8,128)(2,1)S(1)} %get-tuple-element.41.v_ref, ...), custom_call_target="tpu_custom_call", output_to_operand_aliasing={{0}: (8, {}), {1}: (9, {})} | custom-call | flops 16777216 | bytes 1572864 | tf_op jit(solution)/shard_map/last_keys/pallas_call | solution.py:621
Async XLA Ops:
  2.4 9.9 %collective-permute-start = (bf16[64,2048]{1,0:T(8,128)(2,1)S(1)}, bf16[64,2048]{1,0:T(8,128)(2,1)S(1)}, u32[]{:S(2)}, u32[]{:S(2)}) collective-permute-start(bf16[64,2048]{1,0:T(8,128)(2,1)S(1)} %get-tuple-element.43), channel_id=1, source_target_pairs={{0,1},{1,2},{2,3},{3,4},{4,5},{5,6},{6,7},{7,8},{8,9},{9,10},{10,1... | collective-permute-start | bytes 786440 | tf_op jit(solution)/shard_map/ppermute | solution.py:521
  7.2 14.2 %collective-permute-start.1 = (bf16[64,2048]{1,0:T(8,128)(2,1)S(1)}, bf16[64,2048]{1,0:T(8,128)(2,1)S(1)}, u32[]{:S(2)}, u32[]{:S(2)}) collective-permute-start(bf16[64,2048]{1,0:T(8,128)(2,1)S(1)} %get-tuple-element.44), channel_id=1, source_target_pairs={{0,1},{1,2},{2,3},{3,4},{4,5},{5,6},{6,7},{7,8},{8,9},{9,10},{10,1... | collective-permute-start | bytes 786440 | tf_op jit(solution)/shard_map/ppermute | solution.py:521
  13.0 10.7 %collective-permute-start.3 = (bf16[64,1024]{1,0:T(8,128)(2,1)S(1)}, bf16[64,1024]{1,0:T(8,128)(2,1)S(1)}, u32[]{:S(2)}, u32[]{:S(2)}) collective-permute-start(bf16[64,1024]{1,0:T(8,128)(2,1)S(1)} %get-tuple-element.57), channel_id=1, source_target_pairs={{1,0},{2,1},{3,2},{4,3},{5,4},{6,5},{7,6},{8,7},{9,8},{10,9},{11,1... | collective-permute-start | bytes 393224 | tf_op jit(solution)/shard_map/ppermute | solution.py:521
  19.5 6.6 %collective-permute-start.2 = (bf16[64,1024]{1,0:T(8,128)(2,1)S(1)}, bf16[64,1024]{1,0:T(8,128)(2,1)S(1)}, u32[]{:S(2)}, u32[]{:S(2)}) collective-permute-start(bf16[64,1024]{1,0:T(8,128)(2,1)S(1)} %get-tuple-element.56), channel_id=1, source_target_pairs={{1,0},{2,1},{3,2},{4,3},{5,4},{6,5},{7,6},{8,7},{9,8},{10,9},{11,1... | collective-permute-start | bytes 393224 | tf_op jit(solution)/shard_map/ppermute | solution.py:521

commit v31 on v30

--- a/solution.py
+++ b/solution.py
@@ -279,39 +279,25 @@
 
 def pack_kernel(prior, len_hbm, k_ref, v_ref, near_ref, *refs):
     *mask_refs, len_ref, sems, len_sem = refs
+    len_copy = pltpu.make_async_copy(len_hbm, len_ref, len_sem)
+    len_copy.start()
     copies = pack_copies(prior, 0, k_ref, v_ref, near_ref, sems)
     for copy in copies:
         copy.start()
-
+    len_copy.wait()
+    fill_masks(prior, k_ref.shape[0], len_ref, *mask_refs)
     for copy in copies:
         copy.wait()
 
-    @pl.when(lax.axis_index("seq") % 2 == 1)
-    def _():
-        len_copy = pltpu.make_async_copy(len_hbm, len_ref, len_sem)
-        len_copy.start()
-        len_copy.wait()
-        fill_masks(prior, k_ref.shape[0], len_ref, *mask_refs)
-
 
 def ready_kernel(
-    prior, len_hbm, q_hbm, k_hbm, v_hbm, do_hbm, _own, _near, _lead, _tail,
-    far_ref, q_ref, k_ref, v_ref, do_ref, *refs,
+    prior, q_hbm, k_hbm, v_hbm, do_hbm, far_ref, q_ref, k_ref, v_ref, do_ref, sems, far_sems
 ):
-    *mask_refs, len_ref, sems, far_sems, len_sem = refs
     pairs = ((q_hbm, q_ref), (k_hbm, k_ref), (v_hbm, v_ref), (do_hbm, do_ref))
     copies = pack_copies(prior, 1, k_hbm, v_hbm, far_ref, far_sems)
     copies += [pltpu.make_async_copy(hbm, ref, sems.at[n]) for n, (hbm, ref) in enumerate(pairs)]
     for copy in copies:
         copy.start()
-
-    @pl.when(lax.axis_index("seq") % 2 == 0)
-    def _():
-        len_copy = pltpu.make_async_copy(len_hbm, len_ref, len_sem)
-        len_copy.start()
-        len_copy.wait()
-        fill_masks(prior, k_ref.shape[0], len_ref, *mask_refs)
-
     for copy in copies:
         copy.wait()
 
@@ -569,7 +555,7 @@
         near32(tok, 2 * prior), near32(prior + prior // 2, 2 * prior),
         near32(2 * prior, 2 * prior), near32(prior, 2 * prior),
     ]
-    near, *masks = call(
+    near, own_bias, near_bias, lead_bias, tail_bias = call(
         functools.partial(pack_kernel, prior), "near_keys",
         [anywhere] * 3, [inside] * 5, [near16(prior, width), *mask_shapes],
         [len_row, pltpu.SemaphoreType.DMA((2,)), pltpu.SemaphoreType.DMA(())],
@@ -577,16 +563,12 @@
     )(*in_hbm(lengths, key_in, value_in))
     near = neighbour(near, 1)
 
-    far, q, k, v, do, own_bias, near_bias, lead_bias, tail_bias = call(
+    far, q, k, v, do = call(
         functools.partial(ready_kernel, prior), "operands",
-        [anywhere] * 5 + [inside] * 4, [inside] * 9,
-        [near16(prior, width)] + [near16(tok, width)] * 4 + mask_shapes,
-        [
-            len_row, pltpu.SemaphoreType.DMA((4,)), pltpu.SemaphoreType.DMA((2,)),
-            pltpu.SemaphoreType.DMA(()),
-        ],
-        (0, 0, 0, 0), 18 * tok * width, {5: 5, 6: 6, 7: 7, 8: 8},
-    )(*in_hbm(lengths, query_in, key_in, value_in, grad_out), *in_vmem(*masks))
+        [anywhere] * 4, [inside] * 5, [near16(prior, width)] + [near16(tok, width)] * 4,
+        [pltpu.SemaphoreType.DMA((4,)), pltpu.SemaphoreType.DMA((2,))],
+        (0, 0, 0, 0), 18 * tok * width,
+    )(*in_hbm(query_in, key_in, value_in, grad_out))
     far = neighbour(far, 1)
 
     attn, gq, gk_part, gv_part = call(

time: 27.6 us -> 26.1 us (0.946)
  the two profiles are of different devices: /device:TPU:11 before, /device:TPU:0 now
where the time goes in v31:
time: 26.1 us; the launch traced here: 25.8 us
  starting transfers between devices  10.8 us (41%)
  Pallas kernels  8.77 us (34%)
  waiting for transfers between devices  5.52 us (21%)
  between operations  0.71 us (3%)
    ppermute x4, starting transfers between devices, neighbour(): return lax.ppermute(value, ('seq', 'head'), pairs)  10.8 us
    ppermute x4, waiting for transfers between devices, neighbour(): return lax.ppermute(value, ('seq', 'head'), pairs)  5.52 us
    pallas_call x1, Pallas kernels, halo_shards(): call(functools.partial(lead_kernel, prior, step), 'lead_rows', [inside] *...  2.2 us
    pallas_call x1, Pallas kernels, halo_shards(): call(functools.partial(ready_kernel, prior), 'operands', [anywhere] * 4,...  1.65 us
    pallas_call x1, Pallas kernels, halo_shards(): call(functools.partial(own_kernel, prior, step), 'own_block', [inside] *...  1.49 us
    pallas_call x1, Pallas kernels, halo_shards(): call(functools.partial(last_kernel, prior), 'last_keys', [inside] * 8 + [...  1.19 us
    pallas_call x1, Pallas kernels, halo_shards(): call(functools.partial(pack_kernel, prior), 'near_keys', [anywhere] * 3,...  1.01 us
    pallas_call x1, Pallas kernels, halo_shards(): call(functools.partial(near_kernel, prior), 'near_terms', [inside] * 7, [...  0.73 us
  transfers between devices with their start and end apart: 4, of which 3 were waited for; matrix products, arithmetic and copies ran while one was open for 0% of the time, Pallas kernels for 25%

profile of v31, /device:TPU:0, one launch (start us, length us, event | category | flops | bytes accessed | tf_op | source)
XLA Modules:
  0.0 25.8 jit_solution(7443920371009664313)
XLA Ops:
  0.6 1.0 %near_keys.1 = (bf16[64,2048]{1,0:T(8,128)(2,1)S(1)}, f32[128,128]{1,0:T(8,128)S(1)}, f32[96,128]{1,0:T(8,128)S(1)}, f32[128,128]{1,0:T(8,128)S(1)}, f32[64,128]{1,0:T(8,128)S(1)}) custom-call(s32[1,128]{1,0:T(1,128)} %bitcast.1, bf16[128,2048]{1,0:T(8,128)(2,1)} %k_hbm.1, bf16[128,2048]{1,0:T(8,128)(2,1)} %v_hbm.1), custom_call_target="tpu_custom_call" | custom-call | bytes 524288 | tf_op jit(solution)/shard_map/near_keys/pallas_call | solution.py:558
  1.7 4.9 %collective-permute-start = (bf16[64,2048]{1,0:T(8,128)(2,1)S(1)}, bf16[64,2048]{1,0:T(8,128)(2,1)S(1)}, u32[]{:S(2)}, u32[]{:S(2)}) collective-permute-start(bf16[64,2048]{1,0:T(8,128)(2,1)S(1)} %get-tuple-element.35), channel_id=1, source_target_pairs={{0,1},{1,2},{2,3},{3,4},{4,5},{5,6},{6,7},{7,8},{8,9},{9,10},{10,1... | collective-permute-start | bytes 786440 | tf_op jit(solution)/shard_map/ppermute | solution.py:507
  6.5 1.7 %operands.1 = (bf16[64,2048]{1,0:T(8,128)(2,1)S(1)}, bf16[128,2048]{1,0:T(8,128)(2,1)S(1)}, bf16[128,2048]{1,0:T(8,128)(2,1)S(1)}, bf16[128,2048]{1,0:T(8,128)(2,1)S(1)}, bf16[128,2048]{1,0:T(8,128)(2,1)S(1)}) custom-call(bf16[128,2048]{1,0:T(8,128)(2,1)} %q_hbm.1, bf16[128,2048]{1,0:T(8,128)(2,1)} %k_hbm.1, bf16[128,2048]{1,0:T(8,128)(2,1)} %v_hbm.1, ...), custom_call_target="tpu_custom_call" | custom-call | bytes 4718592 | tf_op jit(solution)/shard_map/operands/pallas_call | solution.py:566
  8.2 3.4 %collective-permute-start.1 = (bf16[64,2048]{1,0:T(8,128)(2,1)S(1)}, bf16[64,2048]{1,0:T(8,128)(2,1)S(1)}, u32[]{:S(2)}, u32[]{:S(2)}) collective-permute-start(bf16[64,2048]{1,0:T(8,128)(2,1)S(1)} %get-tuple-element.36), channel_id=1, source_target_pairs={{0,1},{1,2},{2,3},{3,4},{4,5},{5,6},{6,7},{7,8},{8,9},{9,10},{10,1... | collective-permute-start | bytes 786440 | tf_op jit(solution)/shard_map/ppermute | solution.py:507
  11.6 1.5 %own_block.1 = (bf16[64,2048]{1,0:T(8,128)(2,1)S(1)}, bf16[64,2048]{1,0:T(8,128)(2,1)S(1)}, f32[128,2048]{1,0:T(8,128)S(1)}, f32[128,2048]{1,0:T(8,128)S(1)}) custom-call(f32[128,128]{1,0:T(8,128)S(1)} %get-tuple-element.37.bias_ref, bf16[128,2048]{1,0:T(8,128)(2,1)S(1)} %get-tuple-element.31.q_ref, bf16[128,2048]{1,0:T(8,128)(2,1)S(1)} %get-tuple-element.32.k_ref, ...), custom_call_target="tpu_custom_call" | custom-call | flops 201326592 | bytes 4718592 | tf_op jit(solution)/shard_map/own_block/pallas_call | solution.py:574
  13.1 0.0 collective-permute-done.near_ref
  13.1 0.7 %near_terms.1 = (bf16[64,1024]{1,0:T(8,128)(2,1)S(1)}, bf16[64,1024]{1,0:T(8,128)(2,1)S(1)}) custom-call(f32[96,128]{1,0:T(8,128)S(1)} %get-tuple-element.47.near_bias_ref, f32[128,128]{1,0:T(8,128)S(1)} %get-tuple-element.30.bias_ref.lead_bias_ref, bf16[128,2048]{1,0:T(8,128)(2,1)S(1)} %get-tuple-element.31.q_ref, ...), custom_call_target="tpu_custom_call" | custom-call | flops 75497472 | bytes 2097152 | tf_op jit(solution)/shard_map/near_terms/pallas_call | solution.py:582
  13.8 1.3 %collective-permute-start.3 = (bf16[64,1024]{1,0:T(8,128)(2,1)S(1)}, bf16[64,1024]{1,0:T(8,128)(2,1)S(1)}, u32[]{:S(2)}, u32[]{:S(2)}) collective-permute-start(bf16[64,1024]{1,0:T(8,128)(2,1)S(1)} %get-tuple-element.49), channel_id=1, source_target_pairs={{1,0},{2,1},{3,2},{4,3},{5,4},{6,5},{7,6},{8,7},{9,8},{10,9},{11,1... | collective-permute-start | bytes 393224 | tf_op jit(solution)/shard_map/ppermute | solution.py:507
  15.1 1.3 %collective-permute-start.2 = (bf16[64,1024]{1,0:T(8,128)(2,1)S(1)}, bf16[64,1024]{1,0:T(8,128)(2,1)S(1)}, u32[]{:S(2)}, u32[]{:S(2)}) collective-permute-start(bf16[64,1024]{1,0:T(8,128)(2,1)S(1)} %get-tuple-element.48), channel_id=1, source_target_pairs={{1,0},{2,1},{3,2},{4,3},{5,4},{6,5},{7,6},{8,7},{9,8},{10,9},{11,1... | collective-permute-start | bytes 393224 | tf_op jit(solution)/shard_map/ppermute | solution.py:507
  16.4 1.2 %collective-permute-done.1.far_ref = bf16[64,2048]{1,0:T(8,128)(2,1)S(1)} collective-permute-done((bf16[64,2048]{1,0:T(8,128)(2,1)S(1)}, bf16[64,2048]{1,0:T(8,128)(2,1)S(1)}, u32[]{:S(2)}, u32[]{:S(2)}) %collective-permute-start.1) | collective-permute-done | bytes 262176 | tf_op jit(solution)/shard_map/ppermute | solution.py:507
  17.7 2.2 %lead_rows.1 = (bf16[128,2048]{1,0:T(8,128)(2,1)}, bf16[128,2048]{1,0:T(8,128)(2,1)}, bf16[128,2048]{1,0:T(8,128)(2,1)}, bf16[128,2048]{1,0:T(8,128)(2,1)}) custom-call(f32[128,128]{1,0:T(8,128)S(1)} %get-tuple-element.30.bias_ref.lead_bias_ref, bf16[128,2048]{1,0:T(8,128)(2,1)S(1)} %get-tuple-element.31.q_ref, ...), custom_call_target="tpu_custom_call" | custom-call | flops 201326592 | bytes 5242880 | tf_op jit(solution)/shard_map/lead_rows/pallas_call | solution.py:589
  19.9 2.6 %collective-permute-done.3.after_ref = bf16[64,1024]{1,0:T(8,128)(2,1)S(1)} collective-permute-done((bf16[64,1024]{1,0:T(8,128)(2,1)S(1)}, bf16[64,1024]{1,0:T(8,128)(2,1)S(1)}, u32[]{:S(2)}, u32[]{:S(2)}) %collective-permute-start.3) | collective-permute-done | bytes 131104 | tf_op jit(solution)/shard_map/ppermute | solution.py:507
  22.4 0.5 %tail_keys.1 = (bf16[64,1024]{1,0:T(8,128)(2,1)S(1)}, bf16[64,1024]{1,0:T(8,128)(2,1)S(1)}) custom-call(f32[64,128]{1,0:T(8,128)S(1)} %get-tuple-element.46.bias_ref, bf16[128,2048]{1,0:T(8,128)(2,1)S(1)} %get-tuple-element.32.k_ref, bf16[128,2048]{1,0:T(8,128)(2,1)S(1)} %get-tuple-element.33.v_ref, f32[128,2048]{1,0:T(8,128)S(1)} %get-tuple-element.38.gk_part_ref, ...), custom_call_target="tpu_custom_call" | custom-call | flops 16777216 | bytes 1048576 | tf_op jit(solution)/shard_map/tail_keys/pallas_call | solution.py:599
  22.9 1.7 %collective-permute-done.2.after_ref = bf16[64,1024]{1,0:T(8,128)(2,1)S(1)} collective-permute-done((bf16[64,1024]{1,0:T(8,128)(2,1)S(1)}, bf16[64,1024]{1,0:T(8,128)(2,1)S(1)}, u32[]{:S(2)}, u32[]{:S(2)}) %collective-permute-start.2) | collective-permute-done | bytes 131104 | tf_op jit(solution)/shard_map/ppermute | solution.py:507
  24.6 1.2 %last_keys.1 = (bf16[128,2048]{1,0:T(8,128)(2,1)}, bf16[128,2048]{1,0:T(8,128)(2,1)}) custom-call(f32[64,128]{1,0:T(8,128)S(1)} %get-tuple-element.46.bias_ref, bf16[128,2048]{1,0:T(8,128)(2,1)S(1)} %get-tuple-element.32.k_ref, bf16[128,2048]{1,0:T(8,128)(2,1)S(1)} %get-tuple-element.33.v_ref, ...), custom_call_target="tpu_custom_call", output_to_operand_aliasing={{0}: (8, {}), {1}: (9, {})} | custom-call | flops 16777216 | bytes 1572864 | tf_op jit(solution)/shard_map/last_keys/pallas_call | solution.py:603
Async XLA Ops:
  1.7 11.4 %collective-permute-start = (bf16[64,2048]{1,0:T(8,128)(2,1)S(1)}, bf16[64,2048]{1,0:T(8,128)(2,1)S(1)}, u32[]{:S(2)}, u32[]{:S(2)}) collective-permute-start(bf16[64,2048]{1,0:T(8,128)(2,1)S(1)} %get-tuple-element.35), channel_id=1, source_target_pairs={{0,1},{1,2},{2,3},{3,4},{4,5},{5,6},{6,7},{7,8},{8,9},{9,10},{10,1... | collective-permute-start | bytes 786440 | tf_op jit(solution)/shard_map/ppermute | solution.py:507
  8.2 9.5 %collective-permute-start.1 = (bf16[64,2048]{1,0:T(8,128)(2,1)S(1)}, bf16[64,2048]{1,0:T(8,128)(2,1)S(1)}, u32[]{:S(2)}, u32[]{:S(2)}) collective-permute-start(bf16[64,2048]{1,0:T(8,128)(2,1)S(1)} %get-tuple-element.36), channel_id=1, source_target_pairs={{0,1},{1,2},{2,3},{3,4},{4,5},{5,6},{6,7},{7,8},{8,9},{9,10},{10,1... | collective-permute-start | bytes 786440 | tf_op jit(solution)/shard_map/ppermute | solution.py:507
  13.8 8.6 %collective-permute-start.3 = (bf16[64,1024]{1,0:T(8,128)(2,1)S(1)}, bf16[64,1024]{1,0:T(8,128)(2,1)S(1)}, u32[]{:S(2)}, u32[]{:S(2)}) collective-permute-start(bf16[64,1024]{1,0:T(8,128)(2,1)S(1)} %get-tuple-element.49), channel_id=1, source_target_pairs={{1,0},{2,1},{3,2},{4,3},{5,4},{6,5},{7,6},{8,7},{9,8},{10,9},{11,1... | collective-permute-start | bytes 393224 | tf_op jit(solution)/shard_map/ppermute | solution.py:507
  15.1 9.5 %collective-permute-start.2 = (bf16[64,1024]{1,0:T(8,128)(2,1)S(1)}, bf16[64,1024]{1,0:T(8,128)(2,1)S(1)}, u32[]{:S(2)}, u32[]{:S(2)}) collective-permute-start(bf16[64,1024]{1,0:T(8,128)(2,1)S(1)} %get-tuple-element.48), channel_id=1, source_target_pairs={{1,0},{2,1},{3,2},{4,3},{5,4},{6,5},{7,6},{8,7},{9,8},{10,9},{11,1... | collective-permute-start | bytes 393224 | tf_op jit(solution)/shard_map/ppermute | solution.py:507

commit v32 on v31

--- a/solution.py
+++ b/solution.py
@@ -572,7 +572,7 @@
     far = neighbour(far, 1)
 
     attn, gq, gk_part, gv_part = call(
-        functools.partial(own_kernel, prior, step), "own_block",
+        functools.partial(own_kernel, prior, width), "own_block",
         [inside] * 5, [inside] * 4,
         [near16(tok - prior, width)] * 2 + [near32(tok, width)] * 2, (),
         (width // HEAD_DIM, tok - prior, tok, 6), 18 * tok * width,

time: 26.1 us -> 26.1 us (level)
  waiting for transfers between devices: 5.52 us -> 5.97 us
  Pallas kernels: 8.77 us -> 8.32 us
    ppermute x4, waiting for transfers between devices: 5.52 us -> 5.97 us  [neighbour(): return lax.ppermute(value, ('seq', 'head'), pairs)]
    pallas_call x1, Pallas kernels: 1.49 us -> 1.04 us  [halo_shards(): call(functools.partial(own_kernel, prior, width), 'own_block', [inside] *...]
  transfers between devices with their start and end apart: 4 -> 4, of which waited for: 3 -> 4; matrix products, arithmetic and copies ran while one was open for 0% -> 0% of each run, Pallas kernels for 25% -> 24%
where the time goes in v32:
time: 26.1 us; the launch traced here: 25.8 us
  starting transfers between devices  10.8 us (41%)
  Pallas kernels  8.32 us (32%)
  waiting for transfers between devices  5.97 us (23%)
  between operations  0.7 us (3%)
    ppermute x4, starting transfers between devices, neighbour(): return lax.ppermute(value, ('seq', 'head'), pairs)  10.8 us
    ppermute x4, waiting for transfers between devices, neighbour(): return lax.ppermute(value, ('seq', 'head'), pairs)  5.97 us
    pallas_call x1, Pallas kernels, halo_shards(): call(functools.partial(lead_kernel, prior, step), 'lead_rows', [inside] *...  2.2 us
    pallas_call x1, Pallas kernels, halo_shards(): call(functools.partial(ready_kernel, prior), 'operands', [anywhere] * 4,...  1.65 us
    pallas_call x1, Pallas kernels, halo_shards(): call(functools.partial(last_kernel, prior), 'last_keys', [inside] * 8 + [...  1.19 us
    pallas_call x1, Pallas kernels, halo_shards(): call(functools.partial(own_kernel, prior, width), 'own_block', [inside] *...  1.04 us
    pallas_call x1, Pallas kernels, halo_shards(): call(functools.partial(pack_kernel, prior), 'near_keys', [anywhere] * 3,...  1.01 us
    pallas_call x1, Pallas kernels, halo_shards(): call(functools.partial(near_kernel, prior), 'near_terms', [inside] * 7, [...  0.73 us
  transfers between devices with their start and end apart: 4, of which 4 were waited for; matrix products, arithmetic and copies ran while one was open for 0% of the time, Pallas kernels for 24%

profile of v32, /device:TPU:0, one launch (start us, length us, event | category | flops | bytes accessed | tf_op | source)
XLA Modules:
  0.0 25.8 jit_solution(8965753372788342425)
XLA Ops:
  0.6 1.0 %near_keys.1 = (bf16[64,2048]{1,0:T(8,128)(2,1)S(1)}, f32[128,128]{1,0:T(8,128)S(1)}, f32[96,128]{1,0:T(8,128)S(1)}, f32[128,128]{1,0:T(8,128)S(1)}, f32[64,128]{1,0:T(8,128)S(1)}) custom-call(s32[1,128]{1,0:T(1,128)} %bitcast.1, bf16[128,2048]{1,0:T(8,128)(2,1)} %k_hbm.1, bf16[128,2048]{1,0:T(8,128)(2,1)} %v_hbm.1), custom_call_target="tpu_custom_call" | custom-call | bytes 524288 | tf_op jit(solution)/shard_map/near_keys/pallas_call | solution.py:558
  1.7 4.9 %collective-permute-start = (bf16[64,2048]{1,0:T(8,128)(2,1)S(1)}, bf16[64,2048]{1,0:T(8,128)(2,1)S(1)}, u32[]{:S(2)}, u32[]{:S(2)}) collective-permute-start(bf16[64,2048]{1,0:T(8,128)(2,1)S(1)} %get-tuple-element.35), channel_id=1, source_target_pairs={{0,1},{1,2},{2,3},{3,4},{4,5},{5,6},{6,7},{7,8},{8,9},{9,10},{10,1... | collective-permute-start | bytes 786440 | tf_op jit(solution)/shard_map/ppermute | solution.py:507
  6.5 1.7 %operands.1 = (bf16[64,2048]{1,0:T(8,128)(2,1)S(1)}, bf16[128,2048]{1,0:T(8,128)(2,1)S(1)}, bf16[128,2048]{1,0:T(8,128)(2,1)S(1)}, bf16[128,2048]{1,0:T(8,128)(2,1)S(1)}, bf16[128,2048]{1,0:T(8,128)(2,1)S(1)}) custom-call(bf16[128,2048]{1,0:T(8,128)(2,1)} %q_hbm.1, bf16[128,2048]{1,0:T(8,128)(2,1)} %k_hbm.1, bf16[128,2048]{1,0:T(8,128)(2,1)} %v_hbm.1, ...), custom_call_target="tpu_custom_call" | custom-call | bytes 4718592 | tf_op jit(solution)/shard_map/operands/pallas_call | solution.py:566
  8.2 3.4 %collective-permute-start.1 = (bf16[64,2048]{1,0:T(8,128)(2,1)S(1)}, bf16[64,2048]{1,0:T(8,128)(2,1)S(1)}, u32[]{:S(2)}, u32[]{:S(2)}) collective-permute-start(bf16[64,2048]{1,0:T(8,128)(2,1)S(1)} %get-tuple-element.36), channel_id=1, source_target_pairs={{0,1},{1,2},{2,3},{3,4},{4,5},{5,6},{6,7},{7,8},{8,9},{9,10},{10,1... | collective-permute-start | bytes 786440 | tf_op jit(solution)/shard_map/ppermute | solution.py:507
  11.6 1.0 %own_block.1 = (bf16[64,2048]{1,0:T(8,128)(2,1)S(1)}, bf16[64,2048]{1,0:T(8,128)(2,1)S(1)}, f32[128,2048]{1,0:T(8,128)S(1)}, f32[128,2048]{1,0:T(8,128)S(1)}) custom-call(f32[128,128]{1,0:T(8,128)S(1)} %get-tuple-element.37.bias_ref, bf16[128,2048]{1,0:T(8,128)(2,1)S(1)} %get-tuple-element.31.q_ref, bf16[128,2048]{1,0:T(8,128)(2,1)S(1)} %get-tuple-element.32.k_ref, ...), custom_call_target="tpu_custom_call" | custom-call | flops 201326592 | bytes 4718592 | tf_op jit(solution)/shard_map/own_block/pallas_call | solution.py:574
  12.6 0.2 collective-permute-done.near_ref
  12.8 0.7 %near_terms.1 = (bf16[64,1024]{1,0:T(8,128)(2,1)S(1)}, bf16[64,1024]{1,0:T(8,128)(2,1)S(1)}) custom-call(f32[96,128]{1,0:T(8,128)S(1)} %get-tuple-element.47.near_bias_ref, f32[128,128]{1,0:T(8,128)S(1)} %get-tuple-element.30.bias_ref.lead_bias_ref, bf16[128,2048]{1,0:T(8,128)(2,1)S(1)} %get-tuple-element.31.q_ref, ...), custom_call_target="tpu_custom_call" | custom-call | flops 75497472 | bytes 2097152 | tf_op jit(solution)/shard_map/near_terms/pallas_call | solution.py:582
  13.5 1.3 %collective-permute-start.3 = (bf16[64,1024]{1,0:T(8,128)(2,1)S(1)}, bf16[64,1024]{1,0:T(8,128)(2,1)S(1)}, u32[]{:S(2)}, u32[]{:S(2)}) collective-permute-start(bf16[64,1024]{1,0:T(8,128)(2,1)S(1)} %get-tuple-element.49), channel_id=1, source_target_pairs={{1,0},{2,1},{3,2},{4,3},{5,4},{6,5},{7,6},{8,7},{9,8},{10,9},{11,1... | collective-permute-start | bytes 393224 | tf_op jit(solution)/shard_map/ppermute | solution.py:507
  14.8 1.3 %collective-permute-start.2 = (bf16[64,1024]{1,0:T(8,128)(2,1)S(1)}, bf16[64,1024]{1,0:T(8,128)(2,1)S(1)}, u32[]{:S(2)}, u32[]{:S(2)}) collective-permute-start(bf16[64,1024]{1,0:T(8,128)(2,1)S(1)} %get-tuple-element.48), channel_id=1, source_target_pairs={{1,0},{2,1},{3,2},{4,3},{5,4},{6,5},{7,6},{8,7},{9,8},{10,9},{11,1... | collective-permute-start | bytes 393224 | tf_op jit(solution)/shard_map/ppermute | solution.py:507
  16.1 1.5 %collective-permute-done.1.far_ref = bf16[64,2048]{1,0:T(8,128)(2,1)S(1)} collective-permute-done((bf16[64,2048]{1,0:T(8,128)(2,1)S(1)}, bf16[64,2048]{1,0:T(8,128)(2,1)S(1)}, u32[]{:S(2)}, u32[]{:S(2)}) %collective-permute-start.1) | collective-permute-done | bytes 262176 | tf_op jit(solution)/shard_map/ppermute | solution.py:507
  17.7 2.2 %lead_rows.1 = (bf16[128,2048]{1,0:T(8,128)(2,1)}, bf16[128,2048]{1,0:T(8,128)(2,1)}, bf16[128,2048]{1,0:T(8,128)(2,1)}, bf16[128,2048]{1,0:T(8,128)(2,1)}) custom-call(f32[128,128]{1,0:T(8,128)S(1)} %get-tuple-element.30.bias_ref.lead_bias_ref, bf16[128,2048]{1,0:T(8,128)(2,1)S(1)} %get-tuple-element.31.q_ref, ...), custom_call_target="tpu_custom_call" | custom-call | flops 201326592 | bytes 5242880 | tf_op jit(solution)/shard_map/lead_rows/pallas_call | solution.py:589
  19.9 2.6 %collective-permute-done.3.after_ref = bf16[64,1024]{1,0:T(8,128)(2,1)S(1)} collective-permute-done((bf16[64,1024]{1,0:T(8,128)(2,1)S(1)}, bf16[64,1024]{1,0:T(8,128)(2,1)S(1)}, u32[]{:S(2)}, u32[]{:S(2)}) %collective-permute-start.3) | collective-permute-done | bytes 131104 | tf_op jit(solution)/shard_map/ppermute | solution.py:507
  22.4 0.5 %tail_keys.1 = (bf16[64,1024]{1,0:T(8,128)(2,1)S(1)}, bf16[64,1024]{1,0:T(8,128)(2,1)S(1)}) custom-call(f32[64,128]{1,0:T(8,128)S(1)} %get-tuple-element.46.bias_ref, bf16[128,2048]{1,0:T(8,128)(2,1)S(1)} %get-tuple-element.32.k_ref, bf16[128,2048]{1,0:T(8,128)(2,1)S(1)} %get-tuple-element.33.v_ref, f32[128,2048]{1,0:T(8,128)S(1)} %get-tuple-element.38.gk_part_ref, ...), custom_call_target="tpu_custom_call" | custom-call | flops 16777216 | bytes 1048576 | tf_op jit(solution)/shard_map/tail_keys/pallas_call | solution.py:599
  22.9 1.7 %collective-permute-done.2.after_ref = bf16[64,1024]{1,0:T(8,128)(2,1)S(1)} collective-permute-done((bf16[64,1024]{1,0:T(8,128)(2,1)S(1)}, bf16[64,1024]{1,0:T(8,128)(2,1)S(1)}, u32[]{:S(2)}, u32[]{:S(2)}) %collective-permute-start.2) | collective-permute-done | bytes 131104 | tf_op jit(solution)/shard_map/ppermute | solution.py:507
  24.6 1.2 %last_keys.1 = (bf16[128,2048]{1,0:T(8,128)(2,1)}, bf16[128,2048]{1,0:T(8,128)(2,1)}) custom-call(f32[64,128]{1,0:T(8,128)S(1)} %get-tuple-element.46.bias_ref, bf16[128,2048]{1,0:T(8,128)(2,1)S(1)} %get-tuple-element.32.k_ref, bf16[128,2048]{1,0:T(8,128)(2,1)S(1)} %get-tuple-element.33.v_ref, ...), custom_call_target="tpu_custom_call", output_to_operand_aliasing={{0}: (8, {}), {1}: (9, {})} | custom-call | flops 16777216 | bytes 1572864 | tf_op jit(solution)/shard_map/last_keys/pallas_call | solution.py:603
Async XLA Ops:
  1.7 11.2 %collective-permute-start = (bf16[64,2048]{1,0:T(8,128)(2,1)S(1)}, bf16[64,2048]{1,0:T(8,128)(2,1)S(1)}, u32[]{:S(2)}, u32[]{:S(2)}) collective-permute-start(bf16[64,2048]{1,0:T(8,128)(2,1)S(1)} %get-tuple-element.35), channel_id=1, source_target_pairs={{0,1},{1,2},{2,3},{3,4},{4,5},{5,6},{6,7},{7,8},{8,9},{9,10},{10,1... | collective-permute-start | bytes 786440 | tf_op jit(solution)/shard_map/ppermute | solution.py:507
  8.2 9.5 %collective-permute-start.1 = (bf16[64,2048]{1,0:T(8,128)(2,1)S(1)}, bf16[64,2048]{1,0:T(8,128)(2,1)S(1)}, u32[]{:S(2)}, u32[]{:S(2)}) collective-permute-start(bf16[64,2048]{1,0:T(8,128)(2,1)S(1)} %get-tuple-element.36), channel_id=1, source_target_pairs={{0,1},{1,2},{2,3},{3,4},{4,5},{5,6},{6,7},{7,8},{8,9},{9,10},{10,1... | collective-permute-start | bytes 786440 | tf_op jit(solution)/shard_map/ppermute | solution.py:507
  13.5 8.9 %collective-permute-start.3 = (bf16[64,1024]{1,0:T(8,128)(2,1)S(1)}, bf16[64,1024]{1,0:T(8,128)(2,1)S(1)}, u32[]{:S(2)}, u32[]{:S(2)}) collective-permute-start(bf16[64,1024]{1,0:T(8,128)(2,1)S(1)} %get-tuple-element.49), channel_id=1, source_target_pairs={{1,0},{2,1},{3,2},{4,3},{5,4},{6,5},{7,6},{8,7},{9,8},{10,9},{11,1... | collective-permute-start | bytes 393224 | tf_op jit(solution)/shard_map/ppermute | solution.py:507
  14.8 9.8 %collective-permute-start.2 = (bf16[64,1024]{1,0:T(8,128)(2,1)S(1)}, bf16[64,1024]{1,0:T(8,128)(2,1)S(1)}, u32[]{:S(2)}, u32[]{:S(2)}) collective-permute-start(bf16[64,1024]{1,0:T(8,128)(2,1)S(1)} %get-tuple-element.48), channel_id=1, source_target_pairs={{1,0},{2,1},{3,2},{4,3},{5,4},{6,5},{7,6},{8,7},{9,8},{10,9},{11,1... | collective-permute-start | bytes 393224 | tf_op jit(solution)/shard_map/ppermute | solution.py:507

commit v33 on v32

--- a/solution.py
+++ b/solution.py
@@ -587,7 +587,7 @@
     backs = [neighbour(back, -1) for back in backs]
 
     attn, gq, gk, gv = call(
-        functools.partial(lead_kernel, prior, step), "lead_rows",
+        functools.partial(lead_kernel, prior, width), "lead_rows",
         [inside] * 11, [anywhere] * 4, [full16] * 4,
         [near16(prior, width)] * 4
         + [pltpu.SemaphoreType.DMA((groups, 4)), pltpu.SemaphoreType.DMA((2,))],

time: 26.1 us -> 26.1 us (level)
  waiting for transfers between devices: 5.97 us -> 6.24 us
  Pallas kernels: 8.32 us -> 8.05 us
    ppermute x4, waiting for transfers between devices: 5.97 us -> 6.24 us  [neighbour(): return lax.ppermute(value, ('seq', 'head'), pairs)]
    pallas_call x1, Pallas kernels: 2.2 us -> 1.93 us  [halo_shards(): call(functools.partial(lead_kernel, prior, width), 'lead_rows', [inside]...]
  transfers between devices with their start and end apart: 4 -> 4, of which waited for: 4 -> 4; matrix products, arithmetic and copies ran while one was open for 0% -> 0% of each run, Pallas kernels for 24% -> 23%
where the time goes in v33:
time: 26.1 us; the launch traced here: 25.8 us
  starting transfers between devices  10.8 us (41%)
  Pallas kernels  8.05 us (31%)
  waiting for transfers between devices  6.24 us (24%)
  between operations  0.7 us (3%)
    ppermute x4, starting transfers between devices, neighbour(): return lax.ppermute(value, ('seq', 'head'), pairs)  10.8 us
    ppermute x4, waiting for transfers between devices, neighbour(): return lax.ppermute(value, ('seq', 'head'), pairs)  6.24 us
    pallas_call x1, Pallas kernels, halo_shards(): call(functools.partial(lead_kernel, prior, width), 'lead_rows', [inside]...  1.93 us
    pallas_call x1, Pallas kernels, halo_shards(): call(functools.partial(ready_kernel, prior), 'operands', [anywhere] * 4,...  1.65 us
    pallas_call x1, Pallas kernels, halo_shards(): call(functools.partial(last_kernel, prior), 'last_keys', [inside] * 8 + [...  1.19 us
    pallas_call x1, Pallas kernels, halo_shards(): call(functools.partial(own_kernel, prior, width), 'own_block', [inside] *...  1.04 us
    pallas_call x1, Pallas kernels, halo_shards(): call(functools.partial(pack_kernel, prior), 'near_keys', [anywhere] * 3,...  1.01 us
    pallas_call x1, Pallas kernels, halo_shards(): call(functools.partial(near_kernel, prior), 'near_terms', [inside] * 7, [...  0.73 us
  transfers between devices with their start and end apart: 4, of which 4 were waited for; matrix products, arithmetic and copies ran while one was open for 0% of the time, Pallas kernels for 23%

profile of v33, /device:TPU:0, one launch (start us, length us, event | category | flops | bytes accessed | tf_op | source)
XLA Modules:
  0.0 25.8 jit_solution(15620510680790560575)
XLA Ops:
  0.6 1.0 %near_keys.1 = (bf16[64,2048]{1,0:T(8,128)(2,1)S(1)}, f32[128,128]{1,0:T(8,128)S(1)}, f32[96,128]{1,0:T(8,128)S(1)}, f32[128,128]{1,0:T(8,128)S(1)}, f32[64,128]{1,0:T(8,128)S(1)}) custom-call(s32[1,128]{1,0:T(1,128)} %bitcast.1, bf16[128,2048]{1,0:T(8,128)(2,1)} %k_hbm.1, bf16[128,2048]{1,0:T(8,128)(2,1)} %v_hbm.1), custom_call_target="tpu_custom_call" | custom-call | bytes 524288 | tf_op jit(solution)/shard_map/near_keys/pallas_call | solution.py:558
  1.7 4.9 %collective-permute-start = (bf16[64,2048]{1,0:T(8,128)(2,1)S(1)}, bf16[64,2048]{1,0:T(8,128)(2,1)S(1)}, u32[]{:S(2)}, u32[]{:S(2)}) collective-permute-start(bf16[64,2048]{1,0:T(8,128)(2,1)S(1)} %get-tuple-element.35), channel_id=1, source_target_pairs={{0,1},{1,2},{2,3},{3,4},{4,5},{5,6},{6,7},{7,8},{8,9},{9,10},{10,1... | collective-permute-start | bytes 786440 | tf_op jit(solution)/shard_map/ppermute | solution.py:507
  6.5 1.7 %operands.1 = (bf16[64,2048]{1,0:T(8,128)(2,1)S(1)}, bf16[128,2048]{1,0:T(8,128)(2,1)S(1)}, bf16[128,2048]{1,0:T(8,128)(2,1)S(1)}, bf16[128,2048]{1,0:T(8,128)(2,1)S(1)}, bf16[128,2048]{1,0:T(8,128)(2,1)S(1)}) custom-call(bf16[128,2048]{1,0:T(8,128)(2,1)} %q_hbm.1, bf16[128,2048]{1,0:T(8,128)(2,1)} %k_hbm.1, bf16[128,2048]{1,0:T(8,128)(2,1)} %v_hbm.1, ...), custom_call_target="tpu_custom_call" | custom-call | bytes 4718592 | tf_op jit(solution)/shard_map/operands/pallas_call | solution.py:566
  8.2 3.4 %collective-permute-start.1 = (bf16[64,2048]{1,0:T(8,128)(2,1)S(1)}, bf16[64,2048]{1,0:T(8,128)(2,1)S(1)}, u32[]{:S(2)}, u32[]{:S(2)}) collective-permute-start(bf16[64,2048]{1,0:T(8,128)(2,1)S(1)} %get-tuple-element.36), channel_id=1, source_target_pairs={{0,1},{1,2},{2,3},{3,4},{4,5},{5,6},{6,7},{7,8},{8,9},{9,10},{10,1... | collective-permute-start | bytes 786440 | tf_op jit(solution)/shard_map/ppermute | solution.py:507
  11.6 1.0 %own_block.1 = (bf16[64,2048]{1,0:T(8,128)(2,1)S(1)}, bf16[64,2048]{1,0:T(8,128)(2,1)S(1)}, f32[128,2048]{1,0:T(8,128)S(1)}, f32[128,2048]{1,0:T(8,128)S(1)}) custom-call(f32[128,128]{1,0:T(8,128)S(1)} %get-tuple-element.37.bias_ref, bf16[128,2048]{1,0:T(8,128)(2,1)S(1)} %get-tuple-element.31.q_ref, bf16[128,2048]{1,0:T(8,128)(2,1)S(1)} %get-tuple-element.32.k_ref, ...), custom_call_target="tpu_custom_call" | custom-call | flops 201326592 | bytes 4718592 | tf_op jit(solution)/shard_map/own_block/pallas_call | solution.py:574
  12.6 0.2 collective-permute-done.near_ref
  12.8 0.7 %near_terms.1 = (bf16[64,1024]{1,0:T(8,128)(2,1)S(1)}, bf16[64,1024]{1,0:T(8,128)(2,1)S(1)}) custom-call(f32[96,128]{1,0:T(8,128)S(1)} %get-tuple-element.47.near_bias_ref, f32[128,128]{1,0:T(8,128)S(1)} %get-tuple-element.30.bias_ref.lead_bias_ref, bf16[128,2048]{1,0:T(8,128)(2,1)S(1)} %get-tuple-element.31.q_ref, ...), custom_call_target="tpu_custom_call" | custom-call | flops 75497472 | bytes 2097152 | tf_op jit(solution)/shard_map/near_terms/pallas_call | solution.py:582
  13.5 1.3 %collective-permute-start.3 = (bf16[64,1024]{1,0:T(8,128)(2,1)S(1)}, bf16[64,1024]{1,0:T(8,128)(2,1)S(1)}, u32[]{:S(2)}, u32[]{:S(2)}) collective-permute-start(bf16[64,1024]{1,0:T(8,128)(2,1)S(1)} %get-tuple-element.49), channel_id=1, source_target_pairs={{1,0},{2,1},{3,2},{4,3},{5,4},{6,5},{7,6},{8,7},{9,8},{10,9},{11,1... | collective-permute-start | bytes 393224 | tf_op jit(solution)/shard_map/ppermute | solution.py:507
  14.8 1.3 %collective-permute-start.2 = (bf16[64,1024]{1,0:T(8,128)(2,1)S(1)}, bf16[64,1024]{1,0:T(8,128)(2,1)S(1)}, u32[]{:S(2)}, u32[]{:S(2)}) collective-permute-start(bf16[64,1024]{1,0:T(8,128)(2,1)S(1)} %get-tuple-element.48), channel_id=1, source_target_pairs={{1,0},{2,1},{3,2},{4,3},{5,4},{6,5},{7,6},{8,7},{9,8},{10,9},{11,1... | collective-permute-start | bytes 393224 | tf_op jit(solution)/shard_map/ppermute | solution.py:507
  16.1 1.5 %collective-permute-done.1.far_ref = bf16[64,2048]{1,0:T(8,128)(2,1)S(1)} collective-permute-done((bf16[64,2048]{1,0:T(8,128)(2,1)S(1)}, bf16[64,2048]{1,0:T(8,128)(2,1)S(1)}, u32[]{:S(2)}, u32[]{:S(2)}) %collective-permute-start.1) | collective-permute-done | bytes 262176 | tf_op jit(solution)/shard_map/ppermute | solution.py:507
  17.7 1.9 %lead_rows.1 = (bf16[128,2048]{1,0:T(8,128)(2,1)}, bf16[128,2048]{1,0:T(8,128)(2,1)}, bf16[128,2048]{1,0:T(8,128)(2,1)}, bf16[128,2048]{1,0:T(8,128)(2,1)}) custom-call(f32[128,128]{1,0:T(8,128)S(1)} %get-tuple-element.30.bias_ref.lead_bias_ref, bf16[128,2048]{1,0:T(8,128)(2,1)S(1)} %get-tuple-element.31.q_ref, ...), custom_call_target="tpu_custom_call" | custom-call | flops 201326592 | bytes 5242880 | tf_op jit(solution)/shard_map/lead_rows/pallas_call | solution.py:589
  19.6 2.8 %collective-permute-done.3.after_ref = bf16[64,1024]{1,0:T(8,128)(2,1)S(1)} collective-permute-done((bf16[64,1024]{1,0:T(8,128)(2,1)S(1)}, bf16[64,1024]{1,0:T(8,128)(2,1)S(1)}, u32[]{:S(2)}, u32[]{:S(2)}) %collective-permute-start.3) | collective-permute-done | bytes 131104 | tf_op jit(solution)/shard_map/ppermute | solution.py:507
  22.4 0.5 %tail_keys.1 = (bf16[64,1024]{1,0:T(8,128)(2,1)S(1)}, bf16[64,1024]{1,0:T(8,128)(2,1)S(1)}) custom-call(f32[64,128]{1,0:T(8,128)S(1)} %get-tuple-element.46.bias_ref, bf16[128,2048]{1,0:T(8,128)(2,1)S(1)} %get-tuple-element.32.k_ref, bf16[128,2048]{1,0:T(8,128)(2,1)S(1)} %get-tuple-element.33.v_ref, f32[128,2048]{1,0:T(8,128)S(1)} %get-tuple-element.38.gk_part_ref, ...), custom_call_target="tpu_custom_call" | custom-call | flops 16777216 | bytes 1048576 | tf_op jit(solution)/shard_map/tail_keys/pallas_call | solution.py:599
  22.9 1.7 %collective-permute-done.2.after_ref = bf16[64,1024]{1,0:T(8,128)(2,1)S(1)} collective-permute-done((bf16[64,1024]{1,0:T(8,128)(2,1)S(1)}, bf16[64,1024]{1,0:T(8,128)(2,1)S(1)}, u32[]{:S(2)}, u32[]{:S(2)}) %collective-permute-start.2) | collective-permute-done | bytes 131104 | tf_op jit(solution)/shard_map/ppermute | solution.py:507
  24.6 1.2 %last_keys.1 = (bf16[128,2048]{1,0:T(8,128)(2,1)}, bf16[128,2048]{1,0:T(8,128)(2,1)}) custom-call(f32[64,128]{1,0:T(8,128)S(1)} %get-tuple-element.46.bias_ref, bf16[128,2048]{1,0:T(8,128)(2,1)S(1)} %get-tuple-element.32.k_ref, bf16[128,2048]{1,0:T(8,128)(2,1)S(1)} %get-tuple-element.33.v_ref, ...), custom_call_target="tpu_custom_call", output_to_operand_aliasing={{0}: (8, {}), {1}: (9, {})} | custom-call | flops 16777216 | bytes 1572864 | tf_op jit(solution)/shard_map/last_keys/pallas_call | solution.py:603
Async XLA Ops:
  1.7 11.2 %collective-permute-start = (bf16[64,2048]{1,0:T(8,128)(2,1)S(1)}, bf16[64,2048]{1,0:T(8,128)(2,1)S(1)}, u32[]{:S(2)}, u32[]{:S(2)}) collective-permute-start(bf16[64,2048]{1,0:T(8,128)(2,1)S(1)} %get-tuple-element.35), channel_id=1, source_target_pairs={{0,1},{1,2},{2,3},{3,4},{4,5},{5,6},{6,7},{7,8},{8,9},{9,10},{10,1... | collective-permute-start | bytes 786440 | tf_op jit(solution)/shard_map/ppermute | solution.py:507
  8.2 9.5 %collective-permute-start.1 = (bf16[64,2048]{1,0:T(8,128)(2,1)S(1)}, bf16[64,2048]{1,0:T(8,128)(2,1)S(1)}, u32[]{:S(2)}, u32[]{:S(2)}) collective-permute-start(bf16[64,2048]{1,0:T(8,128)(2,1)S(1)} %get-tuple-element.36), channel_id=1, source_target_pairs={{0,1},{1,2},{2,3},{3,4},{4,5},{5,6},{6,7},{7,8},{8,9},{9,10},{10,1... | collective-permute-start | bytes 786440 | tf_op jit(solution)/shard_map/ppermute | solution.py:507
  13.5 8.9 %collective-permute-start.3 = (bf16[64,1024]{1,0:T(8,128)(2,1)S(1)}, bf16[64,1024]{1,0:T(8,128)(2,1)S(1)}, u32[]{:S(2)}, u32[]{:S(2)}) collective-permute-start(bf16[64,1024]{1,0:T(8,128)(2,1)S(1)} %get-tuple-element.49), channel_id=1, source_target_pairs={{1,0},{2,1},{3,2},{4,3},{5,4},{6,5},{7,6},{8,7},{9,8},{10,9},{11,1... | collective-permute-start | bytes 393224 | tf_op jit(solution)/shard_map/ppermute | solution.py:507
  14.8 9.8 %collective-permute-start.2 = (bf16[64,1024]{1,0:T(8,128)(2,1)S(1)}, bf16[64,1024]{1,0:T(8,128)(2,1)S(1)}, u32[]{:S(2)}, u32[]{:S(2)}) collective-permute-start(bf16[64,1024]{1,0:T(8,128)(2,1)S(1)} %get-tuple-element.48), channel_id=1, source_target_pairs={{1,0},{2,1},{3,2},{4,3},{5,4},{6,5},{7,6},{8,7},{9,8},{10,9},{11,1... | collective-permute-start | bytes 393224 | tf_op jit(solution)/shard_map/ppermute | solution.py:507

commit v34 on v33

--- a/solution.py
+++ b/solution.py
@@ -488,15 +488,15 @@
         copies.append(pltpu.make_async_copy(ref, hbm.at[rows, cols], sems.at[len(copies)]))
         copies[-1].start()
 
-    send(gv_first_ref, gv_hbm, 0)
-    send(gk_first_ref, gk_hbm, 0)
     fill_gv, fill_gk = tail_half(
         prior, low, bias_ref, k_ref, v_ref, gk_part_ref, gv_part_ref, after_ref
     )
     fill_gv(gv_ref)
     send(gv_ref, gv_hbm, low)
+    send(gv_first_ref, gv_hbm, 0)
     fill_gk(gk_ref)
     send(gk_ref, gk_hbm, low)
+    send(gk_first_ref, gk_hbm, 0)
     for copy in copies:
         copy.wait()
 

time: 26.1 us -> 26.2 us (level)
  no operation moved by 1% of the time
where the time goes in v34:
time: 26.2 us; the launch traced here: 25.9 us
  starting transfers between devices  10.8 us (41%)
  Pallas kernels  8.14 us (31%)
  waiting for transfers between devices  6.24 us (24%)
  between operations  0.7 us (3%)
    ppermute x4, starting transfers between devices, neighbour(): return lax.ppermute(value, ('seq', 'head'), pairs)  10.8 us
    ppermute x4, waiting for transfers between devices, neighbour(): return lax.ppermute(value, ('seq', 'head'), pairs)  6.24 us
    pallas_call x1, Pallas kernels, halo_shards(): call(functools.partial(lead_kernel, prior, width), 'lead_rows', [inside]...  1.93 us
    pallas_call x1, Pallas kernels, halo_shards(): call(functools.partial(ready_kernel, prior), 'operands', [anywhere] * 4,...  1.65 us
    pallas_call x1, Pallas kernels, halo_shards(): call(functools.partial(last_kernel, prior), 'last_keys', [inside] * 8 + [...  1.28 us
    pallas_call x1, Pallas kernels, halo_shards(): call(functools.partial(own_kernel, prior, width), 'own_block', [inside] *...  1.04 us
    pallas_call x1, Pallas kernels, halo_shards(): call(functools.partial(pack_kernel, prior), 'near_keys', [anywhere] * 3,...  1.01 us
    pallas_call x1, Pallas kernels, halo_shards(): call(functools.partial(near_kernel, prior), 'near_terms', [inside] * 7, [...  0.73 us
  transfers between devices with their start and end apart: 4, of which 4 were waited for; matrix products, arithmetic and copies ran while one was open for 0% of the time, Pallas kernels for 23%

profile of v34, /device:TPU:0, one launch (start us, length us, event | category | flops | bytes accessed | tf_op | source)
XLA Modules:
  0.0 25.9 jit_solution(4065105559348213834)
XLA Ops:
  0.6 1.0 %near_keys.1 = (bf16[64,2048]{1,0:T(8,128)(2,1)S(1)}, f32[128,128]{1,0:T(8,128)S(1)}, f32[96,128]{1,0:T(8,128)S(1)}, f32[128,128]{1,0:T(8,128)S(1)}, f32[64,128]{1,0:T(8,128)S(1)}) custom-call(s32[1,128]{1,0:T(1,128)} %bitcast.1, bf16[128,2048]{1,0:T(8,128)(2,1)} %k_hbm.1, bf16[128,2048]{1,0:T(8,128)(2,1)} %v_hbm.1), custom_call_target="tpu_custom_call" | custom-call | bytes 524288 | tf_op jit(solution)/shard_map/near_keys/pallas_call | solution.py:558
  1.7 4.9 %collective-permute-start = (bf16[64,2048]{1,0:T(8,128)(2,1)S(1)}, bf16[64,2048]{1,0:T(8,128)(2,1)S(1)}, u32[]{:S(2)}, u32[]{:S(2)}) collective-permute-start(bf16[64,2048]{1,0:T(8,128)(2,1)S(1)} %get-tuple-element.35), channel_id=1, source_target_pairs={{0,1},{1,2},{2,3},{3,4},{4,5},{5,6},{6,7},{7,8},{8,9},{9,10},{10,1... | collective-permute-start | bytes 786440 | tf_op jit(solution)/shard_map/ppermute | solution.py:507
  6.5 1.7 %operands.1 = (bf16[64,2048]{1,0:T(8,128)(2,1)S(1)}, bf16[128,2048]{1,0:T(8,128)(2,1)S(1)}, bf16[128,2048]{1,0:T(8,128)(2,1)S(1)}, bf16[128,2048]{1,0:T(8,128)(2,1)S(1)}, bf16[128,2048]{1,0:T(8,128)(2,1)S(1)}) custom-call(bf16[128,2048]{1,0:T(8,128)(2,1)} %q_hbm.1, bf16[128,2048]{1,0:T(8,128)(2,1)} %k_hbm.1, bf16[128,2048]{1,0:T(8,128)(2,1)} %v_hbm.1, ...), custom_call_target="tpu_custom_call" | custom-call | bytes 4718592 | tf_op jit(solution)/shard_map/operands/pallas_call | solution.py:566
  8.2 3.4 %collective-permute-start.1 = (bf16[64,2048]{1,0:T(8,128)(2,1)S(1)}, bf16[64,2048]{1,0:T(8,128)(2,1)S(1)}, u32[]{:S(2)}, u32[]{:S(2)}) collective-permute-start(bf16[64,2048]{1,0:T(8,128)(2,1)S(1)} %get-tuple-element.36), channel_id=1, source_target_pairs={{0,1},{1,2},{2,3},{3,4},{4,5},{5,6},{6,7},{7,8},{8,9},{9,10},{10,1... | collective-permute-start | bytes 786440 | tf_op jit(solution)/shard_map/ppermute | solution.py:507
  11.6 1.0 %own_block.1 = (bf16[64,2048]{1,0:T(8,128)(2,1)S(1)}, bf16[64,2048]{1,0:T(8,128)(2,1)S(1)}, f32[128,2048]{1,0:T(8,128)S(1)}, f32[128,2048]{1,0:T(8,128)S(1)}) custom-call(f32[128,128]{1,0:T(8,128)S(1)} %get-tuple-element.37.bias_ref, bf16[128,2048]{1,0:T(8,128)(2,1)S(1)} %get-tuple-element.31.q_ref, bf16[128,2048]{1,0:T(8,128)(2,1)S(1)} %get-tuple-element.32.k_ref, ...), custom_call_target="tpu_custom_call" | custom-call | flops 201326592 | bytes 4718592 | tf_op jit(solution)/shard_map/own_block/pallas_call | solution.py:574
  12.6 0.2 collective-permute-done.near_ref
  12.8 0.7 %near_terms.1 = (bf16[64,1024]{1,0:T(8,128)(2,1)S(1)}, bf16[64,1024]{1,0:T(8,128)(2,1)S(1)}) custom-call(f32[96,128]{1,0:T(8,128)S(1)} %get-tuple-element.47.near_bias_ref, f32[128,128]{1,0:T(8,128)S(1)} %get-tuple-element.30.bias_ref.lead_bias_ref, bf16[128,2048]{1,0:T(8,128)(2,1)S(1)} %get-tuple-element.31.q_ref, ...), custom_call_target="tpu_custom_call" | custom-call | flops 75497472 | bytes 2097152 | tf_op jit(solution)/shard_map/near_terms/pallas_call | solution.py:582
  13.5 1.3 %collective-permute-start.3 = (bf16[64,1024]{1,0:T(8,128)(2,1)S(1)}, bf16[64,1024]{1,0:T(8,128)(2,1)S(1)}, u32[]{:S(2)}, u32[]{:S(2)}) collective-permute-start(bf16[64,1024]{1,0:T(8,128)(2,1)S(1)} %get-tuple-element.49), channel_id=1, source_target_pairs={{1,0},{2,1},{3,2},{4,3},{5,4},{6,5},{7,6},{8,7},{9,8},{10,9},{11,1... | collective-permute-start | bytes 393224 | tf_op jit(solution)/shard_map/ppermute | solution.py:507
  14.8 1.3 %collective-permute-start.2 = (bf16[64,1024]{1,0:T(8,128)(2,1)S(1)}, bf16[64,1024]{1,0:T(8,128)(2,1)S(1)}, u32[]{:S(2)}, u32[]{:S(2)}) collective-permute-start(bf16[64,1024]{1,0:T(8,128)(2,1)S(1)} %get-tuple-element.48), channel_id=1, source_target_pairs={{1,0},{2,1},{3,2},{4,3},{5,4},{6,5},{7,6},{8,7},{9,8},{10,9},{11,1... | collective-permute-start | bytes 393224 | tf_op jit(solution)/shard_map/ppermute | solution.py:507
  16.1 1.5 %collective-permute-done.1.far_ref = bf16[64,2048]{1,0:T(8,128)(2,1)S(1)} collective-permute-done((bf16[64,2048]{1,0:T(8,128)(2,1)S(1)}, bf16[64,2048]{1,0:T(8,128)(2,1)S(1)}, u32[]{:S(2)}, u32[]{:S(2)}) %collective-permute-start.1) | collective-permute-done | bytes 262176 | tf_op jit(solution)/shard_map/ppermute | solution.py:507
  17.7 1.9 %lead_rows.1 = (bf16[128,2048]{1,0:T(8,128)(2,1)}, bf16[128,2048]{1,0:T(8,128)(2,1)}, bf16[128,2048]{1,0:T(8,128)(2,1)}, bf16[128,2048]{1,0:T(8,128)(2,1)}) custom-call(f32[128,128]{1,0:T(8,128)S(1)} %get-tuple-element.30.bias_ref.lead_bias_ref, bf16[128,2048]{1,0:T(8,128)(2,1)S(1)} %get-tuple-element.31.q_ref, ...), custom_call_target="tpu_custom_call" | custom-call | flops 201326592 | bytes 5242880 | tf_op jit(solution)/shard_map/lead_rows/pallas_call | solution.py:589
  19.6 2.8 %collective-permute-done.3.after_ref = bf16[64,1024]{1,0:T(8,128)(2,1)S(1)} collective-permute-done((bf16[64,1024]{1,0:T(8,128)(2,1)S(1)}, bf16[64,1024]{1,0:T(8,128)(2,1)S(1)}, u32[]{:S(2)}, u32[]{:S(2)}) %collective-permute-start.3) | collective-permute-done | bytes 131104 | tf_op jit(solution)/shard_map/ppermute | solution.py:507
  22.4 0.5 %tail_keys.1 = (bf16[64,1024]{1,0:T(8,128)(2,1)S(1)}, bf16[64,1024]{1,0:T(8,128)(2,1)S(1)}) custom-call(f32[64,128]{1,0:T(8,128)S(1)} %get-tuple-element.46.bias_ref, bf16[128,2048]{1,0:T(8,128)(2,1)S(1)} %get-tuple-element.32.k_ref, bf16[128,2048]{1,0:T(8,128)(2,1)S(1)} %get-tuple-element.33.v_ref, f32[128,2048]{1,0:T(8,128)S(1)} %get-tuple-element.38.gk_part_ref, ...), custom_call_target="tpu_custom_call" | custom-call | flops 16777216 | bytes 1048576 | tf_op jit(solution)/shard_map/tail_keys/pallas_call | solution.py:599
  22.9 1.7 %collective-permute-done.2.after_ref = bf16[64,1024]{1,0:T(8,128)(2,1)S(1)} collective-permute-done((bf16[64,1024]{1,0:T(8,128)(2,1)S(1)}, bf16[64,1024]{1,0:T(8,128)(2,1)S(1)}, u32[]{:S(2)}, u32[]{:S(2)}) %collective-permute-start.2) | collective-permute-done | bytes 131104 | tf_op jit(solution)/shard_map/ppermute | solution.py:507
  24.6 1.3 %last_keys.1 = (bf16[128,2048]{1,0:T(8,128)(2,1)}, bf16[128,2048]{1,0:T(8,128)(2,1)}) custom-call(f32[64,128]{1,0:T(8,128)S(1)} %get-tuple-element.46.bias_ref, bf16[128,2048]{1,0:T(8,128)(2,1)S(1)} %get-tuple-element.32.k_ref, bf16[128,2048]{1,0:T(8,128)(2,1)S(1)} %get-tuple-element.33.v_ref, ...), custom_call_target="tpu_custom_call", output_to_operand_aliasing={{0}: (8, {}), {1}: (9, {})} | custom-call | flops 16777216 | bytes 1572864 | tf_op jit(solution)/shard_map/last_keys/pallas_call | solution.py:603
Async XLA Ops:
  1.7 11.2 %collective-permute-start = (bf16[64,2048]{1,0:T(8,128)(2,1)S(1)}, bf16[64,2048]{1,0:T(8,128)(2,1)S(1)}, u32[]{:S(2)}, u32[]{:S(2)}) collective-permute-start(bf16[64,2048]{1,0:T(8,128)(2,1)S(1)} %get-tuple-element.35), channel_id=1, source_target_pairs={{0,1},{1,2},{2,3},{3,4},{4,5},{5,6},{6,7},{7,8},{8,9},{9,10},{10,1... | collective-permute-start | bytes 786440 | tf_op jit(solution)/shard_map/ppermute | solution.py:507
  8.2 9.5 %collective-permute-start.1 = (bf16[64,2048]{1,0:T(8,128)(2,1)S(1)}, bf16[64,2048]{1,0:T(8,128)(2,1)S(1)}, u32[]{:S(2)}, u32[]{:S(2)}) collective-permute-start(bf16[64,2048]{1,0:T(8,128)(2,1)S(1)} %get-tuple-element.36), channel_id=1, source_target_pairs={{0,1},{1,2},{2,3},{3,4},{4,5},{5,6},{6,7},{7,8},{8,9},{9,10},{10,1... | collective-permute-start | bytes 786440 | tf_op jit(solution)/shard_map/ppermute | solution.py:507
  13.5 8.9 %collective-permute-start.3 = (bf16[64,1024]{1,0:T(8,128)(2,1)S(1)}, bf16[64,1024]{1,0:T(8,128)(2,1)S(1)}, u32[]{:S(2)}, u32[]{:S(2)}) collective-permute-start(bf16[64,1024]{1,0:T(8,128)(2,1)S(1)} %get-tuple-element.49), channel_id=1, source_target_pairs={{1,0},{2,1},{3,2},{4,3},{5,4},{6,5},{7,6},{8,7},{9,8},{10,9},{11,1... | collective-permute-start | bytes 393224 | tf_op jit(solution)/shard_map/ppermute | solution.py:507
  14.8 9.8 %collective-permute-start.2 = (bf16[64,1024]{1,0:T(8,128)(2,1)S(1)}, bf16[64,1024]{1,0:T(8,128)(2,1)S(1)}, u32[]{:S(2)}, u32[]{:S(2)}) collective-permute-start(bf16[64,1024]{1,0:T(8,128)(2,1)S(1)} %get-tuple-element.48), channel_id=1, source_target_pairs={{1,0},{2,1},{3,2},{4,3},{5,4},{6,5},{7,6},{8,7},{9,8},{10,9},{11,1... | collective-permute-start | bytes 393224 | tf_op jit(solution)/shard_map/ppermute | solution.py:507
